TPU v7x, 32 devices: a whole 2x2x4 slice. The times are simulated.
32 devices in a mesh: dp: 8 (over y, x, core), mp: 4 (over z).
Axes of the slice: x: 2, y: 2, z: 4, core: 2. Of those that a mesh axis runs over, the one named last changes fastest.
Arguments:
- answers: bfloat16 [32, 32, 1024], P('dp'), may hold values from -6 to 6
- targets: int32 [32, 32], P('dp'), may hold values from 0 to 25599
- doc_scores: float32 [32, 8], P('dp'), may hold values from -6 to 6
- memory: bfloat16 [256, 400, 1024], P('dp', 'mp'), may hold values from -6 to 6
- lengths: int32 [256], P('dp'), may hold values from 1 to 400, as said below
- self_query: bfloat16 [1024, 1024], P('dp', 'mp'), may hold values from -0.1875 to 0.1875
- self_key: bfloat16 [1024, 1024], P('dp', 'mp'), may hold values from -0.1875 to 0.1875
- self_value: bfloat16 [1024, 1024], P('dp', 'mp'), may hold values from -0.1875 to 0.1875
- query_bias: bfloat16 [16, 64], P('mp', 'dp'), may hold values from -2 to 2
- value_bias: bfloat16 [16, 64], P('mp', 'dp'), may hold values from -2 to 2
- self_output: bfloat16 [1024, 1024], P('mp', 'dp'), may hold values from -0.375 to 0.375
- output_bias: bfloat16 [1024], P('dp'), may hold values from -2 to 2
- first_gain: bfloat16 [1024], P('dp'), may hold values from 0.5 to 1.5
- first_shift: bfloat16 [1024], P('dp'), may hold values from -2 to 2
- cross_query: bfloat16 [1024, 1024], P('dp', 'mp'), may hold values from -0.1875 to 0.1875
- crossq_bias: bfloat16 [16, 64], P('mp', 'dp'), may hold values from -2 to 2
- cross_key: bfloat16 [1024, 1024], P(('dp', 'mp')), may hold values from -0.1875 to 0.1875
- cross_value: bfloat16 [1024, 1024], P(('dp', 'mp')), may hold values from -0.1875 to 0.1875
- crossv_bias: bfloat16 [1024], P(('dp', 'mp')), may hold values from -2 to 2
- cross_output: bfloat16 [1024, 1024], P('mp', 'dp'), may hold values from -0.5 to 0.5
- crosso_bias: bfloat16 [1024], P('dp'), may hold values from -2 to 2
- second_gain: bfloat16 [1024], P('dp'), may hold values from 0.5 to 1.5
- second_shift: bfloat16 [1024], P('dp'), may hold values from -2 to 2
- expand_weight: bfloat16 [1024, 4096], P('dp', 'mp'), may hold values from -0.1875 to 0.1875
- expand_bias: bfloat16 [32, 128], P('mp', 'dp'), may hold values from -2 to 2
- shrink_weight: bfloat16 [4096, 1024], P('mp', 'dp'), may hold values from -0.09375 to 0.09375
- shrink_bias: bfloat16 [1024], P('dp'), may hold values from -2 to 2
- third_gain: bfloat16 [1024], P('dp'), may hold values from 0.5 to 1.5
- third_shift: bfloat16 [1024], P('dp'), may hold values from -2 to 2
- word_table: bfloat16 [25600, 1024], P('mp', 'dp'), may hold values from -0.375 to 0.375
Outputs:
- question_loss: float32 [32], P('dp')
- answer_grad: float32 [32, 32, 1024], P('dp')
- memory_grad: float32 [256, 400, 1024], P('dp', 'mp')
- self_query_grad: float32 [1024, 1024], P('dp', 'mp')
- self_key_grad: float32 [1024, 1024], P('dp', 'mp')
- self_value_grad: float32 [1024, 1024], P('dp', 'mp')
- query_bias_grad: float32 [16, 64], P('mp', 'dp')
- value_bias_grad: float32 [16, 64], P('mp', 'dp')
- self_output_grad: float32 [1024, 1024], P('mp', 'dp')
- output_bias_grad: float32 [1024], P('dp')
- first_gain_grad: float32 [1024], P('dp')
- first_shift_grad: float32 [1024], P('dp')
- cross_query_grad: float32 [1024, 1024], P('dp', 'mp')
- crossq_bias_grad: float32 [16, 64], P('mp', 'dp')
- cross_key_grad: float32 [1024, 1024], P(('dp', 'mp'))
- cross_value_grad: float32 [1024, 1024], P(('dp', 'mp'))
- crossv_bias_grad: float32 [1024], P(('dp', 'mp'))
- cross_output_grad: float32 [1024, 1024], P('mp', 'dp')
- crosso_bias_grad: float32 [1024], P('dp')
- second_gain_grad: float32 [1024], P('dp')
- second_shift_grad: float32 [1024], P('dp')
- expand_weight_grad: float32 [1024, 4096], P('dp', 'mp')
- expand_bias_grad: float32 [32, 128], P('mp', 'dp')
- shrink_weight_grad: float32 [4096, 1024], P('mp', 'dp')
- shrink_bias_grad: float32 [1024], P('dp')
- third_gain_grad: float32 [1024], P('dp')
- third_shift_grad: float32 [1024], P('dp')
Inputs may be any that keep to these rules, and one draw needn't show every extreme that they name: `lengths`: slot j of a row's memory is used when j < its length; some row has all 400 slots used.
All inputs are finite; a program needn't handle non-finite values.
Results may differ from a plain program's by a relative error of at most 0.02.
Values may be sent and summed in bfloat16 or wider, within the bound.
A program may use at most 320 MiB of HBM per device.

v0:
```python
import jax
import jax.numpy as jnp
from jax import lax
from jax.sharding import PartitionSpec as P

D = 1024
H = 16
HD = 64
TOK = 32
K = 8


EPS = 1e-05
NEG = -1e30
SCALE = 0.125


def combined_all(part, axis, combine):
    gathered = jax.tree.map(lambda a: lax.all_gather(a, axis), part)

    def take(source):
        return jax.tree.map(lambda a: lax.dynamic_index_in_dim(a, source, 0, False), gathered)

    return lax.fori_loop(
        1, lax.axis_size(axis), lambda source, state: combine(state, take(source)), take(0)
    )


def product(former, latter):
    return jnp.dot(former, latter, preferred_element_type=jnp.float32)


def product_back(former, latter):
    return lax.dot_general(
        former, latter, (((1,), (1,)), ((), ())), preferred_element_type=jnp.float32
    )


def weight_grad(former, latter):
    return lax.dot_general(
        former, latter, (((0,), (0,)), ((), ())), preferred_element_type=jnp.float32
    )


def column_sum(entries):
    return jnp.sum(entries, axis=0, dtype=jnp.float32)


def gelu_exact(entries):
    return jax.nn.gelu(entries, approximate=False)


def layer_norm(entries, norm_gain, norm_shift):
    center = entries - jnp.mean(entries, axis=-1, keepdims=True)
    inverse = lax.rsqrt(jnp.mean(center * center, axis=-1, keepdims=True) + EPS)
    normed = center * inverse
    return (normed * norm_gain + norm_shift, normed, inverse)


def norm_back(upstream, normed, inverse, norm_gain):
    scaled = upstream * norm_gain
    dentries = inverse * (
        scaled
        - jnp.mean(scaled, axis=-1, keepdims=True)
        - normed * jnp.mean(scaled * normed, axis=-1, keepdims=True)
    )
    return (dentries, jnp.sum(upstream * normed, axis=0), jnp.sum(upstream, axis=0))


def scores_of(queries, key_heads, allowed):
    scores = jnp.einsum("rqhe,rkhe->rhqk", queries, key_heads, preferred_element_type=jnp.float32)
    return jnp.where(allowed, scores, NEG)


def attend(queries, key_heads, value_heads, allowed):
    scores = scores_of(queries, key_heads, allowed)
    score_peak = jnp.max(scores, axis=-1, keepdims=True)
    exponent = jnp.exp(scores - score_peak)
    score_total = jnp.sum(exponent, axis=-1, keepdims=True)
    attn_probs = (exponent / score_total).astype(jnp.bfloat16)
    context = jnp.einsum(
        "rhqk,rkhe->rqhe", attn_probs, value_heads, preferred_element_type=jnp.float32
    )
    return (context.astype(jnp.bfloat16), score_peak, score_total)


def attend_back(queries, key_heads, value_heads, allowed, score_peak, score_total, dcontext):
    scores = scores_of(queries, key_heads, allowed)
    attn_probs = jnp.exp(scores - score_peak) / score_total
    dvalue_heads = jnp.einsum(
        "rhqk,rqhe->rkhe",
        attn_probs.astype(jnp.bfloat16),
        dcontext,
        preferred_element_type=jnp.float32,
    )
    dprobs = jnp.einsum(
        "rqhe,rkhe->rhqk", dcontext, value_heads, preferred_element_type=jnp.float32
    )
    middle = jnp.sum(attn_probs * dprobs, axis=-1, keepdims=True)
    dscores = (attn_probs * (dprobs - middle)).astype(jnp.bfloat16)
    dqueries = jnp.einsum("rhqk,rkhe->rqhe", dscores, key_heads, preferred_element_type=jnp.float32)
    dkey_heads = jnp.einsum("rhqk,rqhe->rkhe", dscores, queries, preferred_element_type=jnp.float32)
    return (dqueries, dkey_heads, dvalue_heads)


def head_sum(partial_term):
    return lax.psum(partial_term, "mp")


def combine_stats(former, latter):
    top_value = jnp.maximum(former[0], latter[0])
    merged = former[1] * jnp.exp(former[0] - top_value) + latter[1] * jnp.exp(latter[0] - top_value)
    return (top_value, merged)


def softmax_stats(local_peak, local_total):
    return combined_all((local_peak, local_total), "mp", combine_stats)


def local(
    answers,
    targets,
    doc_scores,
    memory,
    lengths,
    self_query,
    self_key,
    self_value,
    query_bias,
    value_bias,
    self_output,
    output_bias,
    first_gain,
    first_shift,
    cross_query,
    crossq_bias,
    cross_key,
    cross_value,
    crossv_bias,
    cross_output,
    crosso_bias,
    second_gain,
    second_shift,
    expand_weight,
    expand_bias,
    shrink_weight,
    shrink_bias,
    third_gain,
    third_shift,
    word_table,
):
    groups = answers.shape[0]
    row_count = groups * K
    token_count = row_count * TOK
    model_ways = lax.axis_size("mp")
    local_heads = H // model_ways
    head_cols = local_heads * HD
    heads_shape = (row_count, TOK, local_heads, HD)
    spread = jnp.broadcast_to(answers[:, None], (groups, K, TOK, D)).reshape(row_count, TOK, D)
    spread_targets = jnp.broadcast_to(targets[:, None], (groups, K, TOK)).reshape(row_count, TOK)
    row_input, row_targets = (
        lax.all_to_all(spread, "dp", split_axis=0, concat_axis=0, tiled=True),
        lax.all_to_all(spread_targets, "dp", split_axis=0, concat_axis=0, tiled=True),
    )
    inputs = row_input.reshape(token_count, D)
    target_flat = row_targets.reshape(token_count)
    layer_set = (
        lax.all_gather(self_query, "dp", axis=0, tiled=True),
        lax.all_gather(self_key, "dp", axis=0, tiled=True),
        lax.all_gather(self_value, "dp", axis=0, tiled=True),
        lax.all_gather(query_bias, "dp", axis=1, tiled=True),
        lax.all_gather(value_bias, "dp", axis=1, tiled=True),
        lax.all_gather(self_output, "dp", axis=1, tiled=True),
        lax.all_gather(output_bias, "dp", axis=0, tiled=True),
        lax.all_gather(first_gain, "dp", axis=0, tiled=True),
        lax.all_gather(first_shift, "dp", axis=0, tiled=True),
        lax.all_gather(cross_query, "dp", axis=0, tiled=True),
        lax.all_gather(crossq_bias, "dp", axis=1, tiled=True),
        lax.all_gather(cross_output, "dp", axis=1, tiled=True),
        lax.all_gather(crosso_bias, "dp", axis=0, tiled=True),
        lax.all_gather(second_gain, "dp", axis=0, tiled=True),
        lax.all_gather(second_shift, "dp", axis=0, tiled=True),
        lax.all_gather(expand_weight, "dp", axis=0, tiled=True),
        lax.all_gather(expand_bias, "dp", axis=1, tiled=True),
        lax.all_gather(shrink_weight, "dp", axis=1, tiled=True),
        lax.all_gather(shrink_bias, "dp", axis=0, tiled=True),
        lax.all_gather(third_gain, "dp", axis=0, tiled=True),
        lax.all_gather(third_shift, "dp", axis=0, tiled=True),
        lax.all_gather(word_table, "dp", axis=1, tiled=True),
    )
    (
        full_query,
        full_key,
        full_value,
        full_qbias,
        full_vbias,
        full_output,
        full_obias,
        gain_one,
        shift_one,
        full_cquery,
        full_cqbias,
        full_cout,
        full_cobias,
        gain_two,
        shift_two,
        full_expand,
        full_ebias,
        full_shrink,
        full_sbias,
        gain_three,
        shift_three,
        full_table,
    ) = layer_set
    memory_set = (
        lax.all_gather(cross_key, ("dp", "mp"), axis=0, tiled=True),
        lax.all_gather(cross_value, ("dp", "mp"), axis=0, tiled=True),
        lax.all_gather(crossv_bias, ("dp", "mp"), axis=0, tiled=True),
    )
    key_weight, value_weight, vbias_full = memory_set
    queries = ((product(inputs, full_query) + full_qbias.reshape(-1)) * SCALE).astype(jnp.bfloat16)
    self_keys = product(inputs, full_key).astype(jnp.bfloat16)
    self_values = (product(inputs, full_value) + full_vbias.reshape(-1)).astype(jnp.bfloat16)
    causal = (
        lax.broadcasted_iota(jnp.int32, (TOK, TOK), 1)
        <= lax.broadcasted_iota(jnp.int32, (TOK, TOK), 0)
    )[None, None]
    context, self_peak, self_total = attend(
        queries.reshape(heads_shape),
        self_keys.reshape(heads_shape),
        self_values.reshape(heads_shape),
        causal,
    )
    context = context.reshape(token_count, head_cols)
    first_in = inputs.astype(jnp.float32) + head_sum(product(context, full_output)) + full_obias
    hidden_one, normed_one, inverse_one = layer_norm(first_in, gain_one, shift_one)
    hidden_low1 = hidden_one.astype(jnp.bfloat16)
    cross_queries = ((product(hidden_low1, full_cquery) + full_cqbias.reshape(-1)) * SCALE).astype(
        jnp.bfloat16
    )
    memory_keys = jnp.einsum(
        "rmd,de->rme", memory, key_weight, preferred_element_type=jnp.float32
    ).astype(jnp.bfloat16)
    memory_values = (
        jnp.einsum("rmd,de->rme", memory, value_weight, preferred_element_type=jnp.float32)
        + vbias_full
    ).astype(jnp.bfloat16)
    head_keys, head_values = (
        lax.all_to_all(memory_keys, "mp", split_axis=2, concat_axis=1, tiled=True),
        lax.all_to_all(memory_values, "mp", split_axis=2, concat_axis=1, tiled=True),
    )
    memory_len = head_keys.shape[1]
    memory_shape = (row_count, memory_len, local_heads, HD)
    visible = (
        lax.broadcasted_iota(jnp.int32, (row_count, 1, 1, memory_len), 3)
        < lengths[:, None, None, None]
    )
    context_two, cross_peak, cross_total = attend(
        cross_queries.reshape(heads_shape),
        head_keys.reshape(memory_shape),
        head_values.reshape(memory_shape),
        visible,
    )
    context_two = context_two.reshape(token_count, head_cols)
    second_in = hidden_one + head_sum(product(context_two, full_cout)) + full_cobias
    hidden_two, normed_two, inverse_two = layer_norm(second_in, gain_two, shift_two)
    hidden_low2 = hidden_two.astype(jnp.bfloat16)
    expanded = product(hidden_low2, full_expand) + full_ebias.reshape(-1)
    activated = gelu_exact(expanded).astype(jnp.bfloat16)
    third_in = hidden_two + head_sum(product(activated, full_shrink)) + full_sbias
    hidden_three, normed_three, inverse_three = layer_norm(third_in, gain_three, shift_three)
    hidden_low3 = hidden_three.astype(jnp.bfloat16)
    logits = product_back(hidden_low3, full_table)
    vocab_local = logits.shape[1]
    local_target = target_flat - lax.axis_index("mp") * vocab_local
    inside = (local_target >= 0) & (local_target < vocab_local)
    picked = jnp.take_along_axis(
        logits, jnp.clip(local_target, 0, vocab_local - 1)[:, None], axis=1
    )[:, 0]
    picked = head_sum(jnp.where(inside, picked, 0.0))
    logit_peak = jnp.max(logits, axis=1)
    logit_total = jnp.sum(jnp.exp(logits - logit_peak[:, None]), axis=1)
    logit_peak, logit_total = softmax_stats(logit_peak, logit_total)
    norm_log = logit_peak + jnp.log(logit_total)
    token_loglik = (picked - norm_log).reshape(row_count, TOK)
    question_rows = lax.all_to_all(token_loglik, "dp", split_axis=0, concat_axis=0, tiled=True)
    doc_logp = jax.nn.log_softmax(doc_scores, axis=1)
    joined = doc_logp[:, :, None] + question_rows.reshape(groups, K, TOK)
    joined_top = jnp.max(joined, axis=1, keepdims=True)
    marginal = joined_top + jnp.log(jnp.sum(jnp.exp(joined - joined_top), axis=1, keepdims=True))
    question_loss = -jnp.mean(marginal[:, 0, :], axis=1)
    posterior = jnp.exp(joined - marginal)
    grad_rows = lax.all_to_all(
        (-posterior).reshape(row_count, TOK), "dp", split_axis=0, concat_axis=0, tiled=True
    )
    vocab_probs = jnp.exp(logits - norm_log[:, None])
    hits = (lax.broadcasted_iota(jnp.int32, logits.shape, 1) == local_target[:, None]).astype(
        jnp.float32
    )
    dlogits = (grad_rows.reshape(token_count)[:, None] * (hits - vocab_probs)).astype(jnp.bfloat16)
    dhidden_three = head_sum(product(dlogits, full_table))
    dthird, dgain_three, dshift_three = norm_back(
        dhidden_three, normed_three, inverse_three, gain_three
    )
    dshrink_in = dthird.astype(jnp.bfloat16)
    dshrink_bias = jnp.sum(dthird, axis=0)
    dshrink = weight_grad(activated, dshrink_in)
    dactivated = product_back(dshrink_in, full_shrink)
    dexpanded = jax.vjp(gelu_exact, expanded)[1](dactivated)[0].astype(jnp.bfloat16)
    dexpand_bias = column_sum(dexpanded).reshape(full_ebias.shape)
    dexpand = weight_grad(hidden_low2, dexpanded)
    dhidden_two = dthird + head_sum(product_back(dexpanded, full_expand))
    dsecond, dgain_two, dshift_two = norm_back(dhidden_two, normed_two, inverse_two, gain_two)
    dcout_in = dsecond.astype(jnp.bfloat16)
    dcout_bias = jnp.sum(dsecond, axis=0)
    dcout = weight_grad(context_two, dcout_in)
    dcontext_two = product_back(dcout_in, full_cout).astype(jnp.bfloat16)
    dcross_q, dhead_keys, dhead_values = attend_back(
        cross_queries.reshape(heads_shape),
        head_keys.reshape(memory_shape),
        head_values.reshape(memory_shape),
        visible,
        cross_peak,
        cross_total,
        dcontext_two.reshape(heads_shape),
    )
    dcross_q = dcross_q.reshape(token_count, head_cols)
    low_dkeys = dhead_keys.astype(jnp.bfloat16).reshape(row_count, memory_len, head_cols)
    low_dvalues = dhead_values.astype(jnp.bfloat16).reshape(row_count, memory_len, head_cols)
    slot_dkeys, slot_dvalues = (
        lax.all_to_all(low_dkeys, "mp", split_axis=1, concat_axis=2, tiled=True),
        lax.all_to_all(low_dvalues, "mp", split_axis=1, concat_axis=2, tiled=True),
    )
    dcross_low = dcross_q.astype(jnp.bfloat16) * SCALE
    dcquery = weight_grad(hidden_low1, dcross_low)
    dcq_bias = column_sum(dcross_low).reshape(local_heads, HD)
    dhidden_one = dsecond + head_sum(product_back(dcross_low, full_cquery))
    memory_grad = jnp.einsum(
        "rme,de->rmd", slot_dkeys, key_weight, preferred_element_type=jnp.float32
    ) + jnp.einsum("rme,de->rmd", slot_dvalues, value_weight, preferred_element_type=jnp.float32)
    dkey_weight = jnp.einsum("rmd,rme->de", memory, slot_dkeys, preferred_element_type=jnp.float32)
    dvalue_weight = jnp.einsum(
        "rmd,rme->de", memory, slot_dvalues, preferred_element_type=jnp.float32
    )
    dvalue_bias = jnp.sum(slot_dvalues, axis=(0, 1), dtype=jnp.float32)
    memory_grads = (
        lax.psum_scatter(dkey_weight, ("dp", "mp"), scatter_dimension=0, tiled=True),
        lax.psum_scatter(dvalue_weight, ("dp", "mp"), scatter_dimension=0, tiled=True),
        lax.psum_scatter(dvalue_bias, ("dp", "mp"), scatter_dimension=0, tiled=True),
    )
    dfirst, dgain_one, dshift_one = norm_back(dhidden_one, normed_one, inverse_one, gain_one)
    dout_in = dfirst.astype(jnp.bfloat16)
    dout_bias = jnp.sum(dfirst, axis=0)
    doutput = weight_grad(context, dout_in)
    dcontext = product_back(dout_in, full_output).astype(jnp.bfloat16)
    dquery_f, dkey_f, dvalue_f = attend_back(
        queries.reshape(heads_shape),
        self_keys.reshape(heads_shape),
        self_values.reshape(heads_shape),
        causal,
        self_peak,
        self_total,
        dcontext.reshape(heads_shape),
    )
    dquery_low = dquery_f.astype(jnp.bfloat16).reshape(token_count, head_cols) * SCALE
    dkey_low = dkey_f.astype(jnp.bfloat16).reshape(token_count, head_cols)
    dvalue_low = dvalue_f.astype(jnp.bfloat16).reshape(token_count, head_cols)
    dquery = weight_grad(inputs, dquery_low)
    dkey = weight_grad(inputs, dkey_low)
    dvalue = weight_grad(inputs, dvalue_low)
    dquery_bias = column_sum(dquery_low).reshape(local_heads, HD)
    dvalue_headbias = column_sum(dvalue_low).reshape(local_heads, HD)
    dinputs = dfirst + head_sum(
        product_back(dquery_low, full_query)
        + product_back(dkey_low, full_key)
        + product_back(dvalue_low, full_value)
    )
    returned = lax.all_to_all(
        dinputs.astype(jnp.bfloat16).reshape(row_count, TOK, D),
        "dp",
        split_axis=0,
        concat_axis=0,
        tiled=True,
    )
    answer_grad = jnp.sum(returned.reshape(groups, K, TOK, D), axis=1, dtype=jnp.float32)
    layer_grads = (
        lax.psum_scatter(dquery.astype(jnp.bfloat16), "dp", scatter_dimension=0, tiled=True).astype(
            jnp.float32
        ),
        lax.psum_scatter(dkey.astype(jnp.bfloat16), "dp", scatter_dimension=0, tiled=True).astype(
            jnp.float32
        ),
        lax.psum_scatter(dvalue.astype(jnp.bfloat16), "dp", scatter_dimension=0, tiled=True).astype(
            jnp.float32
        ),
        lax.psum_scatter(
            dquery_bias.astype(jnp.bfloat16), "dp", scatter_dimension=1, tiled=True
        ).astype(jnp.float32),
        lax.psum_scatter(
            dvalue_headbias.astype(jnp.bfloat16), "dp", scatter_dimension=1, tiled=True
        ).astype(jnp.float32),
        lax.psum_scatter(
            doutput.astype(jnp.bfloat16), "dp", scatter_dimension=1, tiled=True
        ).astype(jnp.float32),
        lax.psum_scatter(
            dout_bias.astype(jnp.bfloat16), "dp", scatter_dimension=0, tiled=True
        ).astype(jnp.float32),
        lax.psum_scatter(
            dgain_one.astype(jnp.bfloat16), "dp", scatter_dimension=0, tiled=True
        ).astype(jnp.float32),
        lax.psum_scatter(
            dshift_one.astype(jnp.bfloat16), "dp", scatter_dimension=0, tiled=True
        ).astype(jnp.float32),
        lax.psum_scatter(
            dcquery.astype(jnp.bfloat16), "dp", scatter_dimension=0, tiled=True
        ).astype(jnp.float32),
        lax.psum_scatter(
            dcq_bias.astype(jnp.bfloat16), "dp", scatter_dimension=1, tiled=True
        ).astype(jnp.float32),
        lax.psum_scatter(dcout.astype(jnp.bfloat16), "dp", scatter_dimension=1, tiled=True).astype(
            jnp.float32
        ),
        lax.psum_scatter(
            dcout_bias.astype(jnp.bfloat16), "dp", scatter_dimension=0, tiled=True
        ).astype(jnp.float32),
        lax.psum_scatter(
            dgain_two.astype(jnp.bfloat16), "dp", scatter_dimension=0, tiled=True
        ).astype(jnp.float32),
        lax.psum_scatter(
            dshift_two.astype(jnp.bfloat16), "dp", scatter_dimension=0, tiled=True
        ).astype(jnp.float32),
        lax.psum_scatter(
            dexpand.astype(jnp.bfloat16), "dp", scatter_dimension=0, tiled=True
        ).astype(jnp.float32),
        lax.psum_scatter(
            dexpand_bias.astype(jnp.bfloat16), "dp", scatter_dimension=1, tiled=True
        ).astype(jnp.float32),
        lax.psum_scatter(
            dshrink.astype(jnp.bfloat16), "dp", scatter_dimension=1, tiled=True
        ).astype(jnp.float32),
        lax.psum_scatter(
            dshrink_bias.astype(jnp.bfloat16), "dp", scatter_dimension=0, tiled=True
        ).astype(jnp.float32),
        lax.psum_scatter(
            dgain_three.astype(jnp.bfloat16), "dp", scatter_dimension=0, tiled=True
        ).astype(jnp.float32),
        lax.psum_scatter(
            dshift_three.astype(jnp.bfloat16), "dp", scatter_dimension=0, tiled=True
        ).astype(jnp.float32),
    )
    return (
        question_loss,
        answer_grad,
        memory_grad,
        layer_grads[0],
        layer_grads[1],
        layer_grads[2],
        layer_grads[3],
        layer_grads[4],
        layer_grads[5],
        layer_grads[6],
        layer_grads[7],
        layer_grads[8],
        layer_grads[9],
        layer_grads[10],
        memory_grads[0],
        memory_grads[1],
        memory_grads[2],
        layer_grads[11],
        layer_grads[12],
        layer_grads[13],
        layer_grads[14],
        layer_grads[15],
        layer_grads[16],
        layer_grads[17],
        layer_grads[18],
        layer_grads[19],
        layer_grads[20],
    )


def solution(mesh):
    placed = (
        P("dp", None, None),
        P("dp", None),
        P("dp", None),
        P("dp", "mp", None),
        P("dp"),
        P("dp", "mp"),
        P("dp", "mp"),
        P("dp", "mp"),
        P("mp", "dp"),
        P("mp", "dp"),
        P("mp", "dp"),
        P("dp"),
        P("dp"),
        P("dp"),
        P("dp", "mp"),
        P("mp", "dp"),
        P(("dp", "mp"), None),
        P(("dp", "mp"), None),
        P(("dp", "mp")),
        P("mp", "dp"),
        P("dp"),
        P("dp"),
        P("dp"),
        P("dp", "mp"),
        P("mp", "dp"),
        P("mp", "dp"),
        P("dp"),
        P("dp"),
        P("dp"),
        P("mp", "dp"),
    )
    return jax.shard_map(
        local,
        mesh=mesh,
        in_specs=placed,
        out_specs=(
            P("dp"),
            P("dp", None, None),
            P("dp", "mp", None),
            P("dp", "mp"),
            P("dp", "mp"),
            P("dp", "mp"),
            P("mp", "dp"),
            P("mp", "dp"),
            P("mp", "dp"),
            P("dp"),
            P("dp"),
            P("dp"),
            P("dp", "mp"),
            P("mp", "dp"),
            P(("dp", "mp"), None),
            P(("dp", "mp"), None),
            P(("dp", "mp")),
            P("mp", "dp"),
            P("dp"),
            P("dp"),
            P("dp"),
            P("dp", "mp"),
            P("mp", "dp"),
            P("mp", "dp"),
            P("dp"),
            P("dp"),
            P("dp"),
        ),
        check_vma=False,
    )
```

profile of v0, /device:TPU:0, one launch (start us, length us, event | category | flops | bytes accessed | tf_op | source)
XLA Modules:
  0.0 2508.0 jit_solution(16686930673122716995)
XLA Ops:
  16.8 62.3 %all-reduce = bf16[1024]{0:T(1024)(128)(2,1)S(1)} all-reduce(bf16[1024]{0:T(1024)(128)(2,1)S(1)} %dynamic-update-slice), channel_id=1, replica_groups=mesh['dp'=8,'mp'=4] {'dp','mp'}, use_global_device_ids=true, to_apply=%add | all-reduce | flops 1024 | bytes 4096
  79.1 21.4 add_convert_fusion
  100.6 12.1 copy.278
  119.1 165.7 %all-gather.23.cloned.1.call-done = bf16[1024,1024]{1,0:T(8,128)(2,1)} async-done(((bf16[32,1024]{1,0:T(8,128)(2,1)}), bf16[1024,1024]{1,0:T(8,128)(2,1)}) %all-gather.23.cloned.1.call-update) | async-done | bytes 2097168 | tf_op jit(solution)/shard_map/all_gather | solution.py:216
  284.8 21.4 convolution_convert_fusion.2
  306.2 12.3 copy.283
  318.5 30.8 %all-to-all-start.3 = ((bf16[32,100,1024]{1,0,2:T(8,128)(2,1)}), bf16[32,100,1024]{1,0,2:T(8,128)(2,1)}, u32[]{:S(2)}, u32[]{:S(2)}) async-start(bf16[32,100,1024]{1,0,2:T(8,128)(2,1)} %copy.283), calls=%async_computation.3 | async-start | bytes 16777216 | tf_op jit(solution)/shard_map/all_to_all | solution.py:249
  349.3 11.7 all-gather.2
  370.2 8.9 all_gather.87
  379.1 9.8 all_gather.91
  388.9 9.9 all_gather.89
  398.8 10.3 all_gather.92
  467.5 8.9 all_gather.98
  476.5 9.9 all_gather.101
  486.4 184.1 %all-reduce.23.cloned.1.call-done = f32[1024,1024]{1,0:T(8,128)} async-done(((f32[1024,1024]{1,0:T(8,128)}), f32[1024,1024]{1,0:T(8,128)}) %all-reduce.23.cloned.1.call-update) | async-done | bytes 4194320 | tf_op jit(solution)/shard_map/psum | solution.py:107
  677.8 12.6 copy.419
  690.3 14.5 reshape.390
  704.8 12.2 copy.418
  717.0 14.5 reshape.392
  740.6 9.2 fusion.40
  756.4 10.0 all-gather.11
  791.6 118.3 %all-reduce.25.cloned.1.call-done = f32[1024,1024]{1,0:T(8,128)} async-done(((f32[1024,1024]{1,0:T(8,128)}), f32[1024,1024]{1,0:T(8,128)}) %all-reduce.25.cloned.1.call-update) | async-done | bytes 4194320 | tf_op jit(solution)/shard_map/psum | solution.py:107
  917.2 15.6 multiply_convert_fusion.3
  944.7 9.3 all-gather.12
  972.0 121.3 %all-reduce.27.cloned.1.call-done = f32[1024,1024]{1,0:T(8,128)} async-done(((f32[1024,1024]{1,0:T(8,128)}), f32[1024,1024]{1,0:T(8,128)}) %all-reduce.27.cloned.1.call-update) | async-done | bytes 4194320 | tf_op jit(solution)/shard_map/psum | solution.py:107
  1100.6 23.9 fusion.121
  1124.4 13.1 all-gather
  1137.6 10.9 exponential_reduce_fusion
  1148.5 13.1 all-gather.1
  1161.7 16.0 gather_fusion
  1177.7 9.5 psum.59
  1206.8 24.5 fusion.2
  1231.3 151.5 %all-reduce.29.cloned.1.call-done = f32[1024,1024]{1,0:T(8,128)} async-done(((f32[1024,1024]{1,0:T(8,128)}), f32[1024,1024]{1,0:T(8,128)}) %all-reduce.29.cloned.1.call-update) | async-done | bytes 4194320 | tf_op jit(solution)/shard_map/psum | solution.py:107
  1404.2 153.8 %all-reduce.31.cloned.1.call-done = f32[1024,1024]{1,0:T(8,128)} async-done(((f32[1024,1024]{1,0:T(8,128)}), f32[1024,1024]{1,0:T(8,128)}) %all-reduce.31.cloned.1.call-update) | async-done | bytes 4194320 | tf_op jit(solution)/shard_map/psum | solution.py:107
  1615.7 14.3 copy.305
  1643.7 218.4 %all-reduce.33.cloned.1.call-done = f32[1024,1024]{1,0:T(8,128)} async-done(((f32[1024,1024]{1,0:T(8,128)}), f32[1024,1024]{1,0:T(8,128)}) %all-reduce.33.cloned.1.call-update) | async-done | bytes 4194320 | tf_op jit(solution)/shard_map/psum | solution.py:107
  1904.8 9.5 convolution_convert_fusion
  1914.3 14.3 copy.309
  1928.6 14.5 all-to-all-start.8
  1958.5 11.2 convolution_bitcast_fusion.1
  1975.3 232.1 %all-to-all-done.8 = bf16[32,400,256]{2,0,1:T(8,128)(2,1)} async-done(((bf16[32,400,256]{2,0,1:T(8,128)(2,1)}), bf16[32,400,256]{2,0,1:T(8,128)(2,1)}, u32[]{:S(2)}, u32[]{:S(2)}) %all-to-all-start.8) | async-done | bytes 6553632 | tf_op jit(solution)/shard_map/all_to_all | solution.py:332
  2214.2 8.9 convolution_bitcast_fusion
  2239.8 26.0 %all-reduce.14 = (bf16[4,64]{1,0:T(4,128)(2,1)S(1)}, bf16[4,64]{1,0:T(4,128)(2,1)S(1)}, bf16[1024]{0:T(1024)(128)(2,1)S(1)}, bf16[1024]{0:T(1024)(128)(2,1)S(1)}...) all-reduce(bf16[4,64]{1,0:T(4,128)(2,1)S(1)} %get-tuple-element.395, ...), channel_id=7, replica_groups=mesh['dp'=8,'mp'=4] {'dp'}, use_global_device_ids=true, to_apply=%region_42.43.clone | all-reduce | flops 9984 | bytes 39936
  2289.2 21.8 fusion.8
  2311.0 24.7 convolution_add_fusion
  2335.7 17.4 copy.312
  2357.5 39.4 %all-reduce.7 = f32[1024]{0:T(1024)S(1)} all-reduce(f32[1024]{0:T(1024)S(1)} %bitcast.258), channel_id=17, replica_groups=mesh['dp'=8,'mp'=4] {'dp','mp'}, use_global_device_ids=true, to_apply=%region_58.59.clone | all-reduce | flops 1024 | bytes 8192
  2398.6 101.8 %reduce-scatter.47.cloned.1.call-done = f32[32,1024]{1,0:T(8,128)} async-done(((f32[1024,1024]{1,0:T(8,128)}), f32[32,1024]{1,0:T(8,128)}) %reduce-scatter.47.cloned.1.call-update) | async-done | bytes 131088
  (461 shorter events, 401.9 us)
Async XLA Ops:
  8.0 71.1 %all-gather.21.cloned.1.call-start = ((), (), s32[]{:S(2)}) async-start(), calls=%async_computation.21 | async-start | bytes 2162688 | tf_op jit(solution)/shard_map/all_gather | solution.py:217
  11.4 101.3 %all-to-all-start.1 = ((bf16[32,32,1024]{2,1,0:T(8,128)(2,1)}), bf16[32,32,1024]{2,1,0:T(8,128)(2,1)S(1)}, u32[]{:S(2)}, u32[]{:S(2)}) async-start(bf16[32,32,1024]{2,1,0:T(8,128)(2,1)} %bitcast.220), calls=%async_computation.1 | async-start | bytes 4194304 | tf_op jit(solution)/shard_map/all_to_all | solution.py:162
  112.7 557.8 %copy-start.8 = (bf16[32,32,1024]{2,1,0:T(8,128)(2,1)}, bf16[32,32,1024]{2,1,0:T(8,128)(2,1)S(1)}, u32[]{:S(2)}) copy-start(bf16[32,32,1024]{2,1,0:T(8,128)(2,1)S(1)} %all-to-all-done.1) | copy-start | bytes 6291460
  112.7 205.8 %all-to-all-start.2 = ((bf16[32,100,1024]{1,0,2:T(8,128)(2,1)}), bf16[32,100,1024]{1,0,2:T(8,128)(2,1)}, u32[]{:S(2)}, u32[]{:S(2)}) async-start(bf16[32,100,1024]{1,0,2:T(8,128)(2,1)} %copy.278), calls=%async_computation.2 | async-start | bytes 16777216 | tf_op jit(solution)/shard_map/all_to_all | solution.py:250
  118.4 166.4 %all-gather.23.cloned.1.call-start = ((), (), s32[]{:S(2)}) async-start(), calls=%async_computation.22 | async-start | bytes 2162688 | tf_op jit(solution)/shard_map/all_gather | solution.py:216
  318.5 51.7 %copy-start.50 = (bf16[128,256]{1,0:T(8,128)(2,1)S(1)}, bf16[128,256]{1,0:T(8,128)(2,1)}, u32[]{:S(2)}) copy-start(bf16[128,256]{1,0:T(8,128)(2,1)} %param.39) | copy-start | bytes 196612
  318.5 60.6 %copy-start.51 = (bf16[128,256]{1,0:T(8,128)(2,1)S(1)}, bf16[128,256]{1,0:T(8,128)(2,1)}, u32[]{:S(2)}) copy-start(bf16[128,256]{1,0:T(8,128)(2,1)} %param.38) | copy-start | bytes 196612
  318.5 70.4 %copy-start.52 = (bf16[128,256]{1,0:T(8,128)(2,1)S(1)}, bf16[128,256]{1,0:T(8,128)(2,1)}, u32[]{:S(2)}) copy-start(bf16[128,256]{1,0:T(8,128)(2,1)} %param.37) | copy-start | bytes 196612
  318.5 80.4 %copy-start.53 = (bf16[256,128]{1,0:T(8,128)(2,1)S(1)}, bf16[256,128]{1,0:T(8,128)(2,1)}, u32[]{:S(2)}) copy-start(bf16[256,128]{1,0:T(8,128)(2,1)} %param.42) | copy-start | bytes 196612
  318.5 386.3 %all-to-all-start.3 = ((bf16[32,100,1024]{1,0,2:T(8,128)(2,1)}), bf16[32,100,1024]{1,0,2:T(8,128)(2,1)}, u32[]{:S(2)}, u32[]{:S(2)}) async-start(bf16[32,100,1024]{1,0,2:T(8,128)(2,1)} %copy.283), calls=%async_computation.3 | async-start | bytes 16777216 | tf_op jit(solution)/shard_map/all_to_all | solution.py:249
  349.3 321.2 %all-reduce.23.cloned.1.call-start = ((), (), s32[]{:S(2)}) async-start(), calls=%async_computation.20 | async-start | bytes 8388608 | tf_op jit(solution)/shard_map/psum | solution.py:107
  433.6 52.8 %copy-start.70 = (s32[32]{0:T(128)S(1)}, s32[32]{0:T(128)}, u32[]{:S(2)}) copy-start(s32[32]{0:T(128)} %param.36) | copy-start | bytes 388
  433.6 476.3 %all-reduce.25.cloned.1.call-start = ((), (), s32[]{:S(2)}) async-start(), calls=%async_computation.23 | async-start | bytes 8388608 | tf_op jit(solution)/shard_map/psum | solution.py:107
  458.5 451.4 %copy-start.44 = (f32[8,1,128]{2,1,0:T(1,128)}, f32[8,1,128]{2,1,0:T(1,128)S(1)}, u32[]{:S(2)}) copy-start(f32[8,1,128]{2,1,0:T(1,128)S(1)} %convert_element_type.448) | copy-start | bytes 12292
  476.5 198.2 %copy-start.32 = (bf16[1024,256]{1,0:T(8,128)(2,1)}, bf16[1024,256]{1,0:T(8,128)(2,1)S(1)}, u32[]{:S(2)}) copy-start(bf16[1024,256]{1,0:T(8,128)(2,1)S(1)} %all_gather.98) | copy-start | bytes 1572868
  486.4 265.9 %copy-start.23 = (bf16[256,1024]{1,0:T(8,128)(2,1)}, bf16[256,1024]{1,0:T(8,128)(2,1)S(1)}, u32[]{:S(2)}) copy-start(bf16[256,1024]{1,0:T(8,128)(2,1)S(1)} %all_gather.101) | copy-start | bytes 1572868
  673.3 236.6 %copy-start.42 = (f32[1024]{0:T(1024)}, f32[1024]{0:T(1024)S(1)}, u32[]{:S(2)}) copy-start(f32[1024]{0:T(1024)S(1)} %broadcast_multiply_fusion.8) | copy-start | bytes 12292
  673.9 236.0 %copy-start.46 = (f32[1024]{0:T(1024)}, f32[1024]{0:T(1024)S(1)}, u32[]{:S(2)}) copy-start(f32[1024]{0:T(1024)S(1)} %add_rsqrt_fusion.2) | copy-start | bytes 12292
  677.7 53.8 %copy-start.13 = (bf16[32,32,4,64]{3,2,1,0:T(4,128)(2,1)}, bf16[32,32,4,64]{3,2,1,0:T(4,128)(2,1)S(1)}, u32[]{:S(2)}) copy-start(bf16[32,32,4,64]{3,2,1,0:T(4,128)(2,1)S(1)} %reshape.391) | copy-start | bytes 1572868
  755.0 162.1 %all-gather.25.cloned.1.call-start = ((), (), s32[]{:S(2)}) async-start(), calls=%async_computation.24 | async-start | bytes 2359296 | tf_op jit(solution)/shard_map/all_gather | solution.py:183
  755.7 177.1 %all-gather.27.cloned.1.call-start = ((), (), s32[]{:S(2)}) async-start(), calls=%async_computation.25 | async-start | bytes 2359296 | tf_op jit(solution)/shard_map/all_gather | solution.py:185
  756.3 337.0 %all-reduce.27.cloned.1.call-start = ((), (), s32[]{:S(2)}) async-start(), calls=%async_computation.26 | async-start | bytes 8388608 | tf_op jit(solution)/shard_map/psum | solution.py:107
  782.9 310.4 %copy-start.57 = (f32[8,1,128]{2,1,0:T(1,128)}, f32[8,1,128]{2,1,0:T(1,128)S(1)}, u32[]{:S(2)}) copy-start(f32[8,1,128]{2,1,0:T(1,128)S(1)} %convert_element_type.452) | copy-start | bytes 12292
  939.4 161.2 %all-gather.29.cloned.1.call-start = ((), (), s32[]{:S(2)}) async-start(), calls=%async_computation.27 | async-start | bytes 14745600 | tf_op jit(solution)/shard_map/all_gather | solution.py:189
  940.7 29.8 %all-to-all-start = ((s32[8,1,128]{2,1,0:T(1,128)}), s32[8,1,128]{2,1,0:T(1,128)S(1)}, u32[]{:S(2)}, u32[]{:S(2)}) async-start(s32[8,1,128]{2,1,0:T(1,128)} %reshape.502), calls=%async_computation | async-start | bytes 8192 | tf_op jit(solution)/shard_map/all_to_all | solution.py:163
  1188.1 8.3 all-to-all-start.4
  1191.9 191.0 %all-reduce.29.cloned.1.call-start = ((), (), s32[]{:S(2)}) async-start(), calls=%async_computation.28 | async-start | bytes 8388608 | tf_op jit(solution)/shard_map/psum | solution.py:107
  1231.3 326.7 %all-reduce.31.cloned.1.call-start = ((), (), s32[]{:S(2)}) async-start(), calls=%async_computation.29 | async-start | bytes 8388608 | tf_op jit(solution)/shard_map/psum | solution.py:107
  1404.1 458.0 %all-reduce.33.cloned.1.call-start = ((), (), s32[]{:S(2)}) async-start(), calls=%async_computation.30 | async-start | bytes 8388608 | tf_op jit(solution)/shard_map/psum | solution.py:107
  1591.8 639.8 %reduce-scatter.51.cloned.1.call-start = ((), (), s32[]{:S(2)}) async-start(), calls=%async_computation.41 | async-start | bytes 36864
  1592.6 640.3 %reduce-scatter.53.cloned.1.call-start = ((), (), s32[]{:S(2)}) async-start(), calls=%async_computation.42 | async-start | bytes 2359296
  1600.5 634.4 %reduce-scatter.35.cloned.1.call-start = ((), (), s32[]{:S(2)}) async-start(), calls=%async_computation.33 | async-start | bytes 2359296 | tf_op jit(solution)/shard_map/reduce_scatter | solution.py:432
  1630.0 298.6 %all-to-all-start.7 = ((bf16[32,400,256]{2,0,1:T(8,128)(2,1)}), bf16[32,400,256]{2,0,1:T(8,128)(2,1)}, u32[]{:S(2)}, u32[]{:S(2)}) async-start(bf16[32,400,256]{2,0,1:T(8,128)(2,1)} %copy.305), calls=%async_computation.7 | async-start | bytes 13107200 | tf_op jit(solution)/shard_map/all_to_all | solution.py:331
  1635.5 601.2 %reduce-scatter.49.cloned.1.call-start = ((), (), s32[]{:S(2)}) async-start(), calls=%async_computation.40 | async-start | bytes 589824
  1639.7 222.4 %copy-start.43 = (f32[1024]{0:T(1024)S(1)}, f32[1024]{0:T(1024)}, u32[]{:S(2)}) copy-start(f32[1024]{0:T(1024)} %copy-done.42) | copy-start | bytes 12292
  1639.7 222.4 %copy-start.45 = (f32[8,1,128]{2,1,0:T(1,128)S(1)}, f32[8,1,128]{2,1,0:T(1,128)}, u32[]{:S(2)}) copy-start(f32[8,1,128]{2,1,0:T(1,128)} %copy-done.44) | copy-start | bytes 12292
  1639.7 222.4 %copy-start.47 = (f32[1024]{0:T(1024)S(1)}, f32[1024]{0:T(1024)}, u32[]{:S(2)}) copy-start(f32[1024]{0:T(1024)} %copy-done.46) | copy-start | bytes 12292
  1641.9 596.4 %reduce-scatter.33.cloned.1.call-start = ((), (), s32[]{:S(2)}) async-start(), calls=%async_computation.32 | async-start | bytes 589824 | tf_op jit(solution)/shard_map/reduce_scatter | solution.py:414
  1643.5 629.5 %reduce-scatter.37.cloned.1.call-start = ((), (), s32[]{:S(2)}) async-start(), calls=%async_computation.34 | async-start | bytes 589824
  1884.0 390.8 %reduce-scatter.39.cloned.1.call-start = ((), (), s32[]{:S(2)}) async-start(), calls=%async_computation.35 | async-start | bytes 589824
  1893.2 383.3 %reduce-scatter.41.cloned.1.call-start = ((), (), s32[]{:S(2)}) async-start(), calls=%async_computation.36 | async-start | bytes 589824
  1928.6 278.9 %all-to-all-start.8 = ((bf16[32,400,256]{2,0,1:T(8,128)(2,1)}), bf16[32,400,256]{2,0,1:T(8,128)(2,1)}, u32[]{:S(2)}, u32[]{:S(2)}) async-start(bf16[32,400,256]{2,0,1:T(8,128)(2,1)} %copy.309), calls=%async_computation.8 | async-start | bytes 13107200 | tf_op jit(solution)/shard_map/all_to_all | solution.py:332
  1943.1 335.1 %reduce-scatter.43.cloned.1.call-start = ((), (), s32[]{:S(2)}) async-start(), calls=%async_computation.37 | async-start | bytes 589824
  1947.2 332.7 %all-reduce.35.cloned.1.call-start = ((), (), s32[]{:S(2)}) async-start(), calls=%async_computation.31 | async-start | bytes 8388608 | tf_op jit(solution)/shard_map/psum | solution.py:107
  1951.5 447.1 %reduce-scatter.45.cloned.1.call-start = ((), (), s32[]{:S(2)}) async-start(), calls=%async_computation.38 | async-start | bytes 4325376
  1969.8 244.4 %slice-start.1 = ((s8[6553600]{0:T(1024)(128)(4,1)}), s8[2359296]{0:T(1024)(128)(4,1)S(1)}, s32[]{:S(2)}) async-start(s8[6553600]{0:T(1024)(128)(4,1)} %bitcast.282), calls=%async_computation.44 | async-start | bytes 4718592
  1975.3 525.1 %reduce-scatter.47.cloned.1.call-start = ((), (), s32[]{:S(2)}) async-start(), calls=%async_computation.39 | async-start | bytes 4325376
  2285.4 112.1 %all-to-all-start.6 = ((bf16[32,32,1024]{2,1,0:T(8,128)(2,1)}), bf16[32,32,1024]{2,1,0:T(8,128)(2,1)S(1)}, u32[]{:S(2)}, u32[]{:S(2)}) async-start(bf16[32,32,1024]{2,1,0:T(8,128)(2,1)} %bitcast.56), calls=%async_computation.6 | async-start | bytes 4194304 | tf_op jit(solution)/shard_map/all_to_all | solution.py:378
  (72 other events, 676.6 us)
Sparse Core Ops, SparseCore 0:
  11.8 60.6 all-gather.20
  122.1 162.5 all-gather.22
  757.7 27.9 all-gather.24
  787.5 28.2 all-gather.26
  941.8 75.8 all-gather.28
  1596.2 30.3 reduce-scatter.50
  1629.8 41.2 reduce-scatter.52
  1674.7 41.2 reduce-scatter.34
  1719.1 34.1 reduce-scatter.48
  1756.4 34.1 reduce-scatter.32
  1884.1 44.9 reduce-scatter.36
  1932.4 34.1 reduce-scatter.38
  1969.6 34.1 reduce-scatter.40
  2007.0 34.1 reduce-scatter.42
  2043.9 306.8 reduce-scatter.44
  2353.5 146.8 reduce-scatter.46
Sparse Core Ops, SparseCore 1:
  433.7 236.7 all-reduce.22
  755.1 154.8 all-reduce.24
  939.4 153.8 all-reduce.26
  1231.4 151.4 all-reduce.28
  1404.2 153.7 all-reduce.30
  1591.9 270.2 all-reduce.32
  1951.6 289.2 all-reduce.34
where the time goes:
time: 2520 us; the launch traced here: 2510 us
  waiting for transfers between devices  1450 us (58%)
  blocking collectives  343 us (14%)
  matrix products  293 us (12%)
  local copies, waits for them, and re-layouts  238 us (9%)
  other arithmetic  85.6 us (3%)
  starting transfers between devices  75 us (3%)
    psum x7, waiting for transfers between devices, head_sum(): return lax.psum(partial_term, 'mp')  947 us
    all_to_all x1, waiting for transfers between devices, local(): lax.all_to_all(low_dvalues, 'mp', split_axis=1, concat_axis=2, tiled=True)  232 us
    all_gather x1, waiting for transfers between devices, local(): lax.all_gather(cross_key, ('dp', 'mp'), axis=0, tiled=True)  166 us
    unnamed x3, blocking collectives  128 us
    unnamed x32, waiting for transfers between devices  105 us
    unnamed x208, local copies, waits for them, and re-layouts  75.5 us
    dot_general x9, matrix products, product(): return jnp.dot(former, latter, preferred_element_type=jnp.float32)  57.5 us
  transfers between devices with their start and end apart: 31, of which 10 were waited for; matrix products, arithmetic and copies ran while one was open for 16% of the time, Pallas kernels for 0%

commit v1 on v0

v1 whole, which is shorter than its diff:
```python
import functools

import jax
import jax.numpy as jnp
from jax import lax
from jax.experimental import pallas as pl
from jax.experimental.pallas import tpu as pltpu
from jax.sharding import PartitionSpec as P

D = 1024
H = 16
HD = 64
TOK = 32
K = 8
G = 4
GH = 4
GC = GH * HD
GL = GH * TOK

EPS = 1e-05
NEG = -1e30
SCALE = 0.125
BF = jnp.bfloat16
F32 = jnp.float32
MESH = pl.DeviceIdType.MESH
VMEM_BYTES = 60 * 1024 * 1024


def product(former, latter):
    return jnp.dot(former, latter, preferred_element_type=F32)


def product_back(former, latter):
    return lax.dot_general(former, latter, (((1,), (1,)), ((), ())), preferred_element_type=F32)


def weight_grad(former, latter):
    return lax.dot_general(former, latter, (((0,), (0,)), ((), ())), preferred_element_type=F32)


def gelu_exact(entries):
    return jax.nn.gelu(entries, approximate=False)


def layer_norm(entries, norm_gain, norm_shift):
    center = entries - jnp.mean(entries, axis=-1, keepdims=True)
    inverse = lax.rsqrt(jnp.mean(center * center, axis=-1, keepdims=True) + EPS)
    normed = center * inverse
    return (normed * norm_gain + norm_shift, normed, inverse)


def norm_back(upstream, normed, inverse, norm_gain):
    scaled = upstream * norm_gain
    dentries = inverse * (
        scaled
        - jnp.mean(scaled, axis=-1, keepdims=True)
        - normed * jnp.mean(scaled * normed, axis=-1, keepdims=True)
    )
    return (dentries, jnp.sum(upstream * normed, axis=0), jnp.sum(upstream, axis=0))


class Exchange:
    def __init__(self, entries):
        self.dp_ways, self.mp_ways = lax.axis_size("dp"), lax.axis_size("mp")
        self.chips = self.dp_ways // 2
        self.ways = {"z": self.mp_ways, "chips": self.chips, "pair": 2, "dp": self.dp_ways}
        self.arrays = [entry[0] for entry in entries]
        self.kinds = [entry[1] for entry in entries]
        self.groups = [entry[2] for entry in entries]
        self.count = len(entries)
        shapes = []
        for array, kind, group in entries:
            shape = array.shape
            if kind == "gather":
                shape = (self.ways[group],) + shape
            elif kind == "move":
                shape = (self.ways[group] - 1,) + shape[1:]
            elif kind == "move1":
                shape = (self.ways[group] - 1, shape[0]) + shape[2:]
            elif kind == "near":
                shape = (self.dp_ways,) + shape
            elif kind == "nearswap":
                shape = (self.dp_ways,) + shape[1:]
            else:
                shape = (self.dp_ways, self.mp_ways) + shape
            shapes.append(jax.ShapeDtypeStruct(shape, array.dtype))
        self.shapes = shapes
        self.specs = [pl.BlockSpec(memory_space=pl.ANY)] * self.count
        dma = pltpu.SemaphoreType.DMA
        most = max(self.dp_ways, self.mp_ways)
        self.scratch = [dma((self.count, most)) for _ in range(6)] + [dma((self.count,))]

    def bind(self, ins, outs, sems):
        self.ins, self.outs = ins, outs
        self.zs, self.zr, self.cs, self.cr, self.ps, self.pr, self.own = sems
        dp, mp = lax.axis_index("dp"), lax.axis_index("mp")
        self.dp, self.mp = dp, mp
        self.parity, self.chip = lax.rem(dp, 2), dp // 2
        self.place = {"z": mp, "chips": self.chip, "pair": self.parity, "dp": dp}

    def device(self, group, j):
        if group == "z":
            return (self.dp, j)
        if group == "chips":
            return (2 * j + self.parity, self.mp)
        if group == "pair":
            return (self.dp - self.parity + j, self.mp)
        return (j, self.mp)

    def peer(self, group, off):
        return lax.rem(self.place[group] + off, self.ways[group])

    def remote(self, source, target, send, recv, device):
        return pltpu.make_async_remote_copy(
            src_ref=source,
            dst_ref=target,
            send_sem=send,
            recv_sem=recv,
            device_id=device,
            device_id_type=MESH,
        )

    def meet(self):
        needed = set()
        for kind, group in zip(self.kinds, self.groups):
            if kind in ("near", "nearswap", "wide"):
                needed |= {"chips", "pair"}
                if kind == "wide":
                    needed.add("z")
            else:
                needed.add(group)
        barrier = pltpu.get_barrier_semaphore()
        total = 0
        for group in sorted(needed):
            for off in range(1, self.ways[group]):
                pl.semaphore_signal(
                    barrier,
                    inc=1,
                    device_id=self.device(group, self.peer(group, off)),
                    device_id_type=MESH,
                )
                total += 1
        pl.semaphore_wait(barrier, total)

    def first(self, i):
        kind, group = self.kinds[i], self.groups[i]
        ref, out = self.ins[i], self.outs[i]
        copies = []
        if kind in ("near", "nearswap"):
            return copies
        if kind == "wide":
            group, slot = "z", out.at[self.dp, self.mp]
        for off in range(1, self.ways[group]):
            peer = self.peer(group, off)
            if kind == "wide":
                source, target = ref, slot
            elif kind == "gather":
                source, target = ref, out.at[self.place[group]]
            elif kind == "move":
                source, target = ref.at[peer], out.at[off - 1]
            else:
                source, target = ref.at[:, peer], out.at[off - 1]
            copies.append(
                self.remote(
                    source,
                    target,
                    self.zs.at[i, off - 1],
                    self.zr.at[i, off - 1],
                    self.device(group, peer),
                )
            )
        return copies

    def local(self, i):
        kind, group = self.kinds[i], self.groups[i]
        ref, out = self.ins[i], self.outs[i]
        if kind == "wide":
            source, target = ref, out.at[self.dp, self.mp]
        elif kind == "gather":
            source, target = ref, out.at[self.place[group]]
        elif kind in ("near", "nearswap"):
            source, target = self.mine(i), out.at[self.dp]
        else:
            return None
        return pltpu.make_async_copy(source, target, self.own.at[i])

    def mine(self, i):
        kind = self.kinds[i]
        if kind == "wide":
            return self.outs[i].at[self.dp]
        return self.ins[i].at[self.chip] if kind == "nearswap" else self.ins[i]

    def spread(self, i):
        copies = []
        for off in range(1, self.chips):
            peer = self.peer("chips", off)
            source = self.ins[i].at[peer] if self.kinds[i] == "nearswap" else self.mine(i)
            copies.append(
                self.remote(
                    source,
                    self.outs[i].at[self.dp],
                    self.cs.at[i, off - 1],
                    self.cr.at[i, off - 1],
                    self.device("chips", peer),
                )
            )
        return copies

    def hand(self, i, off):
        owner = 2 * lax.rem(self.chip + self.chips - off, self.chips) + self.parity
        return self.remote(
            self.mine(i) if off == 0 else self.outs[i].at[owner],
            self.outs[i].at[owner],
            self.ps.at[i, off],
            self.pr.at[i, off],
            self.device("pair", 1 - self.parity),
        )

    def begin(self):
        self.meet()
        for i in range(self.count):
            for copy in self.first(i):
                copy.start()
            if self.kinds[i] in ("near", "nearswap"):
                for copy in self.spread(i):
                    copy.start()
                self.hand(i, 0).start()
        for i in range(self.count):
            local = self.local(i)
            if local is not None:
                local.start()

    def finish(self):
        shared = [i for i in range(self.count) if self.kinds[i] in ("near", "nearswap", "wide")]
        for i in shared:
            if self.kinds[i] == "wide":
                for copy in self.first(i):
                    copy.wait()
                self.local(i).wait()
                for copy in self.spread(i):
                    copy.start()
                self.hand(i, 0).start()
        for i in shared:
            for off, copy in enumerate(self.spread(i), 1):
                copy.wait_recv()
                self.hand(i, off).start()
        for i in range(self.count):
            if i in shared:
                for copy in self.spread(i):
                    copy.wait_send()
                for off in range(self.chips):
                    self.hand(i, off).wait()
                if self.kinds[i] != "wide":
                    self.local(i).wait()
            else:
                for copy in self.first(i):
                    copy.wait()
                local = self.local(i)
                if local is not None:
                    local.wait()


def exchange_kernel(plan, *refs):
    count = plan.count
    plan.bind(refs[:count], refs[count : 2 * count], refs[2 * count :])
    plan.begin()
    plan.finish()


def exchange(entries, cid):
    plan = Exchange(entries)
    return pl.pallas_call(
        functools.partial(exchange_kernel, plan),
        out_shape=plan.shapes,
        in_specs=plan.specs,
        out_specs=plan.specs,
        scratch_shapes=plan.scratch,
        compiler_params=pltpu.CompilerParams(collective_id=cid, has_side_effects=True),
        name=f"exchange_{cid}",
    )(*plan.arrays)


def added(array, received, group):
    place = {
        "z": lax.axis_index("mp"),
        "chips": lax.axis_index("dp") // 2,
        "pair": lax.rem(lax.axis_index("dp"), 2),
    }[group]
    axis = 1 if group == "pair" else 0
    own = lax.dynamic_index_in_dim(array, place, axis, keepdims=False)
    return own.astype(F32) + jnp.sum(received.astype(F32), axis=0)


def beside(plan, kernel, inputs, outputs, scratches, *refs):
    n = plan.count
    first, last = pl.program_id(0) == 0, pl.program_id(0) == pl.num_programs(0) - 1
    ins = refs[:inputs]
    sends = refs[inputs : inputs + n]
    outs = refs[inputs + n : inputs + n + outputs]
    lands = refs[inputs + n + outputs : inputs + 2 * n + outputs]
    own = refs[inputs + 2 * n + outputs : inputs + 2 * n + outputs + scratches]
    plan.bind(sends, lands, refs[inputs + 2 * n + outputs + scratches :])
    pl.when(first)(plan.begin)
    kernel(*ins, *outs, *own)
    pl.when(last)(plan.finish)


def memory_call(plan, cid, kernel, name, grid, inputs, in_specs, out_specs, out_shape, scratch, flops):
    return pl.pallas_call(
        functools.partial(beside, plan, kernel, len(inputs), len(out_shape), len(scratch)),
        grid=(grid,),
        in_specs=in_specs + plan.specs,
        out_specs=out_specs + plan.specs,
        out_shape=out_shape + plan.shapes,
        scratch_shapes=scratch + plan.scratch,
        compiler_params=pltpu.CompilerParams(
            vmem_limit_bytes=VMEM_BYTES, collective_id=cid, has_side_effects=True
        ),
        cost_estimate=pl.CostEstimate(flops=flops, bytes_accessed=flops // 200, transcendentals=0),
        name=name,
    )(*inputs, *plan.arrays)


MEM_BLOCK = 16
BACK_BLOCK = 8


def memory_kernel(slots, padded, mem_ref, wk_ref, wv_ref, vb_ref, k_ref, v_ref, rows_ref, wide):
    for c in range(0, D, 128):
        cols = slice(c, c + 128)
        wide[...] = mem_ref[:, :, cols].reshape(slots * MEM_BLOCK, 128).astype(F32)
        for r in range(MEM_BLOCK):
            own = wide[pl.ds(r, slots, stride=MEM_BLOCK), :]
            rows_ref[r * padded : (r + 1) * padded, cols] = jnp.concatenate(
                [own, jnp.zeros((padded - slots, 128), F32)], axis=0
            ).astype(BF)
    rows = rows_ref[...]
    for c in range(0, D, 512):
        cols = slice(c, c + 512)
        k_ref[:, cols] = product(rows, wk_ref[:, cols]).astype(BF)
        v_ref[:, cols] = (product(rows, wv_ref[:, cols]) + vb_ref[:, cols]).astype(BF)


def memory_products(memory, key_weight, value_weight, vbias, padded, plan, cid):
    rows, slots, _ = memory.shape
    whole = lambda a: pl.BlockSpec(a.shape, lambda i: (0,) * a.ndim)
    out = jax.ShapeDtypeStruct((rows * padded, D), BF)
    out_spec = pl.BlockSpec((MEM_BLOCK * padded, D), lambda i: (i, 0))
    return memory_call(
        plan,
        cid,
        functools.partial(memory_kernel, slots, padded),
        "memory_products",
        rows // MEM_BLOCK,
        [jnp.transpose(memory, (1, 0, 2)), key_weight, value_weight, vbias],
        [
            pl.BlockSpec((slots, MEM_BLOCK, D), lambda i: (0, i, 0)),
            whole(key_weight),
            whole(value_weight),
            whole(vbias),
        ],
        [out_spec] * 3,
        [out] * 3,
        [pltpu.VMEM((slots * MEM_BLOCK, 128), F32)],
        4 * rows * padded * D * D,
    )


def memory_weight_kernel(rows_ref, dk_ref, dv_ref, wk_ref, wv_ref, vb_ref, key_sum, value_sum):
    step = pl.program_id(0)

    @pl.when(step == 0)
    def _():
        key_sum[...] = jnp.zeros_like(key_sum)
        value_sum[...] = jnp.zeros_like(value_sum)
        vb_ref[...] = jnp.zeros_like(vb_ref)

    rows = rows_ref[...]
    vb_ref[...] += jnp.sum(dv_ref[...].astype(F32), axis=0, keepdims=True)
    for c in range(0, D, 512):
        cols = slice(c, c + 512)
        key_sum[:, cols] += weight_grad(rows, dk_ref[:, cols])
        value_sum[:, cols] += weight_grad(rows, dv_ref[:, cols])

    @pl.when(step == pl.num_programs(0) - 1)
    def _():
        wk_ref[...] = key_sum[...].astype(BF)
        wv_ref[...] = value_sum[...].astype(BF)


def memory_weights(memory_rows, dkeys, dvalues, rows, padded):
    spec = pl.BlockSpec((BACK_BLOCK * padded, D), lambda i: (i, 0))
    whole = pl.BlockSpec((D, D), lambda i: (0, 0))
    return pl.pallas_call(
        memory_weight_kernel,
        grid=(rows // BACK_BLOCK,),
        in_specs=[spec, spec, spec],
        out_specs=[whole, whole, pl.BlockSpec((1, D), lambda i: (0, 0))],
        out_shape=[
            jax.ShapeDtypeStruct((D, D), BF),
            jax.ShapeDtypeStruct((D, D), BF),
            jax.ShapeDtypeStruct((1, D), F32),
        ],
        scratch_shapes=[pltpu.VMEM((D, D), F32), pltpu.VMEM((D, D), F32)],
        compiler_params=pltpu.CompilerParams(vmem_limit_bytes=VMEM_BYTES),
        cost_estimate=pl.CostEstimate(
            flops=4 * rows * padded * D * D, bytes_accessed=6 * rows * padded * D, transcendentals=0
        ),
        name="memory_weights",
    )(memory_rows, dkeys, dvalues)


def memory_grad_kernel(slots, padded, dk_ref, dv_ref, wk_ref, wv_ref, out_ref, wide):
    for c in range(0, D, 256):
        cols = slice(c, c + 256)
        term = product_back(dk_ref[...], wk_ref[cols, :]) + product_back(dv_ref[...], wv_ref[cols, :])
        for part in range(0, 256, 128):
            for r in range(BACK_BLOCK):
                wide[pl.ds(r, slots, stride=BACK_BLOCK), :] = term[
                    r * padded : r * padded + slots, part : part + 128
                ]
            out_ref[:, :, c + part : c + part + 128] = wide[...].reshape(slots, BACK_BLOCK, 128)


def memory_back(dkeys, dvalues, key_weight, value_weight, rows, slots, padded, plan, cid):
    spec = pl.BlockSpec((BACK_BLOCK * padded, D), lambda i: (i, 0))
    whole = pl.BlockSpec((D, D), lambda i: (0, 0))
    out, *rest = memory_call(
        plan,
        cid,
        functools.partial(memory_grad_kernel, slots, padded),
        "memory_back",
        rows // BACK_BLOCK,
        [dkeys, dvalues, key_weight, value_weight],
        [spec, spec, whole, whole],
        [pl.BlockSpec((slots, BACK_BLOCK, D), lambda i: (0, i, 0))],
        [jax.ShapeDtypeStruct((slots, rows, D), F32)],
        [pltpu.VMEM((slots * BACK_BLOCK, 128), F32)],
        4 * rows * padded * D * D,
    )
    return jnp.transpose(out, (1, 0, 2)), rest


def own_heads(result, keep):
    kept = result * keep
    total = kept[0:TOK]
    for h in range(1, GH):
        total = total + kept[h * TOK : (h + 1) * TOK]
    return total


def cross_kernel(piece, padded, used, k_ref, v_ref, q_ref, keep_ref, ctx_ref, peak_ref, total_ref):
    step = pl.program_id(0)
    keep = keep_ref[...]
    keep_wide = keep.astype(F32)
    slot = lax.broadcasted_iota(jnp.int32, (padded, GL), 0)
    for g in range(G):
        cols = slice(g * GC, (g + 1) * GC)
        query = jnp.concatenate([q_ref[:, cols]] * GH, axis=0) * keep
        scores = product_back(k_ref[:, cols], query)
        for r in range(piece):
            rows = slice(r * padded, (r + 1) * padded)
            seen = slot < used[step * piece + r]
            own = jnp.where(seen, scores[rows], NEG)
            peak = jnp.max(own, axis=0, keepdims=True)
            exponent = jnp.where(seen, jnp.exp(own - peak), 0.0)
            total = jnp.sum(exponent, axis=0, keepdims=True)
            probs = (exponent * (1.0 / jnp.maximum(total, 1e-30))).astype(BF)
            ctx = own_heads(weight_grad(probs, v_ref[rows, cols]), keep_wide)
            ctx_ref[r * TOK : (r + 1) * TOK, cols] = ctx.astype(BF)
            peak_ref[r, g : g + 1, :] = peak
            total_ref[r, g : g + 1, :] = total


def cross_forward(used, keys, values, queries, keep, piece, padded):
    steps = queries.shape[0] // TOK
    rows = steps * piece
    big = pl.BlockSpec((piece * padded, D), lambda i, u: (i, 0))
    stat = pl.BlockSpec((piece, G, GL), lambda i, u: (i, 0, 0))
    return pl.pallas_call(
        functools.partial(cross_kernel, piece, padded),
        grid_spec=pltpu.PrefetchScalarGridSpec(
            num_scalar_prefetch=1,
            grid=(steps,),
            in_specs=[
                big,
                big,
                pl.BlockSpec((TOK, D), lambda i, u: (i, 0)),
                pl.BlockSpec((GL, GC), lambda i, u: (0, 0)),
            ],
            out_specs=[pl.BlockSpec((piece * TOK, D), lambda i, u: (i, 0)), stat, stat],
        ),
        out_shape=[
            jax.ShapeDtypeStruct((rows * TOK, D), BF),
            jax.ShapeDtypeStruct((rows, G, GL), F32),
            jax.ShapeDtypeStruct((rows, G, GL), F32),
        ],
        compiler_params=pltpu.CompilerParams(vmem_limit_bytes=VMEM_BYTES),
        cost_estimate=pl.CostEstimate(
            flops=4 * rows * padded * GL * D,
            bytes_accessed=4 * rows * padded * D,
            transcendentals=rows * padded * G * GL,
        ),
        name="cross_forward",
    )(used, keys, values, queries, keep)


def cross_back_kernel(
    piece, padded, used, k_ref, v_ref, q_ref, dc_ref, norm_ref, mid_ref, keep_ref, dq_ref, dk_ref, dv_ref
):
    step = pl.program_id(0)
    keep = keep_ref[...]
    keep_wide = keep.astype(F32)
    slot = lax.broadcasted_iota(jnp.int32, (padded, GL), 0)
    for g in range(G):
        cols = slice(g * GC, (g + 1) * GC)
        query = jnp.concatenate([q_ref[:, cols]] * GH, axis=0) * keep
        scores = product_back(k_ref[:, cols], query)
        parts = []
        for r in range(piece):
            rows = slice(r * padded, (r + 1) * padded)
            dctx = jnp.concatenate([dc_ref[r * TOK : (r + 1) * TOK, cols]] * GH, axis=0) * keep
            dprobs = product_back(v_ref[rows, cols], dctx)
            seen = slot < used[step * piece + r]
            probs = jnp.where(seen, jnp.exp(scores[rows] - norm_ref[r, g : g + 1, :]), 0.0)
            parts.append((probs * (dprobs - mid_ref[r, g : g + 1, :])).astype(BF))
            dv_ref[rows, cols] = product(probs.astype(BF), dctx).astype(BF)
        dscores = jnp.concatenate(parts, axis=0)
        dk_ref[:, cols] = product(dscores, query).astype(BF)
        dq_ref[:, cols] = own_heads(weight_grad(dscores, k_ref[:, cols]), keep_wide).astype(BF)


def cross_back(used, keys, values, queries, dctx, norm, middle, keep, piece, padded):
    steps = queries.shape[0] // TOK
    rows = steps * piece
    big = pl.BlockSpec((piece * padded, D), lambda i, u: (i, 0))
    stat = pl.BlockSpec((piece, G, GL), lambda i, u: (i, 0, 0))
    small = pl.BlockSpec((TOK, D), lambda i, u: (i, 0))
    return pl.pallas_call(
        functools.partial(cross_back_kernel, piece, padded),
        grid_spec=pltpu.PrefetchScalarGridSpec(
            num_scalar_prefetch=1,
            grid=(steps,),
            in_specs=[
                big,
                big,
                small,
                pl.BlockSpec((piece * TOK, D), lambda i, u: (i, 0)),
                stat,
                stat,
                pl.BlockSpec((GL, GC), lambda i, u: (0, 0)),
            ],
            out_specs=[small, big, big],
        ),
        out_shape=[
            jax.ShapeDtypeStruct((steps * TOK, D), BF),
            jax.ShapeDtypeStruct((rows * padded, D), BF),
            jax.ShapeDtypeStruct((rows * padded, D), BF),
        ],
        compiler_params=pltpu.CompilerParams(vmem_limit_bytes=VMEM_BYTES),
        cost_estimate=pl.CostEstimate(
            flops=10 * rows * padded * GL * D,
            bytes_accessed=8 * rows * padded * D,
            transcendentals=rows * padded * G * GL,
        ),
        name="cross_back",
    )(used, keys, values, queries, dctx, norm, middle, keep)


def words_of(table_ref):
    return jnp.concatenate([table_ref[i] for i in range(table_ref.shape[0])], axis=-1)


def vocab_kernel(tile, h_ref, target_ref, table_ref, peak_ref, total_ref, pick_ref):
    step = pl.program_id(0)

    @pl.when(step == 0)
    def _():
        peak_ref[...] = jnp.full_like(peak_ref, NEG)
        total_ref[...] = jnp.zeros_like(total_ref)
        pick_ref[...] = jnp.zeros_like(pick_ref)

    words = words_of(table_ref)
    block = 256
    word = lax.broadcasted_iota(jnp.int32, (block, tile), 1) + step * tile
    for t in range(0, h_ref.shape[0], block):
        rows = slice(t, t + block)
        logits = product_back(h_ref[rows, :], words)
        former = peak_ref[rows, :]
        peak = jnp.maximum(former, jnp.max(logits, axis=1, keepdims=True))
        total = jnp.sum(jnp.exp(logits - peak), axis=1, keepdims=True)
        total_ref[rows, :] = total_ref[rows, :] * jnp.exp(former - peak) + total
        peak_ref[rows, :] = peak
        hit = jnp.where(word == target_ref[rows, :], logits, 0.0)
        pick_ref[rows, :] += jnp.sum(hit, axis=1, keepdims=True)


def vocab_forward(hidden, target, table, tile):
    tokens = hidden.shape[0]
    parts, words, width = table.shape
    col = pl.BlockSpec((tokens, 1), lambda i: (0, 0))
    return pl.pallas_call(
        functools.partial(vocab_kernel, tile),
        grid=(words // tile,),
        in_specs=[
            pl.BlockSpec((tokens, D), lambda i: (0, 0)),
            col,
            pl.BlockSpec((parts, tile, width), lambda i: (0, i, 0)),
        ],
        out_specs=[col, col, col],
        out_shape=[jax.ShapeDtypeStruct((tokens, 1), F32)] * 3,
        compiler_params=pltpu.CompilerParams(vmem_limit_bytes=VMEM_BYTES),
        cost_estimate=pl.CostEstimate(
            flops=2 * tokens * words * D, bytes_accessed=2 * words * D, transcendentals=tokens * words
        ),
        name="vocab_forward",
    )(hidden, target, table)


def vocab_back_kernel(tile, h_ref, target_ref, norm_ref, rate_ref, table_ref, out_ref):
    step = pl.program_id(0)

    @pl.when(step == 0)
    def _():
        out_ref[...] = jnp.zeros_like(out_ref)

    words = words_of(table_ref)
    block = 256
    word = lax.broadcasted_iota(jnp.int32, (block, tile), 1) + step * tile
    for t in range(0, h_ref.shape[0], block):
        rows = slice(t, t + block)
        logits = product_back(h_ref[rows, :], words)
        probs = jnp.exp(logits - norm_ref[rows, :])
        hit = jnp.where(word == target_ref[rows, :], 1.0, 0.0)
        dlogits = (rate_ref[rows, :] * (hit - probs)).astype(BF)
        out_ref[rows, :] += product(dlogits, words)


def vocab_back(hidden, target, norm, rate, table, tile):
    tokens = hidden.shape[0]
    parts, words, width = table.shape
    col = pl.BlockSpec((tokens, 1), lambda i: (0, 0))
    return pl.pallas_call(
        functools.partial(vocab_back_kernel, tile),
        grid=(words // tile,),
        in_specs=[
            pl.BlockSpec((tokens, D), lambda i: (0, 0)),
            col,
            col,
            col,
            pl.BlockSpec((parts, tile, width), lambda i: (0, i, 0)),
        ],
        out_specs=pl.BlockSpec((tokens, D), lambda i: (0, 0)),
        out_shape=jax.ShapeDtypeStruct((tokens, D), F32),
        compiler_params=pltpu.CompilerParams(vmem_limit_bytes=VMEM_BYTES),
        cost_estimate=pl.CostEstimate(
            flops=4 * tokens * words * D, bytes_accessed=2 * words * D, transcendentals=tokens * words
        ),
        name="vocab_back",
    )(hidden, target, norm, rate, table)


def self_probs(queries, key_heads):
    causal = (
        lax.broadcasted_iota(jnp.int32, (TOK, TOK), 1)
        <= lax.broadcasted_iota(jnp.int32, (TOK, TOK), 0)
    )[None, None]
    scores = jnp.einsum("rqhe,rkhe->rhqk", queries, key_heads, preferred_element_type=F32)
    return jax.nn.softmax(jnp.where(causal, scores, NEG), axis=-1)


def column_parts(gathered):
    return jnp.concatenate([gathered[i] for i in range(gathered.shape[0])], axis=-1)


def block_rows(array, ways):
    rows, columns = array.shape
    width = columns // ways
    return jnp.stack([array[:, i * width : (i + 1) * width] for i in range(ways)])


def local(
    answers,
    targets,
    doc_scores,
    memory,
    lengths,
    self_query,
    self_key,
    self_value,
    query_bias,
    value_bias,
    self_output,
    output_bias,
    first_gain,
    first_shift,
    cross_query,
    crossq_bias,
    cross_key,
    cross_value,
    crossv_bias,
    cross_output,
    crosso_bias,
    second_gain,
    second_shift,
    expand_weight,
    expand_bias,
    shrink_weight,
    shrink_bias,
    third_gain,
    third_shift,
    word_table,
):
    dp_ways, mp_ways = lax.axis_size("dp"), lax.axis_size("mp")
    chips = dp_ways // 2
    dp, mp = lax.axis_index("dp"), lax.axis_index("mp")
    groups = answers.shape[0]
    rows, slots, _ = memory.shape
    piece = rows // dp_ways
    own_q = dp_ways
    uniq = own_q * TOK
    tokens = rows * TOK
    padded = -(-slots // 16) * 16
    shard_rows = rows // mp_ways
    shard_tokens = shard_rows * TOK
    shard_q = own_q // mp_ways
    shard_uniq = shard_q * TOK
    local_heads = H // mp_ways
    head_cols = local_heads * HD
    hidden_cols = expand_weight.shape[1]
    vec = D // dp_ways

    small = jnp.concatenate(
        [
            output_bias,
            first_gain,
            first_shift,
            crosso_bias,
            second_gain,
            second_shift,
            shrink_bias,
            third_gain,
            third_shift,
            query_bias.reshape(-1),
            value_bias.reshape(-1),
            crossq_bias.reshape(-1),
            expand_bias.reshape(-1),
            crossv_bias,
        ]
    )
    sizes = [vec] * 9 + [a.size for a in (query_bias, value_bias, crossq_bias, expand_bias, crossv_bias)]
    small_rows = -(-small.shape[0] // 2048) * 16
    small = jnp.pad(small, (0, small_rows * 128 - small.shape[0])).reshape(small_rows, 128)
    memory_shard = jnp.concatenate([cross_key, cross_value], axis=0)
    wide_rows = cross_key.shape[0]
    self_shard = jnp.concatenate([self_query, self_key, self_value], axis=1)
    target_rows = jnp.pad(targets.reshape(1, -1), ((0, 7), (0, 0)))
    doc_rows = jnp.pad(doc_scores.reshape(1, -1), ((0, 7), (0, 128 - doc_scores.size)))
    wanted = jnp.stack([answers[(2 * c * piece) // K] for c in range(chips)])
    memory_all, small_all, cquery_z, cout_z = exchange(
        [
            (memory_shard, "wide", ""),
            (small, "wide", ""),
            (cross_query, "gather", "z"),
            (cross_output, "gather", "z"),
        ],
        0,
    )
    small_all = small_all.reshape(dp_ways, mp_ways, -1)
    starts = [sum(sizes[:i]) for i in range(len(sizes) + 1)]
    taken = [small_all[:, :, starts[i] : starts[i + 1]] for i in range(len(sizes))]
    (full_obias, gain_one, shift_one, full_cobias, gain_two, shift_two, full_sbias, gain_three, shift_three) = [
        taken[i][:, 0].reshape(D) for i in range(9)
    ]

    def head_bias(part, count, width):
        part = part.reshape(dp_ways, mp_ways, count, width)
        return jnp.transpose(part, (1, 2, 0, 3)).reshape(mp_ways, -1)

    mine = lambda a: lax.dynamic_index_in_dim(a, mp, 0, keepdims=False)
    qbias = mine(head_bias(taken[9], *query_bias.shape))
    vbias = mine(head_bias(taken[10], *value_bias.shape))
    cqbias = head_bias(taken[11], *crossq_bias.shape).reshape(-1)
    ebias = head_bias(taken[12], *expand_bias.shape).reshape(-1)
    cvbias = taken[13].reshape(1, D)
    key_weight = memory_all[:, :, :wide_rows].reshape(D, D)
    value_weight = memory_all[:, :, wide_rows:].reshape(D, D)

    plan = Exchange(
        [
            (expand_weight, "gather", "z"),
            (shrink_weight, "gather", "z"),
            (self_shard, "near", ""),
            (self_output, "near", ""),
            (target_rows, "near", ""),
            (doc_rows, "near", ""),
            (wanted, "nearswap", ""),
            (cquery_z, "near", ""),
            (cout_z, "near", ""),
        ]
    )
    (keys, values, memory_rows, expand_z, shrink_z, self_all, output_all, target_all, doc_all, x_all, cquery_all, cout_all) = (
        memory_products(memory, key_weight, value_weight, cvbias, padded, plan, 1)
    )
    expand_all = lax.all_gather(expand_z, "dp", axis=0, tiled=False)
    shrink_all = lax.all_gather(shrink_z, "dp", axis=0, tiled=False)
    table_all = lax.all_gather(word_table, "dp", axis=0, tiled=False)
    if word_table.shape[1] < 128:
        table_all = column_parts(table_all)[None]
    rows_first = lambda a: jnp.transpose(a, (0, 2, 1, 3)).reshape(dp_ways * a.shape[2], -1)
    columns_first = lambda a: column_parts(a.reshape(dp_ways, -1, a.shape[-1]))
    full_expand = rows_first(expand_all)
    full_shrink = columns_first(shrink_all)
    full_cquery = rows_first(cquery_all)
    full_cout = columns_first(cout_all)
    self_weight = self_all.reshape(D, 3 * head_cols)
    full_output = column_parts(output_all)
    my_group = (dp * piece) // K
    row_targets = lax.dynamic_index_in_dim(
        target_all[:, 0].reshape(dp_ways, groups, TOK), my_group, 1, keepdims=False
    )
    x_rows = x_all.reshape(uniq, D)

    qkv = product(x_rows, self_weight)
    queries = ((qkv[:, :head_cols] + qbias) * SCALE).astype(BF)
    self_keys = qkv[:, head_cols : 2 * head_cols].astype(BF)
    self_values = (qkv[:, 2 * head_cols :] + vbias).astype(BF)
    heads = lambda a: a.reshape(own_q, TOK, local_heads, HD)
    probs = self_probs(heads(queries), heads(self_keys))
    context = jnp.einsum(
        "rhqk,rkhe->rqhe", probs.astype(BF), heads(self_values), preferred_element_type=F32
    )
    context = context.astype(BF).reshape(uniq, head_cols)
    partial = product(context, full_output).astype(BF).reshape(mp_ways, shard_uniq, D)
    (received,) = exchange([(partial, "move", "z")], 2)
    x_own = lax.dynamic_slice_in_dim(x_rows, mp * shard_uniq, shard_uniq, 0)
    first_in = x_own.astype(F32) + added(partial, received, "z") + full_obias
    hidden_one, normed_one, inverse_one = layer_norm(first_in, gain_one, shift_one)
    hidden_low1 = hidden_one.astype(BF)
    cross_queries = ((product(hidden_low1, full_cquery) + cqbias) * SCALE).astype(BF)
    (cross_queries,) = exchange([(cross_queries, "gather", "z")], 3)
    cross_queries = cross_queries.reshape(uniq, D)

    used = jnp.clip(lengths - mp * slots, 0, slots).astype(jnp.int32)
    keep = (
        lax.broadcasted_iota(jnp.int32, (GL, GC), 0) // TOK
        == lax.broadcasted_iota(jnp.int32, (GL, GC), 1) // HD
    ).astype(BF)
    ctx_part, peak_part, total_part = cross_forward(
        used, keys, values, cross_queries, keep, piece, padded
    )
    ctx_part = ctx_part.reshape(mp_ways, shard_tokens, D)
    stat_part = jnp.stack([peak_part, total_part], axis=1).reshape(mp_ways, shard_rows, 2, G, GL)
    ctx_got, stat_got = exchange([(ctx_part, "move", "z"), (stat_part, "move", "z")], 4)
    stat_own = lax.dynamic_index_in_dim(stat_part, mp, 0, keepdims=True)
    stat_got = jnp.concatenate([stat_own, stat_got], axis=0)
    peak_got, total_got = stat_got[:, :, 0], stat_got[:, :, 1]
    peak = jnp.max(peak_got, axis=0)
    weight = total_got * jnp.exp(peak_got - peak)
    total = jnp.sum(weight, axis=0)
    cross_norm = peak + jnp.log(total)
    weight = weight / total

    def to_token_heads(a):
        lead = a.shape[:-3]
        a = a.reshape(lead + (shard_rows, H, TOK))
        return jnp.swapaxes(a, -1, -2).reshape(lead + (shard_tokens, H))

    weight = jnp.repeat(to_token_heads(weight), HD, axis=-1)
    ctx_own = lax.dynamic_index_in_dim(ctx_part, mp, 0, keepdims=False)
    context_two = (
        ctx_own.astype(F32) * weight[0] + jnp.sum(ctx_got.astype(F32) * weight[1:], axis=0)
    ).astype(BF)

    def to_rows(a):
        a = jnp.broadcast_to(a.reshape(shard_q, 1, TOK, D), (shard_q, piece, TOK, D))
        return a.reshape(shard_tokens, D)

    second_in = to_rows(hidden_one) + product(context_two, full_cout) + full_cobias
    hidden_two, normed_two, inverse_two = layer_norm(second_in, gain_two, shift_two)
    hidden_low2 = hidden_two.astype(BF)

    expanded = product(hidden_low2, full_expand) + ebias
    activated = gelu_exact(expanded).astype(BF)
    third_in = hidden_two + product(activated, full_shrink) + full_sbias
    hidden_three, normed_three, inverse_three = layer_norm(third_in, gain_three, shift_three)
    (hidden_low3,) = exchange([(hidden_three.astype(BF), "gather", "z")], 5)
    hidden_low3 = hidden_low3.reshape(tokens, D)

    vocab_local = table_all.shape[1]
    tile = 640 if vocab_local % 640 == 0 else vocab_local
    token_targets = jnp.broadcast_to(
        row_targets.reshape(own_q, 1, TOK), (own_q, piece, TOK)
    ).reshape(tokens, 1)
    local_target = token_targets - mp * vocab_local
    peak, total, picked = vocab_forward(hidden_low3, local_target, table_all, tile)
    stats = jnp.concatenate([peak, total, picked], axis=1).T.reshape(3, tokens // 128, 128)
    (stats,) = exchange([(stats, "gather", "z")], 6)
    stats = stats.reshape(mp_ways, 3, tokens)
    top = jnp.max(stats[:, 0], axis=0)
    norm_log = top + jnp.log(jnp.sum(stats[:, 1] * jnp.exp(stats[:, 0] - top), axis=0))
    loglik = jnp.sum(stats[:, 2], axis=0) - norm_log
    (loglik_all,) = exchange([(loglik.reshape(tokens // 128, 128), "gather", "dp")], 7)
    loglik_all = loglik_all.reshape(dp_ways, own_q, piece, TOK)
    loglik_all = jnp.transpose(loglik_all, (1, 0, 2, 3)).reshape(own_q, groups, K, TOK)
    doc_logp = jax.nn.log_softmax(doc_all[:, 0, : groups * K].reshape(own_q, groups, K), axis=2)
    joined = doc_logp[..., None] + loglik_all
    marginal = jax.nn.logsumexp(joined, axis=2, keepdims=True)
    question_loss = -jnp.mean(
        lax.dynamic_index_in_dim(marginal[:, :, 0], dp, 0, keepdims=False), axis=1
    )
    posterior = jnp.exp(joined - marginal).reshape(own_q, groups * K, TOK)
    rate = -lax.dynamic_slice_in_dim(posterior, dp * piece, piece, 1).reshape(tokens, 1)
    dthree = vocab_back(hidden_low3, local_target, norm_log.reshape(tokens, 1), rate, table_all, tile)
    dthree = dthree.astype(BF).reshape(mp_ways, shard_tokens, D)
    (received,) = exchange([(dthree, "move", "z")], 8)
    dhidden_three = added(dthree, received, "z")

    dthird, dgain_three, dshift_three = norm_back(
        dhidden_three, normed_three, inverse_three, gain_three
    )
    dshrink_bias = jnp.sum(dthird, axis=0)
    dshrink_in = dthird.astype(BF)
    dactivated = product_back(dshrink_in, full_shrink)
    dexpanded = jax.vjp(gelu_exact, expanded)[1](dactivated)[0].astype(BF)
    dexpand_bias = jnp.sum(dexpanded, axis=0, dtype=F32)
    dshrink = weight_grad(activated, dshrink_in)
    dexpand = weight_grad(hidden_low2, dexpanded)
    shrink_dp = lax.psum_scatter(
        block_rows(dshrink.astype(BF), dp_ways), "dp", scatter_dimension=0, tiled=False
    )
    expand_dp = lax.psum_scatter(dexpand.astype(BF), "dp", scatter_dimension=0, tiled=True)
    dhidden_two = dthird + product_back(dexpanded, full_expand)

    dsecond, dgain_two, dshift_two = norm_back(dhidden_two, normed_two, inverse_two, gain_two)
    dcout_bias = jnp.sum(dsecond, axis=0)
    dcout_in = dsecond.astype(BF)
    dcontext_two = product_back(dcout_in, full_cout).astype(BF)
    middle = jnp.sum(
        (dcontext_two.astype(F32) * context_two.astype(F32)).reshape(shard_tokens, H, HD), axis=-1
    )
    middle = jnp.swapaxes(middle.reshape(shard_rows, TOK, H), 1, 2).reshape(shard_rows, G, GL)
    stat_all = jnp.stack([cross_norm, middle])
    dctx_all, stat_all = exchange([(dcontext_two, "gather", "z"), (stat_all, "gather", "z")], 9)
    norm_all = stat_all[:, 0].reshape(rows, G, GL)
    middle_all = stat_all[:, 1].reshape(rows, G, GL)
    dcout = weight_grad(context_two, dcout_in)
    dcross_q, dkeys, dvalues = cross_back(
        used,
        keys,
        values,
        cross_queries,
        dctx_all.reshape(tokens, D),
        norm_all,
        middle_all,
        keep,
        piece,
        padded,
    )
    dcross_q = dcross_q.reshape(mp_ways, shard_uniq, D)
    (received,) = exchange([(dcross_q, "move", "z")], 10)
    dkey_weight, dvalue_weight, dvalue_bias = memory_weights(
        memory_rows, dkeys, dvalues, rows, padded
    )
    dcross_low = (added(dcross_q, received, "z") * SCALE).astype(BF)
    dcquery = weight_grad(hidden_low1, dcross_low)
    dcq_bias = jnp.sum(dcross_low, axis=0, dtype=F32)
    dhidden_one = jnp.sum(dsecond.reshape(shard_q, piece, TOK, D), axis=1).reshape(
        shard_uniq, D
    ) + product_back(dcross_low, full_cquery)

    dfirst, dgain_one, dshift_one = norm_back(dhidden_one, normed_one, inverse_one, gain_one)
    dout_bias = jnp.sum(dfirst, axis=0)
    owners = lambda a: a.reshape(chips, 2, -1, a.shape[-1])
    key_blocks = owners(dkey_weight)
    value_blocks = owners(dvalue_weight)
    cq_blocks = owners(
        jnp.transpose(
            dcquery.astype(BF).reshape(dp_ways, vec, mp_ways, head_cols), (0, 2, 1, 3)
        ).reshape(-1, head_cols)
    )
    co_blocks = owners(block_rows(dcout.astype(BF), dp_ways).reshape(-1, vec))
    first_blocks = [key_blocks, value_blocks, cq_blocks, co_blocks]
    dout_in, *received = exchange(
        [(dfirst.astype(BF), "gather", "z")] + [(a, "move1", "pair") for a in first_blocks], 11
    )
    first_blocks = [added(a, b, "pair").astype(BF) for a, b in zip(first_blocks, received)]
    dout_in = dout_in.reshape(uniq, D)
    doutput = weight_grad(context, dout_in)
    dcontext = heads(product_back(dout_in, full_output).astype(BF))
    dvalue_h = jnp.einsum("rhqk,rqhe->rkhe", probs.astype(BF), dcontext, preferred_element_type=F32)
    dprobs = jnp.einsum("rqhe,rkhe->rhqk", dcontext, heads(self_values), preferred_element_type=F32)
    dscores = (probs * (dprobs - jnp.sum(probs * dprobs, axis=-1, keepdims=True))).astype(BF)
    dquery_h = jnp.einsum("rhqk,rkhe->rqhe", dscores, heads(self_keys), preferred_element_type=F32)
    dkey_h = jnp.einsum("rhqk,rqhe->rkhe", dscores, heads(queries), preferred_element_type=F32)
    flat = lambda a: a.reshape(uniq, head_cols)
    dqkv = jnp.concatenate(
        [flat(dquery_h * SCALE).astype(BF), flat(dkey_h).astype(BF), flat(dvalue_h).astype(BF)], axis=1
    )
    dself = weight_grad(x_rows, dqkv)
    dqkv_bias = jnp.sum(dqkv, axis=0, dtype=F32)
    partial = product_back(dqkv, self_weight).astype(BF).reshape(mp_ways, shard_uniq, D)
    received, key_got = exchange([(partial, "move", "z"), (first_blocks[0], "move", "chips")], 12)
    dinputs = (dfirst + added(partial, received, "z")).astype(BF)

    cast = lambda a: a.astype(BF)
    vectors = jnp.stack(
        [
            dout_bias,
            dgain_one,
            dshift_one,
            dcout_bias,
            dgain_two,
            dshift_two,
            dshrink_bias,
            dgain_three,
            dshift_three,
            dvalue_bias[0],
        ]
    )
    by_dp = lambda a, width: jnp.swapaxes(a.reshape(-1, dp_ways, width), 0, 1).reshape(dp_ways, -1)
    vector_parts = [
        by_dp(vectors, vec),
        by_dp(dcq_bias, crossq_bias.shape[1]),
        by_dp(dexpand_bias, expand_bias.shape[1]),
        by_dp(dqkv_bias[:head_cols], query_bias.shape[1]),
        by_dp(dqkv_bias[2 * head_cols :], value_bias.shape[1]),
    ]
    ends = [sum(a.shape[1] for a in vector_parts[: i + 1]) for i in range(5)]
    vector_blocks = jnp.concatenate(vector_parts, axis=1)
    length = vector_blocks.shape[1]
    vector_rows = -(-length // 1024) * 8
    vector_blocks = owners(
        jnp.pad(vector_blocks, ((0, 0), (0, vector_rows * 128 - length))).reshape(-1, 128)
    )
    dinputs, value_got = exchange(
        [(dinputs, "gather", "z"), (first_blocks[1], "move", "chips")], 13
    )
    answer_blocks = dinputs.reshape(chips, 2, TOK, D)
    self_blocks = owners(cast(dself))
    out_blocks = owners(block_rows(cast(doutput), dp_ways).reshape(-1, vec))
    last_blocks = [self_blocks, out_blocks, answer_blocks, vector_blocks]
    received = exchange([(a, "move1", "pair") for a in last_blocks], 14)
    last_blocks = [added(a, b, "pair").astype(a.dtype) for a, b in zip(last_blocks, received)]
    last_blocks = first_blocks[2:] + last_blocks
    expand_blocks = jnp.transpose(
        expand_dp.reshape(vec, mp_ways, -1), (1, 0, 2)
    )
    shrink_blocks = shrink_dp.reshape(mp_ways, -1, vec)
    plan = Exchange(
        [(a, "move", "chips") for a in last_blocks]
        + [(expand_blocks, "move", "z"), (shrink_blocks, "move", "z")]
    )
    memory_grad, received = memory_back(
        dkeys, dvalues, key_weight, value_weight, rows, slots, padded, plan, 15
    )
    expand_grad = added(expand_blocks, received[6], "z")
    shrink_grad = added(shrink_blocks, received[7], "z")
    cq_sum, co_sum, self_grad, out_grad, answers_own, vector_sum = [
        added(a, b, "chips") if i != 4 else (a, b)
        for i, (a, b) in enumerate(zip(last_blocks, received[:6]))
    ]
    key_sum = added(first_blocks[0], key_got, "chips")
    value_sum = added(first_blocks[1], value_got, "chips")
    zblocks = [
        cast(key_sum).reshape(mp_ways, wide_rows, D),
        cast(value_sum).reshape(mp_ways, wide_rows, D),
        cast(cq_sum).reshape(mp_ways, vec, head_cols),
        cast(co_sum).reshape(mp_ways, head_cols, vec),
    ]
    *got_z, vector_all = exchange(
        [(a, "move", "z") for a in zblocks] + [(vector_sum, "gather", "z")], 16
    )
    key_grad, value_grad, cquery_grad, cout_grad = [
        added(a, b, "z") for a, b in zip(zblocks, got_z)
    ]
    vector_all = vector_all.reshape(mp_ways, -1)
    vector_own = jnp.sum(vector_all, axis=0)
    head_own = lax.dynamic_index_in_dim(vector_all, mp, 0, keepdims=False)

    mine_a, others = answers_own
    mine_a = lax.dynamic_index_in_dim(mine_a, dp // 2, 0, keepdims=False)
    returned = jnp.concatenate([mine_a[None], others], axis=0).astype(F32)
    source = lax.rem(dp // 2 + chips - jnp.arange(chips), chips)
    place = (2 * source * piece) // K
    pick = (place[None, :] == jnp.arange(groups)[:, None]).astype(F32)
    answer_grad = jnp.sum(pick[:, :, None, None] * returned[None], axis=1)

    def vec_of(i):
        return vector_own[i * vec : (i + 1) * vec]

    def mp_rows(start, shape):
        part = vector_own[start : start + mp_ways * shape[0] * shape[1]]
        part = part.reshape(mp_ways, shape[0], shape[1])
        return lax.dynamic_index_in_dim(part, mp, 0, keepdims=False)

    return (
        question_loss,
        answer_grad,
        memory_grad,
        self_grad[:, :head_cols],
        self_grad[:, head_cols : 2 * head_cols],
        self_grad[:, 2 * head_cols :],
        head_own[ends[2] : ends[3]].reshape(query_bias.shape),
        head_own[ends[3] : ends[4]].reshape(value_bias.shape),
        out_grad,
        vec_of(0),
        vec_of(1),
        vec_of(2),
        cquery_grad,
        mp_rows(ends[0], crossq_bias.shape),
        key_grad,
        value_grad,
        lax.dynamic_slice_in_dim(vec_of(9), mp * wide_rows, wide_rows, 0),
        cout_grad,
        vec_of(3),
        vec_of(4),
        vec_of(5),
        expand_grad,
        mp_rows(ends[1], expand_bias.shape),
        shrink_grad,
        vec_of(6),
        vec_of(7),
        vec_of(8),
    )


def solution(mesh):
    placed = (
        P("dp", None, None),
        P("dp", None),
        P("dp", None),
        P("dp", "mp", None),
        P("dp"),
        P("dp", "mp"),
        P("dp", "mp"),
        P("dp", "mp"),
        P("mp", "dp"),
        P("mp", "dp"),
        P("mp", "dp"),
        P("dp"),
        P("dp"),
        P("dp"),
        P("dp", "mp"),
        P("mp", "dp"),
        P(("dp", "mp"), None),
        P(("dp", "mp"), None),
        P(("dp", "mp")),
        P("mp", "dp"),
        P("dp"),
        P("dp"),
        P("dp"),
        P("dp", "mp"),
        P("mp", "dp"),
        P("mp", "dp"),
        P("dp"),
        P("dp"),
        P("dp"),
        P("mp", "dp"),
    )
    return jax.shard_map(
        local,
        mesh=mesh,
        in_specs=placed,
        out_specs=(
            P("dp"),
            P("dp", None, None),
            P("dp", "mp", None),
            P("dp", "mp"),
            P("dp", "mp"),
            P("dp", "mp"),
            P("mp", "dp"),
            P("mp", "dp"),
            P("mp", "dp"),
            P("dp"),
            P("dp"),
            P("dp"),
            P("dp", "mp"),
            P("mp", "dp"),
            P(("dp", "mp"), None),
            P(("dp", "mp"), None),
            P(("dp", "mp")),
            P("mp", "dp"),
            P("dp"),
            P("dp"),
            P("dp"),
            P("dp", "mp"),
            P("mp", "dp"),
            P("mp", "dp"),
            P("dp"),
            P("dp"),
            P("dp"),
        ),
        check_vma=False,
    )
```

time: 2520 us -> 931 us (0.37)
  waiting for transfers between devices: 1450 us -> 1.47 us
  Pallas kernels: 0 us -> 634 us
  blocking collectives: 343 us -> 0 us
  matrix products: 293 us -> 63.9 us
  local copies, waits for them, and re-layouts: 238 us -> 132 us
  starting transfers between devices: 75 us -> 0.54 us
    psum x7 -> x0, waiting for transfers between devices: 947 us -> none  [head_sum(): return lax.psum(partial_term, 'mp')]
    pallas_call x0 -> x22, Pallas kernels: none -> 634 us  [the longest x15 389 us: exchange(): pl.pallas_call(functools.partial(exchange_kernel, plan), out_shape=plan.s...]
    all_to_all x8 -> x0, waiting for transfers between devices: 237 us -> none  [the longest x1 232 us: local(): lax.all_to_all(low_dvalues, 'mp', split_axis=1, concat_axis=2, tiled=True)]
    dot_general x26 -> x12, matrix products: 222 us -> 23.4 us  [the longest x6 20.5 us: product(): return jnp.dot(former, latter, preferred_element_type=F32)]
    all_gather x21 -> x0, blocking collectives: 199 us -> none  [the longest x2 26.2 us: combined_all(): gathered = jax.tree.map(lambda a: lax.all_gather(a, axis), part)]
    all_gather x5 -> x3, waiting for transfers between devices: 166 us -> 0.04 us  [the longest x1 0.02 us: local(): expand_all = lax.all_gather(expand_z, 'dp', axis=0, tiled=False)]
    unnamed x3 -> x0, blocking collectives: 128 us -> none
    unnamed x32 -> x5, waiting for transfers between devices: 105 us -> 1.43 us
  transfers between devices with their start and end apart: 31 -> 5, of which waited for: 10 -> 0; matrix products, arithmetic and copies ran while one was open for 16% -> 17% of each run, Pallas kernels for 0% -> 34%
where the time goes in v1:
time: 931 us; the launch traced here: 918 us
  Pallas kernels  634 us (68%)
  local copies, waits for them, and re-layouts  132 us (14%)
  other arithmetic  69.5 us (7%)
  matrix products  63.9 us (7%)
  between operations  16.6 us (2%)
    pallas_call x15, Pallas kernels, exchange(): pl.pallas_call(functools.partial(exchange_kernel, plan), out_shape=plan.s...  389 us
    pallas_call x2, Pallas kernels, memory_call(): pl.pallas_call(functools.partial(beside, plan, kernel, len(inputs), len(o...  117 us
    pallas_call x1, Pallas kernels, vocab_back(): pl.pallas_call(functools.partial(vocab_back_kernel, tile), grid=(words //...  42.7 us
    unnamed x266, local copies, waits for them, and re-layouts  39.2 us
    dot_general x6, matrix products, product_back(): lax.dot_general(former, latter, (((1,), (1,)), ((), ())), preferred_eleme...  28.5 us
    pallas_call x1, Pallas kernels, memory_weights(): pl.pallas_call(memory_weight_kernel, grid=(rows // BACK_BLOCK,), in_specs...  25.1 us
    pallas_call x1, Pallas kernels, vocab_forward(): pl.pallas_call(functools.partial(vocab_kernel, tile), grid=(words // tile...  25 us
    pallas_call x1, Pallas kernels, cross_back(): pl.pallas_call(functools.partial(cross_back_kernel, piece, padded), grid_...  20.6 us
  transfers between devices with their start and end apart: 5, of which 0 were waited for; matrix products, arithmetic and copies ran while one was open for 17% of the time, Pallas kernels for 34%

profile of v1, /device:TPU:0, one launch (start us, length us, event | category | flops | bytes accessed | tf_op | source)
XLA Modules:
  0.0 918.0 jit_solution(745623744200172190)
XLA Ops:
  11.8 6.8 concatenate.40
  20.7 44.2 %exchange_0.1 = (bf16[8,4,64,1024]{3,2,1,0:T(8,128)(2,1)}, bf16[8,4,16,128]{3,2,1,0:T(8,128)(2,1)}, bf16[4,128,256]{2,1,0:T(8,128)(2,1)}, bf16[4,256,128]{2,1,0:T(8,128)(2,1)}) custom-call(bf16[64,1024]{1,0:T(8,128)(2,1)} %pad_maximum_fusion.2.refs_0_, bf16[16,128]{1,0:T(8,128)(2,1)} %pad_bitcast_fusion.1.refs_1_, bf16[128,256]{1,0:T(8,128)(2,1)} %refs_2_.1, ...), custom_call_target="tpu_custom_call" | custom-call | tf_op jit(solution)/shard_map/exchange_0/pallas_call | solution.py:272
  65.0 5.1 fusion.154
  72.8 63.4 %memory_products.1 = (bf16[3584,1024]{1,0:T(8,128)(2,1)}, bf16[3584,1024]{1,0:T(8,128)(2,1)}, bf16[3584,1024]{1,0:T(8,128)(2,1)}, bf16[4,128,1024]{2,1,0:T(8,128...) custom-call(bf16[100,32,1024]{2,1,0:T(8,128)(2,1)} %bitcast.686, ...), custom_call_target="tpu_custom_call" | custom-call | flops 15032385536 | bytes 75161928 | tf_op jit(solution)/shard_map/memory_products/pallas_call | solution.py:309
  145.3 17.2 %exchange_2.1 = bf16[3,64,1024]{2,1,0:T(8,128)(2,1)} custom-call(bf16[4,64,1024]{2,1,0:T(8,128)(2,1)} %bitcast.588), custom_call_target="tpu_custom_call" | custom-call | tf_op jit(solution)/shard_map/exchange_2/pallas_call | solution.py:272
  162.6 3.2 copy.331
  169.5 15.7 %exchange_3.1 = bf16[4,64,1024]{2,1,0:T(8,128)(2,1)} custom-call(bf16[64,1024]{1,0:T(8,128)(2,1)} %fusion.48.refs_0_), custom_call_target="tpu_custom_call" | custom-call | tf_op jit(solution)/shard_map/exchange_3/pallas_call | solution.py:272
  186.6 15.3 %cross_forward.1 = (bf16[1024,1024]{1,0:T(8,128)(2,1)}, f32[32,4,128]{2,1,0:T(4,128)}, f32[32,4,128]{2,1,0:T(4,128)}) custom-call(s32[32]{0:T(128)} %subtract_clamp_fusion.used, bf16[3584,1024]{1,0:T(8,128)(2,1)} %get-tuple-element.94.k_ref, bf16[3584,1024]{1,0:T(8,128)(2,1)} %get-tuple-element.95.v_ref, bf16[256,1024]{1,0:T(8,128)(2,1)} %bitcast.567, ...), custom_call_target="tpu_custom_call" | custom-call | flops 1879048192 | bytes 14680064 | tf_op jit(solution)/shard_map/cross_forward/pallas_call | solution.py:480
  203.5 52.1 %exchange_4.1 = (bf16[3,256,1024]{2,1,0:T(8,128)(2,1)}, f32[3,8,2,4,128]{4,3,2,1,0:T(4,128)}) custom-call(bf16[4,256,1024]{2,1,0:T(8,128)(2,1)} %bitcast.584, f32[4,8,2,4,128]{4,3,2,1,0:T(4,128)} %pad_maximum_fusion.1.refs_1_), custom_call_target="tpu_custom_call" | custom-call | tf_op jit(solution)/shard_map/exchange_4/pallas_call | solution.py:272
  266.7 2.4 copy.340
  269.8 1.9 fusion.155
  276.6 12.4 %copy.341 = bf16[8,4,128,1024]{2,0,3,1:T(8,128)(2,1)} copy(bf16[8,4,128,1024]{3,2,1,0:T(8,128)(2,1)} %bitcast.556) | data formatting | bytes 16777216 | tf_op jit(solution)/shard_map/all_gather | solution.py:805
  289.0 4.6 fusion.153
  297.5 14.1 %multiply_convert_fusion = (bf16[256,4096]{1,0:T(8,128)(2,1)S(1)}, f32[256,4096]{1,0:T(8,128)}, f32[256,4096]{1,0:T(8,128)}) fusion(f32[4096]{0:T(1024)S(1)} %copy-done.87, bf16[512,8,8,128]{3,2,1,0:T(8,128)(2,1)S(1)} %bitcast.559, f32[256,1024]{1,0:T(8,128)S(1)} %get-tuple-element.291, f32[1024]{0:T(1024)S(1)} %bitcast.654, f32[1024]{0:T(1024)S(1)} %bitcast.645, ...), kind=kOutput, calls=%fused_computation.14 | convolution fusion | flops 2218000384 | bytes 19949568 | tf_op jit(solution)/shard_map/dot_general | solution.py:30
  311.7 2.5 fusion.162
  315.5 38.9 %exchange_5.1 = bf16[4,256,1024]{2,1,0:T(8,128)(2,1)} custom-call(bf16[256,1024]{1,0:T(8,128)(2,1)} %add_convert_fusion.1.refs_0_), custom_call_target="tpu_custom_call" | custom-call | tf_op jit(solution)/shard_map/exchange_5/pallas_call | solution.py:272
  354.4 25.0 %vocab_forward.1 = (f32[1024,1]{1,0:T(8,128)}, f32[1024,1]{1,0:T(8,128)}, f32[1024,1]{1,0:T(8,128)}) custom-call(bf16[1024,1024]{1,0:T(8,128)(2,1)} %bitcast.595, s32[1024,1]{1,0:T(8,128)} %sub.311.target_ref, bf16[8,6400,128]{2,1,0:T(8,128)(2,1)} %bitcast.684), custom_call_target="tpu_custom_call" | custom-call | flops 13421772800 | bytes 13107200 | tf_op jit(solution)/shard_map/vocab_forward/pallas_call | solution.py:602
  383.8 15.6 %exchange_6.1 = f32[4,3,8,128]{3,2,1,0:T(8,128)} custom-call(f32[3,8,128]{2,1,0:T(8,128)} %bitcast.669), custom_call_target="tpu_custom_call" | custom-call | tf_op jit(solution)/shard_map/exchange_6/pallas_call | solution.py:272
  400.9 5.3 exchange_7.1
  412.0 42.7 %vocab_back.1 = f32[1024,1024]{1,0:T(8,128)} custom-call(bf16[1024,1024]{1,0:T(8,128)(2,1)} %bitcast.596, s32[1024,1]{1,0:T(8,128)} %sub.311.target_ref, f32[1024,1]{1,0:T(8,128)} %copy.352.norm_ref, f32[1024,1]{1,0:T(8,128)} %neg.21.rate_ref, bf16[8,6400,128]{2,1,0:T(8,128)(2,1)} %bitcast.685), custom_call_target="tpu_custom_call" | custom-call | flops 26843545600 | bytes 13107200 | tf_op jit(solution)/shard_map/vocab_back/pallas_call | solution.py:643
  454.6 3.9 convert_element_type.586
  458.5 39.1 %exchange_8.1 = bf16[3,256,1024]{2,1,0:T(8,128)(2,1)} custom-call(bf16[4,256,1024]{2,1,0:T(8,128)(2,1)} %bitcast.550), custom_call_target="tpu_custom_call" | custom-call | tf_op jit(solution)/shard_map/exchange_8/pallas_call | solution.py:272
  497.6 1.8 convert_reduce_fusion.1
  499.4 2.3 multiply_reduce_fusion.2
  502.7 13.2 %convert_reduce_fusion = (f32[4096]{0:T(1024)S(1)}, bf16[256,4096]{1,0:T(8,128)(2,1)}) fusion(f32[256,4096]{1,0:T(8,128)} %get-tuple-element.227, f32[256,4096]{1,0:T(8,128)} %get-tuple-element.292, bf16[4096,1024]{1,0:T(8,128)(2,1)} %copy-done.63, f32[256,1024]{1,0:T(8,128)S(1)} %get-tuple-element.218), kind=kOutput, calls=%fused_computation.12 | convolution fusion | flops 2164518912 | bytes 19939328 | tf_op jit(solution)/shard_map/dot_general | solution.py:34
  516.0 5.9 multiply_reduce_fusion.3
  521.9 5.9 convolution_convert_fusion.1
  527.9 2.2 fusion.147
  530.1 3.1 convert_multiply_fusion.1
  536.7 61.9 %exchange_9.1 = (bf16[4,256,1024]{2,1,0:T(8,128)(2,1)}, f32[4,2,8,4,128]{4,3,2,1,0:T(4,128)}) custom-call(bf16[256,1024]{1,0:T(8,128)(2,1)} %get-tuple-element.297.refs_0_, f32[2,8,4,128]{3,2,1,0:T(4,128)} %pad_maximum_fusion.4.refs_1_), custom_call_target="tpu_custom_call" | custom-call | tf_op jit(solution)/shard_map/exchange_9/pallas_call | solution.py:272
  600.2 20.6 %cross_back.1 = (bf16[256,1024]{1,0:T(8,128)(2,1)}, bf16[3584,1024]{1,0:T(8,128)(2,1)}, bf16[3584,1024]{1,0:T(8,128)(2,1)}) custom-call(s32[32]{0:T(128)} %subtract_clamp_fusion.used, bf16[3584,1024]{1,0:T(8,128)(2,1)} %get-tuple-element.94.k_ref, bf16[3584,1024]{1,0:T(8,128)(2,1)} %get-tuple-element.95.v_ref, bf16[256,1024]{1,0:T(8,128)(2,1)} %bitcast.568, ...), custom_call_target="tpu_custom_call" | custom-call | flops 4697620480 | bytes 29360128 | tf_op jit(solution)/shard_map/cross_back/pallas_call | solution.py:539
  620.7 13.7 %exchange_10.1 = bf16[3,64,1024]{2,1,0:T(8,128)(2,1)} custom-call(bf16[4,64,1024]{2,1,0:T(8,128)(2,1)} %bitcast.612), custom_call_target="tpu_custom_call" | custom-call | tf_op jit(solution)/shard_map/exchange_10/pallas_call | solution.py:272
  635.6 3.5 multiply_reduce_fusion.11
  643.5 2.4 convolution_convert_fusion
  661.8 2.8 reshape.842
  664.6 3.8 copy.356
  668.3 25.1 %memory_weights.1 = (bf16[1024,1024]{1,0:T(8,128)(2,1)}, bf16[1024,1024]{1,0:T(8,128)(2,1)}, f32[1,1024]{1,0:T(1,128)}) custom-call(bf16[3584,1024]{1,0:T(8,128)(2,1)} %get-tuple-element.112.rows_ref, bf16[3584,1024]{1,0:T(8,128)(2,1)} %get-tuple-element.113.dk_ref.refs_0_, bf16[3584,1024]{1,0:T(8,128)(2,1)} %get-tuple-element.114.dv_ref.refs_1_), custom_call_target="tpu_custom_call" | custom-call | flops 15032385536 | bytes 22020096 | tf_op jit(solution)/shard_map/memory_weights/pallas_call | solution.py:394
  693.4 15.8 %exchange_11.1 = (bf16[4,64,1024]{2,1,0:T(8,128)(2,1)}, bf16[1,4,128,1024]{3,2,1,0:T(8,128)(2,1)}, bf16[1,4,128,1024]{3,2,1,0:T(8,128)(2,1)}, bf16[1,4,512,256]{3,2,1,0:T(8,128)(2,1)}, bf16[1,4,1024,128]{3,2,1,0:T(8,128)(2,1)}) custom-call(bf16[64,1024]{1,0:T(8,128)(2,1)} %convert_element_type.600.refs_0_, bf16[4,2,128,1024]{3,2,1,0:T(8,128)(2,1)} %bitcast.571, ...), custom_call_target="tpu_custom_call" | custom-call | tf_op jit(solution)/shard_map/exchange_11/pallas_call | solution.py:272
  726.4 2.6 fusion.23.refs_1_
  730.4 17.2 %exchange_12.1 = (bf16[3,64,1024]{2,1,0:T(8,128)(2,1)}, bf16[3,128,1024]{2,1,0:T(8,128)(2,1)}) custom-call(bf16[4,64,1024]{2,1,0:T(8,128)(2,1)} %bitcast.586, bf16[4,128,1024]{2,1,0:T(8,128)(2,1)} %fusion.23.refs_1_), custom_call_target="tpu_custom_call" | custom-call | tf_op jit(solution)/shard_map/exchange_12/pallas_call | solution.py:272
  750.3 2.9 fusion.22.refs_1_
  753.2 15.2 %exchange_13.1 = (bf16[4,64,1024]{2,1,0:T(8,128)(2,1)}, bf16[3,128,1024]{2,1,0:T(8,128)(2,1)}) custom-call(bf16[64,1024]{1,0:T(8,128)(2,1)} %fusion.85.refs_0_, bf16[4,128,1024]{2,1,0:T(8,128)(2,1)} %fusion.22.refs_1_), custom_call_target="tpu_custom_call" | custom-call | tf_op jit(solution)/shard_map/exchange_13/pallas_call | solution.py:272
  769.1 1.9 convolution_convert_fusion.4
  770.9 5.2 exchange_14.1
  790.8 53.1 %memory_back.1 = (f32[100,32,1024]{2,1,0:T(8,128)}, bf16[3,512,256]{2,1,0:T(8,128)(2,1)}, bf16[3,1024,128]{2,1,0:T(8,128)(2,1)}, bf16[3,128,768]{2,1,0:T(8,128)(...) custom-call(bf16[3584,1024]{1,0:T(8,128)(2,1)} %get-tuple-element.11, ...), custom_call_target="tpu_custom_call" | custom-call | flops 15032385536 | bytes 75161928 | tf_op jit(solution)/shard_map/memory_back/pallas_call | solution.py:309
  850.3 32.3 %exchange_16.1 = (bf16[3,32,1024]{2,1,0:T(8,128)(2,1)}, bf16[3,32,1024]{2,1,0:T(8,128)(2,1)}, bf16[3,128,256]{2,1,0:T(8,128)(2,1)}, bf16[3,256,128]{2,1,0:T(8,128)(2,1)}, f32[4,16,128]{2,1,0:T(8,128)}) custom-call(bf16[4,32,1024]{2,1,0:T(8,128)(2,1)} %fusion.65.refs_0_, bf16[4,32,1024]{2,1,0:T(8,128)(2,1)} %fusion.64.refs_1_, ...), custom_call_target="tpu_custom_call" | custom-call | tf_op jit(solution)/shard_map/exchange_16/pallas_call | solution.py:272
  885.3 1.8 convert_add_fusion.7
  898.5 12.5 %copy.523 = f32[32,100,1024]{2,0,1:T(8,128)} copy(f32[32,100,1024]{2,0,1:T(8,128)} %bitcast.546) | data formatting | bytes 26214400
  (532 shorter events, 141.7 us)
Async XLA Ops:
  7.2 269.4 %all-gather.7.cloned.1.call-start = ((), (), s32[]{:S(2)}) async-start(), calls=%async_computation.4 | async-start | bytes 9437184 | tf_op jit(solution)/shard_map/all_gather | solution.py:805
  136.2 152.8 %all-gather.9.cloned.1.call-start = ((), (), s32[]{:S(2)}) async-start(), calls=%async_computation.5 | async-start | bytes 9437184 | tf_op jit(solution)/shard_map/all_gather | solution.py:806
  136.9 217.5 %all-gather.11.cloned.1.call-start = ((), (), s32[]{:S(2)}) async-start(), calls=%async_computation.6 | async-start | bytes 14745600 | tf_op jit(solution)/shard_map/all_gather | solution.py:807
  137.7 650.2 %reduce-scatter.3.cloned.1.call-start = ((), (), s32[]{:S(2)}) async-start(), calls=%async_computation.2 | async-start | bytes 9437184 | tf_op jit(solution)/shard_map/reduce_scatter | solution.py:932
  140.5 22.1 %copy-start.23 = (bf16[8,32,4,64]{3,2,1,0:T(4,128)(2,1)}, bf16[8,32,4,64]{3,2,1,0:T(4,128)(2,1)S(1)}, u32[]{:S(2)}) copy-start(bf16[8,32,4,64]{3,2,1,0:T(4,128)(2,1)S(1)} %reshape.820) | copy-start | bytes 393220
  140.9 21.7 %copy-start.28 = (f32[8,4,32,32]{2,3,1,0:T(8,128)}, f32[8,4,32,32]{2,3,1,0:T(8,128)S(1)}, u32[]{:S(2)}) copy-start(f32[8,4,32,32]{2,3,1,0:T(8,128)S(1)} %convolution_select_fusion) | copy-start | bytes 393220
  143.2 19.4 %copy-start.37 = (bf16[256,256]{1,0:T(8,128)(2,1)}, bf16[256,256]{1,0:T(8,128)(2,1)S(1)}, u32[]{:S(2)}) copy-start(bf16[256,256]{1,0:T(8,128)(2,1)S(1)} %reshape.821) | copy-start | bytes 393220
  162.6 22.7 %copy-start.98 = (s32[32]{0:T(128)S(1)}, s32[32]{0:T(128)}, u32[]{:S(2)}) copy-start(s32[32]{0:T(128)} %param.34) | copy-start | bytes 388
  165.8 36.1 %copy-start.5 = (bf16[8,128,4,256]{1,0,3,2:T(8,128)(2,1)}, bf16[8,128,4,256]{1,0,3,2:T(8,128)(2,1)S(1)}, u32[]{:S(2)}) copy-start(bf16[8,128,4,256]{1,0,3,2:T(8,128)(2,1)S(1)} %copy.331) | copy-start | bytes 6291460
  166.6 35.3 %copy-start.70 = (f32[8,1,128]{2,1,0:T(1,128)}, f32[8,1,128]{2,1,0:T(1,128)S(1)}, u32[]{:S(2)}) copy-start(f32[8,1,128]{2,1,0:T(1,128)S(1)} %get-tuple-element.263) | copy-start | bytes 12292
  166.6 145.0 %copy-start.61 = (f32[8,1,128]{2,1,0:T(1,128)}, f32[8,1,128]{2,1,0:T(1,128)S(1)}, u32[]{:S(2)}) copy-start(f32[8,1,128]{2,1,0:T(1,128)S(1)} %get-tuple-element.260) | copy-start | bytes 12292
  166.6 145.0 %copy-start.66 = (f32[8,1,128]{2,1,0:T(1,128)}, f32[8,1,128]{2,1,0:T(1,128)S(1)}, u32[]{:S(2)}) copy-start(f32[8,1,128]{2,1,0:T(1,128)S(1)} %get-tuple-element.259) | copy-start | bytes 12292
  166.6 147.8 %copy-start.75 = (f32[8,1,128]{2,1,0:T(1,128)}, f32[8,1,128]{2,1,0:T(1,128)S(1)}, u32[]{:S(2)}) copy-start(f32[8,1,128]{2,1,0:T(1,128)S(1)} %get-tuple-element.257) | copy-start | bytes 12292
  167.7 18.9 %copy-start.93 = (f32[64]{0:T(128)}, f32[64]{0:T(128)S(1)}, u32[]{:S(2)}) copy-start(f32[64]{0:T(128)S(1)} %broadcast_multiply_fusion.8) | copy-start | bytes 772
  167.9 18.7 %copy-start.95 = (f32[64]{0:T(128)}, f32[64]{0:T(128)S(1)}, u32[]{:S(2)}) copy-start(f32[64]{0:T(128)S(1)} %add_rsqrt_fusion.2) | copy-start | bytes 772
  168.1 33.8 %copy-start.19 = (f32[64,1024]{1,0:T(8,128)}, f32[64,1024]{1,0:T(8,128)S(1)}, u32[]{:S(2)}) copy-start(f32[64,1024]{1,0:T(8,128)S(1)} %multiply_add_fusion.1) | copy-start | bytes 786436
  201.9 56.9 %copy-start.79 = (bf16[8,4,128]{2,1,0:T(4,128)(2,1)S(1)}, bf16[8,4,128]{2,1,0:T(4,128)(2,1)}, u32[]{:S(2)}) copy-start(bf16[8,4,128]{2,1,0:T(4,128)(2,1)} %slice.530) | copy-start | bytes 24580
  275.7 36.0 %copy-start.80 = (f32[256]{0:T(256)}, f32[256]{0:T(256)S(1)}, u32[]{:S(2)}) copy-start(f32[256]{0:T(256)S(1)} %broadcast_multiply_fusion.5) | copy-start | bytes 3076
  276.0 35.7 %copy-start.84 = (f32[256]{0:T(256)}, f32[256]{0:T(256)S(1)}, u32[]{:S(2)}) copy-start(f32[256]{0:T(256)S(1)} %add_rsqrt_fusion.1) | copy-start | bytes 3076
  296.5 15.1 %copy-start.63 = (bf16[4096,1024]{1,0:T(8,128)(2,1)}, bf16[4096,1024]{1,0:T(8,128)(2,1)S(1)}, u32[]{:S(2)}) copy-start(bf16[4096,1024]{1,0:T(8,128)(2,1)S(1)} %constant_dynamic-update-slice_fusion.16) | copy-start | bytes 25165828
  297.5 14.2 %copy-start.97 = (f32[8,1,128]{2,1,0:T(1,128)S(1)}, f32[8,1,128]{2,1,0:T(1,128)}, u32[]{:S(2)}) copy-start(f32[8,1,128]{2,1,0:T(1,128)} %get-tuple-element.258) | copy-start | bytes 12292
  314.2 65.3 %copy-start.82 = (f32[256]{0:T(256)}, f32[256]{0:T(256)S(1)}, u32[]{:S(2)}) copy-start(f32[256]{0:T(256)S(1)} %broadcast_multiply_fusion.4) | copy-start | bytes 3076
  314.4 65.0 %copy-start.90 = (f32[256]{0:T(256)}, f32[256]{0:T(256)S(1)}, u32[]{:S(2)}) copy-start(f32[256]{0:T(256)S(1)} %add_rsqrt_fusion) | copy-start | bytes 3076
  458.5 40.9 %copy-start.76 = (f32[8,1,128]{2,1,0:T(1,128)S(1)}, f32[8,1,128]{2,1,0:T(1,128)}, u32[]{:S(2)}) copy-start(f32[8,1,128]{2,1,0:T(1,128)} %copy-done.75) | copy-start | bytes 12292
  458.5 40.9 %copy-start.83 = (f32[256]{0:T(256)S(1)}, f32[256]{0:T(256)}, u32[]{:S(2)}) copy-start(f32[256]{0:T(256)} %copy-done.82) | copy-start | bytes 3076
  458.5 40.9 %copy-start.91 = (f32[256]{0:T(256)S(1)}, f32[256]{0:T(256)}, u32[]{:S(2)}) copy-start(f32[256]{0:T(256)} %copy-done.90) | copy-start | bytes 3076
  499.4 16.5 %slice-start.2 = ((s8[8388608]{0:T(1024)(128)(4,1)}), s8[4194304]{0:T(1024)(128)(4,1)S(1)}, s32[]{:S(2)}) async-start(s8[8388608]{0:T(1024)(128)(4,1)} %bitcast.560), calls=%async_computation.9 | async-start | bytes 8388608
  502.7 13.2 %copy-start.11 = (f32[256,1024]{1,0:T(8,128)}, f32[256,1024]{1,0:T(8,128)S(1)}, u32[]{:S(2)}) copy-start(f32[256,1024]{1,0:T(8,128)S(1)} %get-tuple-element.218) | copy-start | bytes 3145732
  502.7 13.2 %slice-start.3 = ((s8[8388608]{0:T(1024)(128)(4,1)}), s8[4194304]{0:T(1024)(128)(4,1)S(1)}, s32[]{:S(2)}) async-start(s8[8388608]{0:T(1024)(128)(4,1)} %bitcast.560), calls=%async_computation.10 | async-start | bytes 8388608
  502.7 13.2 %copy-start.62 = (f32[8,1,128]{2,1,0:T(1,128)S(1)}, f32[8,1,128]{2,1,0:T(1,128)}, u32[]{:S(2)}) copy-start(f32[8,1,128]{2,1,0:T(1,128)} %copy-done.61) | copy-start | bytes 12292
  502.7 13.3 %copy-start.81 = (f32[256]{0:T(256)S(1)}, f32[256]{0:T(256)}, u32[]{:S(2)}) copy-start(f32[256]{0:T(256)} %copy-done.80) | copy-start | bytes 3076
  502.7 13.3 %copy-start.85 = (f32[256]{0:T(256)S(1)}, f32[256]{0:T(256)}, u32[]{:S(2)}) copy-start(f32[256]{0:T(256)} %copy-done.84) | copy-start | bytes 3076
  527.8 263.0 %reduce-scatter.5.cloned.1.call-start = ((), (), s32[]{:S(2)}) async-start(), calls=%async_computation.3 | async-start | bytes 9437184 | tf_op jit(solution)/shard_map/reduce_scatter | solution.py:929
  600.1 35.4 %copy-start.71 = (f32[8,1,128]{2,1,0:T(1,128)S(1)}, f32[8,1,128]{2,1,0:T(1,128)}, u32[]{:S(2)}) copy-start(f32[8,1,128]{2,1,0:T(1,128)} %copy-done.70) | copy-start | bytes 12292
  600.2 35.4 %copy-start.94 = (f32[64]{0:T(128)S(1)}, f32[64]{0:T(128)}, u32[]{:S(2)}) copy-start(f32[64]{0:T(128)} %copy-done.93) | copy-start | bytes 772
  600.2 35.4 %copy-start.96 = (f32[64]{0:T(128)S(1)}, f32[64]{0:T(128)}, u32[]{:S(2)}) copy-start(f32[64]{0:T(128)} %copy-done.95) | copy-start | bytes 772
  693.4 15.8 %copy-start.18 = (bf16[256,1024]{1,0:T(8,128)(2,1)S(1)}, bf16[256,1024]{1,0:T(8,128)(2,1)}, u32[]{:S(2)}) copy-start(bf16[256,1024]{1,0:T(8,128)(2,1)} %copy-done.17) | copy-start | bytes 1572868
  693.4 17.4 %copy-start.69 = (f32[8,4,32]{2,1,0:T(4,128)S(1)}, f32[8,4,32]{2,1,0:T(4,128)}, u32[]{:S(2)}) copy-start(f32[8,4,32]{2,1,0:T(4,128)} %copy-done.68) | copy-start | bytes 12292
  713.9 15.1 %copy-start.7 = (bf16[8,128,768]{2,1,0:T(8,128)(2,1)S(1)}, bf16[8,128,768]{2,1,0:T(8,128)(2,1)}, u32[]{:S(2)}) copy-start(bf16[8,128,768]{2,1,0:T(8,128)(2,1)} %get-tuple-element.92) | copy-start | bytes 4718596
  718.0 30.7 %copy-start.26 = (f32[64,1024]{1,0:T(8,128)S(1)}, f32[64,1024]{1,0:T(8,128)}, u32[]{:S(2)}) copy-start(f32[64,1024]{1,0:T(8,128)} %copy-done.25) | copy-start | bytes 786436
  730.4 38.1 %copy-start.29 = (bf16[4,64,1024]{2,1,0:T(8,128)(2,1)S(1)}, bf16[4,64,1024]{2,1,0:T(8,128)(2,1)}, u32[]{:S(2)}) copy-start(bf16[4,64,1024]{2,1,0:T(8,128)(2,1)} %get-tuple-element.117) | copy-start | bytes 1572868
  730.4 38.1 %copy-start.38 = (bf16[256,256]{1,0:T(8,128)(2,1)S(1)}, bf16[256,256]{1,0:T(8,128)(2,1)}, u32[]{:S(2)}) copy-start(bf16[256,256]{1,0:T(8,128)(2,1)} %copy-done.37) | copy-start | bytes 393220
  747.5 21.5 %copy-start.16 = (bf16[8,32,1024]{2,1,0:T(8,128)(2,1)S(1)}, bf16[8,32,1024]{2,1,0:T(8,128)(2,1)}, u32[]{:S(2)}) copy-start(bf16[8,32,1024]{2,1,0:T(8,128)(2,1)} %get-tuple-element.91) | copy-start | bytes 1572868
  790.8 58.7 %copy-start.42 = (bf16[1,1024,128]{2,1,0:T(8,128)(2,1)S(1)}, bf16[1,1024,128]{2,1,0:T(8,128)(2,1)}, u32[]{:S(2)}) copy-start(bf16[1,1024,128]{2,1,0:T(8,128)(2,1)} %constant_dynamic-slice_fusion.6) | copy-start | bytes 786436
  844.0 40.0 %copy-start.58 = (bf16[3,256,128]{2,1,0:T(8,128)(2,1)S(1)}, bf16[3,256,128]{2,1,0:T(8,128)(2,1)}, u32[]{:S(2)}) copy-start(bf16[3,256,128]{2,1,0:T(8,128)(2,1)} %get-tuple-element.138) | copy-start | bytes 589828
  844.0 40.1 %copy-start.48 = (bf16[3,128,768]{2,1,0:T(8,128)(2,1)S(1)}, bf16[3,128,768]{2,1,0:T(8,128)(2,1)}, u32[]{:S(2)}) copy-start(bf16[3,128,768]{2,1,0:T(8,128)(2,1)} %get-tuple-element.131) | copy-start | bytes 1769476
  844.0 41.2 %copy-start.46 = (bf16[3,128,1024]{2,1,0:T(8,128)(2,1)S(1)}, bf16[3,128,1024]{2,1,0:T(8,128)(2,1)}, u32[]{:S(2)}) copy-start(bf16[3,128,1024]{2,1,0:T(8,128)(2,1)} %get-tuple-element.143) | copy-start | bytes 2359300
  848.7 38.4 %copy-start.45 = (bf16[3,1024,128]{2,1,0:T(8,128)(2,1)S(1)}, bf16[3,1024,128]{2,1,0:T(8,128)(2,1)}, u32[]{:S(2)}) copy-start(bf16[3,1024,128]{2,1,0:T(8,128)(2,1)} %get-tuple-element.144) | copy-start | bytes 2359300
  (60 other events, 260.4 us)
Sparse Core Ops, SparseCore 0:
  136.3 58.5 all-gather.6
  196.8 54.3 all-gather.8
  253.1 74.3 all-gather.10
  528.0 81.1 reduce-scatter.2
  656.2 71.6 reduce-scatter.4

commit v2 on v1

--- a/solution.py
+++ b/solution.py
@@ -36,10 +36,6 @@
 
 def weight_grad(former, latter):
     return lax.dot_general(former, latter, (((0,), (0,)), ((), ())), preferred_element_type=F32)
-
-
-def gelu_exact(entries):
-    return jax.nn.gelu(entries, approximate=False)
 
 
 def layer_norm(entries, norm_gain, norm_shift):
@@ -388,26 +384,26 @@
         wv_ref[...] = value_sum[...].astype(BF)
 
 
-def memory_weights(memory_rows, dkeys, dvalues, rows, padded):
+def memory_weights(memory_rows, dkeys, dvalues, rows, padded, plan, cid):
     spec = pl.BlockSpec((BACK_BLOCK * padded, D), lambda i: (i, 0))
     whole = pl.BlockSpec((D, D), lambda i: (0, 0))
-    return pl.pallas_call(
+    return memory_call(
+        plan,
+        cid,
         memory_weight_kernel,
-        grid=(rows // BACK_BLOCK,),
-        in_specs=[spec, spec, spec],
-        out_specs=[whole, whole, pl.BlockSpec((1, D), lambda i: (0, 0))],
-        out_shape=[
+        "memory_weights",
+        rows // BACK_BLOCK,
+        [memory_rows, dkeys, dvalues],
+        [spec, spec, spec],
+        [whole, whole, pl.BlockSpec((1, D), lambda i: (0, 0))],
+        [
             jax.ShapeDtypeStruct((D, D), BF),
             jax.ShapeDtypeStruct((D, D), BF),
             jax.ShapeDtypeStruct((1, D), F32),
         ],
-        scratch_shapes=[pltpu.VMEM((D, D), F32), pltpu.VMEM((D, D), F32)],
-        compiler_params=pltpu.CompilerParams(vmem_limit_bytes=VMEM_BYTES),
-        cost_estimate=pl.CostEstimate(
-            flops=4 * rows * padded * D * D, bytes_accessed=6 * rows * padded * D, transcendentals=0
-        ),
-        name="memory_weights",
-    )(memory_rows, dkeys, dvalues)
+        [pltpu.VMEM((D, D), F32), pltpu.VMEM((D, D), F32)],
+        4 * rows * padded * D * D,
+    )
 
 
 def memory_grad_kernel(slots, padded, dk_ref, dv_ref, wk_ref, wv_ref, out_ref, wide):
@@ -567,97 +563,468 @@
     )(used, keys, values, queries, dctx, norm, middle, keep)
 
 
-def words_of(table_ref):
-    return jnp.concatenate([table_ref[i] for i in range(table_ref.shape[0])], axis=-1)
-
-
-def vocab_kernel(tile, h_ref, target_ref, table_ref, peak_ref, total_ref, pick_ref):
-    step = pl.program_id(0)
-
-    @pl.when(step == 0)
-    def _():
-        peak_ref[...] = jnp.full_like(peak_ref, NEG)
-        total_ref[...] = jnp.zeros_like(total_ref)
-        pick_ref[...] = jnp.zeros_like(pick_ref)
-
-    words = words_of(table_ref)
-    block = 256
-    word = lax.broadcasted_iota(jnp.int32, (block, tile), 1) + step * tile
-    for t in range(0, h_ref.shape[0], block):
-        rows = slice(t, t + block)
-        logits = product_back(h_ref[rows, :], words)
-        former = peak_ref[rows, :]
-        peak = jnp.maximum(former, jnp.max(logits, axis=1, keepdims=True))
-        total = jnp.sum(jnp.exp(logits - peak), axis=1, keepdims=True)
-        total_ref[rows, :] = total_ref[rows, :] * jnp.exp(former - peak) + total
-        peak_ref[rows, :] = peak
-        hit = jnp.where(word == target_ref[rows, :], logits, 0.0)
-        pick_ref[rows, :] += jnp.sum(hit, axis=1, keepdims=True)
-
-
-def vocab_forward(hidden, target, table, tile):
-    tokens = hidden.shape[0]
+def z_copy(source, target, send, recv, device):
+    return pltpu.make_async_remote_copy(
+        src_ref=source,
+        dst_ref=target,
+        send_sem=send,
+        recv_sem=recv,
+        device_id=(lax.axis_index("dp"), device),
+        device_id_type=MESH,
+    )
+
+
+def z_meet(ways):
+    dp, mp = lax.axis_index("dp"), lax.axis_index("mp")
+    barrier = pltpu.get_barrier_semaphore()
+    for off in range(1, ways):
+        pl.semaphore_signal(
+            barrier, inc=1, device_id=(dp, lax.rem(mp + off, ways)), device_id_type=MESH
+        )
+    pl.semaphore_wait(barrier, ways - 1)
+
+
+def nearest(c, ways):
+    mp = lax.axis_index("mp")
+    left_n, right_n = mp, ways - 1 - mp
+    fewer = jnp.minimum(left_n, right_n)
+    paired = c <= 2 * fewer
+    distance = jnp.where(paired, (c + 1) // 2, c - fewer)
+    left = jnp.where(paired, lax.rem(c, 2) == 1, left_n > right_n)
+    return jnp.where(left, mp - distance, mp + distance), distance, left, paired
+
+
+def table_words(table, start, count):
+    if table.shape[0] == 1:
+        return table[0, pl.ds(start, count), :]
+    return jnp.concatenate([table[i, pl.ds(start, count), :] for i in range(table.shape[0])], axis=-1)
+
+
+def table_load(table_ref, table, sems, tile, c, t):
+    tiles = table.shape[1] // tile
+
+    def copy(k):
+        rows = pl.ds(k * tile, tile)
+        return pltpu.make_async_copy(table_ref.at[:, rows, :], table.at[:, rows, :], sems.at[k])
+
+    @pl.when((c == 0) & (t == 0))
+    def _():
+        for k in range(tiles):
+            copy(k).start()
+
+    for k in range(tiles):
+
+        @pl.when((c == 0) & (t == k))
+        def _(k=k):
+            copy(k).wait()
+
+
+def vocab_kernel(
+    ways, tile, sub, chunk, h_ref, target_ref, table_ref, exp_ref, tops_ref, stats_ref,
+    table, held, run, stats, table_sem, left_send, left_recv, right_send, right_recv,
+    stat_send, stat_recv, own,
+):
+    c, t = pl.program_id(0), pl.program_id(1)
+    last = pl.num_programs(1) - 1
+    mp = lax.axis_index("mp")
+    slot, distance, left, paired = nearest(c, ways)
+
+    def to_right(source, place, hop):
+        return z_copy(source, held.at[place], right_send.at[hop], right_recv.at[hop], mp + 1)
+
+    def to_left(source, place, hop):
+        return z_copy(source, held.at[place], left_send.at[hop], left_recv.at[hop], mp - 1)
+
+    def stats_copy(off):
+        return z_copy(
+            stats,
+            stats_ref.at[mp],
+            stat_send.at[off - 1],
+            stat_recv.at[off - 1],
+            lax.rem(mp + off, ways),
+        )
+
+    @pl.when((c == 0) & (t == 0))
+    def _():
+        z_meet(ways)
+
+        @pl.when(mp < ways - 1)
+        def _():
+            to_right(h_ref, mp, 0).start()
+
+        @pl.when(mp > 0)
+        def _():
+            to_left(h_ref, mp, 0).start()
+
+        local = pltpu.make_async_copy(h_ref, held.at[mp], own.at[0])
+        local.start()
+        local.wait()
+
+    from_left = left | (paired & (lax.rem(c, 2) == 1))
+    from_right = jnp.logical_not(left) | (paired & (lax.rem(c, 2) == 1))
+    due = (c > 0) & (t == 0) & jnp.logical_not(paired & (lax.rem(c, 2) == 0))
+
+    @pl.when(due & from_left)
+    def _():
+        place = mp - distance
+        to_right(held.at[place], place, distance - 1).wait_recv()
+
+        @pl.when(mp < ways - 1)
+        def _():
+            to_right(held.at[place], place, distance).start()
+
+    @pl.when(due & from_right)
+    def _():
+        place = mp + distance
+        to_left(held.at[place], place, distance - 1).wait_recv()
+
+        @pl.when(mp > 0)
+        def _():
+            to_left(held.at[place], place, distance).start()
+
+    table_load(table_ref, table, table_sem, tile, c, t)
+
+    @pl.when(t == 0)
+    def _():
+        run[0:1, :] = jnp.full((1, chunk), NEG, F32)
+        run[1:3, :] = jnp.zeros((2, chunk), F32)
+
+    tokens = held[slot]
+    target = target_ref[slot]
+    parts = []
+    for i in range(tile // sub):
+        start = t * tile + i * sub
+        logits = product_back(table_words(table, start, sub), tokens)
+        top = jnp.max(logits, axis=0, keepdims=True)
+        exponent = jnp.exp(logits - top)
+        word = lax.broadcasted_iota(jnp.int32, (sub, chunk), 0) + start
+        hit = jnp.where(word == target, logits, 0.0)
+        exp_ref[0, i * sub : (i + 1) * sub, :] = exponent.astype(BF)
+        tops_ref[0, pl.ds(t * (tile // sub) + i, 1), :] = top
+        parts.append(
+            (top, jnp.sum(exponent, axis=0, keepdims=True), jnp.sum(hit, axis=0, keepdims=True))
+        )
+    former = run[0:1, :]
+    peak = former
+    for top, total, hit in parts:
+        peak = jnp.maximum(peak, top)
+    sums = run[1:2, :] * jnp.exp(former - peak)
+    hits = run[2:3, :]
+    for top, total, hit in parts:
+        sums += total * jnp.exp(top - peak)
+        hits += hit
+    run[0:1, :] = peak
+    run[1:2, :] = sums
+    run[2:3, :] = hits
+
+    @pl.when(t == last)
+    def _():
+        stats[slot] = run[...]
+
+    @pl.when((c == ways - 1) & (t == last))
+    def _():
+        for off in range(1, ways):
+            stats_copy(off).start()
+        local = pltpu.make_async_copy(stats, stats_ref.at[mp], own.at[1])
+        local.start()
+        for hop in range(ways - 1):
+
+            @pl.when((mp < ways - 1) & (hop <= mp))
+            def _(hop=hop):
+                to_right(held.at[mp - hop], mp - hop, hop).wait_send()
+
+            @pl.when((mp > 0) & (hop <= ways - 1 - mp))
+            def _(hop=hop):
+                to_left(held.at[mp + hop], mp + hop, hop).wait_send()
+
+        for off in range(1, ways):
+            stats_copy(off).wait()
+        local.wait()
+
+
+def vocab_sizes(words):
+    tile = 1280 if words % 1280 == 0 else words
+    sub = 256 if tile % 256 == 0 else tile
+    return tile, sub
+
+
+def vocab_forward(hidden, target, table, cid):
+    ways = lax.axis_size("mp")
+    chunk = hidden.shape[0]
     parts, words, width = table.shape
-    col = pl.BlockSpec((tokens, 1), lambda i: (0, 0))
+    tile, sub = vocab_sizes(words)
+    tiles = words // tile
+    top_rows = -(-(words // sub) // 8) * 8
+    dma = pltpu.SemaphoreType.DMA
     return pl.pallas_call(
-        functools.partial(vocab_kernel, tile),
-        grid=(words // tile,),
+        functools.partial(vocab_kernel, ways, tile, sub, chunk),
+        grid=(ways, tiles),
         in_specs=[
-            pl.BlockSpec((tokens, D), lambda i: (0, 0)),
-            col,
-            pl.BlockSpec((parts, tile, width), lambda i: (0, i, 0)),
+            pl.BlockSpec(memory_space=pl.ANY),
+            pl.BlockSpec((ways, 1, chunk), lambda c, t: (0, 0, 0)),
+            pl.BlockSpec(memory_space=pl.ANY),
         ],
-        out_specs=[col, col, col],
-        out_shape=[jax.ShapeDtypeStruct((tokens, 1), F32)] * 3,
-        compiler_params=pltpu.CompilerParams(vmem_limit_bytes=VMEM_BYTES),
+        out_specs=[
+            pl.BlockSpec((1, tile, chunk), lambda c, t: (c, t, 0)),
+            pl.BlockSpec((1, top_rows, chunk), lambda c, t: (c, 0, 0)),
+            pl.BlockSpec(memory_space=pl.ANY),
+        ],
+        out_shape=[
+            jax.ShapeDtypeStruct((ways, words, chunk), BF),
+            jax.ShapeDtypeStruct((ways, top_rows, chunk), F32),
+            jax.ShapeDtypeStruct((ways, ways, 8, chunk), F32),
+        ],
+        scratch_shapes=[
+            pltpu.VMEM(table.shape, BF),
+            pltpu.VMEM((ways, chunk, D), BF),
+            pltpu.VMEM((8, chunk), F32),
+            pltpu.VMEM((ways, 8, chunk), F32),
+            dma((tiles,)),
+            dma((ways,)),
+            dma((ways,)),
+            dma((ways,)),
+            dma((ways,)),
+            dma((ways,)),
+            dma((ways,)),
+            dma((2,)),
+        ],
+        compiler_params=pltpu.CompilerParams(
+            vmem_limit_bytes=VMEM_BYTES, collective_id=cid, has_side_effects=True
+        ),
         cost_estimate=pl.CostEstimate(
-            flops=2 * tokens * words * D, bytes_accessed=2 * words * D, transcendentals=tokens * words
+            flops=2 * ways * chunk * words * D,
+            bytes_accessed=2 * ways * words * D,
+            transcendentals=ways * chunk * words,
         ),
         name="vocab_forward",
     )(hidden, target, table)
 
 
-def vocab_back_kernel(tile, h_ref, target_ref, norm_ref, rate_ref, table_ref, out_ref):
-    step = pl.program_id(0)
-
-    @pl.when(step == 0)
-    def _():
-        out_ref[...] = jnp.zeros_like(out_ref)
-
-    words = words_of(table_ref)
-    block = 256
-    word = lax.broadcasted_iota(jnp.int32, (block, tile), 1) + step * tile
-    for t in range(0, h_ref.shape[0], block):
-        rows = slice(t, t + block)
-        logits = product_back(h_ref[rows, :], words)
-        probs = jnp.exp(logits - norm_ref[rows, :])
-        hit = jnp.where(word == target_ref[rows, :], 1.0, 0.0)
-        dlogits = (rate_ref[rows, :] * (hit - probs)).astype(BF)
-        out_ref[rows, :] += product(dlogits, words)
-
-
-def vocab_back(hidden, target, norm, rate, table, tile):
+def vocab_back_kernel(
+    ways, tile, sub, chunk, exp_ref, tops_ref, target_ref, norm_ref, rate_ref, table_ref, out_ref,
+    table, total, leaving, landing, table_sem, send, recv,
+):
+    c, t = pl.program_id(0), pl.program_id(1)
+    last = pl.num_programs(1) - 1
+    mp = lax.axis_index("mp")
+    slot = nearest(ways - 1 - c, ways)[0]
+
+    def copy(k):
+        to = nearest(ways - 1 - k, ways)[0]
+        off = lax.rem(to - mp + ways, ways)
+        return z_copy(leaving.at[k], landing.at[off - 1], send.at[k], recv.at[off - 1], to)
+
+    @pl.when((c == 0) & (t == 0))
+    def _():
+        z_meet(ways)
+
+    table_load(table_ref, table, table_sem, tile, c, t)
+    target, norm, rate = target_ref[slot], norm_ref[slot], rate_ref[slot]
+    term = None
+    for i in range(tile // sub):
+        start = t * tile + i * sub
+        factor = jnp.exp(tops_ref[0, pl.ds(t * (tile // sub) + i, 1), :] - norm) * -rate
+        word = lax.broadcasted_iota(jnp.int32, (sub, chunk), 0) + start
+        hit = jnp.where(word == target, rate, 0.0)
+        dlogits = hit + exp_ref[0, i * sub : (i + 1) * sub, :].astype(F32) * factor
+        part = weight_grad(dlogits.astype(BF), table_words(table, start, sub))
+        term = part if term is None else term + part
+
+    @pl.when(t == 0)
+    def _():
+        total[...] = term
+
+    @pl.when(t > 0)
+    def _():
+        total[...] += term
+
+    for k in range(ways - 1):
+
+        @pl.when((c == k) & (t == last))
+        def _(k=k):
+            leaving[k] = total[...].astype(BF)
+            copy(k).start()
+
+    @pl.when((c == ways - 1) & (t == last))
+    def _():
+        for k in range(ways - 1):
+            copy(k).wait_send()
+        for off in range(1, ways):
+            z_copy(
+                leaving.at[0], landing.at[off - 1], send.at[0], recv.at[off - 1], lax.rem(mp + off, ways)
+            ).wait_recv()
+        out = total[...]
+        for k in range(ways - 1):
+            out += landing[k].astype(F32)
+        out_ref[...] = out
+
+
+def vocab_back(exponents, tops, target, norm, rate, table, cid):
+    ways, words, chunk = exponents.shape
+    tile, sub = vocab_sizes(words)
+    tiles = words // tile
+    whole = pl.BlockSpec((ways, 1, chunk), lambda c, t: (0, 0, 0))
+    dma = pltpu.SemaphoreType.DMA
+    return pl.pallas_call(
+        functools.partial(vocab_back_kernel, ways, tile, sub, chunk),
+        grid=(ways, tiles),
+        in_specs=[
+            pl.BlockSpec((1, tile, chunk), lambda c, t: (ways - 1 - c, t, 0)),
+            pl.BlockSpec((1, tops.shape[1], chunk), lambda c, t: (ways - 1 - c, 0, 0)),
+            whole,
+            whole,
+            whole,
+            pl.BlockSpec(memory_space=pl.ANY),
+        ],
+        out_specs=pl.BlockSpec((chunk, D), lambda c, t: (0, 0)),
+        out_shape=jax.ShapeDtypeStruct((chunk, D), F32),
+        scratch_shapes=[
+            pltpu.VMEM(table.shape, BF),
+            pltpu.VMEM((chunk, D), F32),
+            pltpu.VMEM((ways - 1, chunk, D), BF),
+            pltpu.VMEM((ways - 1, chunk, D), BF),
+            dma((tiles,)),
+            dma((ways,)),
+            dma((ways,)),
+        ],
+        compiler_params=pltpu.CompilerParams(
+            vmem_limit_bytes=VMEM_BYTES, collective_id=cid, has_side_effects=True
+        ),
+        cost_estimate=pl.CostEstimate(
+            flops=2 * ways * chunk * words * D, bytes_accessed=2 * ways * words * D, transcendentals=0
+        ),
+        name="vocab_back",
+    )(exponents, tops, target, norm, rate, table)
+
+
+HIDDEN_TILE = 512
+ROOT_HALF = 0.7071067811865476
+ROOT_TAU = 0.3989422804014327
+
+
+def expand_tile(ref):
+    return ref[...].reshape(D, ref.shape[-1])
+
+
+def shrink_tile(ref):
+    if ref.shape[0] == 1:
+        return ref[0, 0]
+    return jnp.concatenate([ref[i, 0] for i in range(ref.shape[0])], axis=-1)
+
+
+def feed_kernel(h_ref, expand_ref, bias_ref, shrink_ref, a_ref, out_ref):
+    t = pl.program_id(0)
+    hidden = product(h_ref[...], expand_tile(expand_ref)) + bias_ref[0]
+    a_ref[...] = hidden
+    active = (hidden * (0.5 + 0.5 * lax.erf(hidden * ROOT_HALF))).astype(BF)
+    term = product(active, shrink_tile(shrink_ref))
+
+    @pl.when(t == 0)
+    def _():
+        out_ref[...] = term
+
+    @pl.when(t > 0)
+    def _():
+        out_ref[...] += term
+
+
+def feed_specs(expand_all, shrink_all):
+    per = expand_all.shape[3] // HIDDEN_TILE
+    parts, _, rows, _ = expand_all.shape
+    return (
+        pl.BlockSpec((parts, 1, rows, HIDDEN_TILE), lambda t: (0, t // per, 0, t % per)),
+        pl.BlockSpec((1, 1, HIDDEN_TILE), lambda t: (t, 0, 0)),
+        pl.BlockSpec(
+            (shrink_all.shape[0], 1, HIDDEN_TILE, shrink_all.shape[3]),
+            lambda t: (0, t // per, t % per, 0),
+        ),
+        expand_all.shape[1] * per,
+    )
+
+
+def feed_forward(hidden, expand_all, bias, shrink_all):
     tokens = hidden.shape[0]
-    parts, words, width = table.shape
-    col = pl.BlockSpec((tokens, 1), lambda i: (0, 0))
+    expand_spec, bias_spec, shrink_spec, tiles = feed_specs(expand_all, shrink_all)
+    whole = pl.BlockSpec((tokens, D), lambda t: (0, 0))
+    units = tiles * HIDDEN_TILE
     return pl.pallas_call(
-        functools.partial(vocab_back_kernel, tile),
-        grid=(words // tile,),
-        in_specs=[
-            pl.BlockSpec((tokens, D), lambda i: (0, 0)),
-            col,
-            col,
-            col,
-            pl.BlockSpec((parts, tile, width), lambda i: (0, i, 0)),
+        feed_kernel,
+        grid=(tiles,),
+        in_specs=[whole, expand_spec, bias_spec, shrink_spec],
+        out_specs=[pl.BlockSpec((tokens, HIDDEN_TILE), lambda t: (0, t)), whole],
+        out_shape=[
+            jax.ShapeDtypeStruct((tokens, units), F32),
+            jax.ShapeDtypeStruct((tokens, D), F32),
         ],
-        out_specs=pl.BlockSpec((tokens, D), lambda i: (0, 0)),
-        out_shape=jax.ShapeDtypeStruct((tokens, D), F32),
         compiler_params=pltpu.CompilerParams(vmem_limit_bytes=VMEM_BYTES),
         cost_estimate=pl.CostEstimate(
-            flops=4 * tokens * words * D, bytes_accessed=2 * words * D, transcendentals=tokens * words
+            flops=4 * tokens * units * D, bytes_accessed=4 * units * D, transcendentals=tokens * units
         ),
-        name="vocab_back",
-    )(hidden, target, norm, rate, table)
+        name="feed_forward",
+    )(hidden, expand_all, bias.reshape(tiles, 1, HIDDEN_TILE), shrink_all)
+
+
+def feed_back_kernel(
+    dout_ref, h_ref, a_ref, expand_ref, shrink_ref, dexpand_ref, dshrink_ref, dbias_ref, dh_ref
+):
+    t = pl.program_id(0)
+    dout = dout_ref[...]
+    hidden = a_ref[...]
+    below = 0.5 + 0.5 * lax.erf(hidden * ROOT_HALF)
+    slope = below + hidden * (ROOT_TAU * jnp.exp(-0.5 * hidden * hidden))
+    active = (hidden * below).astype(BF)
+    dhidden = (slope * product_back(dout, shrink_tile(shrink_ref))).astype(BF)
+    dbias_ref[0] = jnp.sum(dhidden.astype(F32), axis=0, keepdims=True)
+    dshrink = weight_grad(active, dout).astype(BF)
+    width = dshrink_ref.shape[2]
+    for i in range(dshrink_ref.shape[0]):
+        dshrink_ref[i] = dshrink[:, i * width : (i + 1) * width]
+    dexpand_ref[...] = weight_grad(h_ref[...], dhidden).astype(BF)
+    term = product_back(dhidden, expand_tile(expand_ref))
+
+    @pl.when(t == 0)
+    def _():
+        dh_ref[...] = term
+
+    @pl.when(t > 0)
+    def _():
+        dh_ref[...] += term
+
+
+def feed_back(dout, hidden, before, expand_all, shrink_all):
+    tokens = hidden.shape[0]
+    expand_spec, bias_spec, shrink_spec, tiles = feed_specs(expand_all, shrink_all)
+    parts, width = shrink_all.shape[0], shrink_all.shape[3]
+    whole = pl.BlockSpec((tokens, D), lambda t: (0, 0))
+    units = tiles * HIDDEN_TILE
+    return pl.pallas_call(
+        feed_back_kernel,
+        grid=(tiles,),
+        in_specs=[
+            whole,
+            whole,
+            pl.BlockSpec((tokens, HIDDEN_TILE), lambda t: (0, t)),
+            expand_spec,
+            shrink_spec,
+        ],
+        out_specs=[
+            pl.BlockSpec((D, HIDDEN_TILE), lambda t: (0, t)),
+            pl.BlockSpec((parts, HIDDEN_TILE, width), lambda t: (0, t, 0)),
+            bias_spec,
+            whole,
+        ],
+        out_shape=[
+            jax.ShapeDtypeStruct((D, units), BF),
+            jax.ShapeDtypeStruct((parts, units, width), BF),
+            jax.ShapeDtypeStruct((tiles, 1, HIDDEN_TILE), F32),
+            jax.ShapeDtypeStruct((tokens, D), F32),
+        ],
+        compiler_params=pltpu.CompilerParams(vmem_limit_bytes=VMEM_BYTES),
+        cost_estimate=pl.CostEstimate(
+            flops=8 * tokens * units * D, bytes_accessed=8 * units * D, transcendentals=2 * tokens * units
+        ),
+        name="feed_back",
+    )(dout, hidden, before, expand_all, shrink_all)
 
 
 def self_probs(queries, key_heads):
@@ -730,61 +1097,67 @@
     hidden_cols = expand_weight.shape[1]
     vec = D // dp_ways
 
-    small = jnp.concatenate(
-        [
-            output_bias,
-            first_gain,
-            first_shift,
-            crosso_bias,
-            second_gain,
-            second_shift,
-            shrink_bias,
-            third_gain,
-            third_shift,
-            query_bias.reshape(-1),
-            value_bias.reshape(-1),
-            crossq_bias.reshape(-1),
-            expand_bias.reshape(-1),
-            crossv_bias,
-        ]
-    )
-    sizes = [vec] * 9 + [a.size for a in (query_bias, value_bias, crossq_bias, expand_bias, crossv_bias)]
-    small_rows = -(-small.shape[0] // 2048) * 16
-    small = jnp.pad(small, (0, small_rows * 128 - small.shape[0])).reshape(small_rows, 128)
-    memory_shard = jnp.concatenate([cross_key, cross_value], axis=0)
+    vectors = (
+        output_bias,
+        first_gain,
+        first_shift,
+        crosso_bias,
+        second_gain,
+        second_shift,
+        shrink_bias,
+        third_gain,
+        third_shift,
+        crossv_bias,
+    )
+    matrices = (query_bias, value_bias, crossq_bias, expand_bias)
+    starts, top = [], 16
+    for matrix in matrices:
+        starts.append(top)
+        top += -(-matrix.shape[0] // 8) * 8
+    small_rows = -(-top // 16) * 16
+    row_of = lax.broadcasted_iota(jnp.int32, (small_rows, 128), 0)
+    small = jnp.zeros((small_rows, 128), BF)
+    for i, vector in enumerate(vectors):
+        vector = jnp.pad(vector, (0, 128 - vector.shape[0]))
+        small = jnp.where(row_of == i, vector[None, :], small)
+    for start, matrix in zip(starts, matrices):
+        count, width = matrix.shape
+        small += jnp.pad(matrix, ((start, small_rows - start - count), (0, 128 - width)))
     wide_rows = cross_key.shape[0]
     self_shard = jnp.concatenate([self_query, self_key, self_value], axis=1)
-    target_rows = jnp.pad(targets.reshape(1, -1), ((0, 7), (0, 0)))
-    doc_rows = jnp.pad(doc_scores.reshape(1, -1), ((0, 7), (0, 128 - doc_scores.size)))
-    wanted = jnp.stack([answers[(2 * c * piece) // K] for c in range(chips)])
-    memory_all, small_all, cquery_z, cout_z = exchange(
+    target_rows = jnp.pad(targets, ((0, 8 - groups), (0, 128 - TOK)))
+    doc_rows = jnp.pad(doc_scores, ((0, 8 - groups), (0, 128 - K)))
+    if chips == groups:
+        wanted = answers
+    else:
+        wanted = jnp.stack([answers[(2 * c * piece) // K] for c in range(chips)])
+    key_all, value_all, small_all, cquery_z, cout_z = exchange(
         [
-            (memory_shard, "wide", ""),
+            (cross_key, "wide", ""),
+            (cross_value, "wide", ""),
             (small, "wide", ""),
             (cross_query, "gather", "z"),
             (cross_output, "gather", "z"),
         ],
         0,
     )
-    small_all = small_all.reshape(dp_ways, mp_ways, -1)
-    starts = [sum(sizes[:i]) for i in range(len(sizes) + 1)]
-    taken = [small_all[:, :, starts[i] : starts[i + 1]] for i in range(len(sizes))]
     (full_obias, gain_one, shift_one, full_cobias, gain_two, shift_two, full_sbias, gain_three, shift_three) = [
-        taken[i][:, 0].reshape(D) for i in range(9)
+        small_all[:, 0, i, :vec].reshape(D) for i in range(9)
     ]
-
-    def head_bias(part, count, width):
-        part = part.reshape(dp_ways, mp_ways, count, width)
+    cvbias = small_all[:, :, 9, :wide_rows].reshape(1, D)
+
+    def head_bias(i):
+        count, width = matrices[i].shape
+        part = small_all[:, :, starts[i] : starts[i] + count, :width]
         return jnp.transpose(part, (1, 2, 0, 3)).reshape(mp_ways, -1)
 
     mine = lambda a: lax.dynamic_index_in_dim(a, mp, 0, keepdims=False)
-    qbias = mine(head_bias(taken[9], *query_bias.shape))
-    vbias = mine(head_bias(taken[10], *value_bias.shape))
-    cqbias = head_bias(taken[11], *crossq_bias.shape).reshape(-1)
-    ebias = head_bias(taken[12], *expand_bias.shape).reshape(-1)
-    cvbias = taken[13].reshape(1, D)
-    key_weight = memory_all[:, :, :wide_rows].reshape(D, D)
-    value_weight = memory_all[:, :, wide_rows:].reshape(D, D)
+    qbias = mine(head_bias(0))
+    vbias = mine(head_bias(1))
+    cqbias = head_bias(2).reshape(-1)
+    ebias = head_bias(3).reshape(-1)
+    key_weight = key_all.reshape(D, D)
+    value_weight = value_all.reshape(D, D)
 
     plan = Exchange(
         [
@@ -802,22 +1175,23 @@
     (keys, values, memory_rows, expand_z, shrink_z, self_all, output_all, target_all, doc_all, x_all, cquery_all, cout_all) = (
         memory_products(memory, key_weight, value_weight, cvbias, padded, plan, 1)
     )
+    table_all = lax.all_gather(word_table, "dp", axis=0, tiled=False)
+    expand_z, shrink_z, table_all = lax.optimization_barrier((expand_z, shrink_z, table_all))
     expand_all = lax.all_gather(expand_z, "dp", axis=0, tiled=False)
     shrink_all = lax.all_gather(shrink_z, "dp", axis=0, tiled=False)
-    table_all = lax.all_gather(word_table, "dp", axis=0, tiled=False)
     if word_table.shape[1] < 128:
         table_all = column_parts(table_all)[None]
     rows_first = lambda a: jnp.transpose(a, (0, 2, 1, 3)).reshape(dp_ways * a.shape[2], -1)
     columns_first = lambda a: column_parts(a.reshape(dp_ways, -1, a.shape[-1]))
-    full_expand = rows_first(expand_all)
-    full_shrink = columns_first(shrink_all)
+    if shrink_all.shape[-1] < 128:
+        shrink_all = columns_first(shrink_all).reshape(1, mp_ways, -1, D)
     full_cquery = rows_first(cquery_all)
     full_cout = columns_first(cout_all)
     self_weight = self_all.reshape(D, 3 * head_cols)
     full_output = column_parts(output_all)
     my_group = (dp * piece) // K
     row_targets = lax.dynamic_index_in_dim(
-        target_all[:, 0].reshape(dp_ways, groups, TOK), my_group, 1, keepdims=False
+        target_all[:, :groups, :TOK], my_group, 1, keepdims=False
     )
     x_rows = x_all.reshape(uniq, D)
 
@@ -880,57 +1254,48 @@
     hidden_two, normed_two, inverse_two = layer_norm(second_in, gain_two, shift_two)
     hidden_low2 = hidden_two.astype(BF)
 
-    expanded = product(hidden_low2, full_expand) + ebias
-    activated = gelu_exact(expanded).astype(BF)
-    third_in = hidden_two + product(activated, full_shrink) + full_sbias
+    expanded, third_in = feed_forward(hidden_low2, expand_all, ebias, shrink_all)
+    third_in = hidden_two + third_in + full_sbias
     hidden_three, normed_three, inverse_three = layer_norm(third_in, gain_three, shift_three)
-    (hidden_low3,) = exchange([(hidden_three.astype(BF), "gather", "z")], 5)
-    hidden_low3 = hidden_low3.reshape(tokens, D)
 
     vocab_local = table_all.shape[1]
-    tile = 640 if vocab_local % 640 == 0 else vocab_local
-    token_targets = jnp.broadcast_to(
-        row_targets.reshape(own_q, 1, TOK), (own_q, piece, TOK)
-    ).reshape(tokens, 1)
-    local_target = token_targets - mp * vocab_local
-    peak, total, picked = vocab_forward(hidden_low3, local_target, table_all, tile)
-    stats = jnp.concatenate([peak, total, picked], axis=1).T.reshape(3, tokens // 128, 128)
-    (stats,) = exchange([(stats, "gather", "z")], 6)
-    stats = stats.reshape(mp_ways, 3, tokens)
+    token_targets = jnp.broadcast_to(row_targets.reshape(own_q, 1, TOK), (own_q, piece, TOK))
+    local_target = token_targets.reshape(mp_ways, 1, shard_tokens) - mp * vocab_local
+    exponents, tops, stats = vocab_forward(hidden_three.astype(BF), local_target, table_all, 5)
+    stats = jnp.transpose(stats[:, :, :3], (0, 2, 1, 3)).reshape(mp_ways, 3, tokens)
     top = jnp.max(stats[:, 0], axis=0)
     norm_log = top + jnp.log(jnp.sum(stats[:, 1] * jnp.exp(stats[:, 0] - top), axis=0))
     loglik = jnp.sum(stats[:, 2], axis=0) - norm_log
     (loglik_all,) = exchange([(loglik.reshape(tokens // 128, 128), "gather", "dp")], 7)
     loglik_all = loglik_all.reshape(dp_ways, own_q, piece, TOK)
     loglik_all = jnp.transpose(loglik_all, (1, 0, 2, 3)).reshape(own_q, groups, K, TOK)
-    doc_logp = jax.nn.log_softmax(doc_all[:, 0, : groups * K].reshape(own_q, groups, K), axis=2)
+    doc_logp = jax.nn.log_softmax(doc_all[:, :groups, :K], axis=2)
     joined = doc_logp[..., None] + loglik_all
     marginal = jax.nn.logsumexp(joined, axis=2, keepdims=True)
     question_loss = -jnp.mean(
         lax.dynamic_index_in_dim(marginal[:, :, 0], dp, 0, keepdims=False), axis=1
     )
     posterior = jnp.exp(joined - marginal).reshape(own_q, groups * K, TOK)
-    rate = -lax.dynamic_slice_in_dim(posterior, dp * piece, piece, 1).reshape(tokens, 1)
-    dthree = vocab_back(hidden_low3, local_target, norm_log.reshape(tokens, 1), rate, table_all, tile)
-    dthree = dthree.astype(BF).reshape(mp_ways, shard_tokens, D)
-    (received,) = exchange([(dthree, "move", "z")], 8)
-    dhidden_three = added(dthree, received, "z")
+    rate = -lax.dynamic_slice_in_dim(posterior, dp * piece, piece, 1)
+    by_slot = lambda a: a.reshape(mp_ways, 1, shard_tokens)
+    dhidden_three = vocab_back(
+        exponents, tops, local_target, by_slot(norm_log), by_slot(rate), table_all, 8
+    )
 
     dthird, dgain_three, dshift_three = norm_back(
         dhidden_three, normed_three, inverse_three, gain_three
     )
     dshrink_bias = jnp.sum(dthird, axis=0)
     dshrink_in = dthird.astype(BF)
-    dactivated = product_back(dshrink_in, full_shrink)
-    dexpanded = jax.vjp(gelu_exact, expanded)[1](dactivated)[0].astype(BF)
-    dexpand_bias = jnp.sum(dexpanded, axis=0, dtype=F32)
-    dshrink = weight_grad(activated, dshrink_in)
-    dexpand = weight_grad(hidden_low2, dexpanded)
-    shrink_dp = lax.psum_scatter(
-        block_rows(dshrink.astype(BF), dp_ways), "dp", scatter_dimension=0, tiled=False
-    )
-    expand_dp = lax.psum_scatter(dexpand.astype(BF), "dp", scatter_dimension=0, tiled=True)
-    dhidden_two = dthird + product_back(dexpanded, full_expand)
+    dexpand, dshrink, dexpand_bias, dhidden_two = feed_back(
+        dshrink_in, hidden_low2, expanded, expand_all, shrink_all
+    )
+    dexpand_bias = dexpand_bias.reshape(-1)
+    if dshrink.shape[0] < dp_ways:
+        dshrink = block_rows(dshrink[0], dp_ways)
+    shrink_dp = lax.psum_scatter(dshrink, "dp", scatter_dimension=0, tiled=False)
+    expand_dp = lax.psum_scatter(dexpand, "dp", scatter_dimension=0, tiled=True)
+    dhidden_two = dthird + dhidden_two
 
     dsecond, dgain_two, dshift_two = norm_back(dhidden_two, normed_two, inverse_two, gain_two)
     dcout_bias = jnp.sum(dsecond, axis=0)
@@ -940,11 +1305,16 @@
         (dcontext_two.astype(F32) * context_two.astype(F32)).reshape(shard_tokens, H, HD), axis=-1
     )
     middle = jnp.swapaxes(middle.reshape(shard_rows, TOK, H), 1, 2).reshape(shard_rows, G, GL)
+    owners = lambda a: a.reshape(chips, 2, -1, a.shape[-1])
+    cast = lambda a: a.astype(BF)
+    co_blocks = owners(cast(weight_grad(dcout_in, context_two)))
     stat_all = jnp.stack([cross_norm, middle])
-    dctx_all, stat_all = exchange([(dcontext_two, "gather", "z"), (stat_all, "gather", "z")], 9)
+    dctx_all, stat_all, received = exchange(
+        [(dcontext_two, "gather", "z"), (stat_all, "gather", "z"), (co_blocks, "move1", "pair")], 9
+    )
+    co_blocks = cast(added(co_blocks, received, "pair"))
     norm_all = stat_all[:, 0].reshape(rows, G, GL)
     middle_all = stat_all[:, 1].reshape(rows, G, GL)
-    dcout = weight_grad(context_two, dcout_in)
     dcross_q, dkeys, dvalues = cross_back(
         used,
         keys,
@@ -958,9 +1328,12 @@
         padded,
     )
     dcross_q = dcross_q.reshape(mp_ways, shard_uniq, D)
-    (received,) = exchange([(dcross_q, "move", "z")], 10)
-    dkey_weight, dvalue_weight, dvalue_bias = memory_weights(
-        memory_rows, dkeys, dvalues, rows, padded
+    expand_blocks = jnp.transpose(expand_dp.reshape(vec, mp_ways, -1), (1, 0, 2))
+    plan = Exchange(
+        [(dcross_q, "move", "z"), (co_blocks, "move", "chips"), (expand_blocks, "move", "z")]
+    )
+    dkey_weight, dvalue_weight, dvalue_bias, received, co_got, expand_got = memory_weights(
+        memory_rows, dkeys, dvalues, rows, padded, plan, 10
     )
     dcross_low = (added(dcross_q, received, "z") * SCALE).astype(BF)
     dcquery = weight_grad(hidden_low1, dcross_low)
@@ -971,22 +1344,15 @@
 
     dfirst, dgain_one, dshift_one = norm_back(dhidden_one, normed_one, inverse_one, gain_one)
     dout_bias = jnp.sum(dfirst, axis=0)
-    owners = lambda a: a.reshape(chips, 2, -1, a.shape[-1])
-    key_blocks = owners(dkey_weight)
-    value_blocks = owners(dvalue_weight)
-    cq_blocks = owners(
-        jnp.transpose(
-            dcquery.astype(BF).reshape(dp_ways, vec, mp_ways, head_cols), (0, 2, 1, 3)
-        ).reshape(-1, head_cols)
-    )
-    co_blocks = owners(block_rows(dcout.astype(BF), dp_ways).reshape(-1, vec))
-    first_blocks = [key_blocks, value_blocks, cq_blocks, co_blocks]
+    first_blocks = [owners(dkey_weight), owners(dvalue_weight), owners(cast(dcquery))]
     dout_in, *received = exchange(
-        [(dfirst.astype(BF), "gather", "z")] + [(a, "move1", "pair") for a in first_blocks], 11
-    )
-    first_blocks = [added(a, b, "pair").astype(BF) for a, b in zip(first_blocks, received)]
+        [(cast(dfirst), "gather", "z")] + [(a, "move1", "pair") for a in first_blocks], 11
+    )
+    key_blocks, value_blocks, cq_blocks = [
+        cast(added(a, b, "pair")) for a, b in zip(first_blocks, received)
+    ]
     dout_in = dout_in.reshape(uniq, D)
-    doutput = weight_grad(context, dout_in)
+    doutput = weight_grad(dout_in, context)
     dcontext = heads(product_back(dout_in, full_output).astype(BF))
     dvalue_h = jnp.einsum("rhqk,rqhe->rkhe", probs.astype(BF), dcontext, preferred_element_type=F32)
     dprobs = jnp.einsum("rqhe,rkhe->rhqk", dcontext, heads(self_values), preferred_element_type=F32)
@@ -1000,10 +1366,9 @@
     dself = weight_grad(x_rows, dqkv)
     dqkv_bias = jnp.sum(dqkv, axis=0, dtype=F32)
     partial = product_back(dqkv, self_weight).astype(BF).reshape(mp_ways, shard_uniq, D)
-    received, key_got = exchange([(partial, "move", "z"), (first_blocks[0], "move", "chips")], 12)
-    dinputs = (dfirst + added(partial, received, "z")).astype(BF)
-
-    cast = lambda a: a.astype(BF)
+    received, key_got = exchange([(partial, "move", "z"), (key_blocks, "move", "chips")], 12)
+    dinputs = cast(dfirst + added(partial, received, "z"))
+
     vectors = jnp.stack(
         [
             dout_bias,
@@ -1033,58 +1398,61 @@
     vector_blocks = owners(
         jnp.pad(vector_blocks, ((0, 0), (0, vector_rows * 128 - length))).reshape(-1, 128)
     )
-    dinputs, value_got = exchange(
-        [(dinputs, "gather", "z"), (first_blocks[1], "move", "chips")], 13
-    )
+    self_blocks = owners(cast(dself))
+    out_blocks = owners(cast(doutput))
+    last_blocks = [self_blocks, out_blocks, vector_blocks]
+    dinputs, value_got, *received = exchange(
+        [(dinputs, "gather", "z"), (value_blocks, "move", "chips")]
+        + [(a, "move1", "pair") for a in last_blocks],
+        13,
+    )
+    last_blocks = [added(a, b, "pair").astype(a.dtype) for a, b in zip(last_blocks, received)]
     answer_blocks = dinputs.reshape(chips, 2, TOK, D)
-    self_blocks = owners(cast(dself))
-    out_blocks = owners(block_rows(cast(doutput), dp_ways).reshape(-1, vec))
-    last_blocks = [self_blocks, out_blocks, answer_blocks, vector_blocks]
-    received = exchange([(a, "move1", "pair") for a in last_blocks], 14)
-    last_blocks = [added(a, b, "pair").astype(a.dtype) for a, b in zip(last_blocks, received)]
-    last_blocks = first_blocks[2:] + last_blocks
-    expand_blocks = jnp.transpose(
-        expand_dp.reshape(vec, mp_ways, -1), (1, 0, 2)
-    )
+    last_blocks = [cq_blocks, *last_blocks, answer_blocks]
     shrink_blocks = shrink_dp.reshape(mp_ways, -1, vec)
     plan = Exchange(
-        [(a, "move", "chips") for a in last_blocks]
-        + [(expand_blocks, "move", "z"), (shrink_blocks, "move", "z")]
+        [(a, "move", "chips") for a in last_blocks] + [(shrink_blocks, "move", "z")]
     )
     memory_grad, received = memory_back(
         dkeys, dvalues, key_weight, value_weight, rows, slots, padded, plan, 15
     )
-    expand_grad = added(expand_blocks, received[6], "z")
-    shrink_grad = added(shrink_blocks, received[7], "z")
-    cq_sum, co_sum, self_grad, out_grad, answers_own, vector_sum = [
-        added(a, b, "chips") if i != 4 else (a, b)
-        for i, (a, b) in enumerate(zip(last_blocks, received[:6]))
+    expand_grad = added(expand_blocks, expand_got, "z")
+    shrink_grad = added(shrink_blocks, received[5], "z")
+    cq_sum, self_grad, out_grad, vector_sum = [
+        added(a, b, "chips") for a, b in zip(last_blocks[:4], received[:4])
     ]
-    key_sum = added(first_blocks[0], key_got, "chips")
-    value_sum = added(first_blocks[1], value_got, "chips")
+
+    own_answers = lax.dynamic_index_in_dim(answer_blocks, dp // 2, 0, keepdims=True)
+    returned = jnp.concatenate([own_answers, received[4]], axis=0).astype(F32)
+    source = lax.rem(dp // 2 + chips - jnp.arange(chips), chips)
+    place = (2 * source * piece) // K
+    pick = (place[None, :] == jnp.arange(groups)[:, None]).astype(F32)
+    answer_part = cast(jnp.sum(pick[:, :, None, None, None] * returned[None], axis=1))
+
+    key_sum = added(key_blocks, key_got, "chips")
+    value_sum = added(value_blocks, value_got, "chips")
+    co_sum = added(co_blocks, co_got, "chips")
+    by_columns = lambda a: jnp.transpose(a.reshape(vec, mp_ways, -1), (1, 0, 2))
     zblocks = [
         cast(key_sum).reshape(mp_ways, wide_rows, D),
         cast(value_sum).reshape(mp_ways, wide_rows, D),
-        cast(cq_sum).reshape(mp_ways, vec, head_cols),
-        cast(co_sum).reshape(mp_ways, head_cols, vec),
+        by_columns(cast(cq_sum)),
+        by_columns(cast(co_sum)),
     ]
-    *got_z, vector_all = exchange(
-        [(a, "move", "z") for a in zblocks] + [(vector_sum, "gather", "z")], 16
+    *got_z, vector_all, answer_got = exchange(
+        [(a, "move", "z") for a in zblocks]
+        + [(vector_sum, "gather", "z"), (answer_part, "move1", "pair")],
+        16,
     )
     key_grad, value_grad, cquery_grad, cout_grad = [
         added(a, b, "z") for a, b in zip(zblocks, got_z)
     ]
+    cout_grad = cout_grad.T
+    out_grad = out_grad.T
+    answer_grad = added(answer_part, answer_got, "pair")
     vector_all = vector_all.reshape(mp_ways, -1)
     vector_own = jnp.sum(vector_all, axis=0)
     head_own = lax.dynamic_index_in_dim(vector_all, mp, 0, keepdims=False)
-
-    mine_a, others = answers_own
-    mine_a = lax.dynamic_index_in_dim(mine_a, dp // 2, 0, keepdims=False)
-    returned = jnp.concatenate([mine_a[None], others], axis=0).astype(F32)
-    source = lax.rem(dp // 2 + chips - jnp.arange(chips), chips)
-    place = (2 * source * piece) // K
-    pick = (place[None, :] == jnp.arange(groups)[:, None]).astype(F32)
-    answer_grad = jnp.sum(pick[:, :, None, None] * returned[None], axis=1)
 
     def vec_of(i):
         return vector_own[i * vec : (i + 1) * vec]

time: 931 us -> 831 us (0.89)
  local copies, waits for them, and re-layouts: 132 us -> 77.4 us
  matrix products: 63.9 us -> 21.4 us
    pallas_call x15 -> x10, Pallas kernels: 389 us -> 290 us  [exchange(): pl.pallas_call(functools.partial(exchange_kernel, plan), out_shape=plan.s...]
    pallas_call x3 -> x4, Pallas kernels: 92.8 us -> 141 us  [the longest x1 59.4 us: vocab_back(): pl.pallas_call(functools.partial(vocab_back_kernel, ways, tile, sub, chun...]
    pallas_call x2 -> x3, Pallas kernels: 117 us -> 158 us  [memory_call(): pl.pallas_call(functools.partial(beside, plan, kernel, len(inputs), len(o...]
    dot_general x6 -> x4, matrix products: 28.5 us -> 6.45 us  [product_back(): lax.dot_general(former, latter, (((1,), (1,)), ((), ())), preferred_eleme...]
    dot_general x6 -> x4, matrix products: 20.5 us -> 3.91 us  [product(): return jnp.dot(former, latter, preferred_element_type=F32)]
    all_gather x1 -> x0, local copies, waits for them, and re-layouts: 12.4 us -> none  [local(): expand_all = lax.all_gather(expand_z, 'dp', axis=0, tiled=False)]
    reshape x14 -> x2, local copies, waits for them, and re-layouts: 12.7 us -> 0.72 us  [the longest x1 0.68 us: local(): by_slot = lambda a: a.reshape(mp_ways, 1, shard_tokens)]
    convert_element_type x10 -> x6, other arithmetic: 14.6 us -> 3.11 us  [the longest x1 1.04 us: local(): hidden_three.astype(BF)]
  transfers between devices with their start and end apart: 5 -> 5, of which waited for: 0 -> 0; matrix products, arithmetic and copies ran while one was open for 17% -> 14% of each run, Pallas kernels for 34% -> 50%
where the time goes in v2:
time: 831 us; the launch traced here: 818 us
  Pallas kernels  626 us (75%)
  local copies, waits for them, and re-layouts  77.4 us (9%)
  other arithmetic  75.5 us (9%)
  matrix products  21.4 us (3%)
  between operations  16.1 us (2%)
    pallas_call x10, Pallas kernels, exchange(): pl.pallas_call(functools.partial(exchange_kernel, plan), out_shape=plan.s...  290 us
    pallas_call x3, Pallas kernels, memory_call(): pl.pallas_call(functools.partial(beside, plan, kernel, len(inputs), len(o...  158 us
    pallas_call x1, Pallas kernels, vocab_back(): pl.pallas_call(functools.partial(vocab_back_kernel, ways, tile, sub, chun...  59.4 us
    pallas_call x1, Pallas kernels, vocab_forward(): pl.pallas_call(functools.partial(vocab_kernel, ways, tile, sub, chunk), g...  49.2 us
    unnamed x203, local copies, waits for them, and re-layouts  31.2 us
    pallas_call x1, Pallas kernels, cross_back(): pl.pallas_call(functools.partial(cross_back_kernel, piece, padded), grid_...  21.1 us
    pallas_call x1, Pallas kernels, feed_back(): pl.pallas_call(feed_back_kernel, grid=(tiles,), in_specs=[whole, whole, p...  18.7 us
  transfers between devices with their start and end apart: 5, of which 0 were waited for; matrix products, arithmetic and copies ran while one was open for 14% of the time, Pallas kernels for 50%

profile of v2, /device:TPU:0, one launch (start us, length us, event | category | flops | bytes accessed | tf_op | source)
XLA Modules:
  0.0 817.8 jit_solution(2940805815346201533)
XLA Ops:
  8.7 1.5 pad_add_fusion.refs_2_
  10.2 58.9 %exchange_0.1 = (bf16[8,4,32,1024]{3,2,1,0:T(8,128)(2,1)}, bf16[8,4,32,1024]{3,2,1,0:T(8,128)(2,1)}, bf16[8,4,48,128]{3,2,1,0:T(8,128)(2,1)}, bf16[4,128,256]{2,1,0:T(8,128)(2,1)}, bf16[4,256,128]{2,1,0:T(8,128)(2,1)}) custom-call(bf16[32,1024]{1,0:T(8,128)(2,1)} %refs_0_.1, bf16[32,1024]{1,0:T(8,128)(2,1)} %refs_1_.1, bf16[48,128]{1,0:T(8,128)(2,1)} %pad_add_fusion.refs_2_, ...), custom_call_target="tpu_custom_call" | custom-call | tf_op jit(solution)/shard_map/exchange_0/pallas_call | solution.py:268
  73.3 1.6 pad_maximum_fusion.refs_6_
  74.9 79.4 %memory_products.1 = (bf16[3584,1024]{1,0:T(8,128)(2,1)}, bf16[3584,1024]{1,0:T(8,128)(2,1)}, bf16[3584,1024]{1,0:T(8,128)(2,1)}, bf16[4,128,1024]{2,1,0:T(8,128...) custom-call(bf16[100,32,1024]{2,1,0:T(8,128)(2,1)} %bitcast.515, ...), custom_call_target="tpu_custom_call" | custom-call | flops 15032385536 | bytes 75161928 | tf_op jit(solution)/shard_map/memory_products/pallas_call | solution.py:305
  162.1 14.1 %exchange_2.1 = bf16[3,64,1024]{2,1,0:T(8,128)(2,1)} custom-call(bf16[4,64,1024]{2,1,0:T(8,128)(2,1)} %bitcast.431), custom_call_target="tpu_custom_call" | custom-call | tf_op jit(solution)/shard_map/exchange_2/pallas_call | solution.py:268
  176.3 3.2 copy.371
  179.6 1.5 slice_convert_fusion.2
  184.7 15.6 %exchange_3.1 = bf16[4,64,1024]{2,1,0:T(8,128)(2,1)} custom-call(bf16[64,1024]{1,0:T(8,128)(2,1)} %fusion.29.refs_0_), custom_call_target="tpu_custom_call" | custom-call | tf_op jit(solution)/shard_map/exchange_3/pallas_call | solution.py:268
  201.7 15.3 %cross_forward.1 = (bf16[1024,1024]{1,0:T(8,128)(2,1)}, f32[32,4,128]{2,1,0:T(4,128)}, f32[32,4,128]{2,1,0:T(4,128)}) custom-call(s32[32]{0:T(128)} %subtract_clamp_fusion.used, bf16[3584,1024]{1,0:T(8,128)(2,1)} %get-tuple-element.106.k_ref, bf16[3584,1024]{1,0:T(8,128)(2,1)} %get-tuple-element.107.v_ref, bf16[256,1024]{1,0:T(8,128)(2,1)} %bitcast.416, ...), custom_call_target="tpu_custom_call" | custom-call | flops 1879048192 | bytes 14680064 | tf_op jit(solution)/shard_map/cross_forward/pallas_call | solution.py:476
  217.0 1.6 pad_maximum_fusion.1.refs_1_
  218.6 52.7 %exchange_4.1 = (bf16[3,256,1024]{2,1,0:T(8,128)(2,1)}, f32[3,8,2,4,128]{4,3,2,1,0:T(4,128)}) custom-call(bf16[4,256,1024]{2,1,0:T(8,128)(2,1)} %bitcast.427, f32[4,8,2,4,128]{4,3,2,1,0:T(4,128)} %pad_maximum_fusion.1.refs_1_), custom_call_target="tpu_custom_call" | custom-call | tf_op jit(solution)/shard_map/exchange_4/pallas_call | solution.py:268
  278.5 2.4 copy.379
  280.9 1.8 fusion.111
  283.5 1.6 copy-done.2
  290.0 13.3 %feed_forward.1 = (f32[256,4096]{1,0:T(8,128)}, f32[256,1024]{1,0:T(8,128)}) custom-call(bf16[256,1024]{1,0:T(8,128)(2,1)} %fusion.34.h_ref, bf16[8,4,128,1024]{3,2,1,0:T(8,128)(2,1)} %bitcast.408, bf16[8,1,512]{2,1,0:T(2,128)(2,1)} %reshape_reshape_reshape.4.bias_ref, bf16[8,4,1024,128]{3,2,1,0:T(8,128)(2,1)} %bitcast.410), custom_call_target="tpu_custom_call" | custom-call | flops 4294967296 | bytes 16777216 | tf_op jit(solution)/shard_map/feed_forward/pallas_call | solution.py:950
  303.4 1.6 fusion.107
  306.4 49.2 %vocab_forward.1 = (bf16[4,6400,256]{2,1,0:T(8,128)(2,1)}, f32[4,32,256]{2,1,0:T(8,128)}, f32[4,4,8,256]{3,2,1,0:T(8,128)}) custom-call(bf16[256,1024]{1,0:T(8,128)(2,1)} %add_convert_fusion.h_ref, s32[4,1,256]{2,1,0:T(1,128)} %sub.237.target_ref, bf16[8,6400,128]{2,1,0:T(8,128)(2,1)} %bitcast.513), custom_call_target="tpu_custom_call" | custom-call | flops 13421772800 | bytes 52428800 | tf_op jit(solution)/shard_map/vocab_forward/pallas_call | solution.py:759
  357.2 5.8 exchange_7.1
  365.7 59.4 %vocab_back.1 = f32[256,1024]{1,0:T(8,128)} custom-call(bf16[4,6400,256]{2,1,0:T(8,128)(2,1)} %get-tuple-element.123.exp_ref, f32[4,32,256]{2,1,0:T(8,128)} %get-tuple-element.124.tops_ref, s32[4,1,256]{2,1,0:T(1,128)} %sub.237.target_ref, f32[4,1,256]{2,1,0:T(1,128)} %bitcast.511, f32[4,1,256]{2,1,0:T(1,128)} %reshape.738.rate_ref, ...), custom_call_target="tpu_custom_call" | custom-call | flops 13421772800 | bytes 52428800 | tf_op jit(solution)/shard_map/vocab_back/pallas_call | solution.py:868
  425.1 2.4 multiply_reduce_fusion.2
  427.5 1.6 fusion.104
  430.0 18.7 %feed_back.1 = (bf16[1024,4096]{1,0:T(8,128)(2,1)}, bf16[8,4096,128]{2,1,0:T(8,128)(2,1)}, f32[8,1,512]{2,1,0:T(1,128)}, f32[256,1024]{1,0:T(8,128)}) custom-call(bf16[256,1024]{1,0:T(8,128)(2,1)} %convert_element_type.542.dout_ref, bf16[256,1024]{1,0:T(8,128)(2,1)} %fusion.34.h_ref, f32[256,4096]{1,0:T(8,128)} %get-tuple-element.125.a_ref, ...), custom_call_target="tpu_custom_call" | custom-call | flops 8589934592 | bytes 33554432 | tf_op jit(solution)/shard_map/feed_back/pallas_call | solution.py:1000
  452.7 1.6 convert_multiply_fusion.1
  459.5 2.1 convolution_convert_fusion.1
  461.6 62.1 %exchange_9.1 = (bf16[4,256,1024]{2,1,0:T(8,128)(2,1)}, f32[4,2,8,4,128]{4,3,2,1,0:T(4,128)}, bf16[1,4,128,1024]{3,2,1,0:T(8,128)(2,1)}) custom-call(bf16[256,1024]{1,0:T(8,128)(2,1)} %get-tuple-element.437.refs_0_, f32[2,8,4,128]{3,2,1,0:T(4,128)} %pad_maximum_fusion.3.refs_1_, bf16[4,2,128,1024]{3,2,1,0:T(8,128)(2,1)} %bitcast.403), custom_call_target="tpu_custom_call" | custom-call | tf_op jit(solution)/shard_map/exchange_9/pallas_call | solution.py:268
  523.7 1.7 fusion.8.refs_4_
  528.8 21.1 %cross_back.1 = (bf16[256,1024]{1,0:T(8,128)(2,1)}, bf16[3584,1024]{1,0:T(8,128)(2,1)}, bf16[3584,1024]{1,0:T(8,128)(2,1)}) custom-call(s32[32]{0:T(128)} %subtract_clamp_fusion.used, bf16[3584,1024]{1,0:T(8,128)(2,1)} %get-tuple-element.106.k_ref, bf16[3584,1024]{1,0:T(8,128)(2,1)} %get-tuple-element.107.v_ref, bf16[256,1024]{1,0:T(8,128)(2,1)} %bitcast.417, ...), custom_call_target="tpu_custom_call" | custom-call | flops 4697620480 | bytes 29360128 | tf_op jit(solution)/shard_map/cross_back/pallas_call | solution.py:535
  549.9 1.7 copy.391
  552.9 39.1 %memory_weights.1 = (bf16[1024,1024]{1,0:T(8,128)(2,1)}, bf16[1024,1024]{1,0:T(8,128)(2,1)}, f32[1,1024]{1,0:T(1,128)}, bf16[3,64,1024]{2,1,0:T(8,128)(2,1)}, bf...) custom-call(bf16[3584,1024]{1,0:T(8,128)(2,1)} %get-tuple-element.130.refs_0_, ...), custom_call_target="tpu_custom_call" | custom-call | flops 15032385536 | bytes 75161928 | tf_op jit(solution)/shard_map/memory_weights/pallas_call | solution.py:305
  593.1 1.6 convert_reduce_fusion.16
  595.5 2.1 multiply_reduce_fusion.11
  600.4 2.1 convolution_convert_fusion
  602.5 18.7 %exchange_11.1 = (bf16[4,64,1024]{2,1,0:T(8,128)(2,1)}, bf16[1,4,128,1024]{3,2,1,0:T(8,128)(2,1)}, bf16[1,4,128,1024]{3,2,1,0:T(8,128)(2,1)}, bf16[1,4,128,1024]{3,2,1,0:T(8,128)(2,1)}) custom-call(bf16[64,1024]{1,0:T(8,128)(2,1)} %convert_element_type.555.refs_0_, bf16[4,2,128,1024]{3,2,1,0:T(8,128)(2,1)} %bitcast.420, bf16[4,2,128,1024]{3,2,1,0:T(8,128)(2,1)} %bitcast.418, ...), custom_call_target="tpu_custom_call" | custom-call | tf_op jit(solution)/shard_map/exchange_11/pallas_call | solution.py:268
  622.8 1.5 fusion.19
  627.4 2.0 convert_element_type.564
  642.0 1.6 fusion.5.refs_4_
  645.9 3.0 fusion.7.refs_1_
  650.3 14.6 %exchange_12.1 = (bf16[3,64,1024]{2,1,0:T(8,128)(2,1)}, bf16[3,128,1024]{2,1,0:T(8,128)(2,1)}) custom-call(bf16[4,64,1024]{2,1,0:T(8,128)(2,1)} %bitcast.429, bf16[4,128,1024]{2,1,0:T(8,128)(2,1)} %fusion.7.refs_1_), custom_call_target="tpu_custom_call" | custom-call | tf_op jit(solution)/shard_map/exchange_12/pallas_call | solution.py:268
  666.0 1.6 fusion.47.refs_0_
  667.6 2.2 convolution_convert_fusion.3
  671.3 1.8 convolution_convert_fusion.2
  673.1 18.1 %exchange_13.1 = (bf16[4,64,1024]{2,1,0:T(8,128)(2,1)}, bf16[3,128,1024]{2,1,0:T(8,128)(2,1)}, bf16[1,4,128,768]{3,2,1,0:T(8,128)(2,1)}, bf16[1,4,128,256]{3,2,1,0:T(8,128)(2,1)}, f32[1,4,16,128]{3,2,1,0:T(8,128)}) custom-call(bf16[64,1024]{1,0:T(8,128)(2,1)} %fusion.47.refs_0_, bf16[4,128,1024]{2,1,0:T(8,128)(2,1)} %fusion.6.refs_1_, ...), custom_call_target="tpu_custom_call" | custom-call | tf_op jit(solution)/shard_map/exchange_13/pallas_call | solution.py:268
  696.9 1.7 fusion.37.refs_6_
  699.7 39.9 %memory_back.1 = (f32[100,32,1024]{2,1,0:T(8,128)}, bf16[3,128,1024]{2,1,0:T(8,128)(2,1)}, bf16[3,128,768]{2,1,0:T(8,128)(2,1)}, bf16[3,128,256]{2,1,0:T(8,128)(...) custom-call(bf16[3584,1024]{1,0:T(8,128)(2,1)} %get-tuple-element.131.refs_1_.refs_0_, ...), custom_call_target="tpu_custom_call" | custom-call | flops 15032385536 | bytes 75161928 | tf_op jit(solution)/shard_map/memory_back/pallas_call | solution.py:305
  749.1 29.5 %exchange_16.1 = (bf16[3,32,1024]{2,1,0:T(8,128)(2,1)}, bf16[3,32,1024]{2,1,0:T(8,128)(2,1)}, bf16[3,128,256]{2,1,0:T(8,128)(2,1)}, bf16[3,128,256]{2,1,0:T(8,12...) custom-call(bf16[4,32,1024]{2,1,0:T(8,128)(2,1)} %fusion.36.refs_0_, ...), custom_call_target="tpu_custom_call" | custom-call | tf_op jit(solution)/shard_map/exchange_16/pallas_call | solution.py:268
  780.2 1.8 convert_add_fusion.6
  785.8 1.9 convert_add_fusion.5
  798.2 12.5 %copy.515 = f32[32,100,1024]{2,0,1:T(8,128)} copy(f32[32,100,1024]{2,0,1:T(8,128)} %bitcast.400) | data formatting | bytes 26214400
  (435 shorter events, 110.7 us)
Async XLA Ops:
  7.2 147.2 %all-gather.7.cloned.1.call-start = ((), (), s32[]{:S(2)}) async-start(), calls=%async_computation.4 | async-start | bytes 14745600 | tf_op jit(solution)/shard_map/all_gather | solution.py:1178
  7.9 282.1 %all-gather.9.cloned.1.call-start = ((), (), s32[]{:S(2)}) async-start(), calls=%async_computation.5 | async-start | bytes 9437184 | tf_op jit(solution)/shard_map/all_gather | solution.py:1180
  154.4 135.6 %all-gather.11.cloned.1.call-start = ((), (), s32[]{:S(2)}) async-start(), calls=%async_computation.6 | async-start | bytes 9437184 | tf_op jit(solution)/shard_map/all_gather | solution.py:1181
  155.2 394.7 %reduce-scatter.3.cloned.1.call-start = ((), (), s32[]{:S(2)}) async-start(), calls=%async_computation.2 | async-start | bytes 9437184 | tf_op jit(solution)/shard_map/reduce_scatter | solution.py:1297
  160.0 19.5 %copy-start.36 = (bf16[256,256]{1,0:T(8,128)(2,1)}, bf16[256,256]{1,0:T(8,128)(2,1)S(1)}, u32[]{:S(2)}) copy-start(bf16[256,256]{1,0:T(8,128)(2,1)S(1)} %reshape.729) | copy-start | bytes 393220
  179.5 5.2 copy-start.6
  181.1 122.2 %copy-start.62 = (f32[8,1,1,128]{3,2,1,0:T(1,128)}, f32[8,1,1,128]{3,2,1,0:T(1,128)S(1)}, u32[]{:S(2)}) copy-start(f32[8,1,1,128]{3,2,1,0:T(1,128)S(1)} %get-tuple-element.406) | copy-start | bytes 12292
  181.1 124.2 %copy-start.69 = (f32[8,1,1,128]{3,2,1,0:T(1,128)}, f32[8,1,1,128]{3,2,1,0:T(1,128)S(1)}, u32[]{:S(2)}) copy-start(f32[8,1,1,128]{3,2,1,0:T(1,128)S(1)} %get-tuple-element.402) | copy-start | bytes 12292
  182.2 18.2 %copy-start.85 = (s32[32]{0:T(128)S(1)}, s32[32]{0:T(128)}, u32[]{:S(2)}) copy-start(s32[32]{0:T(128)} %param.34) | copy-start | bytes 388
  182.2 34.7 %copy-start.81 = (f32[64]{0:T(128)}, f32[64]{0:T(128)S(1)}, u32[]{:S(2)}) copy-start(f32[64]{0:T(128)S(1)} %broadcast_multiply_fusion.8) | copy-start | bytes 772
  182.5 34.5 %copy-start.83 = (f32[64]{0:T(128)}, f32[64]{0:T(128)S(1)}, u32[]{:S(2)}) copy-start(f32[64]{0:T(128)S(1)} %add_rsqrt_fusion.2) | copy-start | bytes 772
  217.0 54.4 %copy-start.52 = (f32[32,4,128]{2,1,0:T(4,128)S(1)}, f32[32,4,128]{2,1,0:T(4,128)}, u32[]{:S(2)}) copy-start(f32[32,4,128]{2,1,0:T(4,128)} %get-tuple-element.110) | copy-start | bytes 196612
  217.0 54.4 %copy-start.53 = (f32[32,4,128]{2,1,0:T(4,128)S(1)}, f32[32,4,128]{2,1,0:T(4,128)}, u32[]{:S(2)}) copy-start(f32[32,4,128]{2,1,0:T(4,128)} %get-tuple-element.111) | copy-start | bytes 196612
  271.4 4.1 copy-start.64
  271.4 4.5 copy-start.80
  283.5 4.4 copy-start.4
  288.7 14.7 %copy-start.72 = (f32[256]{0:T(256)}, f32[256]{0:T(256)S(1)}, u32[]{:S(2)}) copy-start(f32[256]{0:T(256)S(1)} %broadcast_multiply_fusion.5) | copy-start | bytes 3076
  288.9 14.4 %copy-start.75 = (f32[256]{0:T(256)}, f32[256]{0:T(256)S(1)}, u32[]{:S(2)}) copy-start(f32[256]{0:T(256)S(1)} %add_rsqrt_fusion.1) | copy-start | bytes 3076
  305.0 120.0 %copy-start.74 = (f32[256]{0:T(256)}, f32[256]{0:T(256)S(1)}, u32[]{:S(2)}) copy-start(f32[256]{0:T(256)S(1)} %broadcast_multiply_fusion.4) | copy-start | bytes 3076
  305.3 119.8 %copy-start.77 = (f32[256]{0:T(256)}, f32[256]{0:T(256)S(1)}, u32[]{:S(2)}) copy-start(f32[256]{0:T(256)S(1)} %add_rsqrt_fusion) | copy-start | bytes 3076
  365.7 59.4 %copy-start.70 = (f32[8,1,1,128]{3,2,1,0:T(1,128)S(1)}, f32[8,1,1,128]{3,2,1,0:T(1,128)}, u32[]{:S(2)}) copy-start(f32[8,1,1,128]{3,2,1,0:T(1,128)} %copy-done.69) | copy-start | bytes 12292
  448.8 250.9 %reduce-scatter.5.cloned.1.call-start = ((), (), s32[]{:S(2)}) async-start(), calls=%async_computation.3 | async-start | bytes 9437184 | tf_op jit(solution)/shard_map/reduce_scatter | solution.py:1296
  461.6 62.1 %copy-start.1 = (bf16[1024,1024]{1,0:T(8,128)(2,1)S(1)}, bf16[1024,1024]{1,0:T(8,128)(2,1)}, u32[]{:S(2)}) copy-start(bf16[1024,1024]{1,0:T(8,128)(2,1)} %convolution_convert_fusion.1) | copy-start | bytes 6291460
  552.9 42.6 %copy-start.7 = (bf16[8,128,4,256]{1,0,3,2:T(8,128)(2,1)S(1)}, bf16[8,128,4,256]{1,0,3,2:T(8,128)(2,1)}, u32[]{:S(2)}) copy-start(bf16[8,128,4,256]{1,0,3,2:T(8,128)(2,1)} %copy-done.6) | copy-start | bytes 6291460
  552.9 42.6 %copy-start.38 = (f32[2,32,1024]{2,1,0:T(8,128)S(1)}, f32[2,32,1024]{2,1,0:T(8,128)}, u32[]{:S(2)}) copy-start(f32[2,32,1024]{2,1,0:T(8,128)} %reduce_sum.569) | copy-start | bytes 786436
  552.9 42.6 %copy-start.68 = (f32[8,1,1,128]{3,2,1,0:T(1,128)S(1)}, f32[8,1,1,128]{3,2,1,0:T(1,128)}, u32[]{:S(2)}) copy-start(f32[8,1,1,128]{3,2,1,0:T(1,128)} %copy-done.67) | copy-start | bytes 12292
  552.9 42.6 %copy-start.82 = (f32[64]{0:T(128)S(1)}, f32[64]{0:T(128)}, u32[]{:S(2)}) copy-start(f32[64]{0:T(128)} %copy-done.81) | copy-start | bytes 772
  552.9 42.6 %copy-start.84 = (f32[64]{0:T(128)S(1)}, f32[64]{0:T(128)}, u32[]{:S(2)}) copy-start(f32[64]{0:T(128)} %copy-done.83) | copy-start | bytes 772
  602.5 18.7 %copy-start.20 = (bf16[256,1024]{1,0:T(8,128)(2,1)S(1)}, bf16[256,1024]{1,0:T(8,128)(2,1)}, u32[]{:S(2)}) copy-start(bf16[256,1024]{1,0:T(8,128)(2,1)} %copy-done.19) | copy-start | bytes 1572868
  602.5 20.3 %copy-start.66 = (f32[8,4,32]{2,1,0:T(4,128)S(1)}, f32[8,4,32]{2,1,0:T(4,128)}, u32[]{:S(2)}) copy-start(f32[8,4,32]{2,1,0:T(4,128)} %copy-done.65) | copy-start | bytes 12292
  626.5 14.1 %copy-start.71 = (f32[8,512]{1,0:T(8,128)S(1)}, f32[8,512]{1,0:T(8,128)}, u32[]{:S(2)}) copy-start(f32[8,512]{1,0:T(8,128)} %reshape.758) | copy-start | bytes 49156
  627.4 14.7 %copy-start = (bf16[1024,1024]{1,0:T(8,128)(2,1)S(1)}, bf16[1024,1024]{1,0:T(8,128)(2,1)}, u32[]{:S(2)}) copy-start(bf16[1024,1024]{1,0:T(8,128)(2,1)} %convolution_convert_fusion) | copy-start | bytes 6291460
  644.9 4.0 copy-start.11
  650.3 17.4 %copy-start.37 = (bf16[256,256]{1,0:T(8,128)(2,1)S(1)}, bf16[256,256]{1,0:T(8,128)(2,1)}, u32[]{:S(2)}) copy-start(bf16[256,256]{1,0:T(8,128)(2,1)} %copy-done.36) | copy-start | bytes 393220
  650.3 19.6 %copy-start.12 = (bf16[1024,1024]{1,0:T(8,128)(2,1)S(1)}, bf16[1024,1024]{1,0:T(8,128)(2,1)}, u32[]{:S(2)}) copy-start(bf16[1024,1024]{1,0:T(8,128)(2,1)} %get-tuple-element.137) | copy-start | bytes 6291460
  664.9 5.0 copy-start.39
  673.1 22.5 %copy-start.48 = (f32[1,8,16,128]{3,2,1,0:T(8,128)S(1)}, f32[1,8,16,128]{3,2,1,0:T(8,128)}, u32[]{:S(2)}) copy-start(f32[1,8,16,128]{3,2,1,0:T(8,128)} %copy.435) | copy-start | bytes 196612
  691.1 5.8 copy-start.16
  691.1 7.5 copy-start.3
  691.2 7.5 copy-start.41
  747.6 32.5 %copy-start.42 = (bf16[3,128,1024]{2,1,0:T(8,128)(2,1)S(1)}, bf16[3,128,1024]{2,1,0:T(8,128)(2,1)}, u32[]{:S(2)}) copy-start(bf16[3,128,1024]{2,1,0:T(8,128)(2,1)} %get-tuple-element.165) | copy-start | bytes 2359300
  749.1 32.9 %copy-start.59 = (bf16[3,128,256]{2,1,0:T(8,128)(2,1)S(1)}, bf16[3,128,256]{2,1,0:T(8,128)(2,1)}, u32[]{:S(2)}) copy-start(bf16[3,128,256]{2,1,0:T(8,128)(2,1)} %get-tuple-element.160) | copy-start | bytes 589828
  778.7 5.1 copy-start.45
  784.9 5.0 copy-start.61
  785.7 5.7 copy-start.58
  785.7 7.2 copy-start.57
  785.8 8.7 %copy-start.56 = (bf16[3,32,1024]{2,1,0:T(8,128)(2,1)S(1)}, bf16[3,32,1024]{2,1,0:T(8,128)(2,1)}, u32[]{:S(2)}) copy-start(bf16[3,32,1024]{2,1,0:T(8,128)(2,1)} %get-tuple-element.163) | copy-start | bytes 589828
  785.8 10.2 %copy-start.55 = (bf16[3,128,256]{2,1,0:T(8,128)(2,1)S(1)}, bf16[3,128,256]{2,1,0:T(8,128)(2,1)}, u32[]{:S(2)}) copy-start(bf16[3,128,256]{2,1,0:T(8,128)(2,1)} %get-tuple-element.164) | copy-start | bytes 589828
  (43 other events, 90.5 us)
Sparse Core Ops, SparseCore 0:
  9.9 137.1 all-gather.6
  154.6 54.6 all-gather.8
  211.1 54.4 all-gather.10
  448.9 80.7 reduce-scatter.2
  533.4 79.7 reduce-scatter.4

commit v3 on v2

v3 whole, which is shorter than its diff:
```python
import functools

import jax
import jax.numpy as jnp
from jax import lax
from jax.experimental import pallas as pl
from jax.experimental.pallas import tpu as pltpu
from jax.sharding import PartitionSpec as P

D = 1024
H = 16
HD = 64
TOK = 32
K = 8
G = 4
GH = 4
GC = GH * HD
GL = GH * TOK

EPS = 1e-05
NEG = -1e30
SCALE = 0.125
BF = jnp.bfloat16
F32 = jnp.float32
MESH = pl.DeviceIdType.MESH
DP, MP = "dp", "mp"
GATHER, LATE, MOVE, MOVE1, COLS, NEAR, NEARSWAP, WIDE = range(8)
Z, CHIPS, PAIR = range(3)
PLAIN, COLUMNS, TURNED = range(3)
VMEM_BYTES = 60 * 1024 * 1024


def product(former, latter):
    return jnp.dot(former, latter, preferred_element_type=F32)


def product_back(former, latter):
    return lax.dot_general(former, latter, (((1,), (1,)), ((), ())), preferred_element_type=F32)


def weight_grad(former, latter):
    return lax.dot_general(former, latter, (((0,), (0,)), ((), ())), preferred_element_type=F32)


def layer_norm(entries, norm_gain, norm_shift):
    center = entries - jnp.mean(entries, axis=-1, keepdims=True)
    inverse = lax.rsqrt(jnp.mean(center * center, axis=-1, keepdims=True) + EPS)
    normed = center * inverse
    return (normed * norm_gain + norm_shift, normed, inverse)


def norm_back(upstream, normed, inverse, norm_gain):
    scaled = upstream * norm_gain
    dentries = inverse * (
        scaled
        - jnp.mean(scaled, axis=-1, keepdims=True)
        - normed * jnp.mean(scaled * normed, axis=-1, keepdims=True)
    )
    return (dentries, jnp.sum(upstream * normed, axis=0), jnp.sum(upstream, axis=0))


class Exchange:
    def __init__(self, entries):
        self.dp_ways, self.mp_ways = lax.axis_size(DP), lax.axis_size(MP)
        self.chips = self.dp_ways // 2
        self.ways = {Z: self.mp_ways, CHIPS: self.chips, PAIR: 2, DP: self.dp_ways}
        self.arrays = [entry[0] for entry in entries]
        self.kinds = [entry[1] for entry in entries]
        self.groups = [entry[2] for entry in entries]
        self.count = len(entries)
        shapes = []
        for array, kind, group in entries:
            shape = array.shape
            if kind in (GATHER, LATE):
                shape = (self.ways[group],) + shape
            elif kind == MOVE:
                shape = (self.ways[group] - 1,) + shape[1:]
            elif kind == MOVE1:
                shape = (self.ways[group] - 1, shape[0]) + shape[2:]
            elif kind == COLS:
                shape = (self.ways[group] - 1,) + shape[:-1] + (shape[-1] // self.ways[group],)
            elif kind == NEAR:
                shape = (self.dp_ways,) + shape
            elif kind == NEARSWAP:
                shape = (self.dp_ways,) + shape[1:]
            else:
                shape = (self.dp_ways, self.mp_ways) + shape
            shapes.append(jax.ShapeDtypeStruct(shape, array.dtype))
        self.shapes = shapes
        self.specs = [pl.BlockSpec(memory_space=pl.ANY)] * self.count
        dma = pltpu.SemaphoreType.DMA
        most = max(self.dp_ways, self.mp_ways)
        self.scratch = [dma((self.count, most)) for _ in range(6)] + [dma((self.count,))]

    def bind(self, ins, outs, sems):
        self.ins, self.outs = ins, outs
        self.zs, self.zr, self.cs, self.cr, self.ps, self.pr, self.own = sems
        dp, mp = lax.axis_index(DP), lax.axis_index(MP)
        self.dp, self.mp = dp, mp
        self.parity, self.chip = lax.rem(dp, 2), dp // 2
        self.place = {Z: mp, CHIPS: self.chip, PAIR: self.parity, DP: dp}

    def device(self, group, j):
        if group == Z:
            return (self.dp, j)
        if group == CHIPS:
            return (2 * j + self.parity, self.mp)
        if group == PAIR:
            return (self.dp - self.parity + j, self.mp)
        return (j, self.mp)

    def peer(self, group, off):
        return lax.rem(self.place[group] + off, self.ways[group])

    def remote(self, source, target, send, recv, device):
        return pltpu.make_async_remote_copy(
            src_ref=source,
            dst_ref=target,
            send_sem=send,
            recv_sem=recv,
            device_id=device,
            device_id_type=MESH,
        )

    def meet(self, also=()):
        needed = set(also)
        for kind, group in zip(self.kinds, self.groups):
            if kind in (NEAR, NEARSWAP, WIDE):
                needed |= {CHIPS, PAIR}
                if kind == WIDE:
                    needed.add(Z)
            else:
                needed.add(group)
        barrier = pltpu.get_barrier_semaphore()
        total = 0
        for group in sorted(needed, key=str):
            for off in range(1, self.ways[group]):
                pl.semaphore_signal(
                    barrier,
                    inc=1,
                    device_id=self.device(group, self.peer(group, off)),
                    device_id_type=MESH,
                )
                total += 1
        pl.semaphore_wait(barrier, total)

    def first(self, i):
        kind, group = self.kinds[i], self.groups[i]
        ref, out = self.ins[i], self.outs[i]
        copies = []
        if kind in (NEAR, NEARSWAP):
            return copies
        if kind == WIDE:
            group, slot = Z, out.at[self.dp, self.mp]
        for off in range(1, self.ways[group]):
            peer = self.peer(group, off)
            if kind == WIDE:
                source, target = ref, slot
            elif kind in (GATHER, LATE):
                source, target = ref, out.at[self.place[group]]
            elif kind == MOVE:
                source, target = ref.at[peer], out.at[off - 1]
            elif kind == COLS:
                width = out.shape[-1]
                part = pl.ds(pl.multiple_of(peer * width, width), width)
                source, target = ref.at[:, :, part], out.at[off - 1]
            else:
                source, target = ref.at[:, peer], out.at[off - 1]
            copies.append(
                self.remote(
                    source,
                    target,
                    self.zs.at[i, off - 1],
                    self.zr.at[i, off - 1],
                    self.device(group, peer),
                )
            )
        return copies

    def local(self, i):
        kind, group = self.kinds[i], self.groups[i]
        ref, out = self.ins[i], self.outs[i]
        if kind == WIDE:
            source, target = ref, out.at[self.dp, self.mp]
        elif kind in (GATHER, LATE):
            source, target = ref, out.at[self.place[group]]
        elif kind in (NEAR, NEARSWAP):
            source, target = self.mine(i), out.at[self.dp]
        else:
            return None
        return pltpu.make_async_copy(source, target, self.own.at[i])

    def mine(self, i):
        kind = self.kinds[i]
        if kind == WIDE:
            return self.outs[i].at[self.dp]
        return self.ins[i].at[self.chip] if kind == NEARSWAP else self.ins[i]

    def spread(self, i):
        copies = []
        for off in range(1, self.chips):
            peer = self.peer(CHIPS, off)
            source = self.ins[i].at[peer] if self.kinds[i] == NEARSWAP else self.mine(i)
            copies.append(
                self.remote(
                    source,
                    self.outs[i].at[self.dp],
                    self.cs.at[i, off - 1],
                    self.cr.at[i, off - 1],
                    self.device(CHIPS, peer),
                )
            )
        return copies

    def hand(self, i, off):
        owner = 2 * lax.rem(self.chip + self.chips - off, self.chips) + self.parity
        return self.remote(
            self.mine(i) if off == 0 else self.outs[i].at[owner],
            self.outs[i].at[owner],
            self.ps.at[i, off],
            self.pr.at[i, off],
            self.device(PAIR, 1 - self.parity),
        )

    def begin(self, also=()):
        self.meet(also)
        for i in range(self.count):
            if self.kinds[i] == LATE:
                continue
            for copy in self.first(i):
                copy.start()
            if self.kinds[i] in (NEAR, NEARSWAP):
                for copy in self.spread(i):
                    copy.start()
                self.hand(i, 0).start()
        for i in range(self.count):
            local = self.local(i)
            if local is not None:
                local.start()

    def finish(self):
        shared = [i for i in range(self.count) if self.kinds[i] in (NEAR, NEARSWAP, WIDE)]
        for i in shared:
            if self.kinds[i] == WIDE:
                for copy in self.first(i):
                    copy.wait()
                self.local(i).wait()
                for copy in self.spread(i):
                    copy.start()
                self.hand(i, 0).start()
        for i in range(self.count):
            if self.kinds[i] == LATE:
                for copy in self.first(i):
                    copy.start()
        for i in shared:
            for off, copy in enumerate(self.spread(i), 1):
                copy.wait_recv()
                self.hand(i, off).start()
        for i in range(self.count):
            if i in shared:
                for copy in self.spread(i):
                    copy.wait_send()
                for off in range(self.chips):
                    self.hand(i, off).wait()
                if self.kinds[i] != WIDE:
                    self.local(i).wait()
            else:
                for copy in self.first(i):
                    copy.wait()
                local = self.local(i)
                if local is not None:
                    local.wait()


def exchange_kernel(plan, *refs):
    count = plan.count
    plan.bind(refs[:count], refs[count : 2 * count], refs[2 * count :])
    plan.begin()
    plan.finish()


def exchange(entries, cid):
    plan = Exchange(entries)
    return pl.pallas_call(
        functools.partial(exchange_kernel, plan),
        out_shape=plan.shapes,
        in_specs=plan.specs,
        out_specs=plan.specs,
        scratch_shapes=plan.scratch,
        compiler_params=pltpu.CompilerParams(collective_id=cid, has_side_effects=True),
    )(*plan.arrays)


def added(array, received, group):
    place = {
        Z: lax.axis_index(MP),
        CHIPS: lax.axis_index(DP) // 2,
        PAIR: lax.rem(lax.axis_index(DP), 2),
        DP: lax.axis_index(DP),
    }[group]
    axis = 1 if group == PAIR else 0
    own = lax.dynamic_index_in_dim(array, place, axis, keepdims=False)
    return own.astype(F32) + jnp.sum(received.astype(F32), axis=0)


def sums_kernel(kinds, shapes, *refs):
    n = len(kinds)
    arrays, received, outs = refs[:n], refs[n : 2 * n], refs[2 * n :]
    dp, mp = lax.axis_index(DP), lax.axis_index(MP)
    place = {Z: mp, CHIPS: dp // 2, PAIR: lax.rem(dp, 2)}
    for array, got, out, (kind, group, form) in zip(arrays, received, outs, kinds):
        if kind == GATHER:
            total = jnp.sum(array[...].astype(F32), axis=0)
        else:
            if kind == MOVE:
                own = array[place[group]]
            elif kind == MOVE1:
                own = array[:, place[group]]
            else:
                width = got.shape[-1]
                own = array[:, :, pl.ds(pl.multiple_of(place[group] * width, width), width)]
            total = own.astype(F32)
            for i in range(got.shape[0]):
                total += got[i].astype(F32)
        if form == COLUMNS:
            width = out.shape[-1]
            for i in range(out.shape[0]):
                out[i] = total[:, i * width : (i + 1) * width].astype(out.dtype)
        elif form == TURNED:
            out[...] = total.T
        else:
            out[...] = total.astype(out.dtype)


def sums(entries):
    mp_ways = lax.axis_size(MP)
    arrays, received, shapes, kinds = [], [], [], []
    for array, got, kind, group, form, dtype in entries:
        shape = got.shape[1:]
        if form == COLUMNS:
            shape = (mp_ways, shape[0], shape[1] // mp_ways)
        elif form == TURNED:
            shape = shape[::-1]
        arrays.append(array)
        received.append(got if kind != GATHER else got[:1])
        shapes.append(jax.ShapeDtypeStruct(shape, dtype))
        kinds.append((kind, group, form))
    vmem = pl.BlockSpec(memory_space=pltpu.VMEM)
    return pl.pallas_call(
        functools.partial(sums_kernel, kinds, shapes),
        in_specs=[vmem] * (2 * len(entries)),
        out_specs=[vmem] * len(entries),
        out_shape=shapes,
        compiler_params=pltpu.CompilerParams(vmem_limit_bytes=VMEM_BYTES),
    )(*arrays, *received)


def beside(plan, kernel, inputs, outputs, scratches, *refs):
    n = plan.count
    first, last = pl.program_id(0) == 0, pl.program_id(0) == pl.num_programs(0) - 1
    ins = refs[:inputs]
    sends = refs[inputs : inputs + n]
    outs = refs[inputs + n : inputs + n + outputs]
    lands = refs[inputs + n + outputs : inputs + 2 * n + outputs]
    own = refs[inputs + 2 * n + outputs : inputs + 2 * n + outputs + scratches]
    plan.bind(sends, lands, refs[inputs + 2 * n + outputs + scratches :])
    pl.when(first)(plan.begin)
    kernel(*ins, *outs, *own)
    pl.when(last)(plan.finish)


def memory_call(plan, cid, kernel, name, grid, inputs, in_specs, out_specs, out_shape, scratch, flops):
    return pl.pallas_call(
        functools.partial(beside, plan, kernel, len(inputs), len(out_shape), len(scratch)),
        grid=(grid,),
        in_specs=in_specs + plan.specs,
        out_specs=out_specs + plan.specs,
        out_shape=out_shape + plan.shapes,
        scratch_shapes=scratch + plan.scratch,
        compiler_params=pltpu.CompilerParams(
            vmem_limit_bytes=VMEM_BYTES, collective_id=cid, has_side_effects=True
        ),
        cost_estimate=pl.CostEstimate(flops=flops, bytes_accessed=flops // 200, transcendentals=0),
        name=name,
    )(*inputs, *plan.arrays)


MEM_BLOCK = 16
BACK_BLOCK = 8


def memory_kernel(slots, padded, mem_ref, wk_ref, wv_ref, vb_ref, k_ref, v_ref, rows_ref, wide):
    for c in range(0, D, 128):
        cols = slice(c, c + 128)
        wide[...] = mem_ref[:, :, cols].reshape(slots * MEM_BLOCK, 128).astype(F32)
        for r in range(MEM_BLOCK):
            own = wide[pl.ds(r, slots, stride=MEM_BLOCK), :]
            rows_ref[r * padded : (r + 1) * padded, cols] = jnp.concatenate(
                [own, jnp.zeros((padded - slots, 128), F32)], axis=0
            ).astype(BF)
    rows = rows_ref[...]
    for c in range(0, D, 512):
        cols = slice(c, c + 512)
        k_ref[:, cols] = product(rows, wk_ref[:, cols]).astype(BF)
        v_ref[:, cols] = (product(rows, wv_ref[:, cols]) + vb_ref[:, cols]).astype(BF)


def memory_products(memory, key_weight, value_weight, vbias, padded, plan, cid):
    rows, slots, _ = memory.shape
    whole = lambda a: pl.BlockSpec(a.shape, lambda i: (0,) * a.ndim)
    out = jax.ShapeDtypeStruct((rows * padded, D), BF)
    out_spec = pl.BlockSpec((MEM_BLOCK * padded, D), lambda i: (i, 0))
    return memory_call(
        plan,
        cid,
        functools.partial(memory_kernel, slots, padded),
        "memory_products",
        rows // MEM_BLOCK,
        [jnp.transpose(memory, (1, 0, 2)), key_weight, value_weight, vbias],
        [
            pl.BlockSpec((slots, MEM_BLOCK, D), lambda i: (0, i, 0)),
            whole(key_weight),
            whole(value_weight),
            whole(vbias),
        ],
        [out_spec] * 3,
        [out] * 3,
        [pltpu.VMEM((slots * MEM_BLOCK, 128), F32)],
        4 * rows * padded * D * D,
    )


def memory_weight_kernel(rows_ref, dk_ref, dv_ref, wk_ref, wv_ref, vb_ref, key_sum, value_sum):
    step = pl.program_id(0)

    @pl.when(step == 0)
    def _():
        key_sum[...] = jnp.zeros_like(key_sum)
        value_sum[...] = jnp.zeros_like(value_sum)
        vb_ref[...] = jnp.zeros_like(vb_ref)

    rows = rows_ref[...]
    vb_ref[...] += jnp.sum(dv_ref[...].astype(F32), axis=0, keepdims=True)
    for c in range(0, D, 512):
        cols = slice(c, c + 512)
        key_sum[:, cols] += weight_grad(rows, dk_ref[:, cols])
        value_sum[:, cols] += weight_grad(rows, dv_ref[:, cols])

    @pl.when(step == pl.num_programs(0) - 1)
    def _():
        wk_ref[...] = key_sum[...].astype(BF)
        wv_ref[...] = value_sum[...].astype(BF)


def memory_weights(memory_rows, dkeys, dvalues, rows, padded, plan, cid):
    spec = pl.BlockSpec((BACK_BLOCK * padded, D), lambda i: (i, 0))
    whole = pl.BlockSpec((D, D), lambda i: (0, 0))
    return memory_call(
        plan,
        cid,
        memory_weight_kernel,
        "memory_weights",
        rows // BACK_BLOCK,
        [memory_rows, dkeys, dvalues],
        [spec, spec, spec],
        [whole, whole, pl.BlockSpec((1, D), lambda i: (0, 0))],
        [
            jax.ShapeDtypeStruct((D, D), BF),
            jax.ShapeDtypeStruct((D, D), BF),
            jax.ShapeDtypeStruct((1, D), F32),
        ],
        [pltpu.VMEM((D, D), F32), pltpu.VMEM((D, D), F32)],
        4 * rows * padded * D * D,
    )


def memory_grad_kernel(slots, padded, dk_ref, dv_ref, wk_ref, wv_ref, out_ref, wide):
    for c in range(0, D, 256):
        cols = slice(c, c + 256)
        term = product_back(dk_ref[...], wk_ref[cols, :]) + product_back(dv_ref[...], wv_ref[cols, :])
        for part in range(0, 256, 128):
            for r in range(BACK_BLOCK):
                wide[pl.ds(r, slots, stride=BACK_BLOCK), :] = term[
                    r * padded : r * padded + slots, part : part + 128
                ]
            out_ref[:, :, c + part : c + part + 128] = wide[...].reshape(slots, BACK_BLOCK, 128)


def memory_back(dkeys, dvalues, key_weight, value_weight, rows, slots, padded, plan, cid):
    spec = pl.BlockSpec((BACK_BLOCK * padded, D), lambda i: (i, 0))
    whole = pl.BlockSpec((D, D), lambda i: (0, 0))
    out, *rest = memory_call(
        plan,
        cid,
        functools.partial(memory_grad_kernel, slots, padded),
        "memory_back",
        rows // BACK_BLOCK,
        [dkeys, dvalues, key_weight, value_weight],
        [spec, spec, whole, whole],
        [pl.BlockSpec((slots, BACK_BLOCK, D), lambda i: (0, i, 0))],
        [jax.ShapeDtypeStruct((slots, rows, D), F32)],
        [pltpu.VMEM((slots * BACK_BLOCK, 128), F32)],
        4 * rows * padded * D * D,
    )
    return jnp.transpose(out, (1, 0, 2)), rest


def z_copy(source, target, send, recv, device):
    return pltpu.make_async_remote_copy(
        src_ref=source,
        dst_ref=target,
        send_sem=send,
        recv_sem=recv,
        device_id=(lax.axis_index(DP), device),
        device_id_type=MESH,
    )


def z_meet(ways):
    dp, mp = lax.axis_index(DP), lax.axis_index(MP)
    barrier = pltpu.get_barrier_semaphore()
    for off in range(1, ways):
        pl.semaphore_signal(
            barrier, inc=1, device_id=(dp, lax.rem(mp + off, ways)), device_id_type=MESH
        )
    pl.semaphore_wait(barrier, ways - 1)


def nearest(c, ways):
    mp = lax.axis_index(MP)
    left_n, right_n = mp, ways - 1 - mp
    fewer = jnp.minimum(left_n, right_n)
    paired = c <= 2 * fewer
    distance = jnp.where(paired, (c + 1) // 2, c - fewer)
    left = jnp.where(paired, lax.rem(c, 2) == 1, left_n > right_n)
    return jnp.where(left, mp - distance, mp + distance), distance, left, paired


class LineGather:
    def __init__(self, entries, sems, ways):
        self.entries, self.ways = entries, ways
        self.left_send, self.left_recv, self.right_send, self.right_recv, self.own = sems
        self.mp = lax.axis_index(MP)

    def to_right(self, i, source, place, hop):
        held = self.entries[i][1]
        return z_copy(
            source, held.at[place], self.right_send.at[i, hop], self.right_recv.at[i, hop], self.mp + 1
        )

    def to_left(self, i, source, place, hop):
        held = self.entries[i][1]
        return z_copy(
            source, held.at[place], self.left_send.at[i, hop], self.left_recv.at[i, hop], self.mp - 1
        )

    def begin(self):
        mp, every = self.mp, range(len(self.entries))

        @pl.when(mp < self.ways - 1)
        def _():
            for i in every:
                self.to_right(i, self.entries[i][0], mp, 0).start()

        @pl.when(mp > 0)
        def _():
            for i in every:
                self.to_left(i, self.entries[i][0], mp, 0).start()

        for i in every:
            local = pltpu.make_async_copy(self.entries[i][0], self.entries[i][1].at[mp], self.own.at[i])
            local.start()
            local.wait()

    def arrive(self, c, first):
        mp, every = self.mp, range(len(self.entries))
        _, distance, left, paired = nearest(c, self.ways)
        odd = lax.rem(c, 2) == 1
        due = (c > 0) & first & jnp.logical_not(paired & jnp.logical_not(odd))

        @pl.when(due & (left | (paired & odd)))
        def _():
            place = mp - distance
            for i in every:
                held = self.entries[i][1].at[place]
                self.to_right(i, held, place, distance - 1).wait_recv()

                @pl.when(mp < self.ways - 1)
                def _(i=i, held=held):
                    self.to_right(i, held, place, distance).start()

        @pl.when(due & (jnp.logical_not(left) | (paired & odd)))
        def _():
            place = mp + distance
            for i in every:
                held = self.entries[i][1].at[place]
                self.to_left(i, held, place, distance - 1).wait_recv()

                @pl.when(mp > 0)
                def _(i=i, held=held):
                    self.to_left(i, held, place, distance).start()

    def finish(self):
        mp = self.mp
        for hop in range(self.ways - 1):

            @pl.when((mp < self.ways - 1) & (hop <= mp))
            def _(hop=hop):
                for i, (_, held) in enumerate(self.entries):
                    self.to_right(i, held.at[mp - hop], mp - hop, hop).wait_send()

            @pl.when((mp > 0) & (hop <= self.ways - 1 - mp))
            def _(hop=hop):
                for i, (_, held) in enumerate(self.entries):
                    self.to_left(i, held.at[mp + hop], mp + hop, hop).wait_send()


def line_sems(count, ways):
    dma = pltpu.SemaphoreType.DMA
    return [dma((count, ways)) for _ in range(4)] + [dma((count,))]


def own_heads(result, keep):
    kept = result * keep
    total = kept[0:TOK]
    for h in range(1, GH):
        total = total + kept[h * TOK : (h + 1) * TOK]
    return total


def cross_kernel(
    ways, per, piece, padded, used_ref, k_ref, v_ref, q_ref, keep_ref, ctx_ref, stat_ref, ctx_got, stat_got,
    ctx_out, stat_out, send, recv,
):
    c, j = pl.program_id(0), pl.program_id(1)
    mp = lax.axis_index(MP)
    span = piece * TOK

    @pl.when((c == 0) & (j == 0))
    def _():
        z_meet(ways)

    keep = keep_ref[...]
    keep_wide = keep.astype(F32)
    slot = lax.broadcasted_iota(jnp.int32, (padded, GL), 0)
    for g in range(G):
        cols = slice(g * GC, (g + 1) * GC)
        query = jnp.concatenate([q_ref[:, cols]] * GH, axis=0) * keep
        scores = product_back(k_ref[:, cols], query)
        for r in range(piece):
            rows = slice(r * padded, (r + 1) * padded)
            seen = slot < used_ref[r]
            own = jnp.where(seen, scores[rows], NEG)
            peak = jnp.max(own, axis=0, keepdims=True)
            exponent = jnp.where(seen, jnp.exp(own - peak), 0.0)
            total = jnp.sum(exponent, axis=0, keepdims=True)
            probs = (exponent * (1.0 / jnp.maximum(total, 1e-30))).astype(BF)
            ctx = own_heads(weight_grad(probs, v_ref[rows, cols]), keep_wide)
            ctx_out[c, pl.ds(j * span + r * TOK, TOK), cols] = ctx.astype(BF)
            stat_out[c, 0, j * piece + r, g : g + 1, :] = peak
            stat_out[c, 1, j * piece + r, g : g + 1, :] = total

    def copies(k):
        to = nearest(ways - 1 - k, ways)[0]
        off = lax.rem(to - mp + ways, ways)
        return [
            z_copy(a.at[k], b.at[off - 1], send.at[i, k], recv.at[i, off - 1], to)
            for i, (a, b) in enumerate([(ctx_out, ctx_got), (stat_out, stat_got)])
        ]

    for k in range(ways - 1):

        @pl.when((c == k) & (j == per - 1))
        def _(k=k):
            for copy in copies(k):
                copy.start()

    @pl.when((c == ways - 1) & (j == per - 1))
    def _():
        ctx_ref[...] = ctx_out[ways - 1]
        stat_ref[...] = stat_out[ways - 1]
        for k in range(ways - 1):
            for copy in copies(k):
                copy.wait_send()
        for off in range(1, ways):
            to = lax.rem(mp + off, ways)
            for i, (a, b) in enumerate([(ctx_out, ctx_got), (stat_out, stat_got)]):
                z_copy(a.at[0], b.at[off - 1], send.at[i, 0], recv.at[i, off - 1], to).wait_recv()


def cross_forward(used, keys, values, queries, keep, piece, padded, cid):
    ways = lax.axis_size(MP)
    per = queries.shape[0] // TOK // ways
    rows = per * ways * piece
    shard = per * piece
    at = lambda c, j: nearest(ways - 1 - c, ways)[0] * per + j
    big = pl.BlockSpec((piece * padded, D), lambda c, j: (at(c, j), 0))
    anywhere = pl.BlockSpec(memory_space=pl.ANY)
    dma = pltpu.SemaphoreType.DMA
    return pl.pallas_call(
        functools.partial(cross_kernel, ways, per, piece, padded),
        grid=(ways, per),
        in_specs=[
            pl.BlockSpec((piece, 1, GL), lambda c, j: (at(c, j), 0, 0)),
            big,
            big,
            pl.BlockSpec((TOK, D), lambda c, j: (at(c, j), 0)),
            pl.BlockSpec((GL, GC), lambda c, j: (0, 0)),
        ],
        out_specs=[
            pl.BlockSpec((shard * TOK, D), lambda c, j: (0, 0)),
            pl.BlockSpec((2, shard, G, GL), lambda c, j: (0, 0, 0, 0)),
            anywhere,
            anywhere,
        ],
        out_shape=[
            jax.ShapeDtypeStruct((shard * TOK, D), BF),
            jax.ShapeDtypeStruct((2, shard, G, GL), F32),
            jax.ShapeDtypeStruct((ways - 1, shard * TOK, D), BF),
            jax.ShapeDtypeStruct((ways - 1, 2, shard, G, GL), F32),
        ],
        scratch_shapes=[
            pltpu.VMEM((ways, shard * TOK, D), BF),
            pltpu.VMEM((ways, 2, shard, G, GL), F32),
            dma((2, ways)),
            dma((2, ways)),
        ],
        compiler_params=pltpu.CompilerParams(
            vmem_limit_bytes=VMEM_BYTES, collective_id=cid, has_side_effects=True
        ),
        cost_estimate=pl.CostEstimate(
            flops=4 * rows * padded * GL * D,
            bytes_accessed=4 * rows * padded * D,
            transcendentals=rows * padded * G * GL,
        ),
    )(used, keys, values, queries, keep)


def cross_back_kernel(
    ways, per, piece, padded, used_ref, k_ref, v_ref, q_ref, keep_ref, dctx_ref, stat_ref,
    dk_ref, dv_ref, dq_ref,
    dctx_all, stat_all, dq_out, dq_got, left_send, left_recv, right_send, right_recv, own, send, recv,
):
    c, j = pl.program_id(0), pl.program_id(1)
    mp = lax.axis_index(MP)
    place = nearest(c, ways)[0]
    span = piece * TOK
    line = LineGather(
        [(dctx_ref, dctx_all), (stat_ref, stat_all)],
        (left_send, left_recv, right_send, right_recv, own),
        ways,
    )

    @pl.when((c == 0) & (j == 0))
    def _():
        z_meet(ways)
        line.begin()

    line.arrive(c, j == 0)
    keep = keep_ref[...]
    keep_wide = keep.astype(F32)
    slot = lax.broadcasted_iota(jnp.int32, (padded, GL), 0)
    for g in range(G):
        cols = slice(g * GC, (g + 1) * GC)
        query = jnp.concatenate([q_ref[:, cols]] * GH, axis=0) * keep
        scores = product_back(k_ref[:, cols], query)
        parts = []
        for r in range(piece):
            rows = slice(r * padded, (r + 1) * padded)
            dctx = dctx_all[place, pl.ds(j * span + r * TOK, TOK), cols]
            dctx = jnp.concatenate([dctx] * GH, axis=0) * keep
            dprobs = product_back(v_ref[rows, cols], dctx)
            seen = slot < used_ref[r]
            norm = stat_all[place, 0, j * piece + r, g : g + 1, :]
            middle = stat_all[place, 1, j * piece + r, g : g + 1, :]
            probs = jnp.where(seen, jnp.exp(scores[rows] - norm), 0.0)
            parts.append((probs * (dprobs - middle)).astype(BF))
            dv_ref[rows, cols] = product(probs.astype(BF), dctx).astype(BF)
        dscores = jnp.concatenate(parts, axis=0)
        dk_ref[:, cols] = product(dscores, query).astype(BF)
        dquery = own_heads(weight_grad(dscores, k_ref[:, cols]), keep_wide)
        dq_out[c, pl.ds(j * TOK, TOK), cols] = dquery.astype(BF)

    def copy(k):
        to = nearest(k, ways)[0]
        off = lax.rem(to - mp + ways, ways)
        return z_copy(dq_out.at[k], dq_got.at[off - 1], send.at[k], recv.at[off - 1], to)

    for k in range(1, ways):

        @pl.when((c == k) & (j == per - 1))
        def _(k=k):
            copy(k).start()

    @pl.when((c == ways - 1) & (j == per - 1))
    def _():
        line.finish()
        for k in range(1, ways):
            copy(k).wait_send()
        total = dq_out[0].astype(F32)
        for off in range(1, ways):
            z_copy(
                dq_out.at[0], dq_got.at[off - 1], send.at[0], recv.at[off - 1], lax.rem(mp + off, ways)
            ).wait_recv()
            total += dq_got[off - 1].astype(F32)
        dq_ref[...] = total


def cross_back(used, keys, values, queries, dctx, stats, keep, piece, padded, cid):
    ways = lax.axis_size(MP)
    per = queries.shape[0] // TOK // ways
    rows = per * ways * piece
    shard = per * piece
    at = lambda c, j: nearest(c, ways)[0] * per + j
    big = pl.BlockSpec((piece * padded, D), lambda c, j: (at(c, j), 0))
    anywhere = pl.BlockSpec(memory_space=pl.ANY)
    dma = pltpu.SemaphoreType.DMA
    return pl.pallas_call(
        functools.partial(cross_back_kernel, ways, per, piece, padded),
        grid=(ways, per),
        in_specs=[
            pl.BlockSpec((piece, 1, GL), lambda c, j: (at(c, j), 0, 0)),
            big,
            big,
            pl.BlockSpec((TOK, D), lambda c, j: (at(c, j), 0)),
            pl.BlockSpec((GL, GC), lambda c, j: (0, 0)),
            anywhere,
            anywhere,
        ],
        out_specs=[big, big, pl.BlockSpec((per * TOK, D), lambda c, j: (0, 0))],
        out_shape=[
            jax.ShapeDtypeStruct((rows * padded, D), BF),
            jax.ShapeDtypeStruct((rows * padded, D), BF),
            jax.ShapeDtypeStruct((per * TOK, D), F32),
        ],
        scratch_shapes=[
            pltpu.VMEM((ways, shard * TOK, D), BF),
            pltpu.VMEM((ways, 2, shard, G, GL), F32),
            pltpu.VMEM((ways, per * TOK, D), BF),
            pltpu.VMEM((ways - 1, per * TOK, D), BF),
            *line_sems(2, ways),
            dma((ways,)),
            dma((ways,)),
        ],
        compiler_params=pltpu.CompilerParams(
            vmem_limit_bytes=VMEM_BYTES, collective_id=cid, has_side_effects=True
        ),
        cost_estimate=pl.CostEstimate(
            flops=10 * rows * padded * GL * D,
            bytes_accessed=8 * rows * padded * D,
            transcendentals=rows * padded * G * GL,
        ),
    )(used, keys, values, queries, keep, dctx, stats)


def table_words(table, start, count):
    if table.shape[0] == 1:
        return table[0, pl.ds(start, count), :]
    return jnp.concatenate([table[i, pl.ds(start, count), :] for i in range(table.shape[0])], axis=-1)


def table_load(table_refs, table, sems, tile, c, t):
    tiles = table.shape[1] // tile
    places = [(ref, j * tile) for ref in table_refs for j in range(ref.shape[1] // tile)]

    def copy(k):
        ref, start = places[k]
        source = ref.at[:, pl.ds(start, tile), :]
        return pltpu.make_async_copy(source, table.at[:, pl.ds(k * tile, tile), :], sems.at[k])

    @pl.when((c == 0) & (t == 0))
    def _():
        for k in range(tiles):
            copy(k).start()

    for k in range(tiles):

        @pl.when((c == 0) & (t == k))
        def _(k=k):
            copy(k).wait()


def vocab_kernel(
    ways, tile, sub, chunk, count, h_ref, target_ref, *refs
):
    table_refs, refs = refs[:count], refs[count:]
    vocab_steps(ways, tile, sub, chunk, table_refs, h_ref, target_ref, *refs)


def vocab_steps(
    ways, tile, sub, chunk, table_refs, h_ref, target_ref, exp_ref, tops_ref, stats_ref,
    table, held, run, stats, table_sem, left_send, left_recv, right_send, right_recv, own,
    stat_send, stat_recv, stat_own,
):
    c, t = pl.program_id(0), pl.program_id(1)
    last = pl.num_programs(1) - 1
    mp = lax.axis_index(MP)
    slot = nearest(c, ways)[0]
    line = LineGather(
        [(h_ref, held)], (left_send, left_recv, right_send, right_recv, own), ways
    )

    def stats_copy(off):
        return z_copy(
            stats,
            stats_ref.at[mp],
            stat_send.at[off - 1],
            stat_recv.at[off - 1],
            lax.rem(mp + off, ways),
        )

    @pl.when((c == 0) & (t == 0))
    def _():
        z_meet(ways)
        line.begin()

    line.arrive(c, t == 0)
    table_load(table_refs, table, table_sem, tile, c, t)

    @pl.when(t == 0)
    def _():
        run[0:1, :] = jnp.full((1, chunk), NEG, F32)
        run[1:3, :] = jnp.zeros((2, chunk), F32)

    tokens = held[slot]
    target = target_ref[slot]
    parts = []
    for i in range(tile // sub):
        start = t * tile + i * sub
        logits = product_back(table_words(table, start, sub), tokens)
        top = jnp.max(logits, axis=0, keepdims=True)
        exponent = jnp.exp(logits - top)
        word = lax.broadcasted_iota(jnp.int32, (sub, chunk), 0) + start
        hit = jnp.where(word == target, logits, 0.0)
        exp_ref[0, i * sub : (i + 1) * sub, :] = exponent.astype(BF)
        tops_ref[0, pl.ds(t * (tile // sub) + i, 1), :] = top
        parts.append(
            (top, jnp.sum(exponent, axis=0, keepdims=True), jnp.sum(hit, axis=0, keepdims=True))
        )
    former = run[0:1, :]
    peak = former
    for top, total, hit in parts:
        peak = jnp.maximum(peak, top)
    sums = run[1:2, :] * jnp.exp(former - peak)
    hits = run[2:3, :]
    for top, total, hit in parts:
        sums += total * jnp.exp(top - peak)
        hits += hit
    run[0:1, :] = peak
    run[1:2, :] = sums
    run[2:3, :] = hits

    @pl.when(t == last)
    def _():
        stats[slot] = run[...]

    @pl.when((c == ways - 1) & (t == last))
    def _():
        for off in range(1, ways):
            stats_copy(off).start()
        local = pltpu.make_async_copy(stats, stats_ref.at[mp], stat_own.at[0])
        local.start()
        line.finish()
        for off in range(1, ways):
            stats_copy(off).wait()
        local.wait()


def vocab_sizes(words):
    tile = 1280 if words % 1280 == 0 else words
    sub = 256 if tile % 256 == 0 else tile
    return tile, sub


def vocab_forward(hidden, target, tables, cid):
    ways = lax.axis_size(MP)
    chunk = hidden.shape[0]
    parts, _, width = tables[0].shape
    words = sum(a.shape[1] for a in tables)
    tile, sub = vocab_sizes(words)
    tiles = words // tile
    top_rows = -(-(words // sub) // 8) * 8
    dma = pltpu.SemaphoreType.DMA
    return pl.pallas_call(
        functools.partial(vocab_kernel, ways, tile, sub, chunk, len(tables)),
        grid=(ways, tiles),
        in_specs=[
            pl.BlockSpec(memory_space=pl.ANY),
            pl.BlockSpec((ways, 1, chunk), lambda c, t: (0, 0, 0)),
            *[pl.BlockSpec(memory_space=pl.ANY)] * len(tables),
        ],
        out_specs=[
            pl.BlockSpec((1, tile, chunk), lambda c, t: (c, t, 0)),
            pl.BlockSpec((1, top_rows, chunk), lambda c, t: (c, 0, 0)),
            pl.BlockSpec(memory_space=pl.ANY),
        ],
        out_shape=[
            jax.ShapeDtypeStruct((ways, words, chunk), BF),
            jax.ShapeDtypeStruct((ways, top_rows, chunk), F32),
            jax.ShapeDtypeStruct((ways, ways, 8, chunk), F32),
        ],
        scratch_shapes=[
            pltpu.VMEM((parts, words, width), BF),
            pltpu.VMEM((ways, chunk, D), BF),
            pltpu.VMEM((8, chunk), F32),
            pltpu.VMEM((ways, 8, chunk), F32),
            dma((tiles,)),
            *line_sems(1, ways),
            dma((ways,)),
            dma((ways,)),
            dma((1,)),
        ],
        compiler_params=pltpu.CompilerParams(
            vmem_limit_bytes=VMEM_BYTES, collective_id=cid, has_side_effects=True
        ),
        cost_estimate=pl.CostEstimate(
            flops=2 * ways * chunk * words * D,
            bytes_accessed=2 * ways * words * D,
            transcendentals=ways * chunk * words,
        ),
    )(hidden, target, *tables)


def vocab_back_kernel(
    ways, tile, sub, chunk, count, exp_ref, tops_ref, target_ref, norm_ref, rate_ref, *refs
):
    table_refs, refs = refs[:count], refs[count:]
    vocab_back_steps(
        ways, tile, sub, chunk, table_refs, exp_ref, tops_ref, target_ref, norm_ref, rate_ref, *refs
    )


def vocab_back_steps(
    ways, tile, sub, chunk, table_refs, exp_ref, tops_ref, target_ref, norm_ref, rate_ref, out_ref,
    table, total, terms, leaving, landing, table_sem, send, recv,
):
    c, t = pl.program_id(0), pl.program_id(1)
    last = pl.num_programs(1) - 1
    mp = lax.axis_index(MP)
    slot = nearest(ways - 1 - c, ways)[0]

    def copy(to):
        right = to > mp
        spot = jnp.where(right | (to < mp - 1), to, ways)
        return z_copy(
            leaving.at[to],
            landing.at[spot],
            send.at[to],
            recv.at[spot],
            jnp.where(right, mp + 1, mp - 1),
        )

    def arrived(spot):
        z_copy(
            leaving.at[0], landing.at[spot], send.at[0], recv.at[spot], lax.rem(mp + 1, ways)
        ).wait_recv()

    @pl.when((c == 0) & (t == 0))
    def _():
        z_meet(ways)

    table_load(table_refs, table, table_sem, tile, c, t)
    target, norm, rate = target_ref[slot], norm_ref[slot], rate_ref[slot]
    term = None
    for i in range(tile // sub):
        start = t * tile + i * sub
        factor = jnp.exp(tops_ref[0, pl.ds(t * (tile // sub) + i, 1), :] - norm) * -rate
        word = lax.broadcasted_iota(jnp.int32, (sub, chunk), 0) + start
        hit = jnp.where(word == target, rate, 0.0)
        dlogits = hit + exp_ref[0, i * sub : (i + 1) * sub, :].astype(F32) * factor
        part = weight_grad(dlogits.astype(BF), table_words(table, start, sub))
        term = part if term is None else term + part

    @pl.when(t == 0)
    def _():
        total[...] = term

    @pl.when(t > 0)
    def _():
        total[...] += term

    for k in range(ways - 1):
        to = nearest(ways - 1 - k, ways)[0]
        beyond = jnp.where(to > mp, mp > 0, mp < ways - 1)

        @pl.when((c == k) & (t == last) & jnp.logical_not(beyond))
        def _(to=to):
            leaving[to] = total[...].astype(BF)
            copy(to).start()

        @pl.when((c == k) & (t == last) & beyond)
        def _(k=k):
            terms[k] = total[...]

    for k in range(ways - 1):
        to = nearest(ways - 1 - k, ways)[0]
        beyond = jnp.where(to > mp, mp > 0, mp < ways - 1)

        @pl.when((c == min(k + 2, ways - 1)) & (t == last) & beyond)
        def _(k=k, to=to):
            arrived(to)
            leaving[to] = (terms[k] + landing[to].astype(F32)).astype(BF)
            copy(to).start()

    @pl.when((c == ways - 1) & (t == last))
    def _():
        out_ref[...] = total[...]

        @pl.when(mp > 0)
        def _():
            arrived(mp)
            out_ref[...] += landing[mp].astype(F32)

        @pl.when(mp < ways - 1)
        def _():
            arrived(ways)
            out_ref[...] += landing[ways].astype(F32)

        for k in range(ways - 1):
            copy(nearest(ways - 1 - k, ways)[0]).wait_send()


def vocab_back(exponents, tops, target, norm, rate, tables, cid):
    ways, words, chunk = exponents.shape
    tile, sub = vocab_sizes(words)
    tiles = words // tile
    whole = pl.BlockSpec((ways, 1, chunk), lambda c, t: (0, 0, 0))
    dma = pltpu.SemaphoreType.DMA
    return pl.pallas_call(
        functools.partial(vocab_back_kernel, ways, tile, sub, chunk, len(tables)),
        grid=(ways, tiles),
        in_specs=[
            pl.BlockSpec((1, tile, chunk), lambda c, t: (ways - 1 - c, t, 0)),
            pl.BlockSpec((1, tops.shape[1], chunk), lambda c, t: (ways - 1 - c, 0, 0)),
            whole,
            whole,
            whole,
            *[pl.BlockSpec(memory_space=pl.ANY)] * len(tables),
        ],
        out_specs=pl.BlockSpec((chunk, D), lambda c, t: (0, 0)),
        out_shape=jax.ShapeDtypeStruct((chunk, D), F32),
        scratch_shapes=[
            pltpu.VMEM((tables[0].shape[0], words, tables[0].shape[2]), BF),
            pltpu.VMEM((chunk, D), F32),
            pltpu.VMEM((ways - 1, chunk, D), F32),
            pltpu.VMEM((ways, chunk, D), BF),
            pltpu.VMEM((ways + 1, chunk, D), BF),
            dma((tiles,)),
            dma((ways,)),
            dma((ways + 1,)),
        ],
        compiler_params=pltpu.CompilerParams(
            vmem_limit_bytes=VMEM_BYTES, collective_id=cid, has_side_effects=True
        ),
        cost_estimate=pl.CostEstimate(
            flops=2 * ways * chunk * words * D, bytes_accessed=2 * ways * words * D, transcendentals=0
        ),
    )(exponents, tops, target, norm, rate, *tables)


HIDDEN_TILE = 512
ROOT_HALF = 0.7071067811865476
ROOT_TAU = 0.3989422804014327


def weight_tile(ref):
    return ref[...].reshape(D, ref.shape[-1])


def feed_kernel(h_ref, expand_ref, bias_ref, shrink_ref, a_ref, out_ref):
    t = pl.program_id(0)
    hidden = product(h_ref[...], weight_tile(expand_ref)) + bias_ref[0]
    a_ref[...] = hidden
    active = (hidden * (0.5 + 0.5 * lax.erf(hidden * ROOT_HALF))).astype(BF)
    term = product_back(active, weight_tile(shrink_ref))

    @pl.when(t == 0)
    def _():
        out_ref[...] = term

    @pl.when(t > 0)
    def _():
        out_ref[...] += term


def feed_specs(weights):
    parts, ways, _, rows, units = weights.shape
    per = units // HIDDEN_TILE
    tile = lambda which: pl.BlockSpec(
        (parts, 1, 1, rows, HIDDEN_TILE), lambda t: (0, t // per, which, 0, t % per)
    )
    bias = pl.BlockSpec((1, 1, HIDDEN_TILE), lambda t: (t, 0, 0))
    return tile(0), bias, tile(1), ways * per


def feed_forward(hidden, weights, bias):
    tokens = hidden.shape[0]
    expand_spec, bias_spec, shrink_spec, tiles = feed_specs(weights)
    whole = pl.BlockSpec((tokens, D), lambda t: (0, 0))
    units = tiles * HIDDEN_TILE
    return pl.pallas_call(
        feed_kernel,
        grid=(tiles,),
        in_specs=[whole, expand_spec, bias_spec, shrink_spec],
        out_specs=[pl.BlockSpec((tokens, HIDDEN_TILE), lambda t: (0, t)), whole],
        out_shape=[
            jax.ShapeDtypeStruct((tokens, units), F32),
            jax.ShapeDtypeStruct((tokens, D), F32),
        ],
        compiler_params=pltpu.CompilerParams(vmem_limit_bytes=VMEM_BYTES),
        cost_estimate=pl.CostEstimate(
            flops=4 * tokens * units * D, bytes_accessed=4 * units * D, transcendentals=tokens * units
        ),
    )(hidden, weights, bias.reshape(tiles, 1, HIDDEN_TILE), weights)


def feed_back_kernel(
    dout_ref, h_ref, a_ref, expand_ref, shrink_ref, dweights_ref, dbias_ref, dh_ref
):
    t = pl.program_id(0)
    dout = dout_ref[...]
    hidden = a_ref[...]
    below = 0.5 + 0.5 * lax.erf(hidden * ROOT_HALF)
    slope = below + hidden * (ROOT_TAU * jnp.exp(-0.5 * hidden * hidden))
    active = (hidden * below).astype(BF)
    dhidden = (slope * product(dout, weight_tile(shrink_ref))).astype(BF)
    dbias_ref[0] = jnp.sum(dhidden.astype(F32), axis=0, keepdims=True)
    parts, _, rows, width = dweights_ref.shape
    dweights_ref[:, 0] = weight_grad(h_ref[...], dhidden).astype(BF).reshape(parts, rows, width)
    dweights_ref[:, 1] = weight_grad(dout, active).astype(BF).reshape(parts, rows, width)
    term = product_back(dhidden, weight_tile(expand_ref))

    @pl.when(t == 0)
    def _():
        dh_ref[...] = term

    @pl.when(t > 0)
    def _():
        dh_ref[...] += term


def feed_back(dout, hidden, before, weights):
    tokens = hidden.shape[0]
    expand_spec, bias_spec, shrink_spec, tiles = feed_specs(weights)
    parts, rows = weights.shape[0], weights.shape[3]
    whole = pl.BlockSpec((tokens, D), lambda t: (0, 0))
    units = tiles * HIDDEN_TILE
    return pl.pallas_call(
        feed_back_kernel,
        grid=(tiles,),
        in_specs=[
            whole,
            whole,
            pl.BlockSpec((tokens, HIDDEN_TILE), lambda t: (0, t)),
            expand_spec,
            shrink_spec,
        ],
        out_specs=[
            pl.BlockSpec((parts, 2, rows, HIDDEN_TILE), lambda t: (0, 0, 0, t)),
            bias_spec,
            whole,
        ],
        out_shape=[
            jax.ShapeDtypeStruct((parts, 2, rows, units), BF),
            jax.ShapeDtypeStruct((tiles, 1, HIDDEN_TILE), F32),
            jax.ShapeDtypeStruct((tokens, D), F32),
        ],
        compiler_params=pltpu.CompilerParams(vmem_limit_bytes=VMEM_BYTES),
        cost_estimate=pl.CostEstimate(
            flops=8 * tokens * units * D, bytes_accessed=8 * units * D, transcendentals=2 * tokens * units
        ),
    )(dout, hidden, before, weights, weights)


def self_back_kernel(
    plan, x_ref, dout_ref, ctx_ref, q_ref, k_ref, v_ref, wo_ref, wqkv_ref, keep_ref, dfirst_ref, *refs
):
    n = plan.count
    sends, rest = refs[:n], refs[n:]
    bias_ref, dself_ref, dwo_ref, din_ref = rest[:4]
    lands, rest = rest[4 : 4 + n], rest[4 + n :]
    dctx, dqkv, part, part_got, din, dself, dself_got, dwo, dwo_got = rest[:9]
    send, recv, own = rest[9:12]
    plan.bind(sends, lands, rest[12:])
    ways = plan.mp_ways
    mp, parity = plan.mp, plan.parity

    def part_copy(off):
        to = plan.peer(Z, off)
        return z_copy(part.at[to], part_got.at[off - 1], send.at[0, off], recv.at[0, off], to)

    def din_copy(off):
        return z_copy(din, din_ref.at[mp], send.at[1, off], recv.at[1, off], plan.peer(Z, off))

    def core_copies():
        return [
            plan.remote(a.at[:, 1 - parity], b, send.at[2, i], recv.at[2, i], plan.device(PAIR, 1 - parity))
            for i, (a, b) in enumerate([(dself, dself_got), (dwo, dwo_got)])
        ]

    plan.begin((Z, PAIR))
    keep = keep_ref[...]
    keep_wide = keep.astype(F32)
    dctx[...] = product_back(dout_ref[...], wo_ref[...]).astype(BF)
    key_place = lax.broadcasted_iota(jnp.int32, (TOK, GL), 0)
    query_place = lax.rem(lax.broadcasted_iota(jnp.int32, (TOK, GL), 1), TOK)
    seen = key_place <= query_place

    @pl.loop(0, x_ref.shape[0] // TOK)
    def _(question):
        rows = pl.ds(pl.multiple_of(question * TOK, TOK), TOK)
        keys, values = k_ref[rows, :], v_ref[rows, :]
        query = jnp.concatenate([q_ref[rows, :]] * GH, axis=0) * keep
        upstream = jnp.concatenate([dctx[rows, :]] * GH, axis=0) * keep
        scores = jnp.where(seen, product_back(keys, query), NEG)
        exponent = jnp.exp(scores - jnp.max(scores, axis=0, keepdims=True))
        probs = exponent / jnp.sum(exponent, axis=0, keepdims=True)
        dprobs = product_back(values, upstream)
        middle = jnp.sum(probs * dprobs, axis=0, keepdims=True)
        dscores = (probs * (dprobs - middle)).astype(BF)
        dquery = own_heads(weight_grad(dscores, keys), keep_wide)
        dqkv[rows, 0:GC] = (dquery * SCALE).astype(BF)
        dqkv[rows, GC : 2 * GC] = product(dscores, query).astype(BF)
        dqkv[rows, 2 * GC : 3 * GC] = product(probs.astype(BF), upstream).astype(BF)

    grads = dqkv[...]
    part[...] = product_back(grads, wqkv_ref[...]).astype(BF).reshape(part.shape)
    for off in range(1, ways):
        part_copy(off).start()
    dself[...] = weight_grad(x_ref[...], grads).astype(BF).reshape(dself.shape)
    dwo[...] = weight_grad(dout_ref[...], ctx_ref[...]).astype(BF).reshape(dwo.shape)
    for copy in core_copies():
        copy.start()
    bias_ref[...] = jnp.sum(grads.astype(F32), axis=0, keepdims=True)
    total = dfirst_ref[...] + part[mp].astype(F32)
    for off in range(1, ways):
        part_copy(off).wait_recv()
        total += part_got[off - 1].astype(F32)
    din[...] = total.astype(BF)
    for off in range(1, ways):
        din_copy(off).start()
    local = pltpu.make_async_copy(din, din_ref.at[mp], own.at[0])
    local.start()
    for copy in core_copies():
        copy.wait()
    dself_ref[...] = (dself[:, parity].astype(F32) + dself_got[...].astype(F32)).astype(BF)
    dwo_ref[...] = (dwo[:, parity].astype(F32) + dwo_got[...].astype(F32)).astype(BF)
    plan.finish()
    for off in range(1, ways):
        part_copy(off).wait_send()
        din_copy(off).wait()
    local.wait()


def self_back(x, dout, ctx, queries, keys, values, wo, wqkv, keep, dfirst, plan, cid):
    uniq, shard = x.shape[0], dfirst.shape[0]
    ways, chips = plan.mp_ways, plan.chips
    vec = D // plan.dp_ways
    inputs = [x, dout, ctx, queries, keys, values, wo, wqkv, keep, dfirst]
    vmem = pl.BlockSpec(memory_space=pltpu.VMEM)
    dma = pltpu.SemaphoreType.DMA
    cols = wqkv.shape[1]
    return pl.pallas_call(
        functools.partial(self_back_kernel, plan),
        in_specs=[vmem] * len(inputs) + plan.specs,
        out_specs=[vmem, vmem, vmem, pl.BlockSpec(memory_space=pl.ANY)] + plan.specs,
        out_shape=[
            jax.ShapeDtypeStruct((1, cols), F32),
            jax.ShapeDtypeStruct((chips, vec, cols), BF),
            jax.ShapeDtypeStruct((chips, vec, GC), BF),
            jax.ShapeDtypeStruct((ways, shard, D), BF),
        ]
        + plan.shapes,
        scratch_shapes=[
            pltpu.VMEM((uniq, GC), BF),
            pltpu.VMEM((uniq, cols), BF),
            pltpu.VMEM((ways, shard, D), BF),
            pltpu.VMEM((ways - 1, shard, D), BF),
            pltpu.VMEM((shard, D), BF),
            pltpu.VMEM((chips, 2, vec, cols), BF),
            pltpu.VMEM((chips, vec, cols), BF),
            pltpu.VMEM((chips, 2, vec, GC), BF),
            pltpu.VMEM((chips, vec, GC), BF),
            dma((3, ways)),
            dma((3, ways)),
            dma((1,)),
            *plan.scratch,
        ],
        compiler_params=pltpu.CompilerParams(
            vmem_limit_bytes=VMEM_BYTES, collective_id=cid, has_side_effects=True
        ),
        cost_estimate=pl.CostEstimate(
            flops=4 * uniq * D * cols, bytes_accessed=8 * uniq * D, transcendentals=uniq * GL
        ),
    )(*inputs, *plan.arrays)


def self_probs(queries, key_heads):
    causal = (
        lax.broadcasted_iota(jnp.int32, (TOK, TOK), 1)
        <= lax.broadcasted_iota(jnp.int32, (TOK, TOK), 0)
    )[None, None]
    scores = jnp.einsum("rqhe,rkhe->rhqk", queries, key_heads, preferred_element_type=F32)
    return jax.nn.softmax(jnp.where(causal, scores, NEG), axis=-1)


def column_parts(gathered):
    return jnp.concatenate([gathered[i] for i in range(gathered.shape[0])], axis=-1)


def block_rows(array, ways):
    rows, columns = array.shape
    width = columns // ways
    return jnp.stack([array[:, i * width : (i + 1) * width] for i in range(ways)])


def local(
    answers,
    targets,
    doc_scores,
    memory,
    lengths,
    self_query,
    self_key,
    self_value,
    query_bias,
    value_bias,
    self_output,
    output_bias,
    first_gain,
    first_shift,
    cross_query,
    crossq_bias,
    cross_key,
    cross_value,
    crossv_bias,
    cross_output,
    crosso_bias,
    second_gain,
    second_shift,
    expand_weight,
    expand_bias,
    shrink_weight,
    shrink_bias,
    third_gain,
    third_shift,
    word_table,
):
    dp_ways, mp_ways = lax.axis_size(DP), lax.axis_size(MP)
    chips = dp_ways // 2
    dp, mp = lax.axis_index(DP), lax.axis_index(MP)
    groups = answers.shape[0]
    rows, slots, _ = memory.shape
    piece = rows // dp_ways
    own_q = dp_ways
    uniq = own_q * TOK
    tokens = rows * TOK
    padded = -(-slots // 16) * 16
    shard_rows = rows // mp_ways
    shard_tokens = shard_rows * TOK
    shard_q = own_q // mp_ways
    shard_uniq = shard_q * TOK
    local_heads = H // mp_ways
    head_cols = local_heads * HD
    hidden_cols = expand_weight.shape[1]
    vec = D // dp_ways

    vectors = (
        output_bias,
        first_gain,
        first_shift,
        crosso_bias,
        second_gain,
        second_shift,
        shrink_bias,
        third_gain,
        third_shift,
        crossv_bias,
    )
    matrices = (query_bias, value_bias, crossq_bias, expand_bias)
    starts, top = [], 16
    for matrix in matrices:
        starts.append(top)
        top += -(-matrix.shape[0] // 8) * 8
    small_rows = -(-top // 16) * 16
    row_of = lax.broadcasted_iota(jnp.int32, (small_rows, 128), 0)
    small = jnp.zeros((small_rows, 128), BF)
    for i, vector in enumerate(vectors):
        vector = jnp.pad(vector, (0, 128 - vector.shape[0]))
        small = jnp.where(row_of == i, vector[None, :], small)
    for start, matrix in zip(starts, matrices):
        count, width = matrix.shape
        small += jnp.pad(matrix, ((start, small_rows - start - count), (0, 128 - width)))
    wide_rows = cross_key.shape[0]
    self_shard = jnp.concatenate([self_query, self_key, self_value], axis=1)
    target_rows = jnp.pad(targets, ((0, 8 - groups), (0, 128 - TOK)))
    doc_rows = jnp.pad(doc_scores, ((0, 8 - groups), (0, 128 - K)))
    if chips == groups:
        wanted = answers
    else:
        wanted = jnp.stack([answers[(2 * c * piece) // K] for c in range(chips)])
    feed_shard = jnp.stack([expand_weight, shrink_weight.T]).reshape(4, vec // 2, -1)
    key_all, value_all, small_all, cquery_z, cout_z, feed_first = exchange(
        [
            (cross_key, WIDE, Z),
            (cross_value, WIDE, Z),
            (small, WIDE, Z),
            (cross_query, LATE, Z),
            (cross_output, LATE, Z),
            (feed_shard[0], LATE, Z),
        ],
        0,
    )
    (full_obias, gain_one, shift_one, full_cobias, gain_two, shift_two, full_sbias, gain_three, shift_three) = [
        small_all[:, 0, i, :vec].reshape(D) for i in range(9)
    ]
    cvbias = small_all[:, :, 9, :wide_rows].reshape(1, D)

    def head_bias(i):
        count, width = matrices[i].shape
        part = small_all[:, :, starts[i] : starts[i] + count, :width]
        return jnp.transpose(part, (1, 2, 0, 3)).reshape(mp_ways, -1)

    mine = lambda a: lax.dynamic_index_in_dim(a, mp, 0, keepdims=False)
    qbias = mine(head_bias(0))
    vbias = mine(head_bias(1))
    cqbias = head_bias(2).reshape(-1)
    ebias = head_bias(3).reshape(-1)
    key_weight = key_all.reshape(D, D)
    value_weight = value_all.reshape(D, D)

    plan = Exchange(
        [
            (feed_shard[1:], GATHER, Z),
            (self_shard, NEAR, Z),
            (self_output, NEAR, Z),
            (target_rows, NEAR, Z),
            (doc_rows, NEAR, Z),
            (wanted, NEARSWAP, Z),
            (cquery_z, NEAR, Z),
            (cout_z, NEAR, Z),
        ]
    )
    (keys, values, memory_rows, feed_rest, self_all, output_all, target_all, doc_all, x_all, cquery_all, cout_all) = (
        memory_products(memory, key_weight, value_weight, cvbias, padded, plan, 1)
    )
    words = word_table.shape[0]
    early = words // 1280 * 3 // 5 * 1280 if words % 1280 == 0 else 0
    feed_z = jnp.concatenate([feed_first[:, None], feed_rest], axis=1)
    tables = []
    if early:
        part, _ = lax.optimization_barrier((word_table[:early], small_all))
        part = lax.all_gather(part, DP, axis=0, tiled=False)
        feed_z, part = lax.optimization_barrier((feed_z, part))
        tables.append(part)
    feed_all = lax.all_gather(feed_z, DP, axis=0, tiled=False)
    feed_all = feed_all.reshape(dp_ways, mp_ways, 2, vec, -1)
    tables.append(lax.all_gather(word_table[early:], DP, axis=0, tiled=False))
    if word_table.shape[1] < 128:
        tables = [column_parts(a)[None] for a in tables]
    rows_first = lambda a: jnp.transpose(a, (0, 2, 1, 3)).reshape(dp_ways * a.shape[2], -1)
    columns_first = lambda a: column_parts(a.reshape(dp_ways, -1, a.shape[-1]))
    self_weight = self_all.reshape(D, 3 * head_cols)
    full_output = column_parts(output_all)
    my_group = (dp * piece) // K
    row_targets = lax.dynamic_index_in_dim(
        target_all[:, :groups, :TOK], my_group, 1, keepdims=False
    )
    x_rows = x_all.reshape(uniq, D)

    qkv = product(x_rows, self_weight)
    queries = ((qkv[:, :head_cols] + qbias) * SCALE).astype(BF)
    self_keys = qkv[:, head_cols : 2 * head_cols].astype(BF)
    self_values = (qkv[:, 2 * head_cols :] + vbias).astype(BF)
    heads = lambda a: a.reshape(own_q, TOK, local_heads, HD)
    probs = self_probs(heads(queries), heads(self_keys))
    context = jnp.einsum(
        "rhqk,rkhe->rqhe", probs.astype(BF), heads(self_values), preferred_element_type=F32
    )
    context = context.astype(BF).reshape(uniq, head_cols)
    partial = product(context, full_output).astype(BF).reshape(mp_ways, shard_uniq, D)
    (received,) = exchange([(partial, MOVE, Z)], 2)
    full_cquery = rows_first(cquery_all)
    x_own = lax.dynamic_slice_in_dim(x_rows, mp * shard_uniq, shard_uniq, 0)
    first_in = x_own.astype(F32) + added(partial, received, Z) + full_obias
    hidden_one, normed_one, inverse_one = layer_norm(first_in, gain_one, shift_one)
    hidden_low1 = hidden_one.astype(BF)
    cross_queries = ((product(hidden_low1, full_cquery) + cqbias) * SCALE).astype(BF)
    (cross_queries,) = exchange([(cross_queries, GATHER, Z)], 3)
    full_cout = columns_first(cout_all)
    cross_queries = cross_queries.reshape(uniq, D)

    used = jnp.clip(lengths - mp * slots, 0, slots).astype(jnp.int32)
    used = jnp.broadcast_to(used[:, None, None], (rows, 1, GL))
    keep = (
        lax.broadcasted_iota(jnp.int32, (GL, GC), 0) // TOK
        == lax.broadcasted_iota(jnp.int32, (GL, GC), 1) // HD
    ).astype(BF)
    ctx_own, stat_own, ctx_got, stat_got = cross_forward(
        used, keys, values, cross_queries, keep, piece, padded, 4
    )
    stat_got = jnp.concatenate([stat_own[None], stat_got], axis=0)
    peak_got, total_got = stat_got[:, 0], stat_got[:, 1]
    peak = jnp.max(peak_got, axis=0)
    weight = total_got * jnp.exp(peak_got - peak)
    total = jnp.sum(weight, axis=0)
    cross_norm = peak + jnp.log(total)
    weight = weight / total

    def to_token_heads(a):
        lead = a.shape[:-3]
        a = a.reshape(lead + (shard_rows, H, TOK))
        return jnp.swapaxes(a, -1, -2).reshape(lead + (shard_tokens, H))

    weight = jnp.repeat(to_token_heads(weight), HD, axis=-1)
    context_two = (
        ctx_own.astype(F32) * weight[0] + jnp.sum(ctx_got.astype(F32) * weight[1:], axis=0)
    ).astype(BF)

    def to_rows(a):
        a = jnp.broadcast_to(a.reshape(shard_q, 1, TOK, D), (shard_q, piece, TOK, D))
        return a.reshape(shard_tokens, D)

    second_in = to_rows(hidden_one) + product(context_two, full_cout) + full_cobias
    hidden_two, normed_two, inverse_two = layer_norm(second_in, gain_two, shift_two)
    hidden_low2 = hidden_two.astype(BF)

    expanded, third_in = feed_forward(hidden_low2, feed_all, ebias)
    third_in = hidden_two + third_in + full_sbias
    hidden_three, normed_three, inverse_three = layer_norm(third_in, gain_three, shift_three)

    vocab_local = words
    token_targets = jnp.broadcast_to(row_targets.reshape(own_q, 1, TOK), (own_q, piece, TOK))
    local_target = token_targets.reshape(mp_ways, 1, shard_tokens) - mp * vocab_local
    exponents, tops, stats = vocab_forward(hidden_three.astype(BF), local_target, tables, 5)
    stats = jnp.transpose(stats[:, :, :3], (0, 2, 1, 3)).reshape(mp_ways, 3, tokens)
    top = jnp.max(stats[:, 0], axis=0)
    norm_log = top + jnp.log(jnp.sum(stats[:, 1] * jnp.exp(stats[:, 0] - top), axis=0))
    loglik = jnp.sum(stats[:, 2], axis=0) - norm_log
    (loglik_all,) = exchange([(loglik.reshape(tokens // 128, 128), GATHER, DP)], 7)
    loglik_all = loglik_all.reshape(dp_ways, own_q, piece, TOK)
    loglik_all = jnp.transpose(loglik_all, (1, 0, 2, 3)).reshape(own_q, groups, K, TOK)
    doc_logp = jax.nn.log_softmax(doc_all[:, :groups, :K], axis=2)
    joined = doc_logp[..., None] + loglik_all
    marginal = jax.nn.logsumexp(joined, axis=2, keepdims=True)
    question_loss = -jnp.mean(
        lax.dynamic_index_in_dim(marginal[:, :, 0], dp, 0, keepdims=False), axis=1
    )
    posterior = jnp.exp(joined - marginal).reshape(own_q, groups * K, TOK)
    rate = -lax.dynamic_slice_in_dim(posterior, dp * piece, piece, 1)
    by_slot = lambda a: a.reshape(mp_ways, 1, shard_tokens)
    dhidden_three = vocab_back(
        exponents, tops, local_target, by_slot(norm_log), by_slot(rate), tables, 8
    )

    dthird, dgain_three, dshift_three = norm_back(
        dhidden_three, normed_three, inverse_three, gain_three
    )
    dshrink_bias = jnp.sum(dthird, axis=0)
    dshrink_in = dthird.astype(BF)
    dfeed, dexpand_bias, dhidden_two = feed_back(dshrink_in, hidden_low2, expanded, feed_all)
    dexpand_bias = dexpand_bias.reshape(-1)
    feed_dp = lax.psum_scatter(dfeed, DP, scatter_dimension=0, tiled=False)
    dhidden_two = dthird + dhidden_two

    dsecond, dgain_two, dshift_two = norm_back(dhidden_two, normed_two, inverse_two, gain_two)
    dcout_bias = jnp.sum(dsecond, axis=0)
    dcout_in = dsecond.astype(BF)
    dcontext_two = product_back(dcout_in, full_cout).astype(BF)
    middle = jnp.sum(
        (dcontext_two.astype(F32) * context_two.astype(F32)).reshape(shard_tokens, H, HD), axis=-1
    )
    middle = jnp.swapaxes(middle.reshape(shard_rows, TOK, H), 1, 2).reshape(shard_rows, G, GL)
    owners = lambda a: a.reshape(chips, 2, -1, a.shape[-1])
    cast = lambda a: a.astype(BF)
    co_blocks = owners(cast(weight_grad(dcout_in, context_two)))
    stat_all = jnp.stack([cross_norm, middle])
    dkeys, dvalues, dcross_q = cross_back(
        used, keys, values, cross_queries, dcontext_two, stat_all, keep, piece, padded, 9
    )
    dcross_low = (dcross_q * SCALE).astype(BF)
    dcquery = weight_grad(hidden_low1, dcross_low)
    dcq_bias = jnp.sum(dcross_low, axis=0, dtype=F32)
    dhidden_one = jnp.sum(dsecond.reshape(shard_q, piece, TOK, D), axis=1).reshape(
        shard_uniq, D
    ) + product_back(dcross_low, full_cquery)

    dfirst, dgain_one, dshift_one = norm_back(dhidden_one, normed_one, inverse_one, gain_one)
    dout_bias = jnp.sum(dfirst, axis=0)
    cq_blocks = owners(cast(dcquery))
    plan = Exchange(
        [
            (cast(dfirst), GATHER, Z),
            (co_blocks, MOVE1, PAIR),
            (cq_blocks, MOVE1, PAIR),
        ]
    )
    dkey_weight, dvalue_weight, dvalue_bias, dout_in, co_got, cq_got = memory_weights(
        memory_rows, dkeys, dvalues, rows, padded, plan, 11
    )
    co_blocks, cq_blocks = sums(
        [
            (co_blocks, co_got, MOVE1, PAIR, PLAIN, BF),
            (cq_blocks, cq_got, MOVE1, PAIR, PLAIN, BF),
        ]
    )
    dout_in = dout_in.reshape(uniq, D)
    memory_blocks = [owners(dkey_weight), owners(dvalue_weight)]
    plan = Exchange(
        [(co_blocks, MOVE, CHIPS), (cq_blocks, MOVE, CHIPS)]
        + [(a, MOVE1, PAIR) for a in memory_blocks]
    )
    dqkv_bias, self_blocks, out_blocks, dinputs, co_got, cq_got, *memory_got = self_back(
        x_rows, dout_in, context, queries, self_keys, self_values, full_output, self_weight, keep,
        dfirst, plan, 12,
    )
    dqkv_bias = dqkv_bias[0]
    key_blocks, value_blocks = sums(
        [(a, b, MOVE1, PAIR, PLAIN, BF) for a, b in zip(memory_blocks, memory_got)]
    )

    vectors = jnp.stack(
        [
            dout_bias,
            dgain_one,
            dshift_one,
            dcout_bias,
            dgain_two,
            dshift_two,
            dshrink_bias,
            dgain_three,
            dshift_three,
            dvalue_bias[0],
            dcq_bias,
            jnp.pad(dqkv_bias, (0, D - 3 * head_cols)),
        ]
    )
    vectors = jnp.concatenate([vectors, dexpand_bias.reshape(-1, D)], axis=0)
    answer_blocks = dinputs.reshape(chips, 2, TOK, D)
    plan = Exchange(
        [(feed_dp, COLS, Z)]
        + [
            (a, MOVE, CHIPS)
            for a in (value_blocks, self_blocks, out_blocks, key_blocks, answer_blocks)
        ]
        + [(vectors, GATHER, DP)]
    )
    memory_grad, received = memory_back(
        dkeys, dvalues, key_weight, value_weight, rows, slots, padded, plan, 15
    )
    feed_got, value_got, self_got, out_got, key_got, answer_got, vector_all = received
    key_sum, value_sum, cq_sum, co_sum, self_grad, out_grad, feed_grad, vector_sum = sums(
        [
            (key_blocks, key_got, MOVE, CHIPS, PLAIN, BF),
            (value_blocks, value_got, MOVE, CHIPS, PLAIN, BF),
            (cq_blocks, cq_got, MOVE, CHIPS, COLUMNS, BF),
            (co_blocks, co_got, MOVE, CHIPS, COLUMNS, BF),
            (self_blocks, self_got, MOVE, CHIPS, PLAIN, F32),
            (out_blocks, out_got, MOVE, CHIPS, TURNED, F32),
            (feed_dp, feed_got, COLS, Z, PLAIN, F32),
            (vector_all, vector_all, GATHER, DP, PLAIN, F32),
        ]
    )

    expand_grad, shrink_grad = feed_grad[0], feed_grad[1].T

    own_answers = lax.dynamic_index_in_dim(answer_blocks, dp // 2, 0, keepdims=True)
    returned = jnp.concatenate([own_answers, answer_got], axis=0).astype(F32)
    source = lax.rem(dp // 2 + chips - jnp.arange(chips), chips)
    place = (2 * source * piece) // K
    pick = (place[None, :] == jnp.arange(groups)[:, None]).astype(F32)
    answer_part = cast(jnp.sum(pick[:, :, None, None, None] * returned[None], axis=1))

    zblocks = [
        key_sum.reshape(mp_ways, wide_rows, D),
        value_sum.reshape(mp_ways, wide_rows, D),
        cq_sum,
        co_sum,
    ]
    feature_part = lax.dynamic_slice_in_dim(vector_sum[:10], dp * vec, vec, 1)
    *got_z, feature_all, head_all, answer_got = exchange(
        [(a, MOVE, Z) for a in zblocks]
        + [(feature_part, GATHER, Z), (vector_sum[10:], GATHER, Z)]
        + [(answer_part, MOVE1, PAIR)],
        16,
    )
    forms = [PLAIN, PLAIN, PLAIN, TURNED]
    key_grad, value_grad, cquery_grad, cout_grad, answer_grad = sums(
        [(a, b, MOVE, Z, form, F32) for a, b, form in zip(zblocks, got_z, forms)]
        + [(answer_part, answer_got, MOVE1, PAIR, PLAIN, F32)]
    )
    feature_own = jnp.sum(feature_all, axis=0)
    head_sums = jnp.sum(head_all, axis=0)
    head_own = lax.dynamic_index_in_dim(head_all, mp, 0, keepdims=False)[1]

    def vec_of(i):
        return feature_own[i]

    def of_dp(a, shape):
        a = a.reshape(-1, dp_ways, shape[1])
        return lax.dynamic_index_in_dim(a, dp, 1, keepdims=False)

    def of_mp(a, shape):
        return lax.dynamic_slice_in_dim(of_dp(a.reshape(-1), shape), mp * shape[0], shape[0], 0)

    return (
        question_loss,
        answer_grad,
        memory_grad,
        self_grad[:, :head_cols],
        self_grad[:, head_cols : 2 * head_cols],
        self_grad[:, 2 * head_cols :],
        of_dp(head_own[:head_cols], query_bias.shape),
        of_dp(head_own[2 * head_cols : 3 * head_cols], value_bias.shape),
        out_grad,
        vec_of(0),
        vec_of(1),
        vec_of(2),
        cquery_grad,
        of_mp(head_sums[0], crossq_bias.shape),
        key_grad,
        value_grad,
        lax.dynamic_slice_in_dim(vec_of(9), mp * wide_rows, wide_rows, 0),
        cout_grad,
        vec_of(3),
        vec_of(4),
        vec_of(5),
        expand_grad,
        of_mp(head_sums[2:], expand_bias.shape),
        shrink_grad,
        vec_of(6),
        vec_of(7),
        vec_of(8),
    )


def solution(mesh):
    placed = (
        P(DP, None, None),
        P(DP, None),
        P(DP, None),
        P(DP, MP, None),
        P(DP),
        P(DP, MP),
        P(DP, MP),
        P(DP, MP),
        P(MP, DP),
        P(MP, DP),
        P(MP, DP),
        P(DP),
        P(DP),
        P(DP),
        P(DP, MP),
        P(MP, DP),
        P((DP, MP), None),
        P((DP, MP), None),
        P((DP, MP)),
        P(MP, DP),
        P(DP),
        P(DP),
        P(DP),
        P(DP, MP),
        P(MP, DP),
        P(MP, DP),
        P(DP),
        P(DP),
        P(DP),
        P(MP, DP),
    )
    return jax.shard_map(
        local,
        mesh=mesh,
        in_specs=placed,
        out_specs=(
            P(DP),
            P(DP, None, None),
            P(DP, MP, None),
            P(DP, MP),
            P(DP, MP),
            P(DP, MP),
            P(MP, DP),
            P(MP, DP),
            P(MP, DP),
            P(DP),
            P(DP),
            P(DP),
            P(DP, MP),
            P(MP, DP),
            P((DP, MP), None),
            P((DP, MP), None),
            P((DP, MP)),
            P(MP, DP),
            P(DP),
            P(DP),
            P(DP),
            P(DP, MP),
            P(MP, DP),
            P(MP, DP),
            P(DP),
            P(DP),
            P(DP),
        ),
        check_vma=False,
    )
```

time: 831 us -> 704 us (0.85)
  Pallas kernels: 626 us -> 563 us
  other arithmetic: 75.5 us -> 29.1 us
  local copies, waits for them, and re-layouts: 77.4 us -> 62.4 us
  matrix products: 21.4 us -> 12.6 us
    pallas_call x10 -> x5, Pallas kernels: 290 us -> 110 us  [exchange(): pl.pallas_call(functools.partial(exchange_kernel, plan), out_shape=plan.s...]
    pallas_call x3 -> x8, Pallas kernels: 85.6 us -> 213 us  [the longest x1 57.1 us: vocab_forward(): pl.pallas_call(functools.partial(vocab_kernel, ways, tile, sub, chunk, le...]
    add x9 -> x0, other arithmetic: 12.8 us -> none  [added(): return own.astype(F32) + jnp.sum(received.astype(F32), axis=0)]
    convert_element_type x10 -> x1, other arithmetic: 13 us -> 0.74 us  [local(): cast = lambda a: a.astype(BF)]
    pallas_call x1, Pallas kernels: 59.4 us -> 49.8 us  [vocab_back(): pl.pallas_call(functools.partial(vocab_back_kernel, ways, tile, sub, chun...]
    unnamed x203 -> x127, local copies, waits for them, and re-layouts: 31.2 us -> 21.7 us
    all_gather x3, waiting for transfers between devices: 0.02 us -> 8.64 us  [the longest x1 4.34 us: local(): tables.append(lax.all_gather(word_table[early:], DP, axis=0, tiled=False))]
  transfers between devices with their start and end apart: 5 -> 4, of which waited for: 0 -> 2; matrix products, arithmetic and copies ran while one was open for 14% -> 9% of each run, Pallas kernels for 50% -> 41%
where the time goes in v3:
time: 704 us; the launch traced here: 692 us
  Pallas kernels  563 us (80%)
  local copies, waits for them, and re-layouts  62.4 us (9%)
  other arithmetic  29.1 us (4%)
  between operations  15.8 us (2%)
  matrix products  12.6 us (2%)
  waiting for transfers between devices  8.7 us (1%)
    pallas_call x3, Pallas kernels, memory_call(): pl.pallas_call(functools.partial(beside, plan, kernel, len(inputs), len(o...  157 us
    pallas_call x5, Pallas kernels, exchange(): pl.pallas_call(functools.partial(exchange_kernel, plan), out_shape=plan.s...  110 us
    pallas_call x1, Pallas kernels, vocab_forward(): pl.pallas_call(functools.partial(vocab_kernel, ways, tile, sub, chunk, le...  57.1 us
    pallas_call x1, Pallas kernels, cross_back(): pl.pallas_call(functools.partial(cross_back_kernel, ways, per, piece, pad...  54.6 us
    pallas_call x1, Pallas kernels, vocab_back(): pl.pallas_call(functools.partial(vocab_back_kernel, ways, tile, sub, chun...  49.8 us
    pallas_call x1, Pallas kernels, cross_forward(): pl.pallas_call(functools.partial(cross_kernel, ways, per, piece, padded),...  47.7 us
    pallas_call x1, Pallas kernels, self_back(): pl.pallas_call(functools.partial(self_back_kernel, plan), in_specs=[vmem]...  34.2 us
    unnamed x127, local copies, waits for them, and re-layouts  21.7 us
  transfers between devices with their start and end apart: 4, of which 2 were waited for; matrix products, arithmetic and copies ran while one was open for 9% of the time, Pallas kernels for 41%

profile of v3, /device:TPU:0, one launch (start us, length us, event | category | flops | bytes accessed | tf_op | source)
XLA Modules:
  0.0 691.8 jit_solution(15737675348196725616)
XLA Ops:
  7.3 1.2 copy.195
  12.6 43.3 %shard_map.493 = (bf16[8,4,32,1024]{3,2,1,0:T(8,128)(2,1)}, bf16[8,4,32,1024]{3,2,1,0:T(8,128)(2,1)}, bf16[8,4,48,128]{3,2,1,0:T(8,128)(2,1)}, bf16[4,128,256]{2...) custom-call(bf16[32,1024]{1,0:T(8,128)(2,1)} %refs_0_.1, bf16[32,1024]{1,0:T(8,128)(2,1)} %refs_1_.1, ...), custom_call_target="tpu_custom_call" | custom-call | tf_op jit(solution)/shard_map/pallas_call | solution.py:284
  60.2 71.8 %memory_products.1 = (bf16[3584,1024]{1,0:T(8,128)(2,1)}, bf16[3584,1024]{1,0:T(8,128)(2,1)}, bf16[3584,1024]{1,0:T(8,128)(2,1)}, bf16[4,3,64,1024]{3,2,1,0:T(8,...) custom-call(bf16[100,32,1024]{2,1,0:T(8,128)(2,1)} %bitcast.341, ...), custom_call_target="tpu_custom_call" | custom-call | flops 15032385536 | bytes 75161928 | tf_op jit(solution)/shard_map/memory_products/pallas_call | solution.py:373
  132.1 2.9 pad_maximum_fusion
  135.0 4.3 all-gather.7.cloned.1.call-done
  139.7 2.2 slice.280
  146.9 1.1 convolution_convert_fusion.2
  148.0 13.8 %shard_map.494 = bf16[3,64,1024]{2,1,0:T(8,128)(2,1)} custom-call(bf16[4,64,1024]{2,1,0:T(8,128)(2,1)} %bitcast.258), custom_call_target="tpu_custom_call" | custom-call | tf_op jit(solution)/shard_map/pallas_call | solution.py:284
  161.8 4.4 copy.205
  166.3 1.3 slice_convert_fusion.2
  169.7 1.4 fusion.20.refs_0_
  171.1 14.4 %shard_map.495 = bf16[4,64,1024]{2,1,0:T(8,128)(2,1)} custom-call(bf16[64,1024]{1,0:T(8,128)(2,1)} %fusion.20.refs_0_), custom_call_target="tpu_custom_call" | custom-call | tf_op jit(solution)/shard_map/pallas_call | solution.py:284
  187.0 47.7 %shard_map.496 = (bf16[256,1024]{1,0:T(8,128)(2,1)}, f32[2,8,4,128]{3,2,1,0:T(4,128)}, bf16[3,256,1024]{2,1,0:T(8,128)(2,1)}, f32[3,2,8,4,128]{4,3,2,1,0:T(4,128)}) custom-call(s32[32,1,128]{2,1,0:T(1,128)} %broadcast_in_dim.173.used_ref, bf16[3584,1024]{1,0:T(8,128)(2,1)} %get-tuple-element.117.k_ref, bf16[3584,1024]{1,0:T(8,128)(2,1)} %get-tuple-element.118.v_ref, ...), custom_call_target="tpu_custom_call" | custom-call | flops 1879048192 | bytes 14680064 | tf_op jit(solution)/shard_map/pallas_call | solution.py:700
  240.2 1.3 copy.212
  241.8 2.4 copy.213
  244.2 1.8 fusion.71
  246.8 1.6 copy-done
  252.4 13.4 %shard_map.497 = (f32[256,4096]{1,0:T(8,128)}, f32[256,1024]{1,0:T(8,128)}) custom-call(bf16[256,1024]{1,0:T(8,128)(2,1)} %fusion.23.h_ref, bf16[8,4,2,128,1024]{4,3,2,1,0:T(8,128)(2,1)} %bitcast.239, bf16[8,1,512]{2,1,0:T(2,128)(2,1)} %reshape_reshape_reshape.4.bias_ref, bf16[8,4,2,128,1024]{4,3,2,1,0:T(8,128)(2,1)} %bitcast.240), custom_call_target="tpu_custom_call" | custom-call | flops 4294967296 | bytes 16777216 | tf_op jit(solution)/shard_map/pallas_call | solution.py:1201
  265.8 1.6 fusion.67
  268.8 4.3 all-gather.11.cloned.1.call-done
  273.1 57.1 %shard_map.498 = (bf16[4,6400,256]{2,1,0:T(8,128)(2,1)}, f32[4,32,256]{2,1,0:T(8,128)}, f32[4,4,8,256]{3,2,1,0:T(8,128)}) custom-call(bf16[256,1024]{1,0:T(8,128)(2,1)} %add_convert_fusion.h_ref, s32[4,1,256]{2,1,0:T(1,128)} %sub.226.target_ref, bf16[8,3840,128]{2,1,0:T(8,128)(2,1)} %bitcast.339, bf16[8,2560,128]{2,1,0:T(8,128)(2,1)} %bitcast.342), custom_call_target="tpu_custom_call" | custom-call | flops 13421772800 | bytes 52428800 | tf_op jit(solution)/shard_map/pallas_call | solution.py:984
  331.9 5.3 shard_map.499
  339.2 49.8 %shard_map.500 = f32[256,1024]{1,0:T(8,128)} custom-call(bf16[4,6400,256]{2,1,0:T(8,128)(2,1)} %get-tuple-element.134.exp_ref, f32[4,32,256]{2,1,0:T(8,128)} %get-tuple-element.135.tops_ref, s32[4,1,256]{2,1,0:T(1,128)} %sub.226.target_ref, f32[4,1,256]{2,1,0:T(1,128)} %bitcast.334, f32[4,1,256]{2,1,0:T(1,128)} %reshape.552.rate_ref, ...), custom_call_target="tpu_custom_call" | custom-call | flops 13421772800 | bytes 52428800 | tf_op jit(solution)/shard_map/pallas_call | solution.py:1129
  389.0 1.8 multiply_reduce_fusion.2
  392.1 19.7 %shard_map.501 = (bf16[8,2,128,4096]{3,2,1,0:T(8,128)(2,1)}, f32[8,1,512]{2,1,0:T(1,128)}, f32[256,1024]{1,0:T(8,128)}) custom-call(bf16[256,1024]{1,0:T(8,128)(2,1)} %convert_element_type.269.dout_ref, bf16[256,1024]{1,0:T(8,128)(2,1)} %fusion.23.h_ref, f32[256,4096]{1,0:T(8,128)} %get-tuple-element.136.a_ref, bf16[8,4,2,128,1024]{4,3,2,1,0:T(8,128)(2,1)} %bitcast.241, ...), custom_call_target="tpu_custom_call" | custom-call | flops 8589934592 | bytes 33554432 | tf_op jit(solution)/shard_map/pallas_call | solution.py:1248
  411.9 1.1 copy-done.24
  414.0 1.5 copy-done.2
  415.7 1.6 convert_multiply_fusion
  417.3 1.3 copy.222
  418.7 1.4 bitcast_reduce_fusion
  421.0 54.6 %shard_map.502 = (bf16[3584,1024]{1,0:T(8,128)(2,1)}, bf16[3584,1024]{1,0:T(8,128)(2,1)}, f32[64,1024]{1,0:T(8,128)}) custom-call(s32[32,1,128]{2,1,0:T(1,128)} %broadcast_in_dim.173.used_ref, bf16[3584,1024]{1,0:T(8,128)(2,1)} %get-tuple-element.117.k_ref, bf16[3584,1024]{1,0:T(8,128)(2,1)} %get-tuple-element.118.v_ref, bf16[256,1024]{1,0:T(8,128)(2,1)} %bitcast.267, ...), custom_call_target="tpu_custom_call" | custom-call | flops 4697620480 | bytes 29360128 | tf_op jit(solution)/shard_map/pallas_call | solution.py:818
  475.7 2.4 multiply_reduce_fusion.10
  479.0 2.0 convolution_convert_fusion
  481.0 2.1 convolution_convert_fusion.1
  483.1 27.5 %memory_weights.1 = (bf16[1024,1024]{1,0:T(8,128)(2,1)}, bf16[1024,1024]{1,0:T(8,128)(2,1)}, f32[1,1024]{1,0:T(1,128)}, bf16[4,64,1024]{2,1,0:T(8,128)(2,1)}, bf...) custom-call(bf16[3584,1024]{1,0:T(8,128)(2,1)} %get-tuple-element.133.refs_0_, ...), custom_call_target="tpu_custom_call" | custom-call | flops 15032385536 | bytes 75161928 | tf_op jit(solution)/shard_map/memory_weights/pallas_call | solution.py:373
  510.6 4.6 shard_map.503
  515.3 34.2 %shard_map.504 = (f32[1,768]{1,0:T(1,128)}, bf16[4,128,768]{2,1,0:T(8,128)(2,1)}, bf16[4,128,256]{2,1,0:T(8,128)(2,1)}, bf16[4,64,1024]{2,1,0:T(8,128)(2,1)}, bf...) custom-call(bf16[256,1024]{1,0:T(8,128)(2,1)} %bitcast.260, ...), custom_call_target="tpu_custom_call" | custom-call | flops 805306368 | bytes 2097152 | tf_op jit(solution)/shard_map/pallas_call | solution.py:1363
  550.2 4.4 shard_map.505
  554.7 1.3 concatenate.30.refs_10_
  557.5 58.0 %memory_back.1 = (f32[100,32,1024]{2,1,0:T(8,128)}, bf16[3,2,128,1024]{3,2,1,0:T(8,128)(2,1)}, bf16[3,128,1024]{2,1,0:T(8,128)(2,1)}, bf16[3,128,768]{2,1,0:T(8,...) custom-call(bf16[3584,1024]{1,0:T(8,128)(2,1)} %get-tuple-element.13, ...), custom_call_target="tpu_custom_call" | custom-call | flops 15032385536 | bytes 75161928 | tf_op jit(solution)/shard_map/memory_back/pallas_call | solution.py:373
  615.5 1.5 slice.285.refs_15_
  617.0 7.4 %shard_map.506 = (bf16[128,1024]{1,0:T(8,128)(2,1)}, bf16[128,1024]{1,0:T(8,128)(2,1)}, bf16[4,128,256]{2,1,0:T(8,128)(2,1)}, bf16[4,128,256]{2,1,0:T(8,128)(2,1...) custom-call(bf16[4,128,1024]{2,1,0:T(8,128)(2,1)} %get-tuple-element.150.refs_8_.refs, ...), custom_call_target="tpu_custom_call" | custom-call | tf_op jit(solution)/shard_map/pallas_call | solution.py:349
  624.3 1.4 slice.287.refs_5_
  625.7 1.3 constant_dynamic-slice_fusion.7.refs_4_
  627.1 1.2 multiply_reduce_fusion.refs_6_.refs_4_
  628.3 32.9 %shard_map.507 = (bf16[3,32,1024]{2,1,0:T(8,128)(2,1)}, bf16[3,32,1024]{2,1,0:T(8,128)(2,1)}, bf16[3,128,256]{2,1,0:T(8,128)(2,1)}, bf16[3,128,256]{2,1,0:T(8,12...) custom-call(bf16[4,32,1024]{2,1,0:T(8,128)(2,1)} %bitcast.273, ...), custom_call_target="tpu_custom_call" | custom-call | tf_op jit(solution)/shard_map/pallas_call | solution.py:284
  669.5 2.7 shard_map.508
  672.3 12.5 %copy.286 = f32[32,100,1024]{2,0,1:T(8,128)} copy(f32[32,100,1024]{2,0,1:T(8,128)} %bitcast.244) | data formatting | bytes 26214400
  (289 shorter events, 46.9 us)
Async XLA Ops:
  7.2 3.5 copy-start.15
  7.2 132.1 %all-gather.7.cloned.1.call-start = ((), (), s32[]{:S(2)}) async-start(), calls=%async_computation.2 | async-start | bytes 8847360 | tf_op jit(solution)/shard_map/all_gather | solution.py:1553
  8.5 3.2 copy-start.53
  8.6 3.2 copy-start.38
  8.6 3.1 copy-start.41
  8.6 3.1 copy-start.42
  8.6 3.1 copy-start.43
  8.6 3.1 copy-start.44
  8.6 3.1 copy-start.45
  8.6 3.1 copy-start.46
  8.6 3.1 copy-start.47
  8.7 3.1 copy-start.48
  8.7 3.1 copy-start.49
  8.7 3.1 copy-start.50
  8.7 3.1 copy-start.51
  8.7 3.1 copy-start.52
  10.7 47.6 %copy-start.39 = (s32[4,32]{1,0:T(4,128)S(1)}, s32[4,32]{1,0:T(4,128)}, u32[]{:S(2)}) copy-start(s32[4,32]{1,0:T(4,128)} %param.31) | copy-start | bytes 1540
  10.7 48.2 %copy-start.40 = (f32[4,8]{1,0:T(4,128)S(1)}, f32[4,8]{1,0:T(4,128)}, u32[]{:S(2)}) copy-start(f32[4,8]{1,0:T(4,128)} %param.32) | copy-start | bytes 388
  10.7 48.8 %copy-start.31 = (bf16[128,256]{1,0:T(8,128)(2,1)S(1)}, bf16[128,256]{1,0:T(8,128)(2,1)}, u32[]{:S(2)}) copy-start(bf16[128,256]{1,0:T(8,128)(2,1)} %param.37) | copy-start | bytes 196612
  10.7 48.8 %copy-start.32 = (bf16[128,256]{1,0:T(8,128)(2,1)S(1)}, bf16[128,256]{1,0:T(8,128)(2,1)}, u32[]{:S(2)}) copy-start(bf16[128,256]{1,0:T(8,128)(2,1)} %param.36) | copy-start | bytes 196612
  10.7 48.8 %copy-start.33 = (bf16[128,256]{1,0:T(8,128)(2,1)S(1)}, bf16[128,256]{1,0:T(8,128)(2,1)}, u32[]{:S(2)}) copy-start(bf16[128,256]{1,0:T(8,128)(2,1)} %param.35) | copy-start | bytes 196612
  55.9 196.5 %all-gather.9.cloned.1.call-start = ((), (), s32[]{:S(2)}) async-start(), calls=%async_computation.3 | async-start | bytes 18874368 | tf_op jit(solution)/shard_map/all_gather | solution.py:1556
  60.2 71.9 %copy-start.27 = (bf16[4,64,1024]{2,1,0:T(8,128)(2,1)S(1)}, bf16[4,64,1024]{2,1,0:T(8,128)(2,1)}, u32[]{:S(2)}) copy-start(bf16[4,64,1024]{2,1,0:T(8,128)(2,1)} %get-tuple-element.125) | copy-start | bytes 1572868
  139.3 4.1 copy-start.25
  139.3 4.2 copy-start.5
  139.3 4.2 copy-start.8
  139.3 133.7 %all-gather.11.cloned.1.call-start = ((), (), s32[]{:S(2)}) async-start(), calls=%async_computation.4 | async-start | bytes 5898240 | tf_op jit(solution)/shard_map/all_gather | solution.py:1558
  142.0 415.6 %reduce-scatter.2.cloned.1.call-start = ((), (), s32[]{:S(2)}) async-start(), calls=%async_computation.1 | async-start | bytes 18874368 | tf_op jit(solution)/shard_map/reduce_scatter | solution.py:1663
  145.9 20.2 %copy-start.18 = (bf16[256,256]{1,0:T(8,128)(2,1)}, bf16[256,256]{1,0:T(8,128)(2,1)S(1)}, u32[]{:S(2)}) copy-start(bf16[256,256]{1,0:T(8,128)(2,1)S(1)} %reshape.543.ctx_ref) | copy-start | bytes 393220
  146.9 19.3 %copy-start.9 = (bf16[256,1024]{1,0:T(8,128)(2,1)}, bf16[256,1024]{1,0:T(8,128)(2,1)S(1)}, u32[]{:S(2)}) copy-start(bf16[256,1024]{1,0:T(8,128)(2,1)S(1)} %bitcast_dynamic-update-slice_fusion.wo_ref) | copy-start | bytes 1572868
  161.8 4.4 copy-start.16
  166.2 3.5 copy-start.14
  168.6 16.9 %copy-start.54 = (s32[32]{0:T(128)S(1)}, s32[32]{0:T(128)}, u32[]{:S(2)}) copy-start(s32[32]{0:T(128)} %param.34) | copy-start | bytes 388
  234.7 4.1 copy-start.30
  234.7 4.5 copy-start.36
  244.2 2.6 copy-start.17
  246.0 2.4 copy-start
  246.8 3.4 copy-start.1
  413.6 1.9 copy-start.2
  413.6 2.2 copy-start.4
  475.7 3.3 copy-start.12
  475.7 3.3 copy-start.22
  478.2 4.9 copy-start.13
  550.2 4.4 copy-start.37
  617.0 10.0 %copy-start.29 = (bf16[3,2,32,1024]{3,2,1,0:T(8,128)(2,1)S(1)}, bf16[3,2,32,1024]{3,2,1,0:T(8,128)(2,1)}, u32[]{:S(2)}) copy-start(bf16[3,2,32,1024]{3,2,1,0:T(8,128)(2,1)} %get-tuple-element.171) | copy-start | bytes 1179652
  627.1 35.1 %copy-start.28 = (f32[128,768]{1,0:T(8,128)S(1)}, f32[128,768]{1,0:T(8,128)}, u32[]{:S(2)}) copy-start(f32[128,768]{1,0:T(8,128)} %get-tuple-element.180) | copy-start | bytes 1179652
  627.1 35.8 %copy-start.23 = (f32[2,128,1024]{2,1,0:T(8,128)S(1)}, f32[2,128,1024]{2,1,0:T(8,128)}, u32[]{:S(2)}) copy-start(f32[2,128,1024]{2,1,0:T(8,128)} %get-tuple-element.188) | copy-start | bytes 3145732
  661.2 3.6 copy-start.34
  (11 other events, 13.7 us)
Sparse Core Ops, SparseCore 0:
  56.0 83.2 all-gather.6
  141.2 88.8 all-gather.8
  231.9 41.1 all-gather.10
  411.9 123.1 reduce-scatter.1

commit v4 on v3

--- a/solution.py
+++ b/solution.py
@@ -224,6 +224,9 @@
 
     def begin(self, also=()):
         self.meet(also)
+        self.start()
+
+    def start(self):
         for i in range(self.count):
             if self.kinds[i] == LATE:
                 continue
@@ -342,7 +345,7 @@
         elif form == TURNED:
             shape = shape[::-1]
         arrays.append(array)
-        received.append(got if kind != GATHER else got[:1])
+        received.append(got)
         shapes.append(jax.ShapeDtypeStruct(shape, dtype))
         kinds.append((kind, group, form))
     vmem = pl.BlockSpec(memory_space=pltpu.VMEM)
@@ -386,7 +389,7 @@
 
 
 MEM_BLOCK = 16
-BACK_BLOCK = 8
+BACK_BLOCK = 16
 
 
 def memory_kernel(slots, padded, mem_ref, wk_ref, wv_ref, vb_ref, k_ref, v_ref, rows_ref, wide):
@@ -430,50 +433,6 @@
     )
 
 
-def memory_weight_kernel(rows_ref, dk_ref, dv_ref, wk_ref, wv_ref, vb_ref, key_sum, value_sum):
-    step = pl.program_id(0)
-
-    @pl.when(step == 0)
-    def _():
-        key_sum[...] = jnp.zeros_like(key_sum)
-        value_sum[...] = jnp.zeros_like(value_sum)
-        vb_ref[...] = jnp.zeros_like(vb_ref)
-
-    rows = rows_ref[...]
-    vb_ref[...] += jnp.sum(dv_ref[...].astype(F32), axis=0, keepdims=True)
-    for c in range(0, D, 512):
-        cols = slice(c, c + 512)
-        key_sum[:, cols] += weight_grad(rows, dk_ref[:, cols])
-        value_sum[:, cols] += weight_grad(rows, dv_ref[:, cols])
-
-    @pl.when(step == pl.num_programs(0) - 1)
-    def _():
-        wk_ref[...] = key_sum[...].astype(BF)
-        wv_ref[...] = value_sum[...].astype(BF)
-
-
-def memory_weights(memory_rows, dkeys, dvalues, rows, padded, plan, cid):
-    spec = pl.BlockSpec((BACK_BLOCK * padded, D), lambda i: (i, 0))
-    whole = pl.BlockSpec((D, D), lambda i: (0, 0))
-    return memory_call(
-        plan,
-        cid,
-        memory_weight_kernel,
-        "memory_weights",
-        rows // BACK_BLOCK,
-        [memory_rows, dkeys, dvalues],
-        [spec, spec, spec],
-        [whole, whole, pl.BlockSpec((1, D), lambda i: (0, 0))],
-        [
-            jax.ShapeDtypeStruct((D, D), BF),
-            jax.ShapeDtypeStruct((D, D), BF),
-            jax.ShapeDtypeStruct((1, D), F32),
-        ],
-        [pltpu.VMEM((D, D), F32), pltpu.VMEM((D, D), F32)],
-        4 * rows * padded * D * D,
-    )
-
-
 def memory_grad_kernel(slots, padded, dk_ref, dv_ref, wk_ref, wv_ref, out_ref, wide):
     for c in range(0, D, 256):
         cols = slice(c, c + 256)
@@ -483,7 +442,9 @@
                 wide[pl.ds(r, slots, stride=BACK_BLOCK), :] = term[
                     r * padded : r * padded + slots, part : part + 128
                 ]
-            out_ref[:, :, c + part : c + part + 128] = wide[...].reshape(slots, BACK_BLOCK, 128)
+            out_ref[:, :, c + part : c + part + 128] = (
+                wide[...].reshape(slots, BACK_BLOCK, 128).astype(BF)
+            )
 
 
 def memory_back(dkeys, dvalues, key_weight, value_weight, rows, slots, padded, plan, cid):
@@ -498,11 +459,11 @@
         [dkeys, dvalues, key_weight, value_weight],
         [spec, spec, whole, whole],
         [pl.BlockSpec((slots, BACK_BLOCK, D), lambda i: (0, i, 0))],
-        [jax.ShapeDtypeStruct((slots, rows, D), F32)],
+        [jax.ShapeDtypeStruct((slots, rows, D), BF)],
         [pltpu.VMEM((slots * BACK_BLOCK, 128), F32)],
         4 * rows * padded * D * D,
     )
-    return jnp.transpose(out, (1, 0, 2)), rest
+    return jnp.transpose(out, (1, 0, 2)).astype(F32), rest
 
 
 def z_copy(source, target, send, recv, device):
@@ -737,12 +698,15 @@
 
 
 def cross_back_kernel(
-    ways, per, piece, padded, used_ref, k_ref, v_ref, q_ref, keep_ref, dctx_ref, stat_ref,
-    dk_ref, dv_ref, dq_ref,
-    dctx_all, stat_all, dq_out, dq_got, left_send, left_recv, right_send, right_recv, own, send, recv,
+    ways, per, piece, padded, used_ref, k_ref, v_ref, q_ref, keep_ref, rows_ref, dctx_ref, stat_ref, co_ref,
+    dk_ref, dv_ref, dq_ref, key_ref, value_ref, vb_ref, co_sum_ref,
+    dctx_all, stat_all, dq_out, dq_got, key_sum, value_sum, low, low_got, co_own, co_got,
+    left_send, left_recv, right_send, right_recv, own, send, recv, core_send, core_recv,
 ):
     c, j = pl.program_id(0), pl.program_id(1)
-    mp = lax.axis_index(MP)
+    dp, mp = lax.axis_index(DP), lax.axis_index(MP)
+    parity = lax.rem(dp, 2)
+    sibling = (dp + 1 - 2 * parity, mp)
     place = nearest(c, ways)[0]
     span = piece * TOK
     line = LineGather(
@@ -751,12 +715,43 @@
         ways,
     )
 
+    def core_copy(i):
+        source, target = [
+            (co_ref, co_got),
+            (low.at[0], low_got.at[0]),
+            (low.at[1], low_got.at[1]),
+        ][i]
+        return pltpu.make_async_remote_copy(
+            src_ref=source.at[:, 1 - parity],
+            dst_ref=target,
+            send_sem=core_send.at[i],
+            recv_sem=core_recv.at[i],
+            device_id=sibling,
+            device_id_type=MESH,
+        )
+
+    def co_local():
+        return pltpu.make_async_copy(co_ref.at[:, parity], co_own, own.at[2])
+
     @pl.when((c == 0) & (j == 0))
     def _():
-        z_meet(ways)
+        barrier = pltpu.get_barrier_semaphore()
+        pl.semaphore_signal(barrier, inc=1, device_id=sibling, device_id_type=MESH)
+        for off in range(1, ways):
+            pl.semaphore_signal(
+                barrier, inc=1, device_id=(dp, lax.rem(mp + off, ways)), device_id_type=MESH
+            )
+        pl.semaphore_wait(barrier, ways)
         line.begin()
-
-    line.arrive(c, j == 0)
+        core_copy(0).start()
+        co_local().start()
+        key_sum[...] = jnp.zeros_like(key_sum)
+        value_sum[...] = jnp.zeros_like(value_sum)
+        vb_ref[...] = jnp.zeros_like(vb_ref)
+
+    middle_place = (mp > 0) & (mp < ways - 1)
+    line.arrive(c, (j == 0) & jnp.logical_not(middle_place & (c == ways - 1)))
+    line.arrive(c + 1, (j == 0) & middle_place & (c == ways - 2))
     keep = keep_ref[...]
     keep_wide = keep.astype(F32)
     slot = lax.broadcasted_iota(jnp.int32, (padded, GL), 0)
@@ -792,8 +787,18 @@
         def _(k=k):
             copy(k).start()
 
+    memory_rows = rows_ref[...]
+    vb_ref[...] += jnp.sum(dv_ref[...].astype(F32), axis=0, keepdims=True)
+    for start in range(0, D, 512):
+        cols = slice(start, start + 512)
+        key_sum[:, cols] += weight_grad(memory_rows, dk_ref[:, cols])
+        value_sum[:, cols] += weight_grad(memory_rows, dv_ref[:, cols])
+
     @pl.when((c == ways - 1) & (j == per - 1))
     def _():
+        for i, total in enumerate((key_sum, value_sum)):
+            low[i] = total[...].astype(BF).reshape(low.shape[1:])
+            core_copy(1 + i).start()
         line.finish()
         for k in range(1, ways):
             copy(k).wait_send()
@@ -804,9 +809,15 @@
             ).wait_recv()
             total += dq_got[off - 1].astype(F32)
         dq_ref[...] = total
-
-
-def cross_back(used, keys, values, queries, dctx, stats, keep, piece, padded, cid):
+        co_local().wait()
+        core_copy(0).wait()
+        co_sum_ref[...] = (co_own[...].astype(F32) + co_got[...].astype(F32)).astype(BF)
+        for i, out in enumerate((key_ref, value_ref)):
+            core_copy(1 + i).wait()
+            out[...] = (low[i, :, parity].astype(F32) + low_got[i].astype(F32)).astype(BF)
+
+
+def cross_back(used, keys, values, queries, memory_rows, dctx, stats, co_blocks, keep, piece, padded, cid):
     ways = lax.axis_size(MP)
     per = queries.shape[0] // TOK // ways
     rows = per * ways * piece
@@ -814,6 +825,11 @@
     at = lambda c, j: nearest(c, ways)[0] * per + j
     big = pl.BlockSpec((piece * padded, D), lambda c, j: (at(c, j), 0))
     anywhere = pl.BlockSpec(memory_space=pl.ANY)
+    chips, _, vec, _ = co_blocks.shape
+    half = (chips, vec, D)
+    half_spec = pl.BlockSpec(half, lambda c, j: (0, 0, 0))
+    half_shape = jax.ShapeDtypeStruct(half, BF)
+    line = line_sems(2, ways)
     dma = pltpu.SemaphoreType.DMA
     return pl.pallas_call(
         functools.partial(cross_back_kernel, ways, per, piece, padded),
@@ -824,33 +840,56 @@
             big,
             pl.BlockSpec((TOK, D), lambda c, j: (at(c, j), 0)),
             pl.BlockSpec((GL, GC), lambda c, j: (0, 0)),
+            big,
             anywhere,
             anywhere,
-        ],
-        out_specs=[big, big, pl.BlockSpec((per * TOK, D), lambda c, j: (0, 0))],
+            anywhere,
+        ],
+        out_specs=[
+            big,
+            big,
+            pl.BlockSpec((per * TOK, D), lambda c, j: (0, 0)),
+            half_spec,
+            half_spec,
+            pl.BlockSpec((1, D), lambda c, j: (0, 0)),
+            half_spec,
+        ],
         out_shape=[
             jax.ShapeDtypeStruct((rows * padded, D), BF),
             jax.ShapeDtypeStruct((rows * padded, D), BF),
             jax.ShapeDtypeStruct((per * TOK, D), F32),
+            half_shape,
+            half_shape,
+            jax.ShapeDtypeStruct((1, D), F32),
+            half_shape,
         ],
         scratch_shapes=[
             pltpu.VMEM((ways, shard * TOK, D), BF),
             pltpu.VMEM((ways, 2, shard, G, GL), F32),
             pltpu.VMEM((ways, per * TOK, D), BF),
             pltpu.VMEM((ways - 1, per * TOK, D), BF),
-            *line_sems(2, ways),
+            pltpu.VMEM((D, D), F32),
+            pltpu.VMEM((D, D), F32),
+            pltpu.VMEM((2, chips, 2, vec, D), BF),
+            pltpu.VMEM((2,) + half, BF),
+            pltpu.VMEM(half, BF),
+            pltpu.VMEM(half, BF),
+            *line[:4],
+            dma((3,)),
             dma((ways,)),
             dma((ways,)),
+            dma((3,)),
+            dma((3,)),
         ],
         compiler_params=pltpu.CompilerParams(
             vmem_limit_bytes=VMEM_BYTES, collective_id=cid, has_side_effects=True
         ),
         cost_estimate=pl.CostEstimate(
-            flops=10 * rows * padded * GL * D,
-            bytes_accessed=8 * rows * padded * D,
+            flops=4 * rows * padded * D * D + 10 * rows * padded * GL * D,
+            bytes_accessed=10 * rows * padded * D,
             transcendentals=rows * padded * G * GL,
         ),
-    )(used, keys, values, queries, keep, dctx, stats)
+    )(used, keys, values, queries, keep, memory_rows, dctx, stats, co_blocks)
 
 
 def table_words(table, start, count):
@@ -1273,15 +1312,15 @@
 
 
 def self_back_kernel(
-    plan, x_ref, dout_ref, ctx_ref, q_ref, k_ref, v_ref, wo_ref, wqkv_ref, keep_ref, dfirst_ref, *refs
+    plan, x_ref, ctx_ref, q_ref, k_ref, v_ref, wo_ref, wqkv_ref, keep_ref, dfirst_ref, *refs
 ):
     n = plan.count
     sends, rest = refs[:n], refs[n:]
     bias_ref, dself_ref, dwo_ref, din_ref = rest[:4]
     lands, rest = rest[4 : 4 + n], rest[4 + n :]
-    dctx, dqkv, part, part_got, din, dself, dself_got, dwo, dwo_got = rest[:9]
-    send, recv, own = rest[9:12]
-    plan.bind(sends, lands, rest[12:])
+    dctx, dqkv, part, part_got, din, dself, dself_got, dwo, dwo_got, dout, dout_all = rest[:11]
+    send, recv, own = rest[11:14]
+    plan.bind(sends, lands, rest[14:])
     ways = plan.mp_ways
     mp, parity = plan.mp, plan.parity
 
@@ -1298,10 +1337,21 @@
             for i, (a, b) in enumerate([(dself, dself_got), (dwo, dwo_got)])
         ]
 
-    plan.begin((Z, PAIR))
+    def dout_copy(off):
+        return z_copy(dout, dout_all.at[mp], send.at[3, off], recv.at[3, off], plan.peer(Z, off))
+
+    plan.meet((Z, PAIR))
+    dout[...] = dfirst_ref[...].astype(BF)
+    for off in range(1, ways):
+        dout_copy(off).start()
+    plan.start()
+    dout_all[mp] = dout[...]
     keep = keep_ref[...]
     keep_wide = keep.astype(F32)
-    dctx[...] = product_back(dout_ref[...], wo_ref[...]).astype(BF)
+    for off in range(1, ways):
+        dout_copy(off).wait()
+    upstreams = dout_all[...].reshape(x_ref.shape)
+    dctx[...] = product_back(upstreams, wo_ref[...]).astype(BF)
     key_place = lax.broadcasted_iota(jnp.int32, (TOK, GL), 0)
     query_place = lax.rem(lax.broadcasted_iota(jnp.int32, (TOK, GL), 1), TOK)
     seen = key_place <= query_place
@@ -1328,7 +1378,7 @@
     for off in range(1, ways):
         part_copy(off).start()
     dself[...] = weight_grad(x_ref[...], grads).astype(BF).reshape(dself.shape)
-    dwo[...] = weight_grad(dout_ref[...], ctx_ref[...]).astype(BF).reshape(dwo.shape)
+    dwo[...] = weight_grad(upstreams, ctx_ref[...]).astype(BF).reshape(dwo.shape)
     for copy in core_copies():
         copy.start()
     bias_ref[...] = jnp.sum(grads.astype(F32), axis=0, keepdims=True)
@@ -1352,11 +1402,11 @@
     local.wait()
 
 
-def self_back(x, dout, ctx, queries, keys, values, wo, wqkv, keep, dfirst, plan, cid):
+def self_back(x, ctx, queries, keys, values, wo, wqkv, keep, dfirst, plan, cid):
     uniq, shard = x.shape[0], dfirst.shape[0]
     ways, chips = plan.mp_ways, plan.chips
     vec = D // plan.dp_ways
-    inputs = [x, dout, ctx, queries, keys, values, wo, wqkv, keep, dfirst]
+    inputs = [x, ctx, queries, keys, values, wo, wqkv, keep, dfirst]
     vmem = pl.BlockSpec(memory_space=pltpu.VMEM)
     dma = pltpu.SemaphoreType.DMA
     cols = wqkv.shape[1]
@@ -1381,8 +1431,10 @@
             pltpu.VMEM((chips, vec, cols), BF),
             pltpu.VMEM((chips, 2, vec, GC), BF),
             pltpu.VMEM((chips, vec, GC), BF),
-            dma((3, ways)),
-            dma((3, ways)),
+            pltpu.VMEM((shard, D), BF),
+            pltpu.VMEM((ways, shard, D), BF),
+            dma((4, ways)),
+            dma((4, ways)),
             dma((1,)),
             *plan.scratch,
         ],
@@ -1499,15 +1551,14 @@
         wanted = answers
     else:
         wanted = jnp.stack([answers[(2 * c * piece) // K] for c in range(chips)])
-    feed_shard = jnp.stack([expand_weight, shrink_weight.T]).reshape(4, vec // 2, -1)
-    key_all, value_all, small_all, cquery_z, cout_z, feed_first = exchange(
+    feed_shard = jnp.stack([expand_weight, shrink_weight.T])
+    key_all, value_all, small_all, cquery_z, cout_z = exchange(
         [
             (cross_key, WIDE, Z),
             (cross_value, WIDE, Z),
             (small, WIDE, Z),
             (cross_query, LATE, Z),
             (cross_output, LATE, Z),
-            (feed_shard[0], LATE, Z),
         ],
         0,
     )
@@ -1531,7 +1582,7 @@
 
     plan = Exchange(
         [
-            (feed_shard[1:], GATHER, Z),
+            (feed_shard, GATHER, Z),
             (self_shard, NEAR, Z),
             (self_output, NEAR, Z),
             (target_rows, NEAR, Z),
@@ -1541,20 +1592,17 @@
             (cout_z, NEAR, Z),
         ]
     )
-    (keys, values, memory_rows, feed_rest, self_all, output_all, target_all, doc_all, x_all, cquery_all, cout_all) = (
+    (keys, values, memory_rows, feed_z, self_all, output_all, target_all, doc_all, x_all, cquery_all, cout_all) = (
         memory_products(memory, key_weight, value_weight, cvbias, padded, plan, 1)
     )
     words = word_table.shape[0]
     early = words // 1280 * 3 // 5 * 1280 if words % 1280 == 0 else 0
-    feed_z = jnp.concatenate([feed_first[:, None], feed_rest], axis=1)
     tables = []
     if early:
-        part, _ = lax.optimization_barrier((word_table[:early], small_all))
-        part = lax.all_gather(part, DP, axis=0, tiled=False)
+        part = lax.all_gather(word_table[:early], DP, axis=0, tiled=False)
         feed_z, part = lax.optimization_barrier((feed_z, part))
         tables.append(part)
     feed_all = lax.all_gather(feed_z, DP, axis=0, tiled=False)
-    feed_all = feed_all.reshape(dp_ways, mp_ways, 2, vec, -1)
     tables.append(lax.all_gather(word_table[early:], DP, axis=0, tiled=False))
     if word_table.shape[1] < 128:
         tables = [column_parts(a)[None] for a in tables]
@@ -1675,8 +1723,9 @@
     cast = lambda a: a.astype(BF)
     co_blocks = owners(cast(weight_grad(dcout_in, context_two)))
     stat_all = jnp.stack([cross_norm, middle])
-    dkeys, dvalues, dcross_q = cross_back(
-        used, keys, values, cross_queries, dcontext_two, stat_all, keep, piece, padded, 9
+    dkeys, dvalues, dcross_q, key_blocks, value_blocks, dvalue_bias, co_blocks = cross_back(
+        used, keys, values, cross_queries, memory_rows, dcontext_two, stat_all, co_blocks, keep, piece,
+        padded, 9,
     )
     dcross_low = (dcross_q * SCALE).astype(BF)
     dcquery = weight_grad(hidden_low1, dcross_low)
@@ -1689,35 +1738,13 @@
     dout_bias = jnp.sum(dfirst, axis=0)
     cq_blocks = owners(cast(dcquery))
     plan = Exchange(
-        [
-            (cast(dfirst), GATHER, Z),
-            (co_blocks, MOVE1, PAIR),
-            (cq_blocks, MOVE1, PAIR),
-        ]
-    )
-    dkey_weight, dvalue_weight, dvalue_bias, dout_in, co_got, cq_got = memory_weights(
-        memory_rows, dkeys, dvalues, rows, padded, plan, 11
-    )
-    co_blocks, cq_blocks = sums(
-        [
-            (co_blocks, co_got, MOVE1, PAIR, PLAIN, BF),
-            (cq_blocks, cq_got, MOVE1, PAIR, PLAIN, BF),
-        ]
-    )
-    dout_in = dout_in.reshape(uniq, D)
-    memory_blocks = [owners(dkey_weight), owners(dvalue_weight)]
-    plan = Exchange(
-        [(co_blocks, MOVE, CHIPS), (cq_blocks, MOVE, CHIPS)]
-        + [(a, MOVE1, PAIR) for a in memory_blocks]
-    )
-    dqkv_bias, self_blocks, out_blocks, dinputs, co_got, cq_got, *memory_got = self_back(
-        x_rows, dout_in, context, queries, self_keys, self_values, full_output, self_weight, keep,
-        dfirst, plan, 12,
+        [(cq_blocks, MOVE1, PAIR), (co_blocks, MOVE, CHIPS)]
+    )
+    dqkv_bias, self_blocks, out_blocks, dinputs, cq_got, co_got = self_back(
+        x_rows, context, queries, self_keys, self_values, full_output, self_weight, keep, dfirst, plan, 12
     )
     dqkv_bias = dqkv_bias[0]
-    key_blocks, value_blocks = sums(
-        [(a, b, MOVE1, PAIR, PLAIN, BF) for a, b in zip(memory_blocks, memory_got)]
-    )
+    (cq_blocks,) = sums([(cq_blocks, cq_got, MOVE1, PAIR, PLAIN, BF)])
 
     vectors = jnp.stack(
         [
@@ -1741,22 +1768,20 @@
         [(feed_dp, COLS, Z)]
         + [
             (a, MOVE, CHIPS)
-            for a in (value_blocks, self_blocks, out_blocks, key_blocks, answer_blocks)
+            for a in (key_blocks, value_blocks, cq_blocks, answer_blocks)
         ]
         + [(vectors, GATHER, DP)]
     )
     memory_grad, received = memory_back(
         dkeys, dvalues, key_weight, value_weight, rows, slots, padded, plan, 15
     )
-    feed_got, value_got, self_got, out_got, key_got, answer_got, vector_all = received
-    key_sum, value_sum, cq_sum, co_sum, self_grad, out_grad, feed_grad, vector_sum = sums(
+    feed_got, key_got, value_got, cq_got, answer_got, vector_all = received
+    key_sum, value_sum, cq_sum, co_sum, feed_grad, vector_sum = sums(
         [
             (key_blocks, key_got, MOVE, CHIPS, PLAIN, BF),
             (value_blocks, value_got, MOVE, CHIPS, PLAIN, BF),
             (cq_blocks, cq_got, MOVE, CHIPS, COLUMNS, BF),
             (co_blocks, co_got, MOVE, CHIPS, COLUMNS, BF),
-            (self_blocks, self_got, MOVE, CHIPS, PLAIN, F32),
-            (out_blocks, out_got, MOVE, CHIPS, TURNED, F32),
             (feed_dp, feed_got, COLS, Z, PLAIN, F32),
             (vector_all, vector_all, GATHER, DP, PLAIN, F32),
         ]
@@ -1778,16 +1803,20 @@
         co_sum,
     ]
     feature_part = lax.dynamic_slice_in_dim(vector_sum[:10], dp * vec, vec, 1)
-    *got_z, feature_all, head_all, answer_got = exchange(
+    *got_z, feature_all, head_all, answer_got, self_got, out_got = exchange(
         [(a, MOVE, Z) for a in zblocks]
         + [(feature_part, GATHER, Z), (vector_sum[10:], GATHER, Z)]
-        + [(answer_part, MOVE1, PAIR)],
+        + [(answer_part, MOVE1, PAIR), (self_blocks, MOVE, CHIPS), (out_blocks, MOVE, CHIPS)],
         16,
     )
     forms = [PLAIN, PLAIN, PLAIN, TURNED]
-    key_grad, value_grad, cquery_grad, cout_grad, answer_grad = sums(
+    key_grad, value_grad, cquery_grad, cout_grad, answer_grad, self_grad, out_grad = sums(
         [(a, b, MOVE, Z, form, F32) for a, b, form in zip(zblocks, got_z, forms)]
-        + [(answer_part, answer_got, MOVE1, PAIR, PLAIN, F32)]
+        + [
+            (answer_part, answer_got, MOVE1, PAIR, PLAIN, F32),
+            (self_blocks, self_got, MOVE, CHIPS, PLAIN, F32),
+            (out_blocks, out_got, MOVE, CHIPS, TURNED, F32),
+        ]
     )
     feature_own = jnp.sum(feature_all, axis=0)
     head_sums = jnp.sum(head_all, axis=0)

time: 704 us -> 676 us (0.960)
  local copies, waits for them, and re-layouts: 62.4 us -> 47.4 us
  Pallas kernels: 563 us -> 552 us
    pallas_call x3 -> x2, Pallas kernels: 157 us -> 125 us  [memory_call(): pl.pallas_call(functools.partial(beside, plan, kernel, len(inputs), len(o...]
    unnamed x127 -> x126, local copies, waits for them, and re-layouts: 21.7 us -> 7.58 us
    pallas_call x5, Pallas kernels: 110 us -> 121 us  [exchange(): pl.pallas_call(functools.partial(exchange_kernel, plan), out_shape=plan.s...]
    pallas_call x1, Pallas kernels: 34.2 us -> 44 us  [self_back(): pl.pallas_call(functools.partial(self_back_kernel, plan), in_specs=[vmem]...]
    convert_element_type x1, other arithmetic: 0.74 us -> 9.56 us  [memory_back(): return (jnp.transpose(out, (1, 0, 2)).astype(F32), rest)]
    pallas_call x4 -> x3, Pallas kernels: 19.1 us -> 12.8 us  [sums(): pl.pallas_call(functools.partial(sums_kernel, kinds, shapes), in_specs=[v...]
  transfers between devices with their start and end apart: 4 -> 4, of which waited for: 2 -> 1; matrix products, arithmetic and copies ran while one was open for 9% -> 9% of each run, Pallas kernels for 41% -> 47%
where the time goes in v4:
time: 676 us; the launch traced here: 665 us
  Pallas kernels  552 us (82%)
  local copies, waits for them, and re-layouts  47.4 us (7%)
  other arithmetic  35.1 us (5%)
  between operations  15.9 us (2%)
  matrix products  11.9 us (2%)
    pallas_call x2, Pallas kernels, memory_call(): pl.pallas_call(functools.partial(beside, plan, kernel, len(inputs), len(o...  125 us
    pallas_call x5, Pallas kernels, exchange(): pl.pallas_call(functools.partial(exchange_kernel, plan), out_shape=plan.s...  121 us
    pallas_call x1, Pallas kernels, cross_back(): pl.pallas_call(functools.partial(cross_back_kernel, ways, per, piece, pad...  60.9 us
    pallas_call x1, Pallas kernels, vocab_forward(): pl.pallas_call(functools.partial(vocab_kernel, ways, tile, sub, chunk, le...  58.3 us
    pallas_call x1, Pallas kernels, vocab_back(): pl.pallas_call(functools.partial(vocab_back_kernel, ways, tile, sub, chun...  50.2 us
    pallas_call x1, Pallas kernels, cross_forward(): pl.pallas_call(functools.partial(cross_kernel, ways, per, piece, padded),...  46.7 us
    pallas_call x1, Pallas kernels, self_back(): pl.pallas_call(functools.partial(self_back_kernel, plan), in_specs=[vmem]...  44 us
    pallas_call x1, Pallas kernels, feed_back(): pl.pallas_call(feed_back_kernel, grid=(tiles,), in_specs=[whole, whole, p...  19.7 us
  transfers between devices with their start and end apart: 4, of which 1 were waited for; matrix products, arithmetic and copies ran while one was open for 9% of the time, Pallas kernels for 47%

profile of v4, /device:TPU:0, one launch (start us, length us, event | category | flops | bytes accessed | tf_op | source)
XLA Modules:
  0.0 664.8 jit_solution(3285799721136610912)
XLA Ops:
  7.5 2.4 slice.263
  11.0 51.9 %shard_map.493 = (bf16[8,4,32,1024]{3,2,1,0:T(8,128)(2,1)}, bf16[8,4,32,1024]{3,2,1,0:T(8,128)(2,1)}, bf16[8,4,48,128]{3,2,1,0:T(8,128)(2,1)}, bf16[4,128,256]{2,1,0:T(8,128)(2,1)}, bf16[4,256,128]{2,1,0:T(8,128)(2,1)}) custom-call(bf16[32,1024]{1,0:T(8,128)(2,1)} %refs_0_.1, bf16[32,1024]{1,0:T(8,128)(2,1)} %refs_1_.1, ...), custom_call_target="tpu_custom_call" | custom-call | tf_op jit(solution)/shard_map/pallas_call | solution.py:287
  67.3 63.4 %memory_products.1 = (bf16[3584,1024]{1,0:T(8,128)(2,1)}, bf16[3584,1024]{1,0:T(8,128)(2,1)}, bf16[3584,1024]{1,0:T(8,128)(2,1)}, bf16[4,2,128,1024]{3,2,1,0:T(8...) custom-call(bf16[100,32,1024]{2,1,0:T(8,128)(2,1)} %bitcast.325, ...), custom_call_target="tpu_custom_call" | custom-call | flops 15032385536 | bytes 75161928 | tf_op jit(solution)/shard_map/memory_products/pallas_call | solution.py:376
  130.8 2.1 slice.269
  138.1 1.1 convolution_convert_fusion.2
  139.2 14.1 %shard_map.494 = bf16[3,64,1024]{2,1,0:T(8,128)(2,1)} custom-call(bf16[4,64,1024]{2,1,0:T(8,128)(2,1)} %bitcast.245), custom_call_target="tpu_custom_call" | custom-call | tf_op jit(solution)/shard_map/pallas_call | solution.py:287
  153.3 4.4 copy.199
  157.8 1.5 slice_convert_fusion.2
  159.3 1.1 fusion.69
  161.4 1.4 fusion.20.refs_0_
  162.9 15.7 %shard_map.495 = bf16[4,64,1024]{2,1,0:T(8,128)(2,1)} custom-call(bf16[64,1024]{1,0:T(8,128)(2,1)} %fusion.20.refs_0_), custom_call_target="tpu_custom_call" | custom-call | tf_op jit(solution)/shard_map/pallas_call | solution.py:287
  180.1 46.7 %shard_map.496 = (bf16[256,1024]{1,0:T(8,128)(2,1)}, f32[2,8,4,128]{3,2,1,0:T(4,128)}, bf16[3,256,1024]{2,1,0:T(8,128)(2,1)}, f32[3,2,8,4,128]{4,3,2,1,0:T(4,128)}) custom-call(s32[32,1,128]{2,1,0:T(1,128)} %broadcast_in_dim.170.used_ref, bf16[3584,1024]{1,0:T(8,128)(2,1)} %get-tuple-element.108.k_ref, bf16[3584,1024]{1,0:T(8,128)(2,1)} %get-tuple-element.109.v_ref, ...), custom_call_target="tpu_custom_call" | custom-call | flops 1879048192 | bytes 14680064 | tf_op jit(solution)/shard_map/pallas_call | solution.py:661
  232.3 1.3 copy.206
  233.9 2.4 copy.207
  236.2 1.8 fusion.71
  238.9 1.6 copy-done
  243.4 1.1 fusion.23.h_ref
  244.4 14.0 %shard_map.497 = (f32[256,4096]{1,0:T(8,128)}, f32[256,1024]{1,0:T(8,128)}) custom-call(bf16[256,1024]{1,0:T(8,128)(2,1)} %fusion.23.h_ref, bf16[8,4,2,128,1024]{4,3,2,1,0:T(8,128)(2,1)} %bitcast.233, bf16[8,1,512]{2,1,0:T(2,128)(2,1)} %reshape_reshape_reshape.4.bias_ref, bf16[8,4,2,128,1024]{4,3,2,1,0:T(8,128)(2,1)} %bitcast.234), custom_call_target="tpu_custom_call" | custom-call | flops 4294967296 | bytes 16777216 | tf_op jit(solution)/shard_map/pallas_call | solution.py:1240
  258.4 1.6 fusion.67
  260.3 1.1 add_convert_fusion.h_ref
  261.4 2.2 all-gather.11.cloned.1.call-done
  263.6 58.3 %shard_map.498 = (bf16[4,6400,256]{2,1,0:T(8,128)(2,1)}, f32[4,32,256]{2,1,0:T(8,128)}, f32[4,4,8,256]{3,2,1,0:T(8,128)}) custom-call(bf16[256,1024]{1,0:T(8,128)(2,1)} %add_convert_fusion.h_ref, s32[4,1,256]{2,1,0:T(1,128)} %sub.226.target_ref, bf16[8,3840,128]{2,1,0:T(8,128)(2,1)} %bitcast.323, bf16[8,2560,128]{2,1,0:T(8,128)(2,1)} %bitcast.326), custom_call_target="tpu_custom_call" | custom-call | flops 13421772800 | bytes 52428800 | tf_op jit(solution)/shard_map/pallas_call | solution.py:1023
  323.6 5.3 shard_map.499
  330.9 50.2 %shard_map.500 = f32[256,1024]{1,0:T(8,128)} custom-call(bf16[4,6400,256]{2,1,0:T(8,128)(2,1)} %get-tuple-element.123.exp_ref, f32[4,32,256]{2,1,0:T(8,128)} %get-tuple-element.124.tops_ref, s32[4,1,256]{2,1,0:T(1,128)} %sub.226.target_ref, f32[4,1,256]{2,1,0:T(1,128)} %bitcast.318, f32[4,1,256]{2,1,0:T(1,128)} %reshape.535.rate_ref, ...), custom_call_target="tpu_custom_call" | custom-call | flops 13421772800 | bytes 52428800 | tf_op jit(solution)/shard_map/pallas_call | solution.py:1168
  381.1 1.8 multiply_reduce_fusion.2
  384.1 19.7 %shard_map.501 = (bf16[8,2,128,4096]{3,2,1,0:T(8,128)(2,1)}, f32[8,1,512]{2,1,0:T(1,128)}, f32[256,1024]{1,0:T(8,128)}) custom-call(bf16[256,1024]{1,0:T(8,128)(2,1)} %convert_element_type.272.dout_ref, bf16[256,1024]{1,0:T(8,128)(2,1)} %fusion.23.h_ref, f32[256,4096]{1,0:T(8,128)} %get-tuple-element.125.a_ref, bf16[8,4,2,128,1024]{4,3,2,1,0:T(8,128)(2,1)} %bitcast.235, ...), custom_call_target="tpu_custom_call" | custom-call | flops 8589934592 | bytes 33554432 | tf_op jit(solution)/shard_map/pallas_call | solution.py:1287
  404.0 1.1 copy-done.23
  406.0 1.2 copy-done.2
  407.3 1.6 convert_multiply_fusion
  408.9 1.3 copy.216
  410.3 1.5 bitcast_reduce_fusion
  412.6 2.1 convolution_convert_fusion.1
  414.7 60.9 %shard_map.502 = (bf16[3584,1024]{1,0:T(8,128)(2,1)}, bf16[3584,1024]{1,0:T(8,128)(2,1)}, f32[64,1024]{1,0:T(8,128)}, bf16[4,128,1024]{2,1,0:T(8,128)(2,1)}, bf1...) custom-call(s32[32,1,128]{2,1,0:T(1,128)} %broadcast_in_dim.170.used_ref, ...), custom_call_target="tpu_custom_call" | custom-call | flops 19730006016 | bytes 36700160 | tf_op jit(solution)/shard_map/pallas_call | solution.py:834
  475.7 1.6 multiply_reduce_fusion.10
  478.2 2.1 convolution_convert_fusion
  480.2 44.0 %shard_map.503 = (f32[1,768]{1,0:T(1,128)}, bf16[4,128,768]{2,1,0:T(8,128)(2,1)}, bf16[4,128,256]{2,1,0:T(8,128)(2,1)}, bf16[4,64,1024]{2,1,0:T(8,128)(2,1)}, bf...) custom-call(bf16[256,1024]{1,0:T(8,128)(2,1)} %bitcast.247, bf16[256,256]{1,0:T(8,128)(2,1)} %copy-done.17, ...), custom_call_target="tpu_custom_call" | custom-call | flops 805306368 | bytes 2097152 | tf_op jit(solution)/shard_map/pallas_call | solution.py:1413
  524.2 3.1 shard_map.504.refs_7_.refs_2_
  527.4 1.3 concatenate.26.refs_9_
  530.3 61.2 %memory_back.1 = (bf16[100,32,1024]{2,1,0:T(8,128)(2,1)}, bf16[3,2,128,1024]{3,2,1,0:T(8,128)(2,1)}, bf16[3,128,1024]{2,1,0:T(8,128)(2,1)}, bf16[3,128,1024]{2,1...) custom-call(bf16[3584,1024]{1,0:T(8,128)(2,1)} %get-tuple-element.133.refs, ...), custom_call_target="tpu_custom_call" | custom-call | flops 15032385536 | bytes 75161928 | tf_op jit(solution)/shard_map/memory_back/pallas_call | solution.py:376
  591.5 6.2 shard_map.505
  597.7 1.4 slice.275.refs_5_
  599.1 1.3 constant_dynamic-slice_fusion.7.refs_4_
  600.4 1.2 multiply_reduce_fusion.refs_6_.refs_4_
  601.7 33.7 %shard_map.506 = (bf16[3,32,1024]{2,1,0:T(8,128)(2,1)}, bf16[3,32,1024]{2,1,0:T(8,128)(2,1)}, bf16[3,128,256]{2,1,0:T(8,128)(2,1)}, bf16[3,128,256]{2,1,0:T(8,12...) custom-call(bf16[4,32,1024]{2,1,0:T(8,128)(2,1)} %bitcast.268, ...), custom_call_target="tpu_custom_call" | custom-call | tf_op jit(solution)/shard_map/pallas_call | solution.py:287
  637.3 1.0 copy.220
  641.2 3.5 shard_map.507
  644.7 1.8 fusion.72
  646.5 9.6 %convert_bitcast_fusion = f32[32,100,1024]{2,0,1:T(8,128)} fusion(bf16[100,32,1024]{2,1,0:T(8,128)(2,1)} %get-tuple-element.161), kind=kLoop, calls=%fused_computation.1 | loop fusion | flops 3276800 | bytes 19660800 | tf_op jit(solution)/shard_map/convert_element_type | solution.py:466
  (281 shorter events, 38.2 us)
Async XLA Ops:
  7.2 2.7 copy-start.27
  7.2 2.8 copy-start.53
  7.2 2.9 copy-start.52
  7.2 2.9 copy-start.51
  7.3 2.9 copy-start.50
  7.3 2.9 copy-start.38
  7.3 2.9 copy-start.49
  7.3 2.9 copy-start.48
  7.3 2.9 copy-start.47
  7.3 2.9 copy-start.41
  7.3 2.9 copy-start.46
  7.3 2.9 copy-start.45
  7.3 2.9 copy-start.44
  7.3 2.9 copy-start.42
  7.4 2.9 copy-start.43
  7.4 57.2 %copy-start.39 = (s32[4,32]{1,0:T(4,128)S(1)}, s32[4,32]{1,0:T(4,128)}, u32[]{:S(2)}) copy-start(s32[4,32]{1,0:T(4,128)} %param.31) | copy-start | bytes 1540
  7.4 57.8 %copy-start.40 = (f32[4,8]{1,0:T(4,128)S(1)}, f32[4,8]{1,0:T(4,128)}, u32[]{:S(2)}) copy-start(f32[4,8]{1,0:T(4,128)} %param.32) | copy-start | bytes 388
  7.4 58.4 %copy-start.30 = (bf16[128,256]{1,0:T(8,128)(2,1)S(1)}, bf16[128,256]{1,0:T(8,128)(2,1)}, u32[]{:S(2)}) copy-start(bf16[128,256]{1,0:T(8,128)(2,1)} %param.37) | copy-start | bytes 196612
  7.4 58.4 %copy-start.31 = (bf16[128,256]{1,0:T(8,128)(2,1)S(1)}, bf16[128,256]{1,0:T(8,128)(2,1)}, u32[]{:S(2)}) copy-start(bf16[128,256]{1,0:T(8,128)(2,1)} %param.36) | copy-start | bytes 196612
  7.4 58.4 %copy-start.32 = (bf16[128,256]{1,0:T(8,128)(2,1)S(1)}, bf16[128,256]{1,0:T(8,128)(2,1)}, u32[]{:S(2)}) copy-start(bf16[128,256]{1,0:T(8,128)(2,1)} %param.35) | copy-start | bytes 196612
  7.4 59.0 %copy-start.28 = (bf16[128,1024]{1,0:T(8,128)(2,1)S(1)}, bf16[128,1024]{1,0:T(8,128)(2,1)}, u32[]{:S(2)}) copy-start(bf16[128,1024]{1,0:T(8,128)(2,1)} %param.53) | copy-start | bytes 786436
  7.4 123.3 %all-gather.7.cloned.1.call-start = ((), (), s32[]{:S(2)}) async-start(), calls=%async_computation.2 | async-start | bytes 8847360 | tf_op jit(solution)/shard_map/all_gather | solution.py:1602
  9.8 234.6 %all-gather.9.cloned.1.call-start = ((), (), s32[]{:S(2)}) async-start(), calls=%async_computation.3 | async-start | bytes 18874368 | tf_op jit(solution)/shard_map/all_gather | solution.py:1605
  130.7 3.9 copy-start.24
  130.8 4.0 copy-start.5
  130.8 4.0 copy-start.8
  130.8 132.8 %all-gather.11.cloned.1.call-start = ((), (), s32[]{:S(2)}) async-start(), calls=%async_computation.4 | async-start | bytes 5898240 | tf_op jit(solution)/shard_map/all_gather | solution.py:1606
  133.0 397.3 %reduce-scatter.2.cloned.1.call-start = ((), (), s32[]{:S(2)}) async-start(), calls=%async_computation.1 | async-start | bytes 18874368 | tf_op jit(solution)/shard_map/reduce_scatter | solution.py:1711
  137.2 20.5 %copy-start.17 = (bf16[256,256]{1,0:T(8,128)(2,1)}, bf16[256,256]{1,0:T(8,128)(2,1)S(1)}, u32[]{:S(2)}) copy-start(bf16[256,256]{1,0:T(8,128)(2,1)S(1)} %reshape.527.ctx_ref) | copy-start | bytes 393220
  138.1 19.6 %copy-start.9 = (bf16[256,1024]{1,0:T(8,128)(2,1)}, bf16[256,1024]{1,0:T(8,128)(2,1)S(1)}, u32[]{:S(2)}) copy-start(bf16[256,1024]{1,0:T(8,128)(2,1)S(1)} %bitcast_dynamic-update-slice_fusion.wo_ref) | copy-start | bytes 1572868
  153.3 4.4 copy-start.15
  157.7 3.7 copy-start.13
  160.4 18.2 %copy-start.54 = (s32[32]{0:T(128)S(1)}, s32[32]{0:T(128)}, u32[]{:S(2)}) copy-start(s32[32]{0:T(128)} %param.34) | copy-start | bytes 388
  226.8 4.1 copy-start.29
  226.8 4.5 copy-start.35
  236.2 2.6 copy-start.16
  238.1 2.4 copy-start
  238.8 3.4 copy-start.1
  381.1 1.8 copy-start.7
  405.6 1.7 copy-start.4
  414.7 60.9 %copy-start.14 = (bf16[8,128,4,256]{1,0,3,2:T(8,128)(2,1)S(1)}, bf16[8,128,4,256]{1,0,3,2:T(8,128)(2,1)}, u32[]{:S(2)}) copy-start(bf16[8,128,4,256]{1,0,3,2:T(8,128)(2,1)} %copy.199) | copy-start | bytes 6291460
  475.6 2.5 copy-start.12
  475.6 2.5 copy-start.21
  524.2 3.1 copy-start.37
  524.2 3.2 copy-start.36
  591.5 8.9 %copy-start.26 = (bf16[3,2,32,1024]{3,2,1,0:T(8,128)(2,1)S(1)}, bf16[3,2,32,1024]{3,2,1,0:T(8,128)(2,1)}, u32[]{:S(2)}) copy-start(bf16[3,2,32,1024]{3,2,1,0:T(8,128)(2,1)} %get-tuple-element.149) | copy-start | bytes 1179652
  600.4 35.9 %copy-start.22 = (f32[2,128,1024]{2,1,0:T(8,128)S(1)}, f32[2,128,1024]{2,1,0:T(8,128)}, u32[]{:S(2)}) copy-start(f32[2,128,1024]{2,1,0:T(8,128)} %get-tuple-element.170) | copy-start | bytes 3145732
  635.4 2.9 copy-start.33
  (11 other events, 13.5 us)
Sparse Core Ops, SparseCore 0:
  10.7 97.4 all-gather.6
  130.9 89.6 all-gather.8
  222.4 41.1 all-gather.10
  404.0 122.5 reduce-scatter.1

commit v5 on v4

--- a/solution.py
+++ b/solution.py
@@ -196,29 +196,59 @@
             return self.outs[i].at[self.dp]
         return self.ins[i].at[self.chip] if kind == NEARSWAP else self.ins[i]
 
+    def square(self, i):
+        shape = self.shapes[i].shape
+        halves = len(shape) > 3 or shape[1] % 32 == 0
+        return self.chips == 4 and self.kinds[i] in (NEAR, WIDE) and halves
+
+    def beside(self, chip, k):
+        return chip + 1 - 2 * lax.rem(chip, 2) if k == 0 else chip + 2 - 4 * (chip // 2)
+
+    def owner(self, i, k):
+        if not self.square(i):
+            chip = lax.rem(self.chip + self.chips - k, self.chips)
+        elif k == 0:
+            chip = self.chip
+        elif k < 3:
+            chip = self.beside(self.chip, k - 1)
+        else:
+            chip = self.beside(self.beside(self.chip, 0), 1)
+        return 2 * chip + self.parity
+
     def spread(self, i):
         copies = []
-        for off in range(1, self.chips):
-            peer = self.peer(CHIPS, off)
+        for k in range(1, 3 if self.square(i) else self.chips):
+            peer = self.beside(self.chip, k - 1) if self.square(i) else self.peer(CHIPS, k)
             source = self.ins[i].at[peer] if self.kinds[i] == NEARSWAP else self.mine(i)
             copies.append(
                 self.remote(
                     source,
                     self.outs[i].at[self.dp],
-                    self.cs.at[i, off - 1],
-                    self.cr.at[i, off - 1],
+                    self.cs.at[i, k - 1],
+                    self.cr.at[i, k - 1],
                     self.device(CHIPS, peer),
                 )
             )
         return copies
 
-    def hand(self, i, off):
-        owner = 2 * lax.rem(self.chip + self.chips - off, self.chips) + self.parity
+    def forward(self, i, k):
+        half = self.outs[i].shape[1] // 2
+        part = self.outs[i].at[self.owner(i, k + 1), pl.ds(k * half, half)]
         return self.remote(
-            self.mine(i) if off == 0 else self.outs[i].at[owner],
+            part,
+            part,
+            self.cs.at[i, 2 + k],
+            self.cr.at[i, 2 + k],
+            self.device(CHIPS, self.beside(self.chip, 1 - k)),
+        )
+
+    def hand(self, i, k):
+        owner = self.owner(i, k)
+        return self.remote(
+            self.mine(i) if k == 0 else self.outs[i].at[owner],
             self.outs[i].at[owner],
-            self.ps.at[i, off],
-            self.pr.at[i, off],
+            self.ps.at[i, k],
+            self.pr.at[i, k],
             self.device(PAIR, 1 - self.parity),
         )
 
@@ -256,13 +286,23 @@
                 for copy in self.first(i):
                     copy.start()
         for i in shared:
-            for off, copy in enumerate(self.spread(i), 1):
+            for k, copy in enumerate(self.spread(i), 1):
                 copy.wait_recv()
-                self.hand(i, off).start()
+                if self.square(i):
+                    self.forward(i, k - 1).start()
+                self.hand(i, k).start()
+        for i in shared:
+            if self.square(i):
+                for k in range(2):
+                    self.forward(i, k).wait_recv()
+                self.hand(i, 3).start()
         for i in range(self.count):
             if i in shared:
                 for copy in self.spread(i):
                     copy.wait_send()
+                if self.square(i):
+                    for k in range(2):
+                        self.forward(i, k).wait_send()
                 for off in range(self.chips):
                     self.hand(i, off).wait()
                 if self.kinds[i] != WIDE:
@@ -395,7 +435,9 @@
 def memory_kernel(slots, padded, mem_ref, wk_ref, wv_ref, vb_ref, k_ref, v_ref, rows_ref, wide):
     for c in range(0, D, 128):
         cols = slice(c, c + 128)
-        wide[...] = mem_ref[:, :, cols].reshape(slots * MEM_BLOCK, 128).astype(F32)
+        wide[0 : slots * MEM_BLOCK, :] = (
+            mem_ref[:, :, cols].reshape(slots * MEM_BLOCK, 128).astype(F32)
+        )
         for r in range(MEM_BLOCK):
             own = wide[pl.ds(r, slots, stride=MEM_BLOCK), :]
             rows_ref[r * padded : (r + 1) * padded, cols] = jnp.concatenate(
@@ -428,7 +470,7 @@
         ],
         [out_spec] * 3,
         [out] * 3,
-        [pltpu.VMEM((slots * MEM_BLOCK, 128), F32)],
+        [pltpu.VMEM((-(-slots // 8) * 8 * MEM_BLOCK, 128), F32)],
         4 * rows * padded * D * D,
     )
 
@@ -443,7 +485,7 @@
                     r * padded : r * padded + slots, part : part + 128
                 ]
             out_ref[:, :, c + part : c + part + 128] = (
-                wide[...].reshape(slots, BACK_BLOCK, 128).astype(BF)
+                wide[0 : slots * BACK_BLOCK, :].reshape(slots, BACK_BLOCK, 128).astype(BF)
             )
 
 
@@ -460,7 +502,7 @@
         [spec, spec, whole, whole],
         [pl.BlockSpec((slots, BACK_BLOCK, D), lambda i: (0, i, 0))],
         [jax.ShapeDtypeStruct((slots, rows, D), BF)],
-        [pltpu.VMEM((slots * BACK_BLOCK, 128), F32)],
+        [pltpu.VMEM((-(-slots // 8) * 8 * BACK_BLOCK, 128), F32)],
         4 * rows * padded * D * D,
     )
     return jnp.transpose(out, (1, 0, 2)).astype(F32), rest
@@ -1309,6 +1351,77 @@
             flops=8 * tokens * units * D, bytes_accessed=8 * units * D, transcendentals=2 * tokens * units
         ),
     )(dout, hidden, before, weights, weights)
+
+
+def query_kernel(
+    ways, part_ref, x_ref, bias_ref, gain_ref, shift_ref, cq_ref, cqb_ref,
+    hidden_ref, normed_ref, inverse_ref, low_ref, full_ref, all_ref, got, queries, send, recv, own,
+):
+    mp = lax.axis_index(MP)
+    count = hidden_ref.shape[0]
+
+    def part_copy(off):
+        to = lax.rem(mp + off, ways)
+        return z_copy(part_ref.at[to], got.at[off - 1], send.at[0, off], recv.at[0, off], to)
+
+    def query_copy(off):
+        to = lax.rem(mp + off, ways)
+        return z_copy(queries, all_ref.at[mp], send.at[1, off], recv.at[1, off], to)
+
+    z_meet(ways)
+    for off in range(1, ways):
+        part_copy(off).start()
+    width = full_ref.shape[1] // ways
+    for m in range(ways):
+        full_ref[:, m * width : (m + 1) * width] = cq_ref[:, m].reshape(D, width)
+    rows = pl.ds(pl.multiple_of(mp * count, count), count)
+    total = x_ref[rows, :].astype(F32) + part_ref[mp].astype(F32) + bias_ref[...]
+    for off in range(1, ways):
+        part_copy(off).wait()
+        total += got[off - 1].astype(F32)
+    hidden, normed, inverse = layer_norm(total, gain_ref[...], shift_ref[...])
+    hidden_ref[...] = hidden
+    normed_ref[...] = normed
+    inverse_ref[...] = inverse
+    low_ref[...] = hidden.astype(BF)
+    queries[...] = ((product(hidden.astype(BF), full_ref[...]) + cqb_ref[...]) * SCALE).astype(BF)
+    for off in range(1, ways):
+        query_copy(off).start()
+    local = pltpu.make_async_copy(queries, all_ref.at[mp], own.at[0])
+    local.start()
+    for off in range(1, ways):
+        query_copy(off).wait()
+    local.wait()
+
+
+def cross_inputs(partial, x, bias, gain, shift, cquery, cqbias, cid):
+    ways, count, _ = partial.shape
+    row = lambda a: a.astype(F32).reshape(1, D)
+    vmem = pl.BlockSpec(memory_space=pltpu.VMEM)
+    dma = pltpu.SemaphoreType.DMA
+    return pl.pallas_call(
+        functools.partial(query_kernel, ways),
+        in_specs=[vmem] * 7,
+        out_specs=[vmem] * 5 + [pl.BlockSpec(memory_space=pl.ANY)],
+        out_shape=[
+            jax.ShapeDtypeStruct((count, D), F32),
+            jax.ShapeDtypeStruct((count, D), F32),
+            jax.ShapeDtypeStruct((count, 1), F32),
+            jax.ShapeDtypeStruct((count, D), BF),
+            jax.ShapeDtypeStruct((D, D), BF),
+            jax.ShapeDtypeStruct((ways, count, D), BF),
+        ],
+        scratch_shapes=[
+            pltpu.VMEM((ways - 1, count, D), BF),
+            pltpu.VMEM((count, D), BF),
+            dma((2, ways)),
+            dma((2, ways)),
+            dma((1,)),
+        ],
+        compiler_params=pltpu.CompilerParams(
+            vmem_limit_bytes=VMEM_BYTES, collective_id=cid, has_side_effects=True
+        ),
+    )(partial, x, row(bias), row(gain), row(shift), cquery, row(cqbias))
 
 
 def self_back_kernel(
@@ -1596,7 +1709,7 @@
         memory_products(memory, key_weight, value_weight, cvbias, padded, plan, 1)
     )
     words = word_table.shape[0]
-    early = words // 1280 * 3 // 5 * 1280 if words % 1280 == 0 else 0
+    early = words // 1280 * 4 // 5 * 1280 if words % 1280 == 0 else 0
     tables = []
     if early:
         part = lax.all_gather(word_table[:early], DP, axis=0, tiled=False)
@@ -1627,14 +1740,9 @@
     )
     context = context.astype(BF).reshape(uniq, head_cols)
     partial = product(context, full_output).astype(BF).reshape(mp_ways, shard_uniq, D)
-    (received,) = exchange([(partial, MOVE, Z)], 2)
-    full_cquery = rows_first(cquery_all)
-    x_own = lax.dynamic_slice_in_dim(x_rows, mp * shard_uniq, shard_uniq, 0)
-    first_in = x_own.astype(F32) + added(partial, received, Z) + full_obias
-    hidden_one, normed_one, inverse_one = layer_norm(first_in, gain_one, shift_one)
-    hidden_low1 = hidden_one.astype(BF)
-    cross_queries = ((product(hidden_low1, full_cquery) + cqbias) * SCALE).astype(BF)
-    (cross_queries,) = exchange([(cross_queries, GATHER, Z)], 3)
+    hidden_one, normed_one, inverse_one, hidden_low1, full_cquery, cross_queries = cross_inputs(
+        partial, x_rows, full_obias, gain_one, shift_one, cquery_all, cqbias, 2
+    )
     full_cout = columns_first(cout_all)
     cross_queries = cross_queries.reshape(uniq, D)
 

time: 676 us -> 666 us (0.985)
    pallas_call x5 -> x3, Pallas kernels: 121 us -> 87.9 us  [exchange(): pl.pallas_call(functools.partial(exchange_kernel, plan), out_shape=plan.s...]
    pallas_call x0 -> x1, Pallas kernels: none -> 30.3 us  [cross_inputs(): pl.pallas_call(functools.partial(query_kernel, ways), in_specs=[vmem] * 7...]
  transfers between devices with their start and end apart: 4 -> 4, of which waited for: 1 -> 0; matrix products, arithmetic and copies ran while one was open for 9% -> 8% of each run, Pallas kernels for 47% -> 47%
where the time goes in v5:
time: 666 us; the launch traced here: 655 us
  Pallas kernels  551 us (83%)
  local copies, waits for them, and re-layouts  42.3 us (6%)
  other arithmetic  34.7 us (5%)
  between operations  15.9 us (2%)
  matrix products  10.7 us (2%)
    pallas_call x2, Pallas kernels, memory_call(): pl.pallas_call(functools.partial(beside, plan, kernel, len(inputs), len(o...  121 us
    pallas_call x3, Pallas kernels, exchange(): pl.pallas_call(functools.partial(exchange_kernel, plan), out_shape=plan.s...  87.9 us
    pallas_call x1, Pallas kernels, vocab_forward(): pl.pallas_call(functools.partial(vocab_kernel, ways, tile, sub, chunk, le...  63.5 us
    pallas_call x1, Pallas kernels, cross_back(): pl.pallas_call(functools.partial(cross_back_kernel, ways, per, piece, pad...  60.9 us
    pallas_call x1, Pallas kernels, vocab_back(): pl.pallas_call(functools.partial(vocab_back_kernel, ways, tile, sub, chun...  50.1 us
    pallas_call x1, Pallas kernels, cross_forward(): pl.pallas_call(functools.partial(cross_kernel, ways, per, piece, padded),...  46.8 us
    pallas_call x1, Pallas kernels, self_back(): pl.pallas_call(functools.partial(self_back_kernel, plan), in_specs=[vmem]...  44.5 us
    pallas_call x1, Pallas kernels, cross_inputs(): pl.pallas_call(functools.partial(query_kernel, ways), in_specs=[vmem] * 7...  30.3 us
  transfers between devices with their start and end apart: 4, of which 0 were waited for; matrix products, arithmetic and copies ran while one was open for 8% of the time, Pallas kernels for 47%

profile of v5, /device:TPU:0, one launch (start us, length us, event | category | flops | bytes accessed | tf_op | source)
XLA Modules:
  0.0 655.0 jit_solution(5107393096845009232)
XLA Ops:
  7.5 2.6 slice.263
  11.3 48.4 %shard_map.493 = (bf16[8,4,32,1024]{3,2,1,0:T(8,128)(2,1)}, bf16[8,4,32,1024]{3,2,1,0:T(8,128)(2,1)}, bf16[8,4,48,128]{3,2,1,0:T(8,128)(2,1)}, bf16[4,128,256]{2,1,0:T(8,128)(2,1)}, bf16[4,256,128]{2,1,0:T(8,128)(2,1)}) custom-call(bf16[32,1024]{1,0:T(8,128)(2,1)} %refs_0_.1, bf16[32,1024]{1,0:T(8,128)(2,1)} %refs_1_.1, ...), custom_call_target="tpu_custom_call" | custom-call | tf_op jit(solution)/shard_map/pallas_call | solution.py:327
  59.7 0.9 slice_reduce_fusion.1
  64.0 60.6 %memory_products.1 = (bf16[3584,1024]{1,0:T(8,128)(2,1)}, bf16[3584,1024]{1,0:T(8,128)(2,1)}, bf16[3584,1024]{1,0:T(8,128)(2,1)}, bf16[4,2,128,1024]{3,2,1,0:T(8...) custom-call(bf16[100,32,1024]{2,1,0:T(8,128)(2,1)} %bitcast.302, ...), custom_call_target="tpu_custom_call" | custom-call | flops 15032385536 | bytes 75161928 | tf_op jit(solution)/shard_map/memory_products/pallas_call | solution.py:416
  124.7 1.9 slice.269
  134.8 1.1 convolution_convert_fusion.2
  136.7 30.3 %shard_map.494 = (f32[64,1024]{1,0:T(8,128)}, f32[64,1024]{1,0:T(8,128)}, f32[64,1]{1,0:T(8,128)}, bf16[64,1024]{1,0:T(8,128)(2,1)}, bf16[1024,1024]{1,0:T(8,128)(2,1)}, /*index=5*/bf16[4,64,1024]{2,1,0:T(8,128)(2,1)}) custom-call(bf16[4,64,1024]{2,1,0:T(8,128)(2,1)} %bitcast.233, bf16[256,1024]{1,0:T(8,128)(2,1)} %bitcast.227, ...), custom_call_target="tpu_custom_call" | custom-call | tf_op jit(solution)/shard_map/pallas_call | solution.py:1402
  167.8 46.8 %shard_map.495 = (bf16[256,1024]{1,0:T(8,128)(2,1)}, f32[2,8,4,128]{3,2,1,0:T(4,128)}, bf16[3,256,1024]{2,1,0:T(8,128)(2,1)}, f32[3,2,8,4,128]{4,3,2,1,0:T(4,128)}) custom-call(s32[32,1,128]{2,1,0:T(1,128)} %broadcast_in_dim.164.used_ref, bf16[3584,1024]{1,0:T(8,128)(2,1)} %get-tuple-element.116.k_ref, bf16[3584,1024]{1,0:T(8,128)(2,1)} %get-tuple-element.117.v_ref, ...), custom_call_target="tpu_custom_call" | custom-call | flops 1879048192 | bytes 14680064 | tf_op jit(solution)/shard_map/pallas_call | solution.py:703
  214.6 0.9 fusion.46
  219.3 1.3 copy.202
  220.9 2.4 copy.203
  223.3 1.9 fusion.47
  226.0 1.6 copy-done
  230.8 1.1 fusion.5.h_ref
  231.8 13.6 %shard_map.496 = (f32[256,4096]{1,0:T(8,128)}, f32[256,1024]{1,0:T(8,128)}) custom-call(bf16[256,1024]{1,0:T(8,128)(2,1)} %fusion.5.h_ref, bf16[8,4,2,128,1024]{4,3,2,1,0:T(8,128)(2,1)} %bitcast.217, bf16[8,1,512]{2,1,0:T(2,128)(2,1)} %reshape_reshape_reshape.4.bias_ref, bf16[8,4,2,128,1024]{4,3,2,1,0:T(8,128)(2,1)} %bitcast.218), custom_call_target="tpu_custom_call" | custom-call | flops 4294967296 | bytes 16777216 | tf_op jit(solution)/shard_map/pallas_call | solution.py:1282
  245.5 1.7 fusion.45
  247.4 1.0 add_convert_fusion.h_ref
  248.5 63.5 %shard_map.497 = (bf16[4,6400,256]{2,1,0:T(8,128)(2,1)}, f32[4,32,256]{2,1,0:T(8,128)}, f32[4,4,8,256]{3,2,1,0:T(8,128)}) custom-call(bf16[256,1024]{1,0:T(8,128)(2,1)} %add_convert_fusion.h_ref, s32[4,1,256]{2,1,0:T(1,128)} %sub.216.target_ref, bf16[8,5120,128]{2,1,0:T(8,128)(2,1)} %bitcast.300, bf16[8,1280,128]{2,1,0:T(8,128)(2,1)} %bitcast.303), custom_call_target="tpu_custom_call" | custom-call | flops 13421772800 | bytes 52428800 | tf_op jit(solution)/shard_map/pallas_call | solution.py:1065
  312.0 0.9 slice_bitcast_fusion.2
  313.7 5.8 shard_map.498
  319.5 0.9 reshape.542
  321.5 50.1 %shard_map.499 = f32[256,1024]{1,0:T(8,128)} custom-call(bf16[4,6400,256]{2,1,0:T(8,128)(2,1)} %get-tuple-element.131.exp_ref, f32[4,32,256]{2,1,0:T(8,128)} %get-tuple-element.132.tops_ref, s32[4,1,256]{2,1,0:T(1,128)} %sub.216.target_ref, f32[4,1,256]{2,1,0:T(1,128)} %bitcast.295, f32[4,1,256]{2,1,0:T(1,128)} %reshape.544.rate_ref, ...), custom_call_target="tpu_custom_call" | custom-call | flops 13421772800 | bytes 52428800 | tf_op jit(solution)/shard_map/pallas_call | solution.py:1210
  371.6 1.8 multiply_reduce_fusion.2
  374.6 19.7 %shard_map.500 = (bf16[8,2,128,4096]{3,2,1,0:T(8,128)(2,1)}, f32[8,1,512]{2,1,0:T(1,128)}, f32[256,1024]{1,0:T(8,128)}) custom-call(bf16[256,1024]{1,0:T(8,128)(2,1)} %convert_element_type.266.dout_ref, bf16[256,1024]{1,0:T(8,128)(2,1)} %fusion.5.h_ref, f32[256,4096]{1,0:T(8,128)} %get-tuple-element.133.a_ref, bf16[8,4,2,128,1024]{4,3,2,1,0:T(8,128)(2,1)} %bitcast.219, ...), custom_call_target="tpu_custom_call" | custom-call | flops 8589934592 | bytes 33554432 | tf_op jit(solution)/shard_map/pallas_call | solution.py:1329
  396.6 1.2 copy-done.2
  397.9 1.6 convert_multiply_fusion
  399.4 1.3 copy.212
  400.8 1.6 bitcast_reduce_fusion
  403.3 2.1 convolution_convert_fusion.1
  405.4 60.9 %shard_map.501 = (bf16[3584,1024]{1,0:T(8,128)(2,1)}, bf16[3584,1024]{1,0:T(8,128)(2,1)}, f32[64,1024]{1,0:T(8,128)}, bf16[4,128,1024]{2,1,0:T(8,128)(2,1)}, bf1...) custom-call(s32[32,1,128]{2,1,0:T(1,128)} %broadcast_in_dim.164.used_ref, ...), custom_call_target="tpu_custom_call" | custom-call | flops 19730006016 | bytes 36700160 | tf_op jit(solution)/shard_map/pallas_call | solution.py:876
  466.3 1.9 multiply_reduce_fusion.10
  469.0 2.0 convolution_convert_fusion
  471.1 44.5 %shard_map.502 = (f32[1,768]{1,0:T(1,128)}, bf16[4,128,768]{2,1,0:T(8,128)(2,1)}, bf16[4,128,256]{2,1,0:T(8,128)(2,1)}, bf16[4,64,1024]{2,1,0:T(8,128)(2,1)}, bf...) custom-call(bf16[256,1024]{1,0:T(8,128)(2,1)} %bitcast.228, bf16[256,256]{1,0:T(8,128)(2,1)} %copy-done.13, ...), custom_call_target="tpu_custom_call" | custom-call | flops 805306368 | bytes 2097152 | tf_op jit(solution)/shard_map/pallas_call | solution.py:1526
  515.6 3.1 shard_map.503.refs_7_.refs_2_
  518.8 1.3 concatenate.26.refs_9_
  520.3 0.9 constant_dynamic-slice_fusion.9
  521.7 60.0 %memory_back.1 = (bf16[100,32,1024]{2,1,0:T(8,128)(2,1)}, bf16[3,2,128,1024]{3,2,1,0:T(8,128)(2,1)}, bf16[3,128,1024]{2,1,0:T(8,128)(2,1)}, bf16[3,128,1024]{2,1...) custom-call(bf16[3584,1024]{1,0:T(8,128)(2,1)} %get-tuple-element.145.refs, ...), custom_call_target="tpu_custom_call" | custom-call | flops 15032385536 | bytes 75161928 | tf_op jit(solution)/shard_map/memory_back/pallas_call | solution.py:416
  581.7 6.2 shard_map.504
  588.0 1.4 slice.275.refs_5_
  589.3 1.3 constant_dynamic-slice_fusion.8.refs_4_
  590.7 1.2 multiply_reduce_fusion.refs_6_.refs_4_
  592.0 33.7 %shard_map.505 = (bf16[3,32,1024]{2,1,0:T(8,128)(2,1)}, bf16[3,32,1024]{2,1,0:T(8,128)(2,1)}, bf16[3,128,256]{2,1,0:T(8,128)(2,1)}, bf16[3,128,256]{2,1,0:T(8,12...) custom-call(bf16[4,32,1024]{2,1,0:T(8,128)(2,1)} %bitcast.246, ...), custom_call_target="tpu_custom_call" | custom-call | tf_op jit(solution)/shard_map/pallas_call | solution.py:327
  625.6 0.9 reduce_sum.339
  626.6 0.9 slice_bitcast_fusion
  627.5 1.0 copy.216
  631.4 3.5 shard_map.506
  634.9 1.8 fusion.48
  636.7 9.6 %convert_bitcast_fusion = f32[32,100,1024]{2,0,1:T(8,128)} fusion(bf16[100,32,1024]{2,1,0:T(8,128)(2,1)} %get-tuple-element.173), kind=kLoop, calls=%fused_computation.1 | loop fusion | flops 3276800 | bytes 19660800 | tf_op jit(solution)/shard_map/convert_element_type | solution.py:508
  (295 shorter events, 34.3 us)
Async XLA Ops:
  7.2 2.9 copy-start.24
  7.2 3.1 copy-start.64
  7.2 3.2 copy-start.59
  7.2 3.2 copy-start.58
  7.3 3.2 copy-start.57
  7.3 3.2 copy-start.45
  7.3 3.2 copy-start.56
  7.3 3.2 copy-start.55
  7.3 3.2 copy-start.54
  7.3 3.2 copy-start.48
  7.3 3.2 copy-start.53
  7.3 3.2 copy-start.52
  7.3 3.2 copy-start.51
  7.3 3.2 copy-start.49
  7.4 3.2 copy-start.50
  7.4 53.9 %copy-start.46 = (s32[4,32]{1,0:T(4,128)S(1)}, s32[4,32]{1,0:T(4,128)}, u32[]{:S(2)}) copy-start(s32[4,32]{1,0:T(4,128)} %param.31) | copy-start | bytes 1540
  7.4 54.5 %copy-start.47 = (f32[4,8]{1,0:T(4,128)S(1)}, f32[4,8]{1,0:T(4,128)}, u32[]{:S(2)}) copy-start(f32[4,8]{1,0:T(4,128)} %param.32) | copy-start | bytes 388
  7.4 55.1 %copy-start.30 = (bf16[128,256]{1,0:T(8,128)(2,1)S(1)}, bf16[128,256]{1,0:T(8,128)(2,1)}, u32[]{:S(2)}) copy-start(bf16[128,256]{1,0:T(8,128)(2,1)} %param.37) | copy-start | bytes 196612
  7.4 55.1 %copy-start.31 = (bf16[128,256]{1,0:T(8,128)(2,1)S(1)}, bf16[128,256]{1,0:T(8,128)(2,1)}, u32[]{:S(2)}) copy-start(bf16[128,256]{1,0:T(8,128)(2,1)} %param.36) | copy-start | bytes 196612
  7.4 55.1 %copy-start.32 = (bf16[128,256]{1,0:T(8,128)(2,1)S(1)}, bf16[128,256]{1,0:T(8,128)(2,1)}, u32[]{:S(2)}) copy-start(bf16[128,256]{1,0:T(8,128)(2,1)} %param.35) | copy-start | bytes 196612
  7.4 55.8 %copy-start.26 = (bf16[128,1024]{1,0:T(8,128)(2,1)S(1)}, bf16[128,1024]{1,0:T(8,128)(2,1)}, u32[]{:S(2)}) copy-start(bf16[128,1024]{1,0:T(8,128)(2,1)} %param.53) | copy-start | bytes 786436
  7.4 117.2 %all-gather.7.cloned.1.call-start = ((), (), s32[]{:S(2)}) async-start(), calls=%async_computation.2 | async-start | bytes 11796480 | tf_op jit(solution)/shard_map/all_gather | solution.py:1715
  10.1 221.7 %all-gather.9.cloned.1.call-start = ((), (), s32[]{:S(2)}) async-start(), calls=%async_computation.3 | async-start | bytes 18874368 | tf_op jit(solution)/shard_map/all_gather | solution.py:1718
  124.6 5.2 copy-start.28
  124.6 7.5 %copy-start.20 = (bf16[8,256,128]{2,1,0:T(8,128)(2,1)S(1)}, bf16[8,256,128]{2,1,0:T(8,128)(2,1)}, u32[]{:S(2)}) copy-start(bf16[8,256,128]{2,1,0:T(8,128)(2,1)} %get-tuple-element.113) | copy-start | bytes 1572868
  124.6 7.7 %copy-start.5 = (bf16[8,128,768]{2,1,0:T(8,128)(2,1)S(1)}, bf16[8,128,768]{2,1,0:T(8,128)(2,1)}, u32[]{:S(2)}) copy-start(bf16[8,128,768]{2,1,0:T(8,128)(2,1)} %get-tuple-element.112) | copy-start | bytes 4718596
  124.6 7.7 %copy-start.6 = (bf16[8,32,1024]{2,1,0:T(8,128)(2,1)S(1)}, bf16[8,32,1024]{2,1,0:T(8,128)(2,1)}, u32[]{:S(2)}) copy-start(bf16[8,32,1024]{2,1,0:T(8,128)(2,1)} %get-tuple-element.111) | copy-start | bytes 1572868
  124.7 123.8 %all-gather.11.cloned.1.call-start = ((), (), s32[]{:S(2)}) async-start(), calls=%async_computation.4 | async-start | bytes 2949120 | tf_op jit(solution)/shard_map/all_gather | solution.py:1719
  126.6 395.1 %reduce-scatter.2.cloned.1.call-start = ((), (), s32[]{:S(2)}) async-start(), calls=%async_computation.1 | async-start | bytes 18874368 | tf_op jit(solution)/shard_map/reduce_scatter | solution.py:1819
  132.3 2.6 copy-start.9
  134.0 1.9 copy-start.41
  134.8 32.2 %copy-start.13 = (bf16[256,256]{1,0:T(8,128)(2,1)}, bf16[256,256]{1,0:T(8,128)(2,1)S(1)}, u32[]{:S(2)}) copy-start(bf16[256,256]{1,0:T(8,128)(2,1)S(1)} %reshape.537.ctx_ref) | copy-start | bytes 393220
  214.6 2.5 copy-start.25
  214.6 3.3 copy-start.29
  214.6 3.7 copy-start.40
  223.2 2.7 copy-start.12
  225.2 2.4 copy-start
  225.9 3.4 copy-start.1
  231.8 13.7 %copy-start.37 = (f32[8,1,1,128]{3,2,1,0:T(1,128)S(1)}, f32[8,1,1,128]{3,2,1,0:T(1,128)}, u32[]{:S(2)}) copy-start(f32[8,1,1,128]{3,2,1,0:T(1,128)} %get-tuple-element.393) | copy-start | bytes 12292
  405.4 60.9 %copy-start.11 = (bf16[1024,1024]{1,0:T(8,128)(2,1)S(1)}, bf16[1024,1024]{1,0:T(8,128)(2,1)}, u32[]{:S(2)}) copy-start(bf16[1024,1024]{1,0:T(8,128)(2,1)} %get-tuple-element.140) | copy-start | bytes 6291460
  405.4 60.9 %copy-start.17 = (f32[64,1024]{1,0:T(8,128)S(1)}, f32[64,1024]{1,0:T(8,128)}, u32[]{:S(2)}) copy-start(f32[64,1024]{1,0:T(8,128)} %get-tuple-element.141) | copy-start | bytes 786436
  466.2 2.8 copy-start.10
  466.3 2.8 copy-start.27
  515.6 3.2 copy-start.44
  515.6 3.2 copy-start.43
  581.7 8.9 %copy-start.22 = (bf16[3,2,32,1024]{3,2,1,0:T(8,128)(2,1)S(1)}, bf16[3,2,32,1024]{3,2,1,0:T(8,128)(2,1)}, u32[]{:S(2)}) copy-start(bf16[3,2,32,1024]{3,2,1,0:T(8,128)(2,1)} %get-tuple-element.161) | copy-start | bytes 1179652
  590.7 35.9 %copy-start.18 = (f32[2,128,1024]{2,1,0:T(8,128)S(1)}, f32[2,128,1024]{2,1,0:T(8,128)}, u32[]{:S(2)}) copy-start(f32[2,128,1024]{2,1,0:T(8,128)} %get-tuple-element.182) | copy-start | bytes 3145732
  625.6 2.9 copy-start.35
  (22 other events, 31.7 us)
Sparse Core Ops, SparseCore 0:
  10.7 93.3 all-gather.6
  124.8 90.2 all-gather.8
  216.9 30.1 all-gather.10
  394.5 121.4 reduce-scatter.1

commit v6 on v5

--- a/solution.py
+++ b/solution.py
@@ -621,6 +621,33 @@
 def line_sems(count, ways):
     dma = pltpu.SemaphoreType.DMA
     return [dma((count, ways)) for _ in range(4)] + [dma((count,))]
+
+
+def feed_sum_kernel(array, got, out):
+    width = got.shape[-1]
+    start = pl.multiple_of(lax.axis_index(MP) * width, width)
+    total = array[:, :, pl.ds(start, width)].astype(F32)
+    for i in range(got.shape[0]):
+        total += got[i].astype(F32)
+    out[...] = total
+
+
+def feed_sum(array, got, plan, cid):
+    whole = lambda shape: pl.BlockSpec(shape, lambda i: (0,) * len(shape))
+    shape = got.shape[1:]
+    return memory_call(
+        plan,
+        cid,
+        feed_sum_kernel,
+        "feed_sum",
+        1,
+        [array, got],
+        [whole(array.shape), whole(got.shape)],
+        [whole(shape)],
+        [jax.ShapeDtypeStruct(shape, F32)],
+        [],
+        4 * array.size,
+    )
 
 
 def own_heads(result, keep):
@@ -1884,18 +1911,15 @@
         dkeys, dvalues, key_weight, value_weight, rows, slots, padded, plan, 15
     )
     feed_got, key_got, value_got, cq_got, answer_got, vector_all = received
-    key_sum, value_sum, cq_sum, co_sum, feed_grad, vector_sum = sums(
+    key_sum, value_sum, cq_sum, co_sum, vector_sum = sums(
         [
             (key_blocks, key_got, MOVE, CHIPS, PLAIN, BF),
             (value_blocks, value_got, MOVE, CHIPS, PLAIN, BF),
             (cq_blocks, cq_got, MOVE, CHIPS, COLUMNS, BF),
             (co_blocks, co_got, MOVE, CHIPS, COLUMNS, BF),
-            (feed_dp, feed_got, COLS, Z, PLAIN, F32),
             (vector_all, vector_all, GATHER, DP, PLAIN, F32),
         ]
     )
-
-    expand_grad, shrink_grad = feed_grad[0], feed_grad[1].T
 
     own_answers = lax.dynamic_index_in_dim(answer_blocks, dp // 2, 0, keepdims=True)
     returned = jnp.concatenate([own_answers, answer_got], axis=0).astype(F32)
@@ -1911,12 +1935,15 @@
         co_sum,
     ]
     feature_part = lax.dynamic_slice_in_dim(vector_sum[:10], dp * vec, vec, 1)
-    *got_z, feature_all, head_all, answer_got, self_got, out_got = exchange(
+    plan = Exchange(
         [(a, MOVE, Z) for a in zblocks]
         + [(feature_part, GATHER, Z), (vector_sum[10:], GATHER, Z)]
-        + [(answer_part, MOVE1, PAIR), (self_blocks, MOVE, CHIPS), (out_blocks, MOVE, CHIPS)],
-        16,
-    )
+        + [(answer_part, MOVE1, PAIR), (self_blocks, MOVE, CHIPS), (out_blocks, MOVE, CHIPS)]
+    )
+    feed_grad, *got_z, feature_all, head_all, answer_got, self_got, out_got = feed_sum(
+        feed_dp, feed_got, plan, 16
+    )
+    expand_grad, shrink_grad = feed_grad[0], feed_grad[1].T
     forms = [PLAIN, PLAIN, PLAIN, TURNED]
     key_grad, value_grad, cquery_grad, cout_grad, answer_grad, self_grad, out_grad = sums(
         [(a, b, MOVE, Z, form, F32) for a, b, form in zip(zblocks, got_z, forms)]

time: 666 us -> 669 us (level)
    pallas_call x2 -> x3, Pallas kernels: 121 us -> 157 us  [memory_call(): pl.pallas_call(functools.partial(beside, plan, kernel, len(inputs), len(o...]
    pallas_call x3 -> x2, Pallas kernels: 87.9 us -> 54.2 us  [exchange(): pl.pallas_call(functools.partial(exchange_kernel, plan), out_shape=plan.s...]
where the time goes in v6:
time: 669 us; the launch traced here: 657 us
  Pallas kernels  552 us (83%)
  local copies, waits for them, and re-layouts  42.3 us (6%)
  other arithmetic  35.5 us (5%)
  between operations  15.9 us (2%)
  matrix products  10.7 us (2%)
    pallas_call x3, Pallas kernels, memory_call(): pl.pallas_call(functools.partial(beside, plan, kernel, len(inputs), len(o...  157 us
    pallas_call x1, Pallas kernels, vocab_forward(): pl.pallas_call(functools.partial(vocab_kernel, ways, tile, sub, chunk, le...  63.5 us
    pallas_call x1, Pallas kernels, cross_back(): pl.pallas_call(functools.partial(cross_back_kernel, ways, per, piece, pad...  60.9 us
    pallas_call x2, Pallas kernels, exchange(): pl.pallas_call(functools.partial(exchange_kernel, plan), out_shape=plan.s...  54.2 us
    pallas_call x1, Pallas kernels, vocab_back(): pl.pallas_call(functools.partial(vocab_back_kernel, ways, tile, sub, chun...  50.1 us
    pallas_call x1, Pallas kernels, cross_forward(): pl.pallas_call(functools.partial(cross_kernel, ways, per, piece, padded),...  46.8 us
    pallas_call x1, Pallas kernels, self_back(): pl.pallas_call(functools.partial(self_back_kernel, plan), in_specs=[vmem]...  44.5 us
    pallas_call x1, Pallas kernels, cross_inputs(): pl.pallas_call(functools.partial(query_kernel, ways), in_specs=[vmem] * 7...  30.3 us
  transfers between devices with their start and end apart: 4, of which 0 were waited for; matrix products, arithmetic and copies ran while one was open for 8% of the time, Pallas kernels for 47%

profile of v6, /device:TPU:0, one launch (start us, length us, event | category | flops | bytes accessed | tf_op | source)
XLA Modules:
  0.0 657.3 jit_solution(17140481886742711317)
XLA Ops:
  7.5 2.6 slice.263
  11.3 48.4 %shard_map.493 = (bf16[8,4,32,1024]{3,2,1,0:T(8,128)(2,1)}, bf16[8,4,32,1024]{3,2,1,0:T(8,128)(2,1)}, bf16[8,4,48,128]{3,2,1,0:T(8,128)(2,1)}, bf16[4,128,256]{2,1,0:T(8,128)(2,1)}, bf16[4,256,128]{2,1,0:T(8,128)(2,1)}) custom-call(bf16[32,1024]{1,0:T(8,128)(2,1)} %refs_0_.1, bf16[32,1024]{1,0:T(8,128)(2,1)} %refs_1_.1, ...), custom_call_target="tpu_custom_call" | custom-call | tf_op jit(solution)/shard_map/pallas_call | solution.py:327
  59.7 0.9 slice_reduce_fusion.1
  64.0 60.6 %memory_products.1 = (bf16[3584,1024]{1,0:T(8,128)(2,1)}, bf16[3584,1024]{1,0:T(8,128)(2,1)}, bf16[3584,1024]{1,0:T(8,128)(2,1)}, bf16[4,2,128,1024]{3,2,1,0:T(8...) custom-call(bf16[100,32,1024]{2,1,0:T(8,128)(2,1)} %bitcast.302, ...), custom_call_target="tpu_custom_call" | custom-call | flops 15032385536 | bytes 75161928 | tf_op jit(solution)/shard_map/memory_products/pallas_call | solution.py:416
  124.7 1.9 slice.269
  134.8 1.1 convolution_convert_fusion.2
  136.7 30.3 %shard_map.494 = (f32[64,1024]{1,0:T(8,128)}, f32[64,1024]{1,0:T(8,128)}, f32[64,1]{1,0:T(8,128)}, bf16[64,1024]{1,0:T(8,128)(2,1)}, bf16[1024,1024]{1,0:T(8,128)(2,1)}, /*index=5*/bf16[4,64,1024]{2,1,0:T(8,128)(2,1)}) custom-call(bf16[4,64,1024]{2,1,0:T(8,128)(2,1)} %bitcast.235, bf16[256,1024]{1,0:T(8,128)(2,1)} %bitcast.227, ...), custom_call_target="tpu_custom_call" | custom-call | tf_op jit(solution)/shard_map/pallas_call | solution.py:1429
  167.8 46.8 %shard_map.495 = (bf16[256,1024]{1,0:T(8,128)(2,1)}, f32[2,8,4,128]{3,2,1,0:T(4,128)}, bf16[3,256,1024]{2,1,0:T(8,128)(2,1)}, f32[3,2,8,4,128]{4,3,2,1,0:T(4,128)}) custom-call(s32[32,1,128]{2,1,0:T(1,128)} %broadcast_in_dim.164.used_ref, bf16[3584,1024]{1,0:T(8,128)(2,1)} %get-tuple-element.116.k_ref, bf16[3584,1024]{1,0:T(8,128)(2,1)} %get-tuple-element.117.v_ref, ...), custom_call_target="tpu_custom_call" | custom-call | flops 1879048192 | bytes 14680064 | tf_op jit(solution)/shard_map/pallas_call | solution.py:730
  214.6 0.9 fusion.46
  219.3 1.3 copy.202
  220.9 2.4 copy.203
  223.3 1.9 fusion.47
  226.0 1.6 copy-done
  230.8 1.1 fusion.5.h_ref
  231.8 13.6 %shard_map.496 = (f32[256,4096]{1,0:T(8,128)}, f32[256,1024]{1,0:T(8,128)}) custom-call(bf16[256,1024]{1,0:T(8,128)(2,1)} %fusion.5.h_ref, bf16[8,4,2,128,1024]{4,3,2,1,0:T(8,128)(2,1)} %bitcast.217, bf16[8,1,512]{2,1,0:T(2,128)(2,1)} %reshape_reshape_reshape.4.bias_ref, bf16[8,4,2,128,1024]{4,3,2,1,0:T(8,128)(2,1)} %bitcast.218), custom_call_target="tpu_custom_call" | custom-call | flops 4294967296 | bytes 16777216 | tf_op jit(solution)/shard_map/pallas_call | solution.py:1309
  245.5 1.7 fusion.45
  247.4 1.0 add_convert_fusion.h_ref
  248.5 63.5 %shard_map.497 = (bf16[4,6400,256]{2,1,0:T(8,128)(2,1)}, f32[4,32,256]{2,1,0:T(8,128)}, f32[4,4,8,256]{3,2,1,0:T(8,128)}) custom-call(bf16[256,1024]{1,0:T(8,128)(2,1)} %add_convert_fusion.h_ref, s32[4,1,256]{2,1,0:T(1,128)} %sub.216.target_ref, bf16[8,5120,128]{2,1,0:T(8,128)(2,1)} %bitcast.300, bf16[8,1280,128]{2,1,0:T(8,128)(2,1)} %bitcast.303), custom_call_target="tpu_custom_call" | custom-call | flops 13421772800 | bytes 52428800 | tf_op jit(solution)/shard_map/pallas_call | solution.py:1092
  312.0 0.9 slice_bitcast_fusion.2
  313.7 5.8 shard_map.498
  319.5 0.9 reshape.542
  321.5 50.1 %shard_map.499 = f32[256,1024]{1,0:T(8,128)} custom-call(bf16[4,6400,256]{2,1,0:T(8,128)(2,1)} %get-tuple-element.131.exp_ref, f32[4,32,256]{2,1,0:T(8,128)} %get-tuple-element.132.tops_ref, s32[4,1,256]{2,1,0:T(1,128)} %sub.216.target_ref, f32[4,1,256]{2,1,0:T(1,128)} %bitcast.295, f32[4,1,256]{2,1,0:T(1,128)} %reshape.544.rate_ref, ...), custom_call_target="tpu_custom_call" | custom-call | flops 13421772800 | bytes 52428800 | tf_op jit(solution)/shard_map/pallas_call | solution.py:1237
  371.6 1.8 multiply_reduce_fusion.2
  374.6 19.7 %shard_map.500 = (bf16[8,2,128,4096]{3,2,1,0:T(8,128)(2,1)}, f32[8,1,512]{2,1,0:T(1,128)}, f32[256,1024]{1,0:T(8,128)}) custom-call(bf16[256,1024]{1,0:T(8,128)(2,1)} %convert_element_type.266.dout_ref, bf16[256,1024]{1,0:T(8,128)(2,1)} %fusion.5.h_ref, f32[256,4096]{1,0:T(8,128)} %get-tuple-element.133.a_ref, bf16[8,4,2,128,1024]{4,3,2,1,0:T(8,128)(2,1)} %bitcast.219, ...), custom_call_target="tpu_custom_call" | custom-call | flops 8589934592 | bytes 33554432 | tf_op jit(solution)/shard_map/pallas_call | solution.py:1356
  396.6 1.2 copy-done.2
  397.9 1.6 convert_multiply_fusion
  399.4 1.3 copy.212
  400.8 1.6 bitcast_reduce_fusion
  403.3 2.1 convolution_convert_fusion.1
  405.4 60.9 %shard_map.501 = (bf16[3584,1024]{1,0:T(8,128)(2,1)}, bf16[3584,1024]{1,0:T(8,128)(2,1)}, f32[64,1024]{1,0:T(8,128)}, bf16[4,128,1024]{2,1,0:T(8,128)(2,1)}, bf1...) custom-call(s32[32,1,128]{2,1,0:T(1,128)} %broadcast_in_dim.164.used_ref, ...), custom_call_target="tpu_custom_call" | custom-call | flops 19730006016 | bytes 36700160 | tf_op jit(solution)/shard_map/pallas_call | solution.py:903
  466.3 1.9 multiply_reduce_fusion.10
  469.0 2.0 convolution_convert_fusion
  471.1 44.5 %shard_map.502 = (f32[1,768]{1,0:T(1,128)}, bf16[4,128,768]{2,1,0:T(8,128)(2,1)}, bf16[4,128,256]{2,1,0:T(8,128)(2,1)}, bf16[4,64,1024]{2,1,0:T(8,128)(2,1)}, bf...) custom-call(bf16[256,1024]{1,0:T(8,128)(2,1)} %bitcast.228, bf16[256,256]{1,0:T(8,128)(2,1)} %copy-done.13, ...), custom_call_target="tpu_custom_call" | custom-call | flops 805306368 | bytes 2097152 | tf_op jit(solution)/shard_map/pallas_call | solution.py:1553
  515.6 3.1 shard_map.503.refs_7_.refs_2_
  518.8 1.3 concatenate.26.refs_9_
  520.3 0.9 constant_dynamic-slice_fusion.9
  521.7 60.0 %memory_back.1 = (bf16[100,32,1024]{2,1,0:T(8,128)(2,1)}, bf16[3,2,128,1024]{3,2,1,0:T(8,128)(2,1)}, bf16[3,128,1024]{2,1,0:T(8,128)(2,1)}, bf16[3,128,1024]{2,1...) custom-call(bf16[3584,1024]{1,0:T(8,128)(2,1)} %get-tuple-element.144.refs, ...), custom_call_target="tpu_custom_call" | custom-call | flops 15032385536 | bytes 75161928 | tf_op jit(solution)/shard_map/memory_back/pallas_call | solution.py:416
  581.7 4.7 shard_map.504
  586.4 1.4 slice.275.refs_7_
  587.8 1.3 constant_dynamic-slice_fusion.8.refs_6_
  589.2 1.2 multiply_reduce_fusion.refs_8_.refs_4_
  590.4 36.7 %feed_sum.1 = (f32[2,128,1024]{2,1,0:T(8,128)}, bf16[3,32,1024]{2,1,0:T(8,128)(2,1)}, bf16[3,32,1024]{2,1,0:T(8,128)(2,1)}, bf16[3,128,256]{2,1,0:T(8,128)(2,1)}...) custom-call(bf16[2,128,4096]{2,1,0:T(8,128)(2,1)} %bitcast.234, ...), custom_call_target="tpu_custom_call" | custom-call | flops 4194304 | bytes 20971 | tf_op jit(solution)/shard_map/feed_sum/pallas_call | solution.py:416
  627.1 0.9 reduce_sum.339
  631.7 3.6 shard_map.505
  635.4 1.8 fusion.48
  637.1 0.9 slice_bitcast_fusion
  638.0 1.0 copy.216
  639.0 9.6 %convert_bitcast_fusion = f32[32,100,1024]{2,0,1:T(8,128)} fusion(bf16[100,32,1024]{2,1,0:T(8,128)(2,1)} %get-tuple-element.173), kind=kLoop, calls=%fused_computation.1 | loop fusion | flops 3276800 | bytes 19660800 | tf_op jit(solution)/shard_map/convert_element_type | solution.py:508
  (293 shorter events, 35.0 us)
Async XLA Ops:
  7.2 2.9 copy-start.24
  7.2 3.1 copy-start.63
  7.2 3.2 copy-start.58
  7.2 3.2 copy-start.57
  7.3 3.2 copy-start.56
  7.3 3.2 copy-start.44
  7.3 3.2 copy-start.55
  7.3 3.2 copy-start.54
  7.3 3.2 copy-start.53
  7.3 3.2 copy-start.47
  7.3 3.2 copy-start.52
  7.3 3.2 copy-start.51
  7.3 3.2 copy-start.50
  7.3 3.2 copy-start.48
  7.4 3.2 copy-start.49
  7.4 53.9 %copy-start.45 = (s32[4,32]{1,0:T(4,128)S(1)}, s32[4,32]{1,0:T(4,128)}, u32[]{:S(2)}) copy-start(s32[4,32]{1,0:T(4,128)} %param.31) | copy-start | bytes 1540
  7.4 54.5 %copy-start.46 = (f32[4,8]{1,0:T(4,128)S(1)}, f32[4,8]{1,0:T(4,128)}, u32[]{:S(2)}) copy-start(f32[4,8]{1,0:T(4,128)} %param.32) | copy-start | bytes 388
  7.4 55.1 %copy-start.30 = (bf16[128,256]{1,0:T(8,128)(2,1)S(1)}, bf16[128,256]{1,0:T(8,128)(2,1)}, u32[]{:S(2)}) copy-start(bf16[128,256]{1,0:T(8,128)(2,1)} %param.37) | copy-start | bytes 196612
  7.4 55.1 %copy-start.31 = (bf16[128,256]{1,0:T(8,128)(2,1)S(1)}, bf16[128,256]{1,0:T(8,128)(2,1)}, u32[]{:S(2)}) copy-start(bf16[128,256]{1,0:T(8,128)(2,1)} %param.36) | copy-start | bytes 196612
  7.4 55.1 %copy-start.32 = (bf16[128,256]{1,0:T(8,128)(2,1)S(1)}, bf16[128,256]{1,0:T(8,128)(2,1)}, u32[]{:S(2)}) copy-start(bf16[128,256]{1,0:T(8,128)(2,1)} %param.35) | copy-start | bytes 196612
  7.4 55.8 %copy-start.26 = (bf16[128,1024]{1,0:T(8,128)(2,1)S(1)}, bf16[128,1024]{1,0:T(8,128)(2,1)}, u32[]{:S(2)}) copy-start(bf16[128,1024]{1,0:T(8,128)(2,1)} %param.53) | copy-start | bytes 786436
  7.4 117.2 %all-gather.7.cloned.1.call-start = ((), (), s32[]{:S(2)}) async-start(), calls=%async_computation.2 | async-start | bytes 11796480 | tf_op jit(solution)/shard_map/all_gather | solution.py:1742
  10.1 221.7 %all-gather.9.cloned.1.call-start = ((), (), s32[]{:S(2)}) async-start(), calls=%async_computation.3 | async-start | bytes 18874368 | tf_op jit(solution)/shard_map/all_gather | solution.py:1745
  124.6 5.2 copy-start.28
  124.6 7.5 %copy-start.20 = (bf16[8,256,128]{2,1,0:T(8,128)(2,1)S(1)}, bf16[8,256,128]{2,1,0:T(8,128)(2,1)}, u32[]{:S(2)}) copy-start(bf16[8,256,128]{2,1,0:T(8,128)(2,1)} %get-tuple-element.113) | copy-start | bytes 1572868
  124.6 7.7 %copy-start.5 = (bf16[8,128,768]{2,1,0:T(8,128)(2,1)S(1)}, bf16[8,128,768]{2,1,0:T(8,128)(2,1)}, u32[]{:S(2)}) copy-start(bf16[8,128,768]{2,1,0:T(8,128)(2,1)} %get-tuple-element.112) | copy-start | bytes 4718596
  124.6 7.7 %copy-start.6 = (bf16[8,32,1024]{2,1,0:T(8,128)(2,1)S(1)}, bf16[8,32,1024]{2,1,0:T(8,128)(2,1)}, u32[]{:S(2)}) copy-start(bf16[8,32,1024]{2,1,0:T(8,128)(2,1)} %get-tuple-element.111) | copy-start | bytes 1572868
  124.7 123.8 %all-gather.11.cloned.1.call-start = ((), (), s32[]{:S(2)}) async-start(), calls=%async_computation.4 | async-start | bytes 2949120 | tf_op jit(solution)/shard_map/all_gather | solution.py:1746
  126.6 395.1 %reduce-scatter.2.cloned.1.call-start = ((), (), s32[]{:S(2)}) async-start(), calls=%async_computation.1 | async-start | bytes 18874368 | tf_op jit(solution)/shard_map/reduce_scatter | solution.py:1846
  132.3 2.6 copy-start.9
  134.0 1.9 copy-start.40
  134.8 32.2 %copy-start.13 = (bf16[256,256]{1,0:T(8,128)(2,1)}, bf16[256,256]{1,0:T(8,128)(2,1)S(1)}, u32[]{:S(2)}) copy-start(bf16[256,256]{1,0:T(8,128)(2,1)S(1)} %reshape.537.ctx_ref) | copy-start | bytes 393220
  214.6 2.5 copy-start.25
  214.6 3.3 copy-start.29
  214.6 3.7 copy-start.39
  223.2 2.7 copy-start.12
  225.2 2.4 copy-start
  225.9 3.4 copy-start.1
  231.8 13.7 %copy-start.36 = (f32[8,1,1,128]{3,2,1,0:T(1,128)S(1)}, f32[8,1,1,128]{3,2,1,0:T(1,128)}, u32[]{:S(2)}) copy-start(f32[8,1,1,128]{3,2,1,0:T(1,128)} %get-tuple-element.393) | copy-start | bytes 12292
  245.5 1.9 copy-start.35
  405.4 60.9 %copy-start.11 = (bf16[1024,1024]{1,0:T(8,128)(2,1)S(1)}, bf16[1024,1024]{1,0:T(8,128)(2,1)}, u32[]{:S(2)}) copy-start(bf16[1024,1024]{1,0:T(8,128)(2,1)} %get-tuple-element.140) | copy-start | bytes 6291460
  405.4 60.9 %copy-start.17 = (f32[64,1024]{1,0:T(8,128)S(1)}, f32[64,1024]{1,0:T(8,128)}, u32[]{:S(2)}) copy-start(f32[64,1024]{1,0:T(8,128)} %get-tuple-element.141) | copy-start | bytes 786436
  466.2 2.8 copy-start.10
  466.3 2.8 copy-start.27
  515.6 3.2 copy-start.43
  515.6 3.2 copy-start.42
  581.7 7.4 %copy-start.22 = (bf16[3,2,32,1024]{3,2,1,0:T(8,128)(2,1)S(1)}, bf16[3,2,32,1024]{3,2,1,0:T(8,128)(2,1)}, u32[]{:S(2)}) copy-start(bf16[3,2,32,1024]{3,2,1,0:T(8,128)(2,1)} %get-tuple-element.160) | copy-start | bytes 1179652
  631.7 5.4 copy-start.18
  (21 other events, 29.8 us)
Sparse Core Ops, SparseCore 0:
  10.7 93.3 all-gather.6
  124.8 90.2 all-gather.8
  216.9 30.1 all-gather.10
  394.5 121.4 reduce-scatter.1
